TPU v7x, 32 devices: a whole 2x2x4 slice. The times are simulated.
32 devices in a mesh: seq: 8 (over z, y), tensor: 4 (over x, core).
Axes of the slice: x: 2, y: 2, z: 4, core: 2. Of those that a mesh axis runs over, the one named last changes fastest.
Arguments:
- block_input: bfloat16 [4096, 2048], P(('seq', 'tensor')), may hold values from -6 to 6
- lengths: int32 [4], replicated, may hold values from 1 to 3840, as said below
- norm1_gain: float32 [2048], replicated, may hold values from 0.5 to 1.5
- q_down: bfloat16 [2048, 1024], replicated, may hold values from -0.125 to 0.125
- q_gain: float32 [1024], replicated, may hold values from 0.5 to 1.5
- q_up: bfloat16 [1024, 4096], P(None, 'tensor'), may hold values from -0.25 to 0.25
- kv_weight: bfloat16 [2048, 512], replicated, may hold values from -0.125 to 0.125
- out_weight: bfloat16 [4096, 2048], P('tensor'), may hold values from -0.5 to 0.5
- norm2_gain: float32 [2048], replicated, may hold values from 0.5 to 1.5
- gate_weight: bfloat16 [2048, 5632], P(None, 'tensor'), may hold values from -0.125 to 0.125
- up_weight: bfloat16 [2048, 5632], P(None, 'tensor'), may hold values from -0.125 to 0.125
- down_weight: bfloat16 [5632, 2048], P('tensor'), may hold values from -0.078125 to 0.078125
- cotangent: bfloat16 [4096, 2048], P(('seq', 'tensor')), may hold values from -6 to 6
Outputs:
- block_output: bfloat16 [4096, 2048], P(('seq', 'tensor'))
- input_grad: float32 [4096, 2048], P(('seq', 'tensor'))
- norm1_gain_grad: float32 [2048], P(('seq', 'tensor'))
- q_down_grad: float32 [2048, 1024], P(('seq', 'tensor'))
- q_gain_grad: float32 [1024], P(('seq', 'tensor'))
- q_up_grad: float32 [1024, 4096], P('seq', 'tensor')
- kv_weight_grad: float32 [2048, 512], P(('seq', 'tensor'))
- out_weight_grad: float32 [4096, 2048], P('tensor', 'seq')
- norm2_gain_grad: float32 [2048], P(('seq', 'tensor'))
- gate_grad: float32 [2048, 5632], P('seq', 'tensor')
- up_grad: float32 [2048, 5632], P('seq', 'tensor')
- down_grad: float32 [5632, 2048], P('tensor', 'seq')
Inputs may be any that keep to these rules, and one draw needn't show every extreme that they name: `lengths`: 4 sequences packed in token order, summing to 4096; one of them, at a place that differs from draw to draw, has exactly 3840 tokens, so that it starts on the first index of seq and ends on the last; the other three together have 512 // 2 tokens.
All inputs are finite; a program needn't handle non-finite values.
Results may differ from a plain program's by a relative error of at most 0.02.
Values may be sent and summed in bfloat16 or wider, within the bound.
No kernel may reach another device: no remote copies, remote signals or barrier semaphores. Data moves between devices by JAX's collectives and lax.ppermute only.
A program may use at most 320 MiB of HBM per device.

v0:
```python
import math

import jax
import jax.numpy as jnp
from jax import lax
from jax.sharding import PartitionSpec as P

HD = 256
KEY_BLOCK = 512


EPS = 1e-06
NEG = -1e30


def locate(token_index, lengths):
    starts = jnp.cumsum(lengths) - lengths
    segment = jnp.sum((token_index[:, None] >= starts[None, 1:]).astype(jnp.int32), axis=1)
    picked = segment[:, None] == jnp.arange(lengths.shape[0], dtype=jnp.int32)[None, :]
    offset = jnp.sum(jnp.where(picked, starts[None, :], 0), axis=1)
    return (segment, offset, (token_index - offset).astype(jnp.float32))


def angles(position):
    halfway = HD // 2
    freq = 10000.0 ** (-(2.0 * jnp.arange(halfway, dtype=jnp.float32)) / HD)
    theta = position[:, None] * freq[None, :]
    return (jnp.cos(theta), jnp.sin(theta))


def rotate(values, cos_table, sin_table):
    halfway = values.shape[-1] // 2
    former = values[..., :halfway]
    latter = values[..., halfway:]
    cos_wide = cos_table[:, None, :]
    sin_wide = sin_table[:, None, :]
    return jnp.concatenate(
        [former * cos_wide - latter * sin_wide, latter * cos_wide + former * sin_wide], axis=-1
    )


def rms_parts(values):
    inverse = lax.rsqrt(jnp.mean(values * values, axis=-1, keepdims=True) + EPS)
    return (values * inverse, inverse)


def rms_back(grad_out, scaled, inverse, gain):
    inner = grad_out * gain
    gain_term = jnp.sum(grad_out * scaled, axis=0)
    grad_in = inverse * (inner - scaled * jnp.mean(inner * scaled, axis=-1, keepdims=True))
    return (grad_in, gain_term)


def contract_first(left, right):
    return lax.dot_general(
        left, right, (((0,), (0,)), ((), ())), preferred_element_type=jnp.float32
    )


def contract_last(left, right):
    return lax.dot_general(
        left, right, (((1,), (1,)), ((), ())), preferred_element_type=jnp.float32
    )


def flatten_heads(values, heads_dev):
    token_count = values.shape[0]
    return (
        values.reshape(token_count, heads_dev, HD)
        .transpose(1, 0, 2)
        .reshape(heads_dev * token_count, HD)
    )


def unflatten_heads(values, heads_dev):
    token_count = values.shape[0] // heads_dev
    return (
        values.reshape(heads_dev, token_count, HD)
        .transpose(1, 0, 2)
        .reshape(token_count, heads_dev * HD)
    )


def fetch_keys(keyval):
    return lax.all_gather(keyval, ("seq", "tensor"), axis=0, tiled=True)


def tile_scores(
    query_flat, key_rows, all_segment, row_index, row_segment, tile_number, score_scale
):
    start_key = tile_number * KEY_BLOCK
    tile_rows = lax.dynamic_slice_in_dim(key_rows, start_key, KEY_BLOCK, 0)
    tile_segment = lax.dynamic_slice_in_dim(all_segment, start_key, KEY_BLOCK, 0)
    tile_index = start_key + jnp.arange(KEY_BLOCK, dtype=jnp.int32)
    logits = contract_last(query_flat, tile_rows[:, :HD]) * score_scale
    allowed = (tile_index[None, :] <= row_index[:, None]) & (
        tile_segment[None, :] == row_segment[:, None]
    )
    return (tile_rows, logits, allowed)


def body(
    block_input,
    lengths,
    norm1_gain,
    q_down,
    q_gain,
    q_up,
    kv_weight,
    out_weight,
    norm2_gain,
    gate_weight,
    up_weight,
    down_weight,
    cotangent,
):
    tensor_count = lax.axis_size("tensor")
    seq_count = lax.axis_size("seq")
    own_rows = block_input.shape[0]
    tok_rows = own_rows * tensor_count
    heads_dev = q_up.shape[1] // HD
    total_tokens = tok_rows * seq_count
    first_query = lax.axis_index("seq") * tok_rows
    first_own = first_query + lax.axis_index("tensor") * own_rows
    score_scale = 1.0 / math.sqrt(HD)
    all_index = jnp.arange(total_tokens, dtype=jnp.int32)
    all_segment, all_offset, all_position = locate(all_index, lengths)
    query_index = first_query + jnp.arange(tok_rows, dtype=jnp.int32)
    query_segment = lax.dynamic_slice_in_dim(all_segment, first_query, tok_rows, 0)
    query_offset = lax.dynamic_slice_in_dim(all_offset, first_query, tok_rows, 0)
    query_cos, query_sin = angles(lax.dynamic_slice_in_dim(all_position, first_query, tok_rows, 0))
    own_cos, own_sin = angles(lax.dynamic_slice_in_dim(all_position, first_own, own_rows, 0))
    row_index = jnp.tile(query_index, heads_dev)
    row_segment = jnp.tile(query_segment, heads_dev)
    tile_low = query_offset[0] // KEY_BLOCK
    tile_high = (first_query + tok_rows - 1) // KEY_BLOCK + 1
    inputs = block_input.astype(jnp.float32)
    scaled_one, inverse_one = rms_parts(inputs)
    normed = (scaled_one * norm1_gain).astype(jnp.bfloat16)
    compressed = jnp.dot(normed, q_down, preferred_element_type=jnp.float32)
    scaled_q, inverse_q = rms_parts(compressed)
    latent = (scaled_q * q_gain).astype(jnp.bfloat16)
    kv_raw = jnp.dot(normed, kv_weight, preferred_element_type=jnp.float32)
    rotated = rotate(kv_raw[:, None, :HD], own_cos, own_sin)[:, 0]
    keyval = jnp.concatenate([rotated, kv_raw[:, HD:]], axis=1).astype(jnp.bfloat16)
    key_rows = fetch_keys(keyval)
    latent_all = lax.all_gather(latent, "tensor", axis=0, tiled=True)
    query_raw = jnp.dot(latent_all, q_up, preferred_element_type=jnp.float32)
    query = (
        rotate(query_raw.reshape(tok_rows, heads_dev, HD), query_cos, query_sin)
        .reshape(tok_rows, heads_dev * HD)
        .astype(jnp.bfloat16)
    )
    query_flat = flatten_heads(query, heads_dev)
    flat_rows = query_flat.shape[0]

    def stat_step(tile_number, carried):
        row_top, row_total = carried
        tile_rows, logits, allowed = tile_scores(
            query_flat, key_rows, all_segment, row_index, row_segment, tile_number, score_scale
        )
        masked = jnp.where(allowed, logits, NEG)
        new_top = jnp.maximum(row_top, jnp.max(masked, axis=1))
        added = jnp.sum(jnp.where(allowed, jnp.exp(masked - new_top[:, None]), 0.0), axis=1)
        return (new_top, row_total * jnp.exp(row_top - new_top) + added)

    row_top, row_total = lax.fori_loop(
        tile_low,
        tile_high,
        stat_step,
        (jnp.full((flat_rows,), NEG, jnp.float32), jnp.zeros((flat_rows,), jnp.float32)),
    )
    log_total = row_top + jnp.log(row_total)

    def value_step(tile_number, running):
        tile_rows, logits, allowed = tile_scores(
            query_flat, key_rows, all_segment, row_index, row_segment, tile_number, score_scale
        )
        probability = jnp.where(allowed, jnp.exp(logits - log_total[:, None]), 0.0).astype(
            jnp.bfloat16
        )
        return running + jnp.dot(probability, tile_rows[:, HD:], preferred_element_type=jnp.float32)

    attended_flat = lax.fori_loop(
        tile_low, tile_high, value_step, jnp.zeros((flat_rows, HD), jnp.float32)
    )
    attended_low = unflatten_heads(attended_flat, heads_dev).astype(jnp.bfloat16)
    branch = lax.psum_scatter(
        jnp.dot(attended_low, out_weight, preferred_element_type=jnp.float32).astype(jnp.bfloat16),
        "tensor",
        scatter_dimension=0,
        tiled=True,
    ).astype(jnp.float32)
    residual = inputs + branch
    scaled_two, inverse_two = rms_parts(residual)
    normed_two = (scaled_two * norm2_gain).astype(jnp.bfloat16)
    normed_all = lax.all_gather(normed_two, "tensor", axis=0, tiled=True)
    gate_pre = jnp.dot(normed_all, gate_weight, preferred_element_type=jnp.float32)
    up_pre = jnp.dot(normed_all, up_weight, preferred_element_type=jnp.float32)
    sigmoid_gate = jax.nn.sigmoid(gate_pre)
    silu_gate = gate_pre * sigmoid_gate
    hidden = (silu_gate * up_pre).astype(jnp.bfloat16)
    feed_out = lax.psum_scatter(
        jnp.dot(hidden, down_weight, preferred_element_type=jnp.float32).astype(jnp.bfloat16),
        "tensor",
        scatter_dimension=0,
        tiled=True,
    ).astype(jnp.float32)
    block_output = (residual + feed_out).astype(jnp.bfloat16)
    grad_all = lax.all_gather(cotangent, "tensor", axis=0, tiled=True)
    down_grad = contract_first(hidden, grad_all)
    grad_hidden = contract_last(grad_all, down_weight)
    grad_gate = (
        grad_hidden * up_pre * sigmoid_gate * (1.0 + gate_pre * (1.0 - sigmoid_gate))
    ).astype(jnp.bfloat16)
    grad_up = (grad_hidden * silu_gate).astype(jnp.bfloat16)
    gate_grad = contract_first(normed_all, grad_gate)
    up_grad = contract_first(normed_all, grad_up)
    grad_normed_two = lax.psum_scatter(
        (contract_last(grad_gate, gate_weight) + contract_last(grad_up, up_weight)).astype(
            jnp.bfloat16
        ),
        "tensor",
        scatter_dimension=0,
        tiled=True,
    ).astype(jnp.float32)
    grad_in_two, gain_two_part = rms_back(grad_normed_two, scaled_two, inverse_two, norm2_gain)
    grad_residual = cotangent.astype(jnp.float32) + grad_in_two
    grad_branch = grad_residual.astype(jnp.bfloat16)
    grad_branch_all = lax.all_gather(grad_branch, "tensor", axis=0, tiled=True)
    out_weight_grad = contract_first(attended_low, grad_branch_all)
    grad_attended = contract_last(grad_branch_all, out_weight).astype(jnp.bfloat16)
    grad_flat = flatten_heads(grad_attended, heads_dev)
    row_delta = jnp.sum(grad_flat.astype(jnp.float32) * attended_flat, axis=1)

    def grad_step(tile_number, carried):
        grad_query_acc, grad_kv_acc = carried
        tile_rows, logits, allowed = tile_scores(
            query_flat, key_rows, all_segment, row_index, row_segment, tile_number, score_scale
        )
        probability = jnp.where(allowed, jnp.exp(logits - log_total[:, None]), 0.0)
        grad_probability = contract_last(grad_flat, tile_rows[:, HD:])
        grad_logits = (probability * (grad_probability - row_delta[:, None])).astype(jnp.bfloat16)
        grad_query_acc = (
            grad_query_acc
            + jnp.dot(grad_logits, tile_rows[:, :HD], preferred_element_type=jnp.float32)
            * score_scale
        )
        grad_keys = contract_first(grad_logits, query_flat) * score_scale
        grad_values = contract_first(probability.astype(jnp.bfloat16), grad_flat)
        start_key = tile_number * KEY_BLOCK
        previous = lax.dynamic_slice_in_dim(grad_kv_acc, start_key, KEY_BLOCK, 0)
        updated = previous + jnp.concatenate([grad_keys, grad_values], axis=1)
        return (grad_query_acc, lax.dynamic_update_slice_in_dim(grad_kv_acc, updated, start_key, 0))

    grad_query_flat, grad_kv_partial = lax.fori_loop(
        tile_low,
        tile_high,
        grad_step,
        (jnp.zeros((flat_rows, HD), jnp.float32), jnp.zeros((total_tokens, 2 * HD), jnp.float32)),
    )
    grad_kv_own = lax.psum_scatter(
        grad_kv_partial, ("seq", "tensor"), scatter_dimension=0, tiled=True
    )
    grad_key_raw = rotate(grad_kv_own[:, None, :HD], own_cos, -own_sin)[:, 0]
    grad_kv_raw = jnp.concatenate([grad_key_raw, grad_kv_own[:, HD:]], axis=1).astype(jnp.bfloat16)
    grad_query = unflatten_heads(grad_query_flat, heads_dev).reshape(tok_rows, heads_dev, HD)
    grad_query_raw = (
        rotate(grad_query, query_cos, -query_sin)
        .reshape(tok_rows, heads_dev * HD)
        .astype(jnp.bfloat16)
    )
    q_up_grad = contract_first(latent_all, grad_query_raw)
    q_up_grad, out_weight_grad, gate_grad, up_grad, down_grad = (
        lax.psum_scatter(
            q_up_grad.astype(jnp.bfloat16), "seq", scatter_dimension=0, tiled=True
        ).astype(jnp.float32),
        lax.psum_scatter(
            out_weight_grad.astype(jnp.bfloat16), "seq", scatter_dimension=1, tiled=True
        ).astype(jnp.float32),
        lax.psum_scatter(
            gate_grad.astype(jnp.bfloat16), "seq", scatter_dimension=0, tiled=True
        ).astype(jnp.float32),
        lax.psum_scatter(
            up_grad.astype(jnp.bfloat16), "seq", scatter_dimension=0, tiled=True
        ).astype(jnp.float32),
        lax.psum_scatter(
            down_grad.astype(jnp.bfloat16), "seq", scatter_dimension=1, tiled=True
        ).astype(jnp.float32),
    )
    grad_latent = lax.psum_scatter(
        contract_last(grad_query_raw, q_up).astype(jnp.bfloat16),
        "tensor",
        scatter_dimension=0,
        tiled=True,
    ).astype(jnp.float32)
    grad_compressed_full, gain_q_part = rms_back(grad_latent, scaled_q, inverse_q, q_gain)
    grad_compressed = grad_compressed_full.astype(jnp.bfloat16)
    q_down_part = contract_first(normed, grad_compressed)
    kv_weight_part = contract_first(normed, grad_kv_raw)
    grad_normed = contract_last(grad_compressed, q_down) + contract_last(grad_kv_raw, kv_weight)
    grad_in_one, gain_one_part = rms_back(grad_normed, scaled_one, inverse_one, norm1_gain)
    input_grad = grad_residual + grad_in_one
    q_down_grad, kv_weight_grad, norm1_gain_grad, q_gain_grad, norm2_gain_grad = (
        lax.psum_scatter(q_down_part, ("seq", "tensor"), scatter_dimension=0, tiled=True),
        lax.psum_scatter(kv_weight_part, ("seq", "tensor"), scatter_dimension=0, tiled=True),
        lax.psum_scatter(gain_one_part, ("seq", "tensor"), scatter_dimension=0, tiled=True),
        lax.psum_scatter(gain_q_part, ("seq", "tensor"), scatter_dimension=0, tiled=True),
        lax.psum_scatter(gain_two_part, ("seq", "tensor"), scatter_dimension=0, tiled=True),
    )
    return (
        block_output,
        input_grad,
        norm1_gain_grad,
        q_down_grad,
        q_gain_grad,
        q_up_grad,
        kv_weight_grad,
        out_weight_grad,
        norm2_gain_grad,
        gate_grad,
        up_grad,
        down_grad,
    )


def solution(mesh):
    placed = (
        P(("seq", "tensor"), None),
        P(),
        P(),
        P(),
        P(),
        P(None, "tensor"),
        P(),
        P("tensor", None),
        P(),
        P(None, "tensor"),
        P(None, "tensor"),
        P("tensor", None),
        P(("seq", "tensor"), None),
    )
    return jax.shard_map(
        body,
        mesh=mesh,
        in_specs=placed,
        out_specs=(
            P(("seq", "tensor"), None),
            P(("seq", "tensor"), None),
            P(("seq", "tensor")),
            P(("seq", "tensor"), None),
            P(("seq", "tensor")),
            P("seq", "tensor"),
            P(("seq", "tensor"), None),
            P("tensor", "seq"),
            P(("seq", "tensor")),
            P("seq", "tensor"),
            P("seq", "tensor"),
            P("tensor", "seq"),
        ),
        check_vma=False,
    )
```

profile of v0, /device:TPU:0, one launch (start us, length us, event | category | flops | bytes accessed | tf_op | source)
XLA Modules:
  0.0 1565.9 jit_solution(11041303233923354387)
XLA Ops:
  8.7 3.3 multiply_reduce_fusion.2
  13.9 2.1 fusion.85
  22.6 10.6 all-gather.8.cloned.1.call-done
  33.1 3.8 fusion.87
  37.0 3.3 reshape.336
  40.3 2.1 subtract_convert_fusion.1
  44.0 54.6 %all-gather.6.cloned.1.call-done = bf16[4096,512]{1,0:T(8,128)(2,1)} async-done(((bf16[128,512]{1,0:T(8,128)(2,1)}), bf16[4096,512]{1,0:T(8,128)(2,1)}) %all-gather.6.cloned.1.call-update) | async-done | bytes 4194320 | tf_op jit(solution)/shard_map/all_gather | solution.py:85
  98.7 4.7 while.37
  98.8 2.5 fusion.155
  101.2 2.0 select_reduce_fusion.3
  104.9 5.7 while.38
  105.0 5.5 convolution_add_fusion.3
  110.6 2.7 convert_element_type.133
  113.2 2.3 copy.44
  115.5 6.3 convolution_convert_fusion.4
  121.9 101.9 %reduce-scatter.13.cloned.1.call-done = bf16[128,2048]{1,0:T(8,128)(2,1)} async-done(((bf16[512,2048]{1,0:T(8,128)(2,1)}), bf16[128,2048]{1,0:T(8,128)(2,1)}) %reduce-scatter.13.cloned.1.call-update) | async-done | bytes 524304 | tf_op jit(solution)/shard_map/reduce_scatter | solution.py:188
  225.0 2.0 multiply_convert_fusion.3
  227.7 22.1 %all-gather.10.cloned.1.call-done = bf16[512,2048]{1,0:T(8,128)(2,1)} async-done(((bf16[128,2048]{1,0:T(8,128)(2,1)}), bf16[512,2048]{1,0:T(8,128)(2,1)}) %all-gather.10.cloned.1.call-update) | async-done | bytes 2097168 | tf_op jit(solution)/shard_map/all_gather | solution.py:197
  249.8 8.5 fusion.89
  258.3 8.0 fusion.88
  266.3 7.6 all-gather.12.cloned.1.call-done
  273.9 10.4 multiply_convert_fusion
  284.3 6.5 fusion.90
  290.9 7.3 add_convert_fusion
  298.3 31.5 %reduce-scatter.17.cloned.1.call-done = bf16[128,2048]{1,0:T(8,128)(2,1)} async-done(((bf16[512,2048]{1,0:T(8,128)(2,1)}), bf16[128,2048]{1,0:T(8,128)(2,1)}) %reduce-scatter.17.cloned.1.call-update) | async-done | bytes 524304 | tf_op jit(solution)/shard_map/reduce_scatter | solution.py:219
  329.8 2.1 fusion.43
  332.0 2.4 fusion.79
  334.7 22.5 %all-gather.14.cloned.1.call-done = bf16[512,2048]{1,0:T(8,128)(2,1)} async-done(((bf16[128,2048]{1,0:T(8,128)(2,1)}), bf16[512,2048]{1,0:T(8,128)(2,1)}) %all-gather.14.cloned.1.call-update) | async-done | bytes 2097168 | tf_op jit(solution)/shard_map/all_gather | solution.py:230
  357.2 5.2 convolution_convert_fusion.8
  367.8 4.3 broadcast_in_dim.46.clone
  372.1 22.6 %while.39 = (s32[]{:T(128)}, f32[2048,256]{1,0:T(8,128)}, f32[4096,512]{1,0:T(8,128)}, s32[]{:T(128)}, s32[4096]{0:T(1024)S(1)}, /*index=5*/bf16[4096,512]{1,0:T...) while((s32[]{:T(128)}, f32[2048,256]{1,0:T(8,128)}, ...), condition=%wide.region_18.19_spmd.clone, body=%wide.region_17.18_spmd.clone.sunk | while | flops 2696544768 | bytes 61700452 | solution.py:256
  372.2 2.3 constant_dynamic-slice_fusion.2
  374.4 2.6 copy.84
  377.0 2.7 bitcast_select_fusion.4
  380.5 1.8 fusion.169
  386.1 2.6 copy.85
  388.7 4.5 fusion.170
  394.7 3.0 copy.69
  400.0 2.3 convolution_convert_fusion.7
  403.7 7.3 convolution_convert_fusion
  412.4 7.5 convolution_convert_fusion.1
  421.2 7.6 convolution_convert_fusion.2
  428.9 4.2 convolution_convert_fusion.6
  433.2 6.0 convolution_convert_fusion.3
  439.3 7.9 convolution_convert_fusion.5
  447.3 135.3 %reduce-scatter.19.cloned.1.call-done = bf16[128,1024]{1,0:T(8,128)(2,1)} async-done(((bf16[512,1024]{1,0:T(8,128)(2,1)}), bf16[128,1024]{1,0:T(8,128)(2,1)}) %reduce-scatter.19.cloned.1.call-update) | async-done | bytes 262160 | tf_op jit(solution)/shard_map/reduce_scatter | solution.py:291
  585.5 4.6 fusion.81
  590.5 143.2 %reduce-scatter.21.cloned.1.call-done = f32[128,512]{1,0:T(8,128)} async-done(((f32[4096,512]{1,0:T(8,128)}), f32[128,512]{1,0:T(8,128)}) %reduce-scatter.21.cloned.1.call-update) | async-done | bytes 262160 | tf_op jit(solution)/shard_map/reduce_scatter | solution.py:262
  735.9 2.8 fusion.67
  738.8 4.9 fusion.91
  743.7 100.2 %reduce-scatter.35.cloned.1.call-done = bf16[1408,256]{1,0:T(8,128)(2,1)} async-done(((bf16[1408,2048]{1,0:T(8,128)(2,1)}), bf16[1408,256]{1,0:T(8,128)(2,1)}) %reduce-scatter.35.cloned.1.call-update) | async-done | bytes 720912 | tf_op jit(solution)/shard_map/reduce_scatter | solution.py:287
  843.9 2.3 convert_element_type.165
  846.2 111.6 %reduce-scatter.33.cloned.1.call-done = bf16[256,1408]{1,0:T(8,128)(2,1)} async-done(((bf16[2048,1408]{1,0:T(8,128)(2,1)}), bf16[256,1408]{1,0:T(8,128)(2,1)}) %reduce-scatter.33.cloned.1.call-update) | async-done | bytes 720912 | tf_op jit(solution)/shard_map/reduce_scatter | solution.py:284
  957.8 2.3 convert_element_type.163
  960.1 111.4 %reduce-scatter.31.cloned.1.call-done = bf16[256,1408]{1,0:T(8,128)(2,1)} async-done(((bf16[2048,1408]{1,0:T(8,128)(2,1)}), bf16[256,1408]{1,0:T(8,128)(2,1)}) %reduce-scatter.31.cloned.1.call-update) | async-done | bytes 720912 | tf_op jit(solution)/shard_map/reduce_scatter | solution.py:281
  1071.5 2.3 convert_element_type.161
  1073.8 69.1 %reduce-scatter.25.cloned.1.call-done = bf16[128,1024]{1,0:T(8,128)(2,1)} async-done(((bf16[1024,1024]{1,0:T(8,128)(2,1)}), bf16[128,1024]{1,0:T(8,128)(2,1)}) %reduce-scatter.25.cloned.1.call-update) | async-done | bytes 262160 | tf_op jit(solution)/shard_map/reduce_scatter | solution.py:275
  1144.8 89.5 %reduce-scatter.29.cloned.1.call-done = bf16[1024,256]{1,0:T(8,128)(2,1)} async-done(((bf16[1024,2048]{1,0:T(8,128)(2,1)}), bf16[1024,256]{1,0:T(8,128)(2,1)}) %reduce-scatter.29.cloned.1.call-update) | async-done | bytes 524304 | tf_op jit(solution)/shard_map/reduce_scatter | solution.py:278
  1234.3 2.1 convert_element_type.159
  1236.4 3.7 fusion.49
  1240.1 40.5 %all-reduce.3 = (f32[2048]{0:T(1024)S(1)}, f32[1024]{0:T(1024)S(1)}, f32[2048]{0:T(1024)S(1)}) all-reduce(f32[2048]{0:T(1024)S(1)} %get-tuple-element.258, f32[1024]{0:T(1024)S(1)} %copy-done.27, f32[2048]{0:T(1024)S(1)} %copy-done.22), channel_id=7, replica_groups=mesh['seq'=8,'tensor'=4] {'seq','tensor'}, use_global_device_ids=true, to_apply=%region_24.25.clone | all-reduce | flops 5120 | bytes 40960
  1282.4 3.6 fusion.48
  1286.0 133.3 %reduce-scatter.23.cloned.1.call-done = f32[64,1024]{1,0:T(8,128)} async-done(((f32[2048,1024]{1,0:T(8,128)}), f32[64,1024]{1,0:T(8,128)}) %reduce-scatter.23.cloned.1.call-update) | async-done | bytes 262160 | tf_op jit(solution)/shard_map/reduce_scatter | solution.py:305
  1419.4 139.8 %reduce-scatter.27.cloned.1.call-done = f32[64,512]{1,0:T(8,128)} async-done(((f32[2048,512]{1,0:T(8,128)}), f32[64,512]{1,0:T(8,128)}) %reduce-scatter.27.cloned.1.call-update) | async-done | bytes 131088 | tf_op jit(solution)/shard_map/reduce_scatter | solution.py:306
  (198 shorter events, 39.7 us)
Async XLA Ops:
  7.2 26.0 %copy-start = (bf16[1024,1024]{1,0:T(8,128)(2,1)S(1)}, bf16[1024,1024]{1,0:T(8,128)(2,1)}, u32[]{:S(2)}) copy-start(bf16[1024,1024]{1,0:T(8,128)(2,1)} %param.24) | copy-start | bytes 6291460
  7.2 5.5 copy-start.20
  7.2 25.9 %all-gather.8.cloned.1.call-start = ((), (), s32[]{:S(2)}) async-start(), calls=%async_computation.13 | async-start | bytes 1310720 | tf_op jit(solution)/shard_map/all_gather | solution.py:147
  8.6 5.3 copy-start.23
  8.6 5.0 copy-start.39
  8.6 5.3 copy-start.4
  8.7 5.2 copy-start.17
  11.9 0.8 copy-start.9
  12.0 1.9 copy-start.30
  13.6 85.1 %all-gather.6.cloned.1.call-start = ((), (), s32[]{:S(2)}) async-start(), calls=%async_computation.12 | async-start | bytes 4325376 | tf_op jit(solution)/shard_map/all_gather | solution.py:85
  16.3 4.5 copy-start.34
  16.3 20.6 %copy-start.32 = (f32[128]{0:T(128)}, f32[128]{0:T(128)S(1)}, u32[]{:S(2)}) copy-start(f32[128]{0:T(128)S(1)} %multiply_power_fusion) | copy-start | bytes 1540
  17.4 206.3 %reduce-scatter.13.cloned.1.call-start = ((), (), s32[]{:S(2)}) async-start(), calls=%async_computation.14 | async-start | bytes 2621440 | tf_op jit(solution)/shard_map/reduce_scatter | solution.py:188
  22.6 17.7 %copy-start.11 = (f32[512,128]{1,0:T(8,128)}, f32[512,128]{1,0:T(8,128)S(1)}, u32[]{:S(2)}) copy-start(f32[512,128]{1,0:T(8,128)S(1)} %get-tuple-element.348) | copy-start | bytes 786436
  121.8 103.2 %copy-start.19 = (f32[2048]{0:T(1024)S(1)}, f32[2048]{0:T(1024)}, u32[]{:S(2)}) copy-start(f32[2048]{0:T(1024)} %param.27) | copy-start | bytes 24580
  121.8 128.0 %all-gather.10.cloned.1.call-start = ((), (), s32[]{:S(2)}) async-start(), calls=%async_computation.15 | async-start | bytes 2621440 | tf_op jit(solution)/shard_map/all_gather | solution.py:197
  225.0 106.9 %copy-start.28 = (f32[128]{0:T(128)}, f32[128]{0:T(128)S(1)}, u32[]{:S(2)}) copy-start(f32[128]{0:T(128)S(1)} %add_rsqrt_fusion) | copy-start | bytes 1540
  227.1 46.8 %all-gather.12.cloned.1.call-start = ((), (), s32[]{:S(2)}) async-start(), calls=%async_computation.17 | async-start | bytes 2621440 | tf_op jit(solution)/shard_map/all_gather | solution.py:210
  227.7 102.1 %reduce-scatter.17.cloned.1.call-start = ((), (), s32[]{:S(2)}) async-start(), calls=%async_computation.18 | async-start | bytes 2621440 | tf_op jit(solution)/shard_map/reduce_scatter | solution.py:219
  249.8 8.5 copy-start.38
  284.3 6.5 copy-start.41
  284.3 6.5 copy-start.43
  290.9 39.0 %copy-start.7 = (bf16[128,2048]{1,0:T(8,128)(2,1)S(1)}, bf16[128,2048]{1,0:T(8,128)(2,1)}, u32[]{:S(2)}) copy-start(bf16[128,2048]{1,0:T(8,128)(2,1)} %reduce-scatter.13.cloned.1.call-done) | copy-start | bytes 1572868
  298.2 59.0 %all-gather.14.cloned.1.call-start = ((), (), s32[]{:S(2)}) async-start(), calls=%async_computation.19 | async-start | bytes 2621440 | tf_op jit(solution)/shard_map/all_gather | solution.py:230
  332.0 30.4 %copy-start.36 = (f32[128]{0:T(128)}, f32[128]{0:T(128)S(1)}, u32[]{:S(2)}) copy-start(f32[128]{0:T(128)S(1)} %broadcast_multiply_fusion.2) | copy-start | bytes 1540
  334.4 248.1 %reduce-scatter.19.cloned.1.call-start = ((), (), s32[]{:S(2)}) async-start(), calls=%async_computation.20 | async-start | bytes 1310720 | tf_op jit(solution)/shard_map/reduce_scatter | solution.py:291
  364.0 1.9 copy-start.6
  380.5 3.2 copy-start.14
  382.3 1.4 copy-start.1
  383.7 1.2 copy-start.2
  388.7 4.5 copy-start.3
  394.7 3.0 copy-start.12
  394.7 3.0 copy-start.13
  399.1 1.0 copy-start.16
  402.3 331.4 %reduce-scatter.21.cloned.1.call-start = ((), (), s32[]{:S(2)}) async-start(), calls=%async_computation.21 | async-start | bytes 8650752 | tf_op jit(solution)/shard_map/reduce_scatter | solution.py:262
  402.4 1.4 copy-start.40
  403.0 440.9 %reduce-scatter.35.cloned.1.call-start = ((), (), s32[]{:S(2)}) async-start(), calls=%async_computation.28 | async-start | bytes 6488064 | tf_op jit(solution)/shard_map/reduce_scatter | solution.py:287
  411.0 1.4 copy-start.44
  411.0 546.8 %reduce-scatter.33.cloned.1.call-start = ((), (), s32[]{:S(2)}) async-start(), calls=%async_computation.27 | async-start | bytes 6488064 | tf_op jit(solution)/shard_map/reduce_scatter | solution.py:284
  419.9 1.4 copy-start.42
  419.9 651.6 %reduce-scatter.31.cloned.1.call-start = ((), (), s32[]{:S(2)}) async-start(), calls=%async_computation.26 | async-start | bytes 6488064 | tf_op jit(solution)/shard_map/reduce_scatter | solution.py:281
  428.9 4.4 copy-start.15
  428.9 714.1 %reduce-scatter.25.cloned.1.call-start = ((), (), s32[]{:S(2)}) async-start(), calls=%async_computation.23 | async-start | bytes 2359296 | tf_op jit(solution)/shard_map/reduce_scatter | solution.py:275
  433.2 801.2 %reduce-scatter.29.cloned.1.call-start = ((), (), s32[]{:S(2)}) async-start(), calls=%async_computation.25 | async-start | bytes 4718592 | tf_op jit(solution)/shard_map/reduce_scatter | solution.py:278
  439.3 143.3 %copy-start.10 = (f32[128,1024]{1,0:T(8,128)S(1)}, f32[128,1024]{1,0:T(8,128)}, u32[]{:S(2)}) copy-start(f32[128,1024]{1,0:T(8,128)} %copy-done.9) | copy-start | bytes 1572868
  439.3 143.3 %copy-start.21 = (f32[1024]{0:T(1024)S(1)}, f32[1024]{0:T(1024)}, u32[]{:S(2)}) copy-start(f32[1024]{0:T(1024)} %param.23) | copy-start | bytes 12292
  439.3 143.3 %copy-start.31 = (f32[128]{0:T(128)S(1)}, f32[128]{0:T(128)}, u32[]{:S(2)}) copy-start(f32[128]{0:T(128)} %copy-done.30) | copy-start | bytes 1540
  439.3 843.1 %reduce-scatter.15.cloned.1.call-start = ((), (), s32[]{:S(2)}) async-start(), calls=%async_computation.16 | async-start | bytes 2621440 | tf_op jit(solution)/shard_map/reduce_scatter | solution.py:203
  447.2 138.3 %copy-start.5 = (bf16[128,2048]{1,0:T(8,128)(2,1)S(1)}, bf16[128,2048]{1,0:T(8,128)(2,1)}, u32[]{:S(2)}) copy-start(bf16[128,2048]{1,0:T(8,128)(2,1)} %param.19) | copy-start | bytes 1572868
  447.2 138.3 %copy-start.18 = (f32[2048]{0:T(1024)S(1)}, f32[2048]{0:T(1024)}, u32[]{:S(2)}) copy-start(f32[2048]{0:T(1024)} %param.21) | copy-start | bytes 24580
  447.2 138.3 %copy-start.24 = (f32[128]{0:T(128)S(1)}, f32[128]{0:T(128)}, u32[]{:S(2)}) copy-start(f32[128]{0:T(128)} %copy-done.23) | copy-start | bytes 1540
  447.3 972.1 %reduce-scatter.23.cloned.1.call-start = ((), (), s32[]{:S(2)}) async-start(), calls=%async_computation.22 | async-start | bytes 8650752 | tf_op jit(solution)/shard_map/reduce_scatter | solution.py:305
  590.2 145.4 %copy-start.33 = (f32[128]{0:T(128)S(1)}, f32[128]{0:T(128)}, u32[]{:S(2)}) copy-start(f32[128]{0:T(128)} %copy-done.32) | copy-start | bytes 1540
  590.2 145.4 %copy-start.35 = (f32[128]{0:T(128)S(1)}, f32[128]{0:T(128)}, u32[]{:S(2)}) copy-start(f32[128]{0:T(128)} %copy-done.34) | copy-start | bytes 1540
  590.2 145.7 %copy-start.25 = (f32[128]{0:T(128)S(1)}, f32[128]{0:T(128)}, u32[]{:S(2)}) copy-start(f32[128]{0:T(128)} %copy-done.23) | copy-start | bytes 1540
  590.2 969.0 %reduce-scatter.27.cloned.1.call-start = ((), (), s32[]{:S(2)}) async-start(), calls=%async_computation.24 | async-start | bytes 4325376 | tf_op jit(solution)/shard_map/reduce_scatter | solution.py:306
  846.2 390.2 %copy-start.26 = (f32[128]{0:T(128)S(1)}, f32[128]{0:T(128)}, u32[]{:S(2)}) copy-start(f32[128]{0:T(128)} %copy-done.23) | copy-start | bytes 1540
  1144.8 95.3 %copy-start.22 = (f32[2048]{0:T(1024)S(1)}, f32[2048]{0:T(1024)}, u32[]{:S(2)}) copy-start(f32[2048]{0:T(1024)} %get-tuple-element.256) | copy-start | bytes 24580
  1144.8 95.3 %copy-start.27 = (f32[1024]{0:T(1024)S(1)}, f32[1024]{0:T(1024)}, u32[]{:S(2)}) copy-start(f32[1024]{0:T(1024)} %get-tuple-element.260) | copy-start | bytes 12292
  1144.8 137.6 %copy-start.8 = (bf16[128,2048]{1,0:T(8,128)(2,1)S(1)}, bf16[128,2048]{1,0:T(8,128)(2,1)}, u32[]{:S(2)}) copy-start(bf16[128,2048]{1,0:T(8,128)(2,1)} %reduce-scatter.13.cloned.1.call-done) | copy-start | bytes 1572868
  1144.8 137.6 %copy-start.29 = (f32[128]{0:T(128)S(1)}, f32[128]{0:T(128)}, u32[]{:S(2)}) copy-start(f32[128]{0:T(128)} %copy-done.28) | copy-start | bytes 1540
  1144.8 137.6 %copy-start.37 = (f32[128]{0:T(128)S(1)}, f32[128]{0:T(128)}, u32[]{:S(2)}) copy-start(f32[128]{0:T(128)} %copy-done.36) | copy-start | bytes 1540
Sparse Core Ops, SparseCore 0:
  13.7 19.4 all-gather.7
  36.6 62.0 all-gather.5
  121.9 101.7 reduce-scatter.12
  227.2 22.5 all-gather.9
  251.3 22.5 all-gather.11
  298.4 31.4 reduce-scatter.16
  334.6 22.5 all-gather.13
  402.4 180.1 reduce-scatter.18
  585.0 148.6 reduce-scatter.20
  737.7 106.1 reduce-scatter.34
  848.0 109.7 reduce-scatter.32
  961.8 109.7 reduce-scatter.30
  1075.5 67.4 reduce-scatter.24
  1146.9 87.3 reduce-scatter.28
  1236.7 31.2 reduce-scatter.14
  1270.9 148.4 reduce-scatter.22
  1422.2 136.9 reduce-scatter.26
where the time goes:
time: 1580 us; the launch traced here: 1570 us
  waiting for transfers between devices  1290 us (82%)
  matrix products  139 us (9%)
  other arithmetic  41 us (3%)
  local copies, waits for them, and re-layouts  40.7 us (3%)
  blocking collectives  40.5 us (3%)
  between operations  17.3 us (1%)
    reduce_scatter x1, waiting for transfers between devices, body(): lax.psum_scatter(grad_kv_partial, ('seq', 'tensor'), scatter_dimension=0,...  143 us
    reduce_scatter x1, waiting for transfers between devices, body(): lax.psum_scatter(kv_weight_part, ('seq', 'tensor'), scatter_dimension=0,...  140 us
    reduce_scatter x1, waiting for transfers between devices, body(): lax.psum_scatter(contract_last(grad_query_raw, q_up).astype(jnp.bfloat16)...  135 us
    reduce_scatter x1, waiting for transfers between devices, body(): lax.psum_scatter(q_down_part, ('seq', 'tensor'), scatter_dimension=0, til...  133 us
    reduce_scatter x1, waiting for transfers between devices, body(): lax.psum_scatter(up_grad.astype(jnp.bfloat16), 'seq', scatter_dimension=0...  112 us
    reduce_scatter x1, waiting for transfers between devices, body(): lax.psum_scatter(gate_grad.astype(jnp.bfloat16), 'seq', scatter_dimension...  111 us
    reduce_scatter x1, waiting for transfers between devices, body(): lax.psum_scatter(jnp.dot(attended_low, out_weight, preferred_element_type...  102 us
    reduce_scatter x1, waiting for transfers between devices, body(): lax.psum_scatter(down_grad.astype(jnp.bfloat16), 'seq', scatter_dimension...  100 us
  transfers between devices with their start and end apart: 17, of which 16 were waited for; matrix products, arithmetic and copies ran while one was open for 7% of the time, Pallas kernels for 0%

commit v1 on v0

v1 whole, which is shorter than its diff:
```python
import functools
import math

import jax
import jax.numpy as jnp
from jax import lax
from jax.experimental import pallas as pl
from jax.experimental.pallas import tpu as pltpu
from jax.sharding import PartitionSpec as P

HD = 256
EPS = 1e-06
NEG = -1e30
F32 = jnp.float32
BF16 = jnp.bfloat16
LOG2_SCALE = math.log2(math.e) / math.sqrt(HD)
SCALE = 1.0 / math.sqrt(HD)
MIB = 1 << 20
BRIEF = pl.CostEstimate(flops=1000, bytes_accessed=1000, transcendentals=0)

NN = (((1,), (0,)), ((), ()))
NT = (((1,), (1,)), ((), ()))
TN = (((0,), (0,)), ((), ()))


def dot(left, right, dims=NN):
    return lax.dot_general(left, right, dims, preferred_element_type=F32)


def first_of_segment(token, starts):
    found = jnp.zeros_like(token)
    for start in starts:
        found = jnp.maximum(found, jnp.where(token >= start, start, 0))
    return found


def angles(position):
    halfway = HD // 2
    freq = 10000.0 ** (-(2.0 * jnp.arange(halfway, dtype=F32)) / HD)
    theta = position[:, None] * freq[None, :]
    return jnp.cos(theta), jnp.sin(theta)


def at_index(values, index, axis, keepdims=True):
    start = [jnp.int32(0)] * values.ndim
    start[axis] = index
    size = values.shape[:axis] + (1,) + values.shape[axis + 1 :]
    taken = lax.dynamic_slice(values, start, size, allow_negative_indices=False)
    return taken if keepdims else lax.squeeze(taken, [axis])


def rms_parts(values):
    inverse = lax.rsqrt(jnp.mean(values * values, axis=-1, keepdims=True) + EPS)
    return values * inverse, inverse


def rms_back(grad_out, scaled, inverse, gain):
    inner = grad_out * gain
    return inverse * (inner - scaled * jnp.mean(inner * scaled, axis=-1, keepdims=True))


def key_bias(meta, slot, qi_ref, ql_ref, keys, rows):
    block = keys // 4
    row = lax.broadcasted_iota(jnp.int32, (keys, rows), 0)
    which = row // block
    other = ((which & 1) << 1) | (which >> 1)
    token = meta[0, slot] + (meta[2, 0] ^ other) * block + (row & (block - 1))
    allowed = (token <= qi_ref[0:1, :]) & (token >= ql_ref[0:1, :])
    return jnp.where(allowed, 0.0, NEG)


def fwd_kernel(heads, first, last, slot, meta, q_ref, a_ref, b_ref, qi_ref, ql_ref, *refs):
    if not first:
        held, refs = refs[:3], refs[3:]
    if last:
        o_ref, ot_ref, lse_ref, m_s, l_s, acc_s, bias_s = refs
    else:
        m_s, l_s, acc_s, bias_s = refs
    step = pl.program_id(0)
    slot = slot + step

    @pl.when(step == 0)
    def _():
        if first:
            m_s[...] = jnp.full_like(m_s, NEG)
            l_s[...] = jnp.zeros_like(l_s)
            acc_s[...] = jnp.zeros_like(acc_s)
        else:
            m_s[...] = held[0][...]
            l_s[...] = held[1][...]
            acc_s[...] = held[2][...]

    def tile(masked):
        key = jnp.concatenate([a_ref[0, :, :HD], b_ref[0, :, :HD]], axis=0)
        value = jnp.concatenate([a_ref[0, :, HD:], b_ref[0, :, HD:]], axis=0)
        value_t = value.T
        if masked:
            bias_s[...] = key_bias(meta, slot, qi_ref, ql_ref, *bias_s.shape)

        def score(h):
            return dot(key, q_ref[:, h * HD : (h + 1) * HD], NT)

        following = score(0)
        for h in range(heads):
            scores = following * LOG2_SCALE
            if h + 1 < heads:
                following = score(h + 1)
            if masked:
                scores = scores + bias_s[...]
            old = m_s[h, 0:1, :]
            new = jnp.maximum(old, jnp.max(scores, axis=0, keepdims=True))
            alpha = jnp.exp2(old - new)
            weight = jnp.exp2(scores - new)
            l_s[h, 0:1, :] = l_s[h, 0:1, :] * alpha + jnp.sum(weight, axis=0, keepdims=True)
            m_s[h, 0:1, :] = new
            acc_s[h] = acc_s[h] * alpha + dot(value_t, weight.astype(BF16))

    pl.when(meta[1, slot] == 1)(lambda: tile(False))
    pl.when(meta[1, slot] == 2)(lambda: tile(True))

    if last:

        @pl.when(step == pl.num_programs(0) - 1)
        def _():
            for h in range(heads):
                total = l_s[h, 0:1, :]
                out_t = (acc_s[h] / total).astype(BF16)
                ot_ref[h * HD : (h + 1) * HD, :] = out_t
                o_ref[:, h * HD : (h + 1) * HD] = out_t.T
                lse_ref[h] = jnp.broadcast_to(m_s[h, 0:1, :] + jnp.log2(total), lse_ref.shape[1:])


def attend(meta, slot, query, kv_a, kv_b, q_index, q_low, held, last):
    rows, width = query.shape
    heads = width // HD
    slots, half, wide = kv_a.shape
    keys = 2 * half
    whole = lambda *shape: pl.BlockSpec(shape, lambda i, m: (0,) * len(shape))
    tile = pl.BlockSpec((1, half, wide), lambda i, m: (i, 0, 0))
    state = [(heads, 8, rows), (heads, 8, rows), (heads, HD, rows)]
    bias = pltpu.VMEM((keys, rows), F32)
    if last:
        out = [((rows, width), BF16), ((width, rows), BF16), ((heads, 8, rows), F32)]
        scratch = [pltpu.VMEM(shape, F32) for shape in state] + [bias]
    else:
        out = [(shape, F32) for shape in state]
        scratch = [bias]
    return pl.pallas_call(
        functools.partial(fwd_kernel, heads, not held, last, slot),
        grid_spec=pltpu.PrefetchScalarGridSpec(
            num_scalar_prefetch=1,
            grid=(slots,),
            in_specs=[whole(rows, width), tile, tile, whole(8, rows), whole(8, rows)]
            + [whole(*shape) for shape in state if held],
            out_specs=[whole(*shape) for shape, _ in out],
            scratch_shapes=scratch,
        ),
        out_shape=[jax.ShapeDtypeStruct(*o) for o in out],
        compiler_params=pltpu.CompilerParams(vmem_limit_bytes=24 * MIB),
        cost_estimate=BRIEF,
        name="attend",
    )(meta, query, kv_a, kv_b, q_index, q_low, *held)


def bwd_kernel(heads, meta, q_ref, do_ref, a_ref, b_ref, qi_ref, ql_ref, lse_ref, delta_ref, cos_ref, sin_ref,
               dq_ref, da_ref, db_ref, dq_s, dk_s, dv_s, bias_s):
    slot = pl.program_id(0)
    half = a_ref.shape[1]

    @pl.when(slot == 0)
    def _():
        dq_s[...] = jnp.zeros_like(dq_s)

    @pl.when(meta[1, slot] == 0)
    def _():
        da_ref[...] = jnp.zeros_like(da_ref)
        db_ref[...] = jnp.zeros_like(db_ref)

    def tile(masked):
        key = jnp.concatenate([a_ref[0, :, :HD], b_ref[0, :, :HD]], axis=0)
        value = jnp.concatenate([a_ref[0, :, HD:], b_ref[0, :, HD:]], axis=0)
        key_t = key.T
        if masked:
            bias_s[...] = key_bias(meta, slot, qi_ref, ql_ref, *bias_s.shape)
        for h in range(heads):
            at = slice(h * HD, (h + 1) * HD)
            scores = dot(key, q_ref[:, at], NT) * LOG2_SCALE
            if masked:
                scores = scores + bias_s[...]
            weight = jnp.exp2(scores - lse_ref[h, 0:1, :])
            grad = dot(value, do_ref[:, at], NT)
            ds = (weight * (grad - delta_ref[h, 0:1, :])).astype(BF16)
            dv = dot(weight.astype(BF16), do_ref[:, at])
            dk = dot(ds, q_ref[:, at])
            if h == 0:
                dv_s[...] = dv
                dk_s[...] = dk
            else:
                dv_s[...] += dv
                dk_s[...] += dk
            dq_s[h] += dot(key_t, ds)
        da_ref[0, :, :HD] = (dk_s[:half, :] * SCALE).astype(BF16)
        db_ref[0, :, :HD] = (dk_s[half:, :] * SCALE).astype(BF16)
        da_ref[0, :, HD:] = dv_s[:half, :].astype(BF16)
        db_ref[0, :, HD:] = dv_s[half:, :].astype(BF16)

    pl.when(meta[1, slot] == 1)(lambda: tile(False))
    pl.when(meta[1, slot] == 2)(lambda: tile(True))

    @pl.when(slot == pl.num_programs(0) - 1)
    def _():
        cos, sin = cos_ref[...], sin_ref[...]
        mid = HD // 2
        for h in range(heads):
            grad = (dq_s[h] * SCALE).T
            former, latter = grad[:, :mid], grad[:, mid:]
            dq_ref[:, h * HD : h * HD + mid] = (former * cos + latter * sin).astype(BF16)
            dq_ref[:, h * HD + mid : (h + 1) * HD] = (latter * cos - former * sin).astype(BF16)


def attend_back(meta, query, grad, kv_a, kv_b, q_index, q_low, lse, delta, cos, sin):
    rows, width = query.shape
    heads = width // HD
    slots, half, wide = kv_a.shape
    keys = 2 * half
    whole = lambda *shape: pl.BlockSpec(shape, lambda i, m: (0,) * len(shape))
    tile = pl.BlockSpec((1, half, wide), lambda i, m: (i, 0, 0))
    out_tile = pl.BlockSpec((1, half, wide), lambda i, m: (m[3, i], 0, 0))
    return pl.pallas_call(
        functools.partial(bwd_kernel, heads),
        grid_spec=pltpu.PrefetchScalarGridSpec(
            num_scalar_prefetch=1,
            grid=(slots,),
            in_specs=[
                whole(rows, width), whole(rows, width), tile, tile, whole(8, rows), whole(8, rows),
                whole(heads, 8, rows), whole(heads, 8, rows), whole(rows, HD // 2), whole(rows, HD // 2),
            ],
            out_specs=[whole(rows, width), out_tile, out_tile],
            scratch_shapes=[
                pltpu.VMEM((heads, HD, rows), F32),
                pltpu.VMEM((keys, HD), F32),
                pltpu.VMEM((keys, HD), F32),
                pltpu.VMEM((keys, rows), F32),
            ],
        ),
        out_shape=[
            jax.ShapeDtypeStruct((rows, width), BF16),
            jax.ShapeDtypeStruct((slots, half, wide), BF16),
            jax.ShapeDtypeStruct((slots, half, wide), BF16),
        ],
        compiler_params=pltpu.CompilerParams(vmem_limit_bytes=32 * MIB),
        cost_estimate=BRIEF,
        name="attend_back",
    )(meta, query, grad, kv_a, kv_b, q_index, q_low, lse, delta, cos, sin)


def attended_grad_kernel(gb_ref, w_ref, att_ref, out_ref, delta_ref):
    grad = dot(gb_ref[...], w_ref[...], NT).astype(BF16)
    out_ref[...] = grad
    term = grad.astype(F32) * att_ref[...].astype(F32)
    delta_ref[0] = jnp.broadcast_to(jnp.sum(term.T, axis=0, keepdims=True), delta_ref.shape[1:])


def attended_grad(grad_branch, weight, attended):
    rows, depth = grad_branch.shape
    width = weight.shape[0]
    return pl.pallas_call(
        attended_grad_kernel,
        grid=(width // HD,),
        in_specs=[
            pl.BlockSpec((rows, depth), lambda i: (0, 0)),
            pl.BlockSpec((HD, depth), lambda i: (i, 0)),
            pl.BlockSpec((rows, HD), lambda i: (0, i)),
        ],
        out_specs=[pl.BlockSpec((rows, HD), lambda i: (0, i)), pl.BlockSpec((1, 8, rows), lambda i: (i, 0, 0))],
        out_shape=[
            jax.ShapeDtypeStruct((rows, width), BF16),
            jax.ShapeDtypeStruct((width // HD, 8, rows), F32),
        ],
        compiler_params=pltpu.CompilerParams(vmem_limit_bytes=12 * MIB),
        cost_estimate=BRIEF,
        name="attended_grad",
    )(grad_branch, weight, attended)


def product(lefts, rights, dims):
    cut = lefts[0].shape[0] // 2
    keep = sum(dot(left[:cut], right, dims) for left, right in zip(lefts, rights))
    send = sum(dot(left[cut:], right, dims) for left, right in zip(lefts, rights))
    return keep.astype(BF16), send.astype(BF16)


def project_kernel(x_ref, w_ref, cos_ref, sin_ref, out_ref):
    raw = dot(x_ref[...], w_ref[...])
    cos, sin = cos_ref[...], sin_ref[...]
    mid = HD // 2
    former, latter = raw[:, :mid], raw[:, mid:]
    out_ref[:, :mid] = (former * cos - latter * sin).astype(BF16)
    out_ref[:, mid:] = (latter * cos + former * sin).astype(BF16)


def project_rotate(latent, weight, cos, sin):
    rows, rank = latent.shape
    width = weight.shape[1]
    whole = lambda *shape: pl.BlockSpec(shape, lambda i: (0,) * len(shape))
    return pl.pallas_call(
        project_kernel,
        grid=(width // HD,),
        in_specs=[
            whole(rows, rank),
            pl.BlockSpec((rank, HD), lambda i: (0, i)),
            whole(rows, HD // 2),
            whole(rows, HD // 2),
        ],
        out_specs=pl.BlockSpec((rows, HD), lambda i: (0, i)),
        out_shape=jax.ShapeDtypeStruct((rows, width), BF16),
        compiler_params=pltpu.CompilerParams(vmem_limit_bytes=10 * MIB),
        cost_estimate=BRIEF,
        name="project_rotate",
    )(latent, weight, cos, sin)


def hidden_kernel(x_ref, gate_ref, up_ref, gh_ref, hidden_ref, hidden_t_ref, gg_ref, gu_ref, gate_s, up_s):
    step = pl.program_id(0)
    gate = dot(x_ref[...], gate_ref[...])
    up = dot(x_ref[...], up_ref[...])

    @pl.when(step == 0)
    def _():
        gate_s[...] = gate
        up_s[...] = up

    @pl.when(step > 0)
    def _():
        gate_s[...] += gate
        up_s[...] += up

    @pl.when(step == pl.num_programs(0) - 1)
    def _():
        for first in range(0, gate_s.shape[0], 128):
            at = slice(first, first + 128)
            gate_pre, up_pre, grad = gate_s[at, :], up_s[at, :], gh_ref[at, :]
            sigmoid = jax.nn.sigmoid(gate_pre)
            silu = gate_pre * sigmoid
            hidden = (silu * up_pre).astype(BF16)
            hidden_ref[at, :] = hidden
            hidden_t_ref[:, at] = hidden.T
            gg_ref[at, :] = (grad * up_pre * sigmoid * (1.0 + gate_pre * (1.0 - sigmoid))).astype(BF16)
            gu_ref[at, :] = (grad * silu).astype(BF16)


def hidden_units(normed, gate_weight, up_weight, grad_hidden):
    rows, depth = normed.shape
    units = gate_weight.shape[1]
    cut = 512
    whole = lambda *shape: pl.BlockSpec(shape, lambda i: (0,) * len(shape))
    weight = pl.BlockSpec((cut, units), lambda i: (i, 0))
    plain = jax.ShapeDtypeStruct((rows, units), BF16)
    return pl.pallas_call(
        hidden_kernel,
        grid=(depth // cut,),
        in_specs=[pl.BlockSpec((rows, cut), lambda i: (0, i)), weight, weight, whole(rows, units)],
        out_specs=[whole(rows, units), whole(units, rows), whole(rows, units), whole(rows, units)],
        out_shape=[plain, jax.ShapeDtypeStruct((units, rows), BF16), plain, plain],
        scratch_shapes=[pltpu.VMEM((rows, units), F32), pltpu.VMEM((rows, units), F32)],
        compiler_params=pltpu.CompilerParams(vmem_limit_bytes=36 * MIB),
        cost_estimate=BRIEF,
        name="hidden_units",
    )(normed, gate_weight, up_weight, grad_hidden)


def in_order(values, owner, axis):
    return jnp.stack(
        [at_index(values, owner[j], axis, keepdims=False) for j in range(owner.shape[0])]
    )


def rows_kernel(owner, left_ref, *refs):
    count = len(refs) // 2
    left = left_ref[...]
    for right_ref, out_ref in zip(refs[:count], refs[count:]):
        out_ref[0] = dot(left, right_ref[...], TN).astype(BF16)


def grad_by_rows(owner, left, rights, count):
    slots = owner.shape[0]
    rows, width = left.shape
    cut = width // count
    if cut % 128:
        return [in_order(dot(left, r, TN).astype(BF16).reshape(count, cut, -1), owner, 0) for r in rights]
    return pl.pallas_call(
        rows_kernel,
        grid_spec=pltpu.PrefetchScalarGridSpec(
            num_scalar_prefetch=1,
            grid=(slots,),
            in_specs=[pl.BlockSpec((rows, cut), lambda i, o: (0, o[i]))]
            + [pl.BlockSpec(r.shape, lambda i, o: (0, 0)) for r in rights],
            out_specs=[pl.BlockSpec((1, cut, r.shape[1]), lambda i, o: (i, 0, 0)) for r in rights],
        ),
        out_shape=[jax.ShapeDtypeStruct((slots, cut, r.shape[1]), BF16) for r in rights],
        compiler_params=pltpu.CompilerParams(vmem_limit_bytes=16 * MIB),
        cost_estimate=BRIEF,
        name="grad_by_rows",
    )(owner, left, *rights)


def columns_kernel(owner, left_ref, right_ref, out_ref):
    out_ref[0] = dot(left_ref[...], right_ref[...]).astype(BF16)


def grad_by_columns(owner, left_t, right, count):
    slots = owner.shape[0]
    rows, width = right.shape
    cut = width // count
    tall = left_t.shape[0]
    if cut % 128:
        return in_order(dot(left_t, right).astype(BF16).reshape(tall, count, cut), owner, 1)
    return pl.pallas_call(
        columns_kernel,
        grid_spec=pltpu.PrefetchScalarGridSpec(
            num_scalar_prefetch=1,
            grid=(slots,),
            in_specs=[
                pl.BlockSpec((tall, rows), lambda i, o: (0, 0)),
                pl.BlockSpec((rows, cut), lambda i, o: (0, o[i])),
            ],
            out_specs=pl.BlockSpec((1, tall, cut), lambda i, o: (i, 0, 0)),
        ),
        out_shape=jax.ShapeDtypeStruct((slots, tall, cut), BF16),
        compiler_params=pltpu.CompilerParams(vmem_limit_bytes=16 * MIB),
        cost_estimate=BRIEF,
        name="grad_by_columns",
    )(owner, left_t, right)


def add(*parts):
    total = parts[0].astype(F32)
    for part in parts[1:]:
        total = total + part.astype(F32)
    return total


def near(values):
    return lax.ppermute(values, "tensor", [(i, i ^ 1) for i in range(4)])


def far(values):
    return lax.ppermute(values, "tensor", [(i, i ^ 2) for i in range(4)])


def ring_order(count):
    return list(range(0, count, 2)) + list(range(count - 1, 0, -2))


def ring_shift(values, step, count):
    order = ring_order(count)
    return lax.ppermute(
        values, "seq", [(order[i], order[(i + step) % count]) for i in range(count)]
    )


def seq_at(place, count):
    return jnp.where(place < count // 2, 2 * place, 2 * (count - 1 - place) + 1)


def swap_seq(values, bit, count):
    return lax.ppermute(values, "seq", [(i, i ^ bit) for i in range(count)])


def bits_of(count, first=1):
    bits = [1 << i for i in range(count.bit_length() - 1)]
    return [first] + [b for b in bits if b != first]


def apart_of(bits):
    apart = [0]
    for bit in reversed(bits):
        apart = apart + [bit | a for a in apart]
    return apart


class Order:
    def __init__(self):
        self.last = ()

    def after(self, *values):
        held = lax.optimization_barrier((values, self.last))[0]
        return held if len(values) > 1 else held[0]

    def ran(self, *values):
        self.last = values

    def wait(self, *values):
        self.last = self.last + values


class Halving:
    def __init__(self, order, bits, count, send, *keep):
        self.order, self.bits, self.count = order, list(bits), count
        self.terms = list(keep)
        self.moving = swap_seq(send, self.bits.pop(0), count)

    def keep(self, *values):
        self.terms += values

    def hop(self, go=True):
        arrived = self.order.after(self.moving)
        self.terms.append(arrived)
        cut = arrived.shape[0] // 2
        send = add(*[t[cut:] for t in self.terms]).astype(BF16)
        self.terms = [t[:cut] for t in self.terms]
        self.order.ran(send)
        self.send = send
        if go:
            self.moving = swap_seq(send, self.bits.pop(0), self.count)

    def go(self):
        self.moving = swap_seq(self.order.after(self.send), self.bits.pop(0), self.count)

    def finish(self):
        while self.bits:
            self.hop()
        arrived = self.order.after(self.moving)
        total = add(*[t[0] for t in self.terms], arrived[0])
        self.order.ran(total)
        return total


def swap(values):
    cut = values.shape[0] // 2
    return jnp.concatenate([values[cut:], values[:cut]], axis=0)


def body(
    block_input, lengths, norm1_gain, q_down, q_gain, q_up, kv_weight, out_weight, norm2_gain,
    gate_weight, up_weight, down_weight, cotangent,
):
    group = lax.axis_size("tensor")
    count = lax.axis_size("seq")
    mine = lax.axis_index("tensor").astype(jnp.int32)
    seq = lax.axis_index("seq").astype(jnp.int32)
    own = block_input.shape[0]
    rows = own * group
    heads = q_up.shape[1] // HD
    place = jnp.where((seq & 1) == 0, seq >> 1, count - 1 - (seq >> 1))

    starts = [jnp.int32(0)]
    for i in range(lengths.shape[0] - 1):
        starts.append(starts[-1] + lengths[i])
    blocks = mine ^ jnp.array([0, 2, 1, 3], jnp.int32)
    token = (seq * rows + blocks[:, None] * own + jnp.arange(own, dtype=jnp.int32)[None, :]).reshape(rows)
    low = first_of_segment(token, starts)
    cos_own, sin_own = angles((token - low)[:own].astype(F32))
    offsets = [0]
    for step in range(1, count // 2):
        offsets += [-step, step]
    offsets.append(count // 2)
    slot_seq = seq_at((place + jnp.array(offsets, jnp.int32)) & (count - 1), count)
    ends = first_of_segment(jnp.stack([seq * rows, seq * rows + rows - 1]), starts)
    base = slot_seq * rows
    needed = (slot_seq <= seq) & (slot_seq >= lax.div(ends[0], jnp.int32(rows)))
    bounded = (slot_seq == seq) | (base < ends[1])
    bits, bits_two = bits_of(count), bits_of(count, 2)
    apart = slot_seq ^ seq
    slot_out = sum(((apart >> (bit.bit_length() - 1)) & 1) << (len(bits) - 1 - i) for i, bit in enumerate(bits))
    meta = jnp.stack([base, needed * (1 + bounded), jnp.full((count,), mine), slot_out]).astype(jnp.int32)
    q_index = jnp.broadcast_to(token[None, :], (8, rows))
    q_low = jnp.broadcast_to(low[None, :], (8, rows))
    owner = seq ^ jnp.array(apart_of(bits), jnp.int32)
    owner_two = seq ^ jnp.array(apart_of(bits_two), jnp.int32)

    order = Order()
    half = count // 2

    inputs = block_input.astype(F32)
    scaled_one, inverse_one = rms_parts(inputs)
    normed = (scaled_one * norm1_gain).astype(BF16)
    kv_raw = dot(normed, kv_weight)
    mid = HD // 2
    former, latter = kv_raw[:, :mid], kv_raw[:, mid:HD]
    keyval = jnp.concatenate(
        [
            former * cos_own - latter * sin_own,
            latter * cos_own + former * sin_own,
            kv_raw[:, HD:],
        ],
        axis=1,
    ).astype(BF16)
    order.ran(keyval)
    keyval_far = far(keyval)
    compressed = dot(order.after(normed), q_down)
    latent = (rms_parts(compressed)[0] * q_gain).astype(BF16)
    order.ran(latent)
    latent_far = far(latent)
    pair = jnp.concatenate([keyval, order.after(keyval_far)], axis=0)
    order.ran(pair)
    ahead, back = ring_shift(pair, 1, count), ring_shift(pair, -1, count)
    pair_near = near(pair)
    cos, sin = angles((order.after(token) - low).astype(F32))
    order.ran(cos, sin)
    latent_half = jnp.concatenate([latent, order.after(latent_far)], axis=0)
    order.ran(latent_half)
    latent_near = near(latent_half)
    input_far = far(order.after(block_input))
    grad_far = far(order.after(cotangent))
    kv_a = jnp.zeros((count,) + pair.shape, BF16)
    kv_b = jnp.zeros((count,) + pair.shape, BF16)

    def put(kept, piece, slot):
        return lax.dynamic_update_slice(kept, piece, (slot, 0, 0))

    kv_a, kv_b = put(kv_a, pair[None], 0), put(kv_b, order.after(pair_near)[None], 0)
    for step in range(1, half + 1):
        ahead, back = order.after(ahead, back)
        slot = 2 * step - 1
        if step < half:
            piece = jnp.stack([ahead, back])
            order.ran(ahead, back)
            if step < half - 1:
                ahead, back = ring_shift(ahead, 1, count), ring_shift(back, -1, count)
            else:
                ahead, back = ring_shift(ahead[:own], 1, count), ring_shift(back[own:], -1, count)
        else:
            piece = jnp.concatenate([ahead, back], axis=0)[None]
        piece_near = near(order.after(piece))
        kv_a = put(kv_a, piece, slot)
        if step == 1:
            latent_all = jnp.concatenate([latent_half, order.after(latent_near)], axis=0)
            query = project_rotate(latent_all, q_up, cos, sin)
            order.ran(query)
        if step == half - 1:
            input_half = jnp.concatenate([block_input, order.after(input_far)], axis=0)
            order.ran(input_half)
        if step == half:
            grad_half = jnp.concatenate([cotangent, order.after(grad_far)], axis=0)
            order.ran(grad_half)
            grad_near = near(grad_half)
        kv_b = put(kv_b, order.after(piece_near), slot)
    kv_a, kv_b = order.after(kv_a, kv_b)
    attended, attended_t, lse = attend(meta, 0, order.after(query), kv_a, kv_b, q_index, q_low, (), True)
    order.ran(attended)

    def sum_half(lefts, rights, dims, meanwhile):
        lefts[0] = order.after(lefts[0])
        keep, send = product(lefts, rights, dims)
        order.ran(send)
        chip = add(keep, order.after(near(send))).astype(BF16)
        order.ran(chip)
        moving = far(swap(chip))
        made = meanwhile()
        return add(chip, order.after(moving)), made

    share = q_down.shape[0] // (count * group)

    def before_residual():
        normed_half = (rms_parts(order.after(input_half).astype(F32))[0] * norm1_gain).astype(BF16)
        scaled_q, inverse_q = rms_parts(dot(normed_half, q_down))
        order.ran(scaled_q)

        def picked(which):
            blocks = normed_half.reshape(2 * own, count, group, share)
            return at_index(blocks, which, 2, keepdims=False).reshape(2 * own, count * share)

        picked_near = near(picked(mine ^ 1))
        grad_all = jnp.concatenate([grad_half, order.after(grad_near)], axis=0)
        grad_hidden = dot(grad_all, down_weight, NT)
        order.ran(grad_hidden)
        picked_all = jnp.concatenate([picked(mine), order.after(picked_near)], axis=0)
        order.ran(picked_all)
        return scaled_q, inverse_q, picked_all, grad_all, grad_hidden

    branch, (scaled_q, inverse_q, picked, grad_all, grad_hidden) = sum_half(
        [attended], [out_weight], NN, before_residual
    )
    residual = input_half.astype(F32) + branch
    scaled_two, inverse_two = rms_parts(residual)
    normed_half = (scaled_two * norm2_gain).astype(BF16)
    order.ran(normed_half)
    normed_two = jnp.concatenate([normed_half, order.after(near(normed_half))], axis=0)

    hidden, hidden_t, grad_gate, grad_up = hidden_units(normed_two, gate_weight, up_weight, grad_hidden)
    order.ran(hidden)

    send = grad_by_columns(owner[half:], order.after(hidden_t), grad_all, count)
    order.ran(send)
    down_sum = Halving(order, bits, count, send)
    keep = grad_by_columns(owner[:half], order.after(hidden_t), grad_all, count)
    order.ran(keep)
    down_sum.keep(keep)

    [send] = grad_by_rows(owner_two[half:], order.after(normed_two), [grad_up], count)
    order.ran(send)
    up_sum = Halving(order, bits_two, count, send)
    [keep] = grad_by_rows(owner_two[:half], order.after(normed_two), [grad_up], count)
    order.ran(keep)
    up_sum.keep(keep)

    def after_feed():
        keep, send = product([order.after(hidden)], [down_weight], NN)
        order.ran(send)
        feed_chip = add(keep, order.after(near(send))).astype(BF16)
        order.ran(feed_chip)
        return feed_chip

    back_two, feed_chip = sum_half([grad_gate, grad_up], [gate_weight, up_weight], NT, after_feed)
    grad_residual = grad_half.astype(F32) + rms_back(back_two, scaled_two, inverse_two, norm2_gain)
    branch_half = grad_residual.astype(BF16)
    order.ran(branch_half)
    branch_near = near(branch_half)
    feed_far = far(order.after(feed_chip)[own:])

    [send] = grad_by_rows(owner[half:], order.after(normed_two), [grad_gate], count)
    order.ran(send)
    gate_sum = Halving(order, bits, count, send)
    grad_branch = jnp.concatenate([branch_half, order.after(branch_near)], axis=0)
    grad_attended, delta = attended_grad(grad_branch, out_weight, attended)
    order.ran(grad_attended)
    send_out = grad_by_columns(owner[half:], order.after(attended_t), grad_branch, count)
    order.ran(send_out)
    down_sum.hop()
    [keep] = grad_by_rows(owner[:half], order.after(normed_two), [grad_gate], count)
    order.ran(keep)
    gate_sum.keep(keep)
    up_sum.hop(go=False)

    grad_query_raw, dkv_a, dkv_b = attend_back(
        meta, query, order.after(grad_attended), kv_a, kv_b, q_index, q_low, lse, delta, cos, sin
    )
    order.ran(grad_query_raw)
    dkv_near = near(dkv_b)

    latent_keep, latent_send = product([order.after(grad_query_raw)], [q_up], NT)
    order.ran(latent_send)
    latent_near = near(latent_send)
    down_sum.hop()
    gate_sum.hop()
    up_sum.go()
    chip_kv = add(dkv_a, order.after(dkv_near)).astype(BF16)
    order.ran(chip_kv)
    kv_far = far(chip_kv[:, own:])
    latent_chip = add(latent_keep, order.after(latent_near)).astype(BF16)
    order.ran(latent_chip)
    latent_far = far(swap(latent_chip))
    feed_out = add(feed_chip[:own], order.after(feed_far))
    block_output = (residual[:own] + feed_out).astype(BF16)
    order.ran(block_output)
    keep = grad_by_columns(owner[:half], order.after(attended_t), grad_branch, count)
    order.ran(keep)
    out_sum = Halving(order, bits, count, order.after(send_out), keep)
    [send_query] = grad_by_rows(owner[half:], order.after(latent_all), [grad_query_raw], count)
    order.ran(send_query)
    [keep_query] = grad_by_rows(owner[:half], order.after(latent_all), [grad_query_raw], count)
    order.ran(keep_query)

    chips_kv = add(chip_kv[:, :own], order.after(kv_far)).astype(BF16)
    order.ran(chips_kv)
    kv_sum = Halving(order, bits, count, chips_kv[half:], chips_kv[:half])
    up_sum.hop()

    grad_latent = add(latent_chip, order.after(latent_far))
    grad_compressed = rms_back(grad_latent, scaled_q, inverse_q, q_gain).astype(BF16)
    order.ran(grad_compressed)
    compressed_near = near(grad_compressed)
    down_grad = down_sum.finish()
    kv_sum.hop()


    def shared(values, size):
        blocks = values.reshape(count, group, size)
        return at_index(blocks, mine, 1, keepdims=False)

    compressed_all = jnp.concatenate([grad_compressed, order.after(compressed_near)], axis=0)
    q_down_parts = dot(picked, compressed_all, TN).astype(BF16).reshape(count, share, -1)
    order.ran(q_down_parts)
    q_down_parts = in_order(q_down_parts, owner, 0)
    q_down_sum = Halving(order, bits, count, q_down_parts[half:], q_down_parts[:half])

    out_sum.hop()
    query_sum = Halving(order, bits, count, order.after(send_query), keep_query)
    kv_sum.hop()
    gate_sum.hop()
    up_grad = up_sum.finish()
    kv_own = kv_sum.finish()
    former, latter = kv_own[:, :mid], kv_own[:, mid:HD]
    grad_kv_raw = jnp.concatenate(
        [
            former * cos_own + latter * sin_own,
            latter * cos_own - former * sin_own,
            kv_own[:, HD:],
        ],
        axis=1,
    ).astype(BF16)
    order.ran(grad_kv_raw)
    kv_raw_far = far(grad_kv_raw)
    grad_normed = dot(grad_compressed[:own], q_down, NT) + dot(order.after(grad_kv_raw), kv_weight, NT)
    input_grad = grad_residual[:own] + rms_back(grad_normed, scaled_one, inverse_one, norm1_gain)
    gain_one = jnp.sum(grad_normed * scaled_one, axis=0)
    order.ran(input_grad, gain_one)
    gain_far = far(gain_one)
    kv_half = jnp.concatenate([grad_kv_raw, order.after(kv_raw_far)], axis=0)
    order.ran(kv_half)
    kv_half_near = near(kv_half)
    gain_one = gain_one + order.after(gain_far)
    gain_two = jnp.sum(back_two * scaled_two, axis=0)
    gain_q = jnp.sum(grad_latent * scaled_q, axis=0)
    gains = jnp.concatenate([gain_one, gain_two, gain_q])
    order.ran(gains)
    gains_near = near(gains)
    kv_parts = dot(
        picked, jnp.concatenate([kv_half, order.after(kv_half_near)], axis=0), TN
    ).astype(BF16).reshape(count, share, -1)
    order.ran(kv_parts)
    kv_parts = in_order(kv_parts, owner, 0)
    kv_weight_sum = Halving(order, bits, count, kv_parts[half:], kv_parts[:half])
    gains = gains + order.after(gains_near)
    width = block_input.shape[1]
    gains = jnp.concatenate(
        [
            shared(gains[:width], share),
            shared(gains[width : 2 * width], share),
            shared(gains[2 * width :], q_gain.shape[0] // (count * group)),
        ],
        axis=1,
    )
    order.ran(gains)
    gains = in_order(gains, owner, 0)[:, None, :]
    gains_sum = Halving(order, bits, count, gains[half:], gains[:half])
    q_down_sum.hop()
    query_sum.hop()
    kv_weight_sum.hop()
    gains_sum.hop()
    out_sum.hop()
    gate_grad = gate_sum.finish()
    q_down_sum.hop()
    kv_weight_sum.hop()
    gains_sum.hop()
    query_sum.hop()
    out_weight_grad = out_sum.finish()
    q_down_grad = q_down_sum.finish()
    kv_weight_grad = kv_weight_sum.finish()
    gains = gains_sum.finish()[0]
    q_up_grad = query_sum.finish()
    return (
        block_output,
        input_grad,
        gains[:share],
        q_down_grad,
        gains[2 * share :],
        q_up_grad,
        kv_weight_grad,
        out_weight_grad,
        gains[share : 2 * share],
        gate_grad,
        up_grad,
        down_grad,
    )


def solution(mesh):
    both = P(("seq", "tensor"))
    rows = P(("seq", "tensor"), None)
    return jax.shard_map(
        body,
        mesh=mesh,
        in_specs=(
            rows, P(), P(), P(), P(), P(None, "tensor"), P(), P("tensor", None), P(),
            P(None, "tensor"), P(None, "tensor"), P("tensor", None), rows,
        ),
        out_specs=(
            rows, rows, both, rows, both, P("seq", "tensor"), rows, P("tensor", "seq"), both,
            P("seq", "tensor"), P("seq", "tensor"), P("tensor", "seq"),
        ),
        check_vma=False,
    )
```

time: 1580 us -> 490 us (0.31)
  waiting for transfers between devices: 1290 us -> 198 us
  matrix products: 139 us -> 33 us
  starting transfers between devices: 1.3 us -> 80.4 us
  Pallas kernels: 0 us -> 59.9 us
  blocking collectives: 40.5 us -> 0 us
  other arithmetic: 41 us -> 68.1 us
    reduce_scatter x12 -> x0, waiting for transfers between devices: 1170 us -> none  [the longest x1 143 us: body(): lax.psum_scatter(grad_kv_partial, ('seq', 'tensor'), scatter_dimension=0,...]
    ppermute x0 -> x64, waiting for transfers between devices: none -> 198 us  [the longest x27 116 us: swap_seq(): return lax.ppermute(values, 'seq', [(i, i ^ bit) for i in range(count)])]
    all_gather x5 -> x0, waiting for transfers between devices: 117 us -> none  [the longest x1 54.6 us: fetch_keys(): return lax.all_gather(keyval, ('seq', 'tensor'), axis=0, tiled=True)]
    dot_general x28 -> x18, matrix products: 139 us -> 33 us  [dot(): return lax.dot_general(left, right, dims, preferred_element_type=F32)]
    ppermute x0 -> x64, starting transfers between devices: none -> 80.4 us  [the longest x27 56 us: swap_seq(): return lax.ppermute(values, 'seq', [(i, i ^ bit) for i in range(count)])]
    pallas_call x0 -> x15, Pallas kernels: none -> 59.9 us  [the longest x6 20.2 us: grad_by_rows(): pl.pallas_call(rows_kernel, grid_spec=pltpu.PrefetchScalarGridSpec(num_sc...]
    unnamed x1 -> x0, blocking collectives: 40.5 us -> none
    add x8 -> x14, other arithmetic: 4.82 us -> 21.8 us  [the longest x9 18 us: add(): total = total + part.astype(F32)]
  transfers between devices with their start and end apart: 17 -> 64, of which waited for: 16 -> 24; matrix products, arithmetic and copies ran while one was open for 7% -> 23% of each run, Pallas kernels for 0% -> 7%
where the time goes in v1:
time: 490 us; the launch traced here: 484 us
  waiting for transfers between devices  198 us (40%)
  starting transfers between devices  80.4 us (16%)
  other arithmetic  68.1 us (14%)
  Pallas kernels  59.9 us (12%)
  local copies, waits for them, and re-layouts  37.6 us (8%)
  matrix products  33 us (7%)
  between operations  6.52 us (1%)
    ppermute x27, waiting for transfers between devices, swap_seq(): return lax.ppermute(values, 'seq', [(i, i ^ bit) for i in range(count)])  116 us
    ppermute x11, waiting for transfers between devices, far(): return lax.ppermute(values, 'tensor', [(i, i ^ 2) for i in range(4)])  60.9 us
    ppermute x27, starting transfers between devices, swap_seq(): return lax.ppermute(values, 'seq', [(i, i ^ bit) for i in range(count)])  56 us
    dot_general x18, matrix products, dot(): return lax.dot_general(left, right, dims, preferred_element_type=F32)  33 us
    convert_element_type x18, other arithmetic, hop(): send = add(*[t[cut:] for t in self.terms]).astype(BF16)  23.5 us
    pallas_call x6, Pallas kernels, grad_by_rows(): pl.pallas_call(rows_kernel, grid_spec=pltpu.PrefetchScalarGridSpec(num_sc...  20.2 us
    add x9, other arithmetic, add(): total = total + part.astype(F32)  18 us
    unnamed x149, local copies, waits for them, and re-layouts  17.5 us
  transfers between devices with their start and end apart: 64, of which 24 were waited for; matrix products, arithmetic and copies ran while one was open for 23% of the time, Pallas kernels for 7%

profile of v1, /device:TPU:0, one launch (start us, length us, event | category | flops | bytes accessed | tf_op | source)
XLA Modules:
  0.0 483.6 jit_solution(8329005649921770910)
XLA Ops:
  9.1 3.0 collective-permute-start.1
  20.9 2.1 collective-permute-start.4
  24.6 5.4 %collective-permute-done.4 = bf16[256,512]{1,0:T(8,128)(2,1)S(1)} collective-permute-done((bf16[256,512]{1,0:T(8,128)(2,1)S(1)}, bf16[256,512]{1,0:T(8,128)(2,1)S(1)}, u32[]{:S(2)}, u32[]{:S(2)}) %collective-permute-start.4) | collective-permute-done | bytes 262176 | tf_op jit(solution)/shard_map/ppermute | solution.py:457
  37.7 2.2 project_rotate.1.q_ref
  39.9 2.2 collective-permute-done.5
  44.7 5.1 %collective-permute-done.8 = bf16[256,512]{1,0:T(8,128)(2,1)S(1)} collective-permute-done((bf16[256,512]{1,0:T(8,128)(2,1)S(1)}, bf16[256,512]{1,0:T(8,128)(2,1)S(1)}, u32[]{:S(2)}, u32[]{:S(2)}) %collective-permute-start.8) | collective-permute-done | bytes 262176 | tf_op jit(solution)/shard_map/ppermute | solution.py:457
  53.3 4.7 collective-permute-done.10
  59.8 3.8 attend.1
  70.6 2.3 multiply_reduce_fusion.5
  72.9 20.9 %collective-permute-done.19 = bf16[256,2048]{1,0:T(8,128)(2,1)S(1)} collective-permute-done((bf16[256,2048]{1,0:T(8,128)(2,1)S(1)}, bf16[256,2048]{1,0:T(8,128)(2,1)S(1)}, u32[]{:S(2)}, u32[]{:S(2)}) %collective-permute-start.19) | collective-permute-done | bytes 1048608 | tf_op jit(solution)/shard_map/ppermute | solution.py:448
  94.9 6.3 %fusion.97.gh_ref = f32[512,1408]{1,0:T(8,128)S(1)} fusion(bf16[512,2048]{1,0:T(8,128)(2,1)S(1)} %constant_dynamic-update-slice_fusion.4.right_ref, bf16[1408,2048]{1,0:T(8,128)(2,1)} %param.28), kind=kOutput, calls=%fused_computation.254 | convolution fusion | flops 2952790016 | bytes 10747904 | tf_op jit(solution)/shard_map/dot_general | solution.py:27
  101.4 12.8 %hidden_units.1 = (bf16[512,1408]{1,0:T(8,128)(2,1)S(1)}, bf16[1408,512]{1,0:T(8,128)(2,1)S(1)}, bf16[512,1408]{1,0:T(8,128)(2,1)S(1)}, bf16[512,1408]{1,0:T(8,128)(2,1)S(1)}) custom-call(bf16[512,2048]{1,0:T(8,128)(2,1)S(1)} %pad_maximum_fusion.x_ref.left_ref, bf16[2048,1408]{1,0:T(8,128)(2,1)S(1)} %bitcast.128, bf16[2048,1408]{1,0:T(8,128)(2,1)} %up_ref.1, ...), custom_call_target="tpu_custom_call" | custom-call | flops 1000 | bytes 1000 | tf_op jit(solution)/shard_map/hidden_units/pallas_call | solution.py:359
  114.3 4.1 grad_by_columns.4
  118.4 2.9 grad_by_columns.5
  122.9 4.3 grad_by_rows.6
  127.2 4.7 collective-permute-start.28
  131.8 4.9 %collective-permute-start.29 = (bf16[4,1408,256]{2,1,0:T(8,128)(2,1)}, bf16[4,1408,256]{2,1,0:T(8,128)(2,1)}, u32[]{:S(2)}, u32[]{:S(2)}) collective-permute-start(bf16[4,1408,256]{2,1,0:T(8,128)(2,1)} %grad_by_columns.4), channel_id=1, source_target_pairs={{0,4},{4,0},{8,12},{12,8},{16,20},{20,16},{24,28},{28,24},{1,5},{5... | collective-permute-start | bytes 8650760 | tf_op jit(solution)/shard_map/ppermute | solution.py:467
  136.8 3.2 grad_by_rows.7
  149.4 4.7 convolution_convert_fusion.2
  159.4 20.5 %collective-permute-done.25 = bf16[256,2048]{1,0:T(8,128)(2,1)S(1)} collective-permute-done((bf16[256,2048]{1,0:T(8,128)(2,1)S(1)}, bf16[256,2048]{1,0:T(8,128)(2,1)S(1)}, u32[]{:S(2)}, u32[]{:S(2)}) %collective-permute-start.25) | collective-permute-done | bytes 1048608 | tf_op jit(solution)/shard_map/ppermute | solution.py:448
  180.7 2.6 fusion.86
  186.3 4.2 grad_by_rows.8
  190.5 3.2 pad_maximum_fusion.1.gb_ref.right_ref
  193.7 2.3 copy.29
  197.5 2.2 copy-done.26
  200.9 3.8 attended_grad.1
  204.8 2.5 grad_by_columns.6
  207.3 3.0 add_convert_fusion.3
  210.5 3.2 grad_by_rows.9
  213.7 2.8 add_convert_fusion.2
  217.4 5.1 %attend_back.1 = (bf16[512,1024]{1,0:T(8,128)(2,1)S(1)}, bf16[8,256,512]{2,1,0:T(8,128)(2,1)S(1)}, bf16[8,256,512]{2,1,0:T(8,128)(2,1)S(1)}) custom-call(s32[4,8]{1,0:T(4,128)S(1)} %pad_add_fusion.meta, bf16[512,1024]{1,0:T(8,128)(2,1)S(1)} %copy-done.17, bf16[512,1024]{1,0:T(8,128)(2,1)S(1)} %get-tuple-element.179.do_ref, ...), custom_call_target="tpu_custom_call" | custom-call | flops 1000 | bytes 1000 | tf_op jit(solution)/shard_map/attend_back/pallas_call | solution.py:229
  223.8 3.2 collective-permute-done.20
  230.3 14.3 %collective-permute-done.33 = bf16[2,1408,256]{2,1,0:T(8,128)(2,1)} collective-permute-done((bf16[2,1408,256]{2,1,0:T(8,128)(2,1)}, bf16[2,1408,256]{2,1,0:T(8,128)(2,1)}, u32[]{:S(2)}, u32[]{:S(2)}) %collective-permute-start.33) | collective-permute-done | bytes 1441824 | tf_op jit(solution)/shard_map/ppermute | solution.py:467
  246.2 10.4 %collective-permute-start.38 = (bf16[1,1408,256]{2,1,0:T(8,128)(2,1)S(1)}, bf16[1,1408,256]{2,1,0:T(8,128)(2,1)S(1)}, u32[]{:S(2)}, u32[]{:S(2)}) collective-permute-start(bf16[1,1408,256]{2,1,0:T(8,128)(2,1)S(1)} %add_convert_fusion.11), channel_id=1, source_target_pairs={{0,16},{4,20},{8,24},{12,28},{16,0},{20,4},{24,8},{28,12},{1,17},{... | collective-permute-start | bytes 2162696 | tf_op jit(solution)/shard_map/ppermute | solution.py:467
  256.7 4.7 collective-permute-done.32
  263.5 5.9 %collective-permute-start.35 = (bf16[2,256,1408]{2,1,0:T(8,128)(2,1)S(1)}, bf16[2,256,1408]{2,1,0:T(8,128)(2,1)S(1)}, u32[]{:S(2)}, u32[]{:S(2)}) collective-permute-start(bf16[2,256,1408]{2,1,0:T(8,128)(2,1)S(1)} %add_convert_fusion.2), channel_id=1, source_target_pairs={{0,4},{4,0},{8,12},{12,8},{16,20},{20,16},{24,28},{28,24},{1,5},{5... | collective-permute-start | bytes 4325384 | tf_op jit(solution)/shard_map/ppermute | solution.py:467
  272.7 2.5 grad_by_columns.7
  276.0 3.1 grad_by_rows.10
  279.1 2.3 grad_by_rows.11
  282.4 13.8 %collective-permute-done.36 = bf16[8,128,512]{2,1,0:T(8,128)(2,1)S(1)} collective-permute-done((bf16[8,128,512]{2,1,0:T(8,128)(2,1)S(1)}, bf16[8,128,512]{2,1,0:T(8,128)(2,1)S(1)}, u32[]{:S(2)}, u32[]{:S(2)}) %collective-permute-start.36) | collective-permute-done | bytes 1048608 | tf_op jit(solution)/shard_map/ppermute | solution.py:448
  296.6 5.2 %collective-permute-done.35 = bf16[2,256,1408]{2,1,0:T(8,128)(2,1)S(1)} collective-permute-done((bf16[2,256,1408]{2,1,0:T(8,128)(2,1)S(1)}, bf16[2,256,1408]{2,1,0:T(8,128)(2,1)S(1)}, u32[]{:S(2)}, u32[]{:S(2)}) %collective-permute-start.35) | collective-permute-done | bytes 1441824 | tf_op jit(solution)/shard_map/ppermute | solution.py:467
  301.7 2.1 collective-permute-start.37
  306.1 5.5 %collective-permute-start.43 = (bf16[1,256,1408]{2,1,0:T(8,128)(2,1)S(1)}, bf16[1,256,1408]{2,1,0:T(8,128)(2,1)S(1)}, u32[]{:S(2)}, u32[]{:S(2)}) collective-permute-start(bf16[1,256,1408]{2,1,0:T(8,128)(2,1)S(1)} %add_convert_fusion.10), channel_id=1, source_target_pairs={{0,16},{4,20},{8,24},{12,28},{16,0},{20,4},{24,8},{28,12},{1,17},{... | collective-permute-start | bytes 2162696 | tf_op jit(solution)/shard_map/ppermute | solution.py:467
  312.5 2.9 add_bitcast_fusion.2
  316.9 40.3 %collective-permute-done.37 = bf16[4,128,512]{2,1,0:T(8,128)(2,1)S(1)} collective-permute-done((bf16[4,128,512]{2,1,0:T(8,128)(2,1)S(1)}, bf16[4,128,512]{2,1,0:T(8,128)(2,1)S(1)}, u32[]{:S(2)}, u32[]{:S(2)}) %collective-permute-start.37) | collective-permute-done | bytes 524320 | tf_op jit(solution)/shard_map/ppermute | solution.py:467
  360.1 4.9 %collective-permute-done.39 = bf16[2,128,512]{2,1,0:T(8,128)(2,1)S(1)} collective-permute-done((bf16[2,128,512]{2,1,0:T(8,128)(2,1)S(1)}, bf16[2,128,512]{2,1,0:T(8,128)(2,1)S(1)}, u32[]{:S(2)}, u32[]{:S(2)}) %collective-permute-start.39) | collective-permute-done | bytes 262176 | tf_op jit(solution)/shard_map/ppermute | solution.py:467
  365.0 5.7 %collective-permute-start.42 = (bf16[1,128,512]{2,1,0:T(8,128)(2,1)S(1)}, bf16[1,128,512]{2,1,0:T(8,128)(2,1)S(1)}, u32[]{:S(2)}, u32[]{:S(2)}) collective-permute-start(bf16[1,128,512]{2,1,0:T(8,128)(2,1)S(1)} %add_convert_fusion.20), channel_id=1, source_target_pairs={{0,16},{4,20},{8,24},{12,28},{16,0},{20,4},{24,8},{28,12},{1,17},{... | collective-permute-start | bytes 393224 | tf_op jit(solution)/shard_map/ppermute | solution.py:467
  370.7 2.8 add_convert_fusion.9
  373.4 2.5 add_bitcast_fusion.1
  378.0 2.0 fusion.19
  380.1 2.4 fusion.18
  382.6 3.9 constant_dynamic-slice_fusion.6
  394.0 9.1 %collective-permute-done.52 = bf16[4,64,1024]{2,1,0:T(8,128)(2,1)} collective-permute-done((bf16[4,64,1024]{2,1,0:T(8,128)(2,1)}, bf16[4,64,1024]{2,1,0:T(8,128)(2,1)}, u32[]{:S(2)}, u32[]{:S(2)}) %collective-permute-start.52) | collective-permute-done | bytes 524320 | tf_op jit(solution)/shard_map/ppermute | solution.py:467
  403.1 3.8 constant_dynamic-slice_fusion.2
  409.8 4.8 %constant_dynamic-slice_fusion.12 = (bf16[1,64,512]{2,1,0:T(8,128)(2,1)S(1)}, bf16[1,64,512]{2,1,0:T(8,128)(2,1)S(1)}, bf16[1,64,512]{2,1,0:T(8,128)(2,1)S(1)}, ...) fusion(bf16[8,64,512]{2,1,0:T(8,128)(2,1)} %bitcast.137, ...), kind=kLoop, calls=%fused_computation.170 | loop fusion | bytes 786456 | tf_op jit(solution)/shard_map/dynamic_slice | solution.py:48
  414.7 10.2 %collective-permute-done.51 = bf16[4,128,1024]{2,1,0:T(8,128)(2,1)} collective-permute-done((bf16[4,128,1024]{2,1,0:T(8,128)(2,1)}, bf16[4,128,1024]{2,1,0:T(8,128)(2,1)}, u32[]{:S(2)}, u32[]{:S(2)}) %collective-permute-start.51) | collective-permute-done | bytes 1048608 | tf_op jit(solution)/shard_map/ppermute | solution.py:467
  427.2 5.2 %collective-permute-done.50 = bf16[4,64,512]{2,1,0:T(8,128)(2,1)S(1)} collective-permute-done((bf16[4,64,512]{2,1,0:T(8,128)(2,1)S(1)}, bf16[4,64,512]{2,1,0:T(8,128)(2,1)S(1)}, u32[]{:S(2)}, u32[]{:S(2)}) %collective-permute-start.50) | collective-permute-done | bytes 262176 | tf_op jit(solution)/shard_map/ppermute | solution.py:467
  438.4 3.0 add_bitcast_fusion
  444.1 18.7 %collective-permute-done.54 = bf16[2,64,512]{2,1,0:T(8,128)(2,1)S(1)} collective-permute-done((bf16[2,64,512]{2,1,0:T(8,128)(2,1)S(1)}, bf16[2,64,512]{2,1,0:T(8,128)(2,1)S(1)}, u32[]{:S(2)}, u32[]{:S(2)}) %collective-permute-start.54) | collective-permute-done | bytes 131104 | tf_op jit(solution)/shard_map/ppermute | solution.py:467
  465.0 3.0 collective-permute-start.58
  469.2 2.4 add_bitcast_fusion.3
  471.6 2.4 add_bitcast_fusion.5
  473.9 2.2 add_bitcast_fusion.7
  477.8 3.6 collective-permute-done.63
  (380 shorter events, 113.6 us)
Async XLA Ops:
  9.1 11.7 %collective-permute-start.1 = (bf16[128,512]{1,0:T(8,128)(2,1)S(1)}, bf16[128,512]{1,0:T(8,128)(2,1)S(1)}, u32[]{:S(2)}, u32[]{:S(2)}) collective-permute-start(bf16[128,512]{1,0:T(8,128)(2,1)S(1)} %pad_maximum_fusion.15), channel_id=1, source_target_pairs={{0,2},{1,3},{2,0},{3,1},{4,6},{5,7},{6,4},{7,5},{8,10},{9,11},{10,... | collective-permute-start | bytes 393224 | tf_op jit(solution)/shard_map/ppermute | solution.py:448
  13.1 11.3 %collective-permute-start = (bf16[128,1024]{1,0:T(8,128)(2,1)S(1)}, bf16[128,1024]{1,0:T(8,128)(2,1)S(1)}, u32[]{:S(2)}, u32[]{:S(2)}) collective-permute-start(bf16[128,1024]{1,0:T(8,128)(2,1)S(1)} %multiply_convert_fusion.2), channel_id=1, source_target_pairs={{0,2},{1,3},{2,0},{3,1},{4,6},{5,7},{6,4},{7,5},{8,10},{9,11},{10,... | collective-permute-start | bytes 786440 | tf_op jit(solution)/shard_map/ppermute | solution.py:448
  20.8 13.4 %collective-permute-start.13 = (bf16[256,512]{1,0:T(8,128)(2,1)S(1)}, bf16[256,512]{1,0:T(8,128)(2,1)S(1)}, u32[]{:S(2)}, u32[]{:S(2)}) collective-permute-start(bf16[256,512]{1,0:T(8,128)(2,1)S(1)} %get-tuple-element.277), channel_id=1, source_target_pairs={{0,1},{1,0},{2,3},{3,2},{4,5},{5,4},{6,7},{7,6},{8,9},{9,8},{10,11... | collective-permute-start | bytes 786440 | tf_op jit(solution)/shard_map/ppermute | solution.py:444
  20.9 9.1 %collective-permute-start.4 = (bf16[256,512]{1,0:T(8,128)(2,1)S(1)}, bf16[256,512]{1,0:T(8,128)(2,1)S(1)}, u32[]{:S(2)}, u32[]{:S(2)}) collective-permute-start(bf16[256,512]{1,0:T(8,128)(2,1)S(1)} %get-tuple-element.277), channel_id=1, source_target_pairs={{0,4},{8,0},{16,8},{24,16},{28,24},{20,28},{12,20},{4,12},{1,5},{9... | collective-permute-start | bytes 786440 | tf_op jit(solution)/shard_map/ppermute | solution.py:457
  23.0 8.4 %collective-permute-start.3 = (bf16[256,512]{1,0:T(8,128)(2,1)S(1)}, bf16[256,512]{1,0:T(8,128)(2,1)S(1)}, u32[]{:S(2)}, u32[]{:S(2)}) collective-permute-start(bf16[256,512]{1,0:T(8,128)(2,1)S(1)} %get-tuple-element.277), channel_id=1, source_target_pairs={{0,8},{8,16},{16,24},{24,28},{28,20},{20,12},{12,4},{4,0},{1,9},{9... | collective-permute-start | bytes 786440 | tf_op jit(solution)/shard_map/ppermute | solution.py:457
  24.4 11.6 %collective-permute-start.7 = (bf16[256,1024]{1,0:T(8,128)(2,1)S(1)}, bf16[256,1024]{1,0:T(8,128)(2,1)S(1)}, u32[]{:S(2)}, u32[]{:S(2)}) collective-permute-start(bf16[256,1024]{1,0:T(8,128)(2,1)S(1)} %pad_maximum_fusion.5), channel_id=1, source_target_pairs={{0,1},{1,0},{2,3},{3,2},{4,5},{5,4},{6,7},{7,6},{8,9},{9,8},{10,11... | collective-permute-start | bytes 1572872 | tf_op jit(solution)/shard_map/ppermute | solution.py:444
  31.4 13.1 %collective-permute-start.14 = (bf16[2,256,512]{2,1,0:T(8,128)(2,1)S(1)}, bf16[2,256,512]{2,1,0:T(8,128)(2,1)S(1)}, u32[]{:S(2)}, u32[]{:S(2)}) collective-permute-start(bf16[2,256,512]{2,1,0:T(8,128)(2,1)S(1)} %get-tuple-element.139), channel_id=1, source_target_pairs={{0,1},{1,0},{2,3},{3,2},{4,5},{5,4},{6,7},{7,6},{8,9},{9,8},{10,11... | collective-permute-start | bytes 1572872 | tf_op jit(solution)/shard_map/ppermute | solution.py:444
  32.3 18.8 %collective-permute-start.2 = (bf16[128,2048]{1,0:T(8,128)(2,1)}, bf16[128,2048]{1,0:T(8,128)(2,1)S(1)}, u32[]{:S(2)}, u32[]{:S(2)}) collective-permute-start(bf16[128,2048]{1,0:T(8,128)(2,1)} %param.17), channel_id=1, source_target_pairs={{0,2},{1,3},{2,0},{3,1},{4,6},{5,7},{6,4},{7,5},{8,10},{9,11},{10,... | collective-permute-start | bytes 1572872 | tf_op jit(solution)/shard_map/ppermute | solution.py:448
  33.8 8.4 %collective-permute-start.5 = (bf16[256,512]{1,0:T(8,128)(2,1)S(1)}, bf16[256,512]{1,0:T(8,128)(2,1)S(1)}, u32[]{:S(2)}, u32[]{:S(2)}) collective-permute-start(bf16[256,512]{1,0:T(8,128)(2,1)S(1)} %collective-permute-done.3), channel_id=1, source_target_pairs={{0,8},{8,16},{16,24},{24,28},{28,20},{20,12},{12,4},{4,0},{1,9},{9... | collective-permute-start | bytes 786440 | tf_op jit(solution)/shard_map/ppermute | solution.py:457
  34.3 8.1 %collective-permute-start.6 = (bf16[256,512]{1,0:T(8,128)(2,1)S(1)}, bf16[256,512]{1,0:T(8,128)(2,1)S(1)}, u32[]{:S(2)}, u32[]{:S(2)}) collective-permute-start(bf16[256,512]{1,0:T(8,128)(2,1)S(1)} %collective-permute-done.4), channel_id=1, source_target_pairs={{0,4},{8,0},{16,8},{24,16},{28,24},{20,28},{12,20},{4,12},{1,5},{9... | collective-permute-start | bytes 786440 | tf_op jit(solution)/shard_map/ppermute | solution.py:457
  36.1 22.0 %collective-permute-start.10 = (bf16[128,2048]{1,0:T(8,128)(2,1)S(1)}, bf16[128,2048]{1,0:T(8,128)(2,1)S(1)}, u32[]{:S(2)}, u32[]{:S(2)}) collective-permute-start(bf16[128,2048]{1,0:T(8,128)(2,1)S(1)} %copy-done.56), channel_id=1, source_target_pairs={{0,2},{1,3},{2,0},{3,1},{4,6},{5,7},{6,4},{7,5},{8,10},{9,11},{10,... | collective-permute-start | bytes 1572872 | tf_op jit(solution)/shard_map/ppermute | solution.py:448
  42.4 7.4 %collective-permute-start.8 = (bf16[256,512]{1,0:T(8,128)(2,1)S(1)}, bf16[256,512]{1,0:T(8,128)(2,1)S(1)}, u32[]{:S(2)}, u32[]{:S(2)}) collective-permute-start(bf16[256,512]{1,0:T(8,128)(2,1)S(1)} %collective-permute-done.5), channel_id=1, source_target_pairs={{0,8},{8,16},{16,24},{24,28},{28,20},{20,12},{12,4},{4,0},{1,9},{9... | collective-permute-start | bytes 786440 | tf_op jit(solution)/shard_map/ppermute | solution.py:457
  44.0 7.0 %collective-permute-start.9 = (bf16[256,512]{1,0:T(8,128)(2,1)S(1)}, bf16[256,512]{1,0:T(8,128)(2,1)S(1)}, u32[]{:S(2)}, u32[]{:S(2)}) collective-permute-start(bf16[256,512]{1,0:T(8,128)(2,1)S(1)} %collective-permute-done.6), channel_id=1, source_target_pairs={{0,4},{8,0},{16,8},{24,16},{28,24},{20,28},{12,20},{4,12},{1,5},{9... | collective-permute-start | bytes 786440 | tf_op jit(solution)/shard_map/ppermute | solution.py:457
  44.5 13.8 %collective-permute-start.15 = (bf16[2,256,512]{2,1,0:T(8,128)(2,1)S(1)}, bf16[2,256,512]{2,1,0:T(8,128)(2,1)S(1)}, u32[]{:S(2)}, u32[]{:S(2)}) collective-permute-start(bf16[2,256,512]{2,1,0:T(8,128)(2,1)S(1)} %get-tuple-element.141), channel_id=1, source_target_pairs={{0,1},{1,0},{2,3},{3,2},{4,5},{5,4},{6,7},{7,6},{8,9},{9,8},{10,11... | collective-permute-start | bytes 1572872 | tf_op jit(solution)/shard_map/ppermute | solution.py:444
  51.0 7.0 %collective-permute-start.12 = (bf16[128,512]{1,0:T(8,128)(2,1)S(1)}, bf16[128,512]{1,0:T(8,128)(2,1)S(1)}, u32[]{:S(2)}, u32[]{:S(2)}) collective-permute-start(bf16[128,512]{1,0:T(8,128)(2,1)S(1)} %slice.524), channel_id=1, source_target_pairs={{0,4},{8,0},{16,8},{24,16},{28,24},{20,28},{12,20},{4,12},{1,5},{9... | collective-permute-start | bytes 393224 | tf_op jit(solution)/shard_map/ppermute | solution.py:457
  51.6 6.4 %collective-permute-start.11 = (bf16[128,512]{1,0:T(8,128)(2,1)S(1)}, bf16[128,512]{1,0:T(8,128)(2,1)S(1)}, u32[]{:S(2)}, u32[]{:S(2)}) collective-permute-start(bf16[128,512]{1,0:T(8,128)(2,1)S(1)} %slice.523), channel_id=1, source_target_pairs={{0,8},{8,16},{16,24},{24,28},{28,20},{20,12},{12,4},{4,0},{1,9},{9... | collective-permute-start | bytes 393224 | tf_op jit(solution)/shard_map/ppermute | solution.py:457
  53.2 6.5 %collective-permute-start.16 = (bf16[2,256,512]{2,1,0:T(8,128)(2,1)S(1)}, bf16[2,256,512]{2,1,0:T(8,128)(2,1)S(1)}, u32[]{:S(2)}, u32[]{:S(2)}) collective-permute-start(bf16[2,256,512]{2,1,0:T(8,128)(2,1)S(1)} %get-tuple-element.143), channel_id=1, source_target_pairs={{0,1},{1,0},{2,3},{3,2},{4,5},{5,4},{6,7},{7,6},{8,9},{9,8},{10,11... | collective-permute-start | bytes 1572872 | tf_op jit(solution)/shard_map/ppermute | solution.py:444
  58.1 1.6 collective-permute-start.17
  64.9 2.7 collective-permute-start.18
  65.3 7.6 %collective-permute-start.21 = (bf16[256,2048]{1,0:T(8,128)(2,1)S(1)}, bf16[256,2048]{1,0:T(8,128)(2,1)S(1)}, u32[]{:S(2)}, u32[]{:S(2)}) collective-permute-start(bf16[256,2048]{1,0:T(8,128)(2,1)S(1)} %get-tuple-element.263), channel_id=1, source_target_pairs={{0,1},{1,0},{2,3},{3,2},{4,5},{5,4},{6,7},{7,6},{8,9},{9,8},{10,11... | collective-permute-start | bytes 3145736 | tf_op jit(solution)/shard_map/ppermute | solution.py:444
  68.5 25.3 %collective-permute-start.19 = (bf16[256,2048]{1,0:T(8,128)(2,1)S(1)}, bf16[256,2048]{1,0:T(8,128)(2,1)S(1)}, u32[]{:S(2)}, u32[]{:S(2)}) collective-permute-start(bf16[256,2048]{1,0:T(8,128)(2,1)S(1)} %pad_maximum_fusion.3), channel_id=1, source_target_pairs={{0,2},{1,3},{2,0},{3,1},{4,6},{5,7},{6,4},{7,5},{8,10},{9,11},{10,... | collective-permute-start | bytes 3145736 | tf_op jit(solution)/shard_map/ppermute | solution.py:448
  94.7 6.5 %collective-permute-start.22 = (bf16[256,2048]{1,0:T(8,128)(2,1)S(1)}, bf16[256,2048]{1,0:T(8,128)(2,1)S(1)}, u32[]{:S(2)}, u32[]{:S(2)}) collective-permute-start(bf16[256,2048]{1,0:T(8,128)(2,1)S(1)} %multiply_convert_fusion), channel_id=1, source_target_pairs={{0,1},{1,0},{2,3},{3,2},{4,5},{5,4},{6,7},{7,6},{8,9},{9,8},{10,11... | collective-permute-start | bytes 3145736 | tf_op jit(solution)/shard_map/ppermute | solution.py:444
  127.2 86.5 %collective-permute-start.28 = (bf16[4,256,1408]{2,1,0:T(8,128)(2,1)}, bf16[4,256,1408]{2,1,0:T(8,128)(2,1)}, u32[]{:S(2)}, u32[]{:S(2)}) collective-permute-start(bf16[4,256,1408]{2,1,0:T(8,128)(2,1)} %grad_by_rows.6), channel_id=1, source_target_pairs={{0,8},{4,12},{8,0},{12,4},{16,24},{20,28},{24,16},{28,20},{1,9},{5... | collective-permute-start | bytes 8650760 | tf_op jit(solution)/shard_map/ppermute | solution.py:467
  131.8 75.5 %collective-permute-start.29 = (bf16[4,1408,256]{2,1,0:T(8,128)(2,1)}, bf16[4,1408,256]{2,1,0:T(8,128)(2,1)}, u32[]{:S(2)}, u32[]{:S(2)}) collective-permute-start(bf16[4,1408,256]{2,1,0:T(8,128)(2,1)} %grad_by_columns.4), channel_id=1, source_target_pairs={{0,4},{4,0},{8,12},{12,8},{16,20},{20,16},{24,28},{28,24},{1,5},{5... | collective-permute-start | bytes 8650760 | tf_op jit(solution)/shard_map/ppermute | solution.py:467
  145.3 3.7 collective-permute-start.23
  154.1 4.1 collective-permute-start.24
  154.8 25.1 %collective-permute-start.25 = (bf16[256,2048]{1,0:T(8,128)(2,1)S(1)}, bf16[256,2048]{1,0:T(8,128)(2,1)S(1)}, u32[]{:S(2)}, u32[]{:S(2)}) collective-permute-start(bf16[256,2048]{1,0:T(8,128)(2,1)S(1)} %pad_maximum_fusion.4), channel_id=1, source_target_pairs={{0,2},{1,3},{2,0},{3,1},{4,6},{5,7},{6,4},{7,5},{8,10},{9,11},{10,... | collective-permute-start | bytes 3145736 | tf_op jit(solution)/shard_map/ppermute | solution.py:448
  183.3 7.2 %collective-permute-start.27 = (bf16[256,2048]{1,0:T(8,128)(2,1)}, bf16[256,2048]{1,0:T(8,128)(2,1)}, u32[]{:S(2)}, u32[]{:S(2)}) collective-permute-start(bf16[256,2048]{1,0:T(8,128)(2,1)} %get-tuple-element.234), channel_id=1, source_target_pairs={{0,1},{1,0},{2,3},{3,2},{4,5},{5,4},{6,7},{7,6},{8,9},{9,8},{10,11... | collective-permute-start | bytes 3145736 | tf_op jit(solution)/shard_map/ppermute | solution.py:444
  190.5 70.9 %collective-permute-start.32 = (bf16[4,256,1408]{2,1,0:T(8,128)(2,1)}, bf16[4,256,1408]{2,1,0:T(8,128)(2,1)}, u32[]{:S(2)}, u32[]{:S(2)}) collective-permute-start(bf16[4,256,1408]{2,1,0:T(8,128)(2,1)} %grad_by_rows.8), channel_id=1, source_target_pairs={{0,4},{4,0},{8,12},{12,8},{16,20},{20,16},{24,28},{28,24},{1,5},{5... | collective-permute-start | bytes 8650760 | tf_op jit(solution)/shard_map/ppermute | solution.py:467
  210.3 34.3 %collective-permute-start.33 = (bf16[2,1408,256]{2,1,0:T(8,128)(2,1)}, bf16[2,1408,256]{2,1,0:T(8,128)(2,1)}, u32[]{:S(2)}, u32[]{:S(2)}) collective-permute-start(bf16[2,1408,256]{2,1,0:T(8,128)(2,1)} %add_convert_fusion.3), channel_id=1, source_target_pairs={{0,8},{4,12},{8,0},{12,4},{16,24},{20,28},{24,16},{28,20},{1,9},{5... | collective-permute-start | bytes 4325384 | tf_op jit(solution)/shard_map/ppermute | solution.py:467
  222.4 41.0 %collective-permute-start.31 = (bf16[8,256,512]{2,1,0:T(8,128)(2,1)S(1)}, bf16[8,256,512]{2,1,0:T(8,128)(2,1)S(1)}, u32[]{:S(2)}, u32[]{:S(2)}) collective-permute-start(bf16[8,256,512]{2,1,0:T(8,128)(2,1)S(1)} %get-tuple-element.185), channel_id=1, source_target_pairs={{0,1},{1,0},{2,3},{3,2},{4,5},{5,4},{6,7},{7,6},{8,9},{9,8},{10,11... | collective-permute-start | bytes 6291464 | tf_op jit(solution)/shard_map/ppermute | solution.py:444
  222.9 4.1 collective-permute-start.20
  227.1 43.7 %collective-permute-start.26 = (bf16[128,2048]{1,0:T(8,128)(2,1)S(1)}, bf16[128,2048]{1,0:T(8,128)(2,1)S(1)}, u32[]{:S(2)}, u32[]{:S(2)}) collective-permute-start(bf16[128,2048]{1,0:T(8,128)(2,1)S(1)} %slice.543), channel_id=1, source_target_pairs={{0,2},{1,3},{2,0},{3,1},{4,6},{5,7},{6,4},{7,5},{8,10},{9,11},{10,... | collective-permute-start | bytes 1572872 | tf_op jit(solution)/shard_map/ppermute | solution.py:448
  229.4 40.6 %collective-permute-start.30 = (bf16[256,1024]{1,0:T(8,128)(2,1)S(1)}, bf16[256,1024]{1,0:T(8,128)(2,1)S(1)}, u32[]{:S(2)}, u32[]{:S(2)}) collective-permute-start(bf16[256,1024]{1,0:T(8,128)(2,1)S(1)} %convolution_convert_fusion.6), channel_id=1, source_target_pairs={{0,1},{1,0},{2,3},{3,2},{4,5},{5,4},{6,7},{7,6},{8,9},{9,8},{10,11... | collective-permute-start | bytes 1572872 | tf_op jit(solution)/shard_map/ppermute | solution.py:444
  246.2 66.2 %collective-permute-start.38 = (bf16[1,1408,256]{2,1,0:T(8,128)(2,1)S(1)}, bf16[1,1408,256]{2,1,0:T(8,128)(2,1)S(1)}, u32[]{:S(2)}, u32[]{:S(2)}) collective-permute-start(bf16[1,1408,256]{2,1,0:T(8,128)(2,1)S(1)} %add_convert_fusion.11), channel_id=1, source_target_pairs={{0,16},{4,20},{8,24},{12,28},{16,0},{20,4},{24,8},{28,12},{1,17},{... | collective-permute-start | bytes 2162696 | tf_op jit(solution)/shard_map/ppermute | solution.py:467
  263.1 107.6 %collective-permute-start.44 = (bf16[2,256,1408]{2,1,0:T(8,128)(2,1)S(1)}, bf16[2,256,1408]{2,1,0:T(8,128)(2,1)S(1)}, u32[]{:S(2)}, u32[]{:S(2)}) collective-permute-start(bf16[2,256,1408]{2,1,0:T(8,128)(2,1)S(1)} %add_convert_fusion.1), channel_id=1, source_target_pairs={{0,8},{4,12},{8,0},{12,4},{16,24},{20,28},{24,16},{28,20},{1,9},{5... | collective-permute-start | bytes 4325384 | tf_op jit(solution)/shard_map/ppermute | solution.py:467
  263.5 38.3 %collective-permute-start.35 = (bf16[2,256,1408]{2,1,0:T(8,128)(2,1)S(1)}, bf16[2,256,1408]{2,1,0:T(8,128)(2,1)S(1)}, u32[]{:S(2)}, u32[]{:S(2)}) collective-permute-start(bf16[2,256,1408]{2,1,0:T(8,128)(2,1)S(1)} %add_convert_fusion.2), channel_id=1, source_target_pairs={{0,4},{4,0},{8,12},{12,8},{16,20},{20,16},{24,28},{28,24},{1,5},{5... | collective-permute-start | bytes 4325384 | tf_op jit(solution)/shard_map/ppermute | solution.py:467
  270.1 26.1 %collective-permute-start.36 = (bf16[8,128,512]{2,1,0:T(8,128)(2,1)S(1)}, bf16[8,128,512]{2,1,0:T(8,128)(2,1)S(1)}, u32[]{:S(2)}, u32[]{:S(2)}) collective-permute-start(bf16[8,128,512]{2,1,0:T(8,128)(2,1)S(1)} %slice.660), channel_id=1, source_target_pairs={{0,2},{1,3},{2,0},{3,1},{4,6},{5,7},{6,4},{7,5},{8,10},{9,11},{10,... | collective-permute-start | bytes 3145736 | tf_op jit(solution)/shard_map/ppermute | solution.py:448
  275.3 30.7 %collective-permute-start.34 = (bf16[256,1024]{1,0:T(8,128)(2,1)S(1)}, bf16[256,1024]{1,0:T(8,128)(2,1)S(1)}, u32[]{:S(2)}, u32[]{:S(2)}) collective-permute-start(bf16[256,1024]{1,0:T(8,128)(2,1)S(1)} %pad_maximum_fusion.10), channel_id=1, source_target_pairs={{0,2},{1,3},{2,0},{3,1},{4,6},{5,7},{6,4},{7,5},{8,10},{9,11},{10,... | collective-permute-start | bytes 1572872 | tf_op jit(solution)/shard_map/ppermute | solution.py:448
  296.2 62.2 %collective-permute-start.40 = (bf16[4,1024,256]{2,1,0:T(8,128)(2,1)S(1)}, bf16[4,1024,256]{2,1,0:T(8,128)(2,1)S(1)}, u32[]{:S(2)}, u32[]{:S(2)}) collective-permute-start(bf16[4,1024,256]{2,1,0:T(8,128)(2,1)S(1)} %grad_by_columns.6), channel_id=1, source_target_pairs={{0,4},{4,0},{8,12},{12,8},{16,20},{20,16},{24,28},{28,24},{1,5},{5... | collective-permute-start | bytes 6291464 | tf_op jit(solution)/shard_map/ppermute | solution.py:467
  301.7 55.5 %collective-permute-start.37 = (bf16[4,128,512]{2,1,0:T(8,128)(2,1)S(1)}, bf16[4,128,512]{2,1,0:T(8,128)(2,1)S(1)}, u32[]{:S(2)}, u32[]{:S(2)}) collective-permute-start(bf16[4,128,512]{2,1,0:T(8,128)(2,1)S(1)} %slice.663), channel_id=1, source_target_pairs={{0,4},{4,0},{8,12},{12,8},{16,20},{20,16},{24,28},{28,24},{1,5},{5... | collective-permute-start | bytes 1572872 | tf_op jit(solution)/shard_map/ppermute | solution.py:467
  306.1 67.4 %collective-permute-start.43 = (bf16[1,256,1408]{2,1,0:T(8,128)(2,1)S(1)}, bf16[1,256,1408]{2,1,0:T(8,128)(2,1)S(1)}, u32[]{:S(2)}, u32[]{:S(2)}) collective-permute-start(bf16[1,256,1408]{2,1,0:T(8,128)(2,1)S(1)} %add_convert_fusion.10), channel_id=1, source_target_pairs={{0,16},{4,20},{8,24},{12,28},{16,0},{20,4},{24,8},{28,12},{1,17},{... | collective-permute-start | bytes 2162696 | tf_op jit(solution)/shard_map/ppermute | solution.py:467
  312.4 45.3 %collective-permute-start.41 = (bf16[256,1024]{1,0:T(8,128)(2,1)S(1)}, bf16[256,1024]{1,0:T(8,128)(2,1)S(1)}, u32[]{:S(2)}, u32[]{:S(2)}) collective-permute-start(bf16[256,1024]{1,0:T(8,128)(2,1)S(1)} %multiply_convert_fusion.1), channel_id=1, source_target_pairs={{0,1},{1,0},{2,3},{3,2},{4,5},{5,4},{6,7},{7,6},{8,9},{9,8},{10,11... | collective-permute-start | bytes 1572872 | tf_op jit(solution)/shard_map/ppermute | solution.py:444
  357.3 7.7 %collective-permute-start.39 = (bf16[2,128,512]{2,1,0:T(8,128)(2,1)S(1)}, bf16[2,128,512]{2,1,0:T(8,128)(2,1)S(1)}, u32[]{:S(2)}, u32[]{:S(2)}) collective-permute-start(bf16[2,128,512]{2,1,0:T(8,128)(2,1)S(1)} %add_convert_fusion.17), channel_id=1, source_target_pairs={{0,8},{4,12},{8,0},{12,4},{16,24},{20,28},{24,16},{28,20},{1,9},{5... | collective-permute-start | bytes 786440 | tf_op jit(solution)/shard_map/ppermute | solution.py:467
  365.0 11.0 %collective-permute-start.42 = (bf16[1,128,512]{2,1,0:T(8,128)(2,1)S(1)}, bf16[1,128,512]{2,1,0:T(8,128)(2,1)S(1)}, u32[]{:S(2)}, u32[]{:S(2)}) collective-permute-start(bf16[1,128,512]{2,1,0:T(8,128)(2,1)S(1)} %add_convert_fusion.20), channel_id=1, source_target_pairs={{0,16},{4,20},{8,24},{12,28},{16,0},{20,4},{24,8},{28,12},{1,17},{... | collective-permute-start | bytes 393224 | tf_op jit(solution)/shard_map/ppermute | solution.py:467
  376.5 6.0 %collective-permute-start.46 = (bf16[128,512]{1,0:T(8,128)(2,1)S(1)}, bf16[128,512]{1,0:T(8,128)(2,1)S(1)}, u32[]{:S(2)}, u32[]{:S(2)}) collective-permute-start(bf16[128,512]{1,0:T(8,128)(2,1)S(1)} %pad_maximum_fusion.16), channel_id=1, source_target_pairs={{0,2},{1,3},{2,0},{3,1},{4,6},{5,7},{6,4},{7,5},{8,10},{9,11},{10,... | collective-permute-start | bytes 393224 | tf_op jit(solution)/shard_map/ppermute | solution.py:448
  382.5 9.7 %collective-permute-start.48 = (bf16[256,512]{1,0:T(8,128)(2,1)S(1)}, bf16[256,512]{1,0:T(8,128)(2,1)S(1)}, u32[]{:S(2)}, u32[]{:S(2)}) collective-permute-start(bf16[256,512]{1,0:T(8,128)(2,1)S(1)} %pad_maximum_fusion.13), channel_id=1, source_target_pairs={{0,1},{1,0},{2,3},{3,2},{4,5},{5,4},{6,7},{7,6},{8,9},{9,8},{10,11... | collective-permute-start | bytes 786440 | tf_op jit(solution)/shard_map/ppermute | solution.py:444
  386.5 5.1 %collective-permute-start.45 = (f32[2048]{0:T(1024)S(1)}, f32[2048]{0:T(1024)S(1)}, u32[]{:S(2)}, u32[]{:S(2)}) collective-permute-start(f32[2048]{0:T(1024)S(1)} %get-tuple-element.232), channel_id=1, source_target_pairs={{0,2},{1,3},{2,0},{3,1},{4,6},{5,7},{6,4},{7,5},{8,10},{9,11},{10,... | collective-permute-start | bytes 24584 | tf_op jit(solution)/shard_map/ppermute | solution.py:448
  388.0 15.1 %collective-permute-start.52 = (bf16[4,64,1024]{2,1,0:T(8,128)(2,1)}, bf16[4,64,1024]{2,1,0:T(8,128)(2,1)}, u32[]{:S(2)}, u32[]{:S(2)}) collective-permute-start(bf16[4,64,1024]{2,1,0:T(8,128)(2,1)} %pad_maximum_fusion.11), channel_id=1, source_target_pairs={{0,4},{4,0},{8,12},{12,8},{16,20},{20,16},{24,28},{28,24},{1,5},{5... | collective-permute-start | bytes 1572872 | tf_op jit(solution)/shard_map/ppermute | solution.py:467
  389.1 47.2 %collective-permute-start.56 = (bf16[1,256,1408]{2,1,0:T(8,128)(2,1)}, bf16[1,256,1408]{2,1,0:T(8,128)(2,1)}, u32[]{:S(2)}, u32[]{:S(2)}) collective-permute-start(bf16[1,256,1408]{2,1,0:T(8,128)(2,1)} %add_convert_fusion.9), channel_id=1, source_target_pairs={{0,16},{4,20},{8,24},{12,28},{16,0},{20,4},{24,8},{28,12},{1,17},{... | collective-permute-start | bytes 2162696 | tf_op jit(solution)/shard_map/ppermute | solution.py:467
  389.8 44.8 %collective-permute-start.57 = (bf16[2,1024,256]{2,1,0:T(8,128)(2,1)}, bf16[2,1024,256]{2,1,0:T(8,128)(2,1)}, u32[]{:S(2)}, u32[]{:S(2)}) collective-permute-start(bf16[2,1024,256]{2,1,0:T(8,128)(2,1)} %add_convert_fusion.4), channel_id=1, source_target_pairs={{0,8},{4,12},{8,0},{12,4},{16,24},{20,28},{24,16},{28,20},{1,9},{5... | collective-permute-start | bytes 3145736 | tf_op jit(solution)/shard_map/ppermute | solution.py:467
  391.6 33.2 %collective-permute-start.51 = (bf16[4,128,1024]{2,1,0:T(8,128)(2,1)}, bf16[4,128,1024]{2,1,0:T(8,128)(2,1)}, u32[]{:S(2)}, u32[]{:S(2)}) collective-permute-start(bf16[4,128,1024]{2,1,0:T(8,128)(2,1)} %grad_by_rows.10), channel_id=1, source_target_pairs={{0,4},{4,0},{8,12},{12,8},{16,20},{20,16},{24,28},{28,24},{1,5},{5... | collective-permute-start | bytes 3145736 | tf_op jit(solution)/shard_map/ppermute | solution.py:467
  392.3 1.3 collective-permute-start.47
  406.9 25.8 %collective-permute-start.49 = (f32[4,1,160]{2,0,1:T(4,128)S(1)}, f32[4,1,160]{2,0,1:T(4,128)S(1)}, u32[]{:S(2)}, u32[]{:S(2)}) collective-permute-start(f32[4,1,160]{2,0,1:T(4,128)S(1)} %maximum_bitcast_fusion.1), channel_id=1, source_target_pairs={{0,4},{4,0},{8,12},{12,8},{16,20},{20,16},{24,28},{28,24},{1,5},{5... | collective-permute-start | bytes 7688 | tf_op jit(solution)/shard_map/ppermute | solution.py:467
  409.1 32.2 %collective-permute-start.55 = (bf16[2,64,1024]{2,1,0:T(8,128)(2,1)S(1)}, bf16[2,64,1024]{2,1,0:T(8,128)(2,1)S(1)}, u32[]{:S(2)}, u32[]{:S(2)}) collective-permute-start(bf16[2,64,1024]{2,1,0:T(8,128)(2,1)S(1)} %add_convert_fusion.16), channel_id=1, source_target_pairs={{0,8},{4,12},{8,0},{12,4},{16,24},{20,28},{24,16},{28,20},{1,9},{5... | collective-permute-start | bytes 786440 | tf_op jit(solution)/shard_map/ppermute | solution.py:467
  424.9 7.6 %collective-permute-start.50 = (bf16[4,64,512]{2,1,0:T(8,128)(2,1)S(1)}, bf16[4,64,512]{2,1,0:T(8,128)(2,1)S(1)}, u32[]{:S(2)}, u32[]{:S(2)}) collective-permute-start(bf16[4,64,512]{2,1,0:T(8,128)(2,1)S(1)} %pad_maximum_fusion.14), channel_id=1, source_target_pairs={{0,4},{4,0},{8,12},{12,8},{16,20},{20,16},{24,28},{28,24},{1,5},{5... | collective-permute-start | bytes 786440 | tf_op jit(solution)/shard_map/ppermute | solution.py:467
  432.4 35.6 %collective-permute-start.62 = (bf16[2,128,1024]{2,1,0:T(8,128)(2,1)S(1)}, bf16[2,128,1024]{2,1,0:T(8,128)(2,1)S(1)}, u32[]{:S(2)}, u32[]{:S(2)}) collective-permute-start(bf16[2,128,1024]{2,1,0:T(8,128)(2,1)S(1)} %add_convert_fusion.13), channel_id=1, source_target_pairs={{0,8},{4,12},{8,0},{12,4},{16,24},{20,28},{24,16},{28,20},{1,9},{5... | collective-permute-start | bytes 1572872 | tf_op jit(solution)/shard_map/ppermute | solution.py:467
  432.7 30.0 %collective-permute-start.54 = (bf16[2,64,512]{2,1,0:T(8,128)(2,1)S(1)}, bf16[2,64,512]{2,1,0:T(8,128)(2,1)S(1)}, u32[]{:S(2)}, u32[]{:S(2)}) collective-permute-start(bf16[2,64,512]{2,1,0:T(8,128)(2,1)S(1)} %add_convert_fusion.19), channel_id=1, source_target_pairs={{0,8},{4,12},{8,0},{12,4},{16,24},{20,28},{24,16},{28,20},{1,9},{5... | collective-permute-start | bytes 393224 | tf_op jit(solution)/shard_map/ppermute | solution.py:467
  434.6 29.8 %collective-permute-start.53 = (bf16[2,1,160]{2,0,1:T(2,128)(2,1)S(1)}, bf16[2,1,160]{2,0,1:T(2,128)(2,1)S(1)}, u32[]{:S(2)}, u32[]{:S(2)}) collective-permute-start(bf16[2,1,160]{2,0,1:T(2,128)(2,1)S(1)} %fusion.70), channel_id=1, source_target_pairs={{0,8},{4,12},{8,0},{12,4},{16,24},{20,28},{24,16},{28,20},{1,9},{5... | collective-permute-start | bytes 1928 | tf_op jit(solution)/shard_map/ppermute | solution.py:467
  436.4 32.8 %collective-permute-start.61 = (bf16[1,1024,256]{2,1,0:T(8,128)(2,1)S(1)}, bf16[1,1024,256]{2,1,0:T(8,128)(2,1)S(1)}, u32[]{:S(2)}, u32[]{:S(2)}) collective-permute-start(bf16[1,1024,256]{2,1,0:T(8,128)(2,1)S(1)} %add_convert_fusion.12), channel_id=1, source_target_pairs={{0,16},{4,20},{8,24},{12,28},{16,0},{20,4},{24,8},{28,12},{1,17},{... | collective-permute-start | bytes 1572872 | tf_op jit(solution)/shard_map/ppermute | solution.py:467
  443.0 28.6 %collective-permute-start.60 = (bf16[1,64,1024]{2,1,0:T(8,128)(2,1)S(1)}, bf16[1,64,1024]{2,1,0:T(8,128)(2,1)S(1)}, u32[]{:S(2)}, u32[]{:S(2)}) collective-permute-start(bf16[1,64,1024]{2,1,0:T(8,128)(2,1)S(1)} %add_convert_fusion.18), channel_id=1, source_target_pairs={{0,16},{4,20},{8,24},{12,28},{16,0},{20,4},{24,8},{28,12},{1,17},{... | collective-permute-start | bytes 393224 | tf_op jit(solution)/shard_map/ppermute | solution.py:467
  464.3 9.7 %collective-permute-start.59 = (bf16[1,64,512]{2,1,0:T(8,128)(2,1)S(1)}, bf16[1,64,512]{2,1,0:T(8,128)(2,1)S(1)}, u32[]{:S(2)}, u32[]{:S(2)}) collective-permute-start(bf16[1,64,512]{2,1,0:T(8,128)(2,1)S(1)} %add_convert_fusion.21), channel_id=1, source_target_pairs={{0,16},{4,20},{8,24},{12,28},{16,0},{20,4},{24,8},{28,12},{1,17},{... | collective-permute-start | bytes 196616 | tf_op jit(solution)/shard_map/ppermute | solution.py:467
  465.0 11.1 %collective-permute-start.58 = (bf16[1,1,160]{2,0,1:T(2,128)(2,1)S(1)}, bf16[1,1,160]{2,0,1:T(2,128)(2,1)S(1)}, u32[]{:S(2)}, u32[]{:S(2)}) collective-permute-start(bf16[1,1,160]{2,0,1:T(2,128)(2,1)S(1)} %fusion.77), channel_id=1, source_target_pairs={{0,16},{4,20},{8,24},{12,28},{16,0},{20,4},{24,8},{28,12},{1,17},{... | collective-permute-start | bytes 968 | tf_op jit(solution)/shard_map/ppermute | solution.py:467
  469.1 12.4 %collective-permute-start.63 = (bf16[1,128,1024]{2,1,0:T(8,128)(2,1)S(1)}, bf16[1,128,1024]{2,1,0:T(8,128)(2,1)S(1)}, u32[]{:S(2)}, u32[]{:S(2)}) collective-permute-start(bf16[1,128,1024]{2,1,0:T(8,128)(2,1)S(1)} %add_convert_fusion.15), channel_id=1, source_target_pairs={{0,16},{4,20},{8,24},{12,28},{16,0},{20,4},{24,8},{28,12},{1,17},{... | collective-permute-start | bytes 786440 | tf_op jit(solution)/shard_map/ppermute | solution.py:467
  (73 other events, 874.1 us)

commit v2 on v1

--- a/solution.py
+++ b/solution.py
@@ -27,20 +27,6 @@
     return lax.dot_general(left, right, dims, preferred_element_type=F32)
 
 
-def first_of_segment(token, starts):
-    found = jnp.zeros_like(token)
-    for start in starts:
-        found = jnp.maximum(found, jnp.where(token >= start, start, 0))
-    return found
-
-
-def angles(position):
-    halfway = HD // 2
-    freq = 10000.0 ** (-(2.0 * jnp.arange(halfway, dtype=F32)) / HD)
-    theta = position[:, None] * freq[None, :]
-    return jnp.cos(theta), jnp.sin(theta)
-
-
 def at_index(values, index, axis, keepdims=True):
     start = [jnp.int32(0)] * values.ndim
     start[axis] = index
@@ -59,43 +45,112 @@
     return inverse * (inner - scaled * jnp.mean(inner * scaled, axis=-1, keepdims=True))
 
 
-def key_bias(meta, slot, qi_ref, ql_ref, keys, rows):
-    block = keys // 4
-    row = lax.broadcasted_iota(jnp.int32, (keys, rows), 0)
-    which = row // block
-    other = ((which & 1) << 1) | (which >> 1)
-    token = meta[0, slot] + (meta[2, 0] ^ other) * block + (row & (block - 1))
-    allowed = (token <= qi_ref[0:1, :]) & (token >= ql_ref[0:1, :])
+def place_in_kernel():
+    return lax.axis_index("seq").astype(jnp.int32), lax.axis_index("tensor").astype(jnp.int32)
+
+
+def group_block(row, own):
+    block = lax.div(row, jnp.int32(own))
+    return ((block & 1) << 1) | (block >> 1), row - block * own
+
+
+def first_in_kernel(token, lengths):
+    found = jnp.zeros_like(token)
+    start = jnp.int32(0)
+    for i in range(lengths.shape[0] - 1):
+        start = start + lengths[i]
+        found = jnp.maximum(found, jnp.where(token >= start, start, 0))
+    return found
+
+
+def angles_in_kernel(rows, own, lengths, freq_ref):
+    seq, mine = place_in_kernel()
+    other, within = group_block(lax.broadcasted_iota(jnp.int32, (rows, HD // 2), 0), own)
+    token = seq * (4 * own) + (mine ^ other) * own + within
+    theta = (token - first_in_kernel(token, lengths)).astype(F32) * freq_ref[0:1, :]
+    return jnp.cos(theta), jnp.sin(theta)
+
+
+def slot_of(slot, count, seq):
+    place = jnp.where((seq & 1) == 0, seq >> 1, count - 1 - (seq >> 1))
+    step = (slot + 1) >> 1
+    place = (place + jnp.where((slot & 1) == 1, -step, step)) & (count - 1)
+    return seq_at(place, count)
+
+
+def slot_state(lengths, slot, count, rows):
+    seq, _ = place_in_kernel()
+    source = slot_of(slot, count, seq)
+    first = first_in_kernel(seq * rows, lengths)
+    last = first_in_kernel(seq * rows + rows - 1, lengths)
+    base = source * rows
+    needed = (source <= seq) & (source >= lax.div(first, jnp.int32(rows)))
+    bounded = (source == seq) | (base < last)
+    return base, needed, bounded
+
+
+def key_bias(lengths, base, keys, rows):
+    seq, mine = place_in_kernel()
+    own = rows // 4
+    other, within = group_block(lax.broadcasted_iota(jnp.int32, (keys, rows), 0), own)
+    token = base + (mine ^ other) * own + within
+    other, within = group_block(lax.broadcasted_iota(jnp.int32, (8, rows), 1), own)
+    query = seq * rows + (mine ^ other) * own + within
+    low = first_in_kernel(query, lengths)
+    allowed = (token <= query[0:1, :]) & (token >= low[0:1, :])
     return jnp.where(allowed, 0.0, NEG)
 
 
-def fwd_kernel(heads, first, last, slot, meta, q_ref, a_ref, b_ref, qi_ref, ql_ref, *refs):
-    if not first:
-        held, refs = refs[:3], refs[3:]
-    if last:
-        o_ref, ot_ref, lse_ref, m_s, l_s, acc_s, bias_s = refs
-    else:
-        m_s, l_s, acc_s, bias_s = refs
-    step = pl.program_id(0)
-    slot = slot + step
-
-    @pl.when(step == 0)
+def keys_kernel(lengths, x_ref, gain_ref, w_ref, freq_ref, out_ref, normed_ref):
+    values = x_ref[...].astype(F32)
+    inverse = lax.rsqrt(jnp.mean(values * values, axis=-1, keepdims=True) + EPS)
+    normed = (values * inverse * gain_ref[...]).astype(BF16)
+    normed_ref[...] = normed
+    raw = dot(normed, w_ref[...])
+    cos, sin = angles_in_kernel(x_ref.shape[0], x_ref.shape[0], lengths, freq_ref)
+    mid = HD // 2
+    former, latter = raw[:, :mid], raw[:, mid:HD]
+    out_ref[:, :mid] = (former * cos - latter * sin).astype(BF16)
+    out_ref[:, mid:HD] = (latter * cos + former * sin).astype(BF16)
+    out_ref[:, HD:] = raw[:, HD:].astype(BF16)
+
+
+def own_keys(lengths, values, gain, weight, freq):
+    own, depth = values.shape
+    whole = lambda *shape: pl.BlockSpec(shape, lambda i, m: (0,) * len(shape))
+    return pl.pallas_call(
+        keys_kernel,
+        grid_spec=pltpu.PrefetchScalarGridSpec(
+            num_scalar_prefetch=1,
+            grid=(1,),
+            in_specs=[whole(own, depth), whole(1, depth), whole(*weight.shape), whole(1, HD // 2)],
+            out_specs=[whole(own, 2 * HD), whole(own, depth)],
+        ),
+        out_shape=[jax.ShapeDtypeStruct((own, 2 * HD), BF16), jax.ShapeDtypeStruct((own, depth), BF16)],
+        compiler_params=pltpu.CompilerParams(vmem_limit_bytes=16 * MIB),
+        cost_estimate=BRIEF,
+        name="own_keys",
+    )(lengths, values, gain, weight, freq)
+
+
+def fwd_kernel(heads, lengths, q_ref, a_ref, b_ref, o_ref, ot_ref, lse_ref, m_s, l_s, acc_s, bias_s):
+    slot = pl.program_id(0)
+    count = pl.num_programs(0)
+    keys, rows = bias_s.shape
+    base, needed, bounded = slot_state(lengths, slot, count, rows)
+
+    @pl.when(slot == 0)
     def _():
-        if first:
-            m_s[...] = jnp.full_like(m_s, NEG)
-            l_s[...] = jnp.zeros_like(l_s)
-            acc_s[...] = jnp.zeros_like(acc_s)
-        else:
-            m_s[...] = held[0][...]
-            l_s[...] = held[1][...]
-            acc_s[...] = held[2][...]
+        m_s[...] = jnp.full_like(m_s, NEG)
+        l_s[...] = jnp.zeros_like(l_s)
+        acc_s[...] = jnp.zeros_like(acc_s)
 
     def tile(masked):
         key = jnp.concatenate([a_ref[0, :, :HD], b_ref[0, :, :HD]], axis=0)
         value = jnp.concatenate([a_ref[0, :, HD:], b_ref[0, :, HD:]], axis=0)
         value_t = value.T
         if masked:
-            bias_s[...] = key_bias(meta, slot, qi_ref, ql_ref, *bias_s.shape)
+            bias_s[...] = key_bias(lengths, base, keys, rows)
 
         def score(h):
             return dot(key, q_ref[:, h * HD : (h + 1) * HD], NT)
@@ -115,63 +170,56 @@
             m_s[h, 0:1, :] = new
             acc_s[h] = acc_s[h] * alpha + dot(value_t, weight.astype(BF16))
 
-    pl.when(meta[1, slot] == 1)(lambda: tile(False))
-    pl.when(meta[1, slot] == 2)(lambda: tile(True))
-
-    if last:
-
-        @pl.when(step == pl.num_programs(0) - 1)
-        def _():
-            for h in range(heads):
-                total = l_s[h, 0:1, :]
-                out_t = (acc_s[h] / total).astype(BF16)
-                ot_ref[h * HD : (h + 1) * HD, :] = out_t
-                o_ref[:, h * HD : (h + 1) * HD] = out_t.T
-                lse_ref[h] = jnp.broadcast_to(m_s[h, 0:1, :] + jnp.log2(total), lse_ref.shape[1:])
-
-
-def attend(meta, slot, query, kv_a, kv_b, q_index, q_low, held, last):
+    pl.when(needed & ~bounded)(lambda: tile(False))
+    pl.when(needed & bounded)(lambda: tile(True))
+
+    @pl.when(slot == count - 1)
+    def _():
+        for h in range(heads):
+            total = l_s[h, 0:1, :]
+            out_t = (acc_s[h] / total).astype(BF16)
+            ot_ref[h * HD : (h + 1) * HD, :] = out_t
+            o_ref[:, h * HD : (h + 1) * HD] = out_t.T
+            lse_ref[h] = jnp.broadcast_to(m_s[h, 0:1, :] + jnp.log2(total), lse_ref.shape[1:])
+
+
+def attend(lengths, query, kv_a, kv_b):
     rows, width = query.shape
     heads = width // HD
     slots, half, wide = kv_a.shape
     keys = 2 * half
     whole = lambda *shape: pl.BlockSpec(shape, lambda i, m: (0,) * len(shape))
     tile = pl.BlockSpec((1, half, wide), lambda i, m: (i, 0, 0))
-    state = [(heads, 8, rows), (heads, 8, rows), (heads, HD, rows)]
-    bias = pltpu.VMEM((keys, rows), F32)
-    if last:
-        out = [((rows, width), BF16), ((width, rows), BF16), ((heads, 8, rows), F32)]
-        scratch = [pltpu.VMEM(shape, F32) for shape in state] + [bias]
-    else:
-        out = [(shape, F32) for shape in state]
-        scratch = [bias]
+    state = [(heads, 8, rows), (heads, 8, rows), (heads, HD, rows), (keys, rows)]
+    out = [((rows, width), BF16), ((width, rows), BF16), ((heads, 8, rows), F32)]
     return pl.pallas_call(
-        functools.partial(fwd_kernel, heads, not held, last, slot),
+        functools.partial(fwd_kernel, heads),
         grid_spec=pltpu.PrefetchScalarGridSpec(
             num_scalar_prefetch=1,
             grid=(slots,),
-            in_specs=[whole(rows, width), tile, tile, whole(8, rows), whole(8, rows)]
-            + [whole(*shape) for shape in state if held],
+            in_specs=[whole(rows, width), tile, tile],
             out_specs=[whole(*shape) for shape, _ in out],
-            scratch_shapes=scratch,
+            scratch_shapes=[pltpu.VMEM(shape, F32) for shape in state],
         ),
         out_shape=[jax.ShapeDtypeStruct(*o) for o in out],
         compiler_params=pltpu.CompilerParams(vmem_limit_bytes=24 * MIB),
         cost_estimate=BRIEF,
         name="attend",
-    )(meta, query, kv_a, kv_b, q_index, q_low, *held)
-
-
-def bwd_kernel(heads, meta, q_ref, do_ref, a_ref, b_ref, qi_ref, ql_ref, lse_ref, delta_ref, cos_ref, sin_ref,
+    )(lengths, query, kv_a, kv_b)
+
+
+def bwd_kernel(heads, lengths, _, q_ref, do_ref, a_ref, b_ref, lse_ref, delta_ref, cos_ref, sin_ref,
                dq_ref, da_ref, db_ref, dq_s, dk_s, dv_s, bias_s):
     slot = pl.program_id(0)
+    keys, rows = bias_s.shape
+    base, needed, bounded = slot_state(lengths, slot, pl.num_programs(0), rows)
     half = a_ref.shape[1]
 
     @pl.when(slot == 0)
     def _():
         dq_s[...] = jnp.zeros_like(dq_s)
 
-    @pl.when(meta[1, slot] == 0)
+    @pl.when(~needed)
     def _():
         da_ref[...] = jnp.zeros_like(da_ref)
         db_ref[...] = jnp.zeros_like(db_ref)
@@ -181,7 +229,7 @@
         value = jnp.concatenate([a_ref[0, :, HD:], b_ref[0, :, HD:]], axis=0)
         key_t = key.T
         if masked:
-            bias_s[...] = key_bias(meta, slot, qi_ref, ql_ref, *bias_s.shape)
+            bias_s[...] = key_bias(lengths, base, keys, rows)
         for h in range(heads):
             at = slice(h * HD, (h + 1) * HD)
             scores = dot(key, q_ref[:, at], NT) * LOG2_SCALE
@@ -204,8 +252,8 @@
         da_ref[0, :, HD:] = dv_s[:half, :].astype(BF16)
         db_ref[0, :, HD:] = dv_s[half:, :].astype(BF16)
 
-    pl.when(meta[1, slot] == 1)(lambda: tile(False))
-    pl.when(meta[1, slot] == 2)(lambda: tile(True))
+    pl.when(needed & ~bounded)(lambda: tile(False))
+    pl.when(needed & bounded)(lambda: tile(True))
 
     @pl.when(slot == pl.num_programs(0) - 1)
     def _():
@@ -218,21 +266,21 @@
             dq_ref[:, h * HD + mid : (h + 1) * HD] = (latter * cos - former * sin).astype(BF16)
 
 
-def attend_back(meta, query, grad, kv_a, kv_b, q_index, q_low, lse, delta, cos, sin):
+def attend_back(lengths, slot_out, query, grad, kv_a, kv_b, lse, delta, cos, sin):
     rows, width = query.shape
     heads = width // HD
     slots, half, wide = kv_a.shape
     keys = 2 * half
-    whole = lambda *shape: pl.BlockSpec(shape, lambda i, m: (0,) * len(shape))
-    tile = pl.BlockSpec((1, half, wide), lambda i, m: (i, 0, 0))
-    out_tile = pl.BlockSpec((1, half, wide), lambda i, m: (m[3, i], 0, 0))
+    whole = lambda *shape: pl.BlockSpec(shape, lambda i, m, o: (0,) * len(shape))
+    tile = pl.BlockSpec((1, half, wide), lambda i, m, o: (i, 0, 0))
+    out_tile = pl.BlockSpec((1, half, wide), lambda i, m, o: (o[i], 0, 0))
     return pl.pallas_call(
         functools.partial(bwd_kernel, heads),
         grid_spec=pltpu.PrefetchScalarGridSpec(
-            num_scalar_prefetch=1,
+            num_scalar_prefetch=2,
             grid=(slots,),
             in_specs=[
-                whole(rows, width), whole(rows, width), tile, tile, whole(8, rows), whole(8, rows),
+                whole(rows, width), whole(rows, width), tile, tile,
                 whole(heads, 8, rows), whole(heads, 8, rows), whole(rows, HD // 2), whole(rows, HD // 2),
             ],
             out_specs=[whole(rows, width), out_tile, out_tile],
@@ -251,7 +299,7 @@
         compiler_params=pltpu.CompilerParams(vmem_limit_bytes=32 * MIB),
         cost_estimate=BRIEF,
         name="attend_back",
-    )(meta, query, grad, kv_a, kv_b, q_index, q_low, lse, delta, cos, sin)
+    )(lengths, slot_out, query, grad, kv_a, kv_b, lse, delta, cos, sin)
 
 
 def attended_grad_kernel(gb_ref, w_ref, att_ref, out_ref, delta_ref):
@@ -290,7 +338,13 @@
     return keep.astype(BF16), send.astype(BF16)
 
 
-def project_kernel(x_ref, w_ref, cos_ref, sin_ref, out_ref):
+def project_kernel(lengths, x_ref, w_ref, freq_ref, out_ref, cos_ref, sin_ref):
+    rows = x_ref.shape[0]
+
+    @pl.when(pl.program_id(0) == 0)
+    def _():
+        cos_ref[...], sin_ref[...] = angles_in_kernel(rows, rows // 4, lengths, freq_ref)
+
     raw = dot(x_ref[...], w_ref[...])
     cos, sin = cos_ref[...], sin_ref[...]
     mid = HD // 2
@@ -299,25 +353,26 @@
     out_ref[:, mid:] = (latter * cos + former * sin).astype(BF16)
 
 
-def project_rotate(latent, weight, cos, sin):
+def project_rotate(lengths, latent, weight, freq):
     rows, rank = latent.shape
     width = weight.shape[1]
-    whole = lambda *shape: pl.BlockSpec(shape, lambda i: (0,) * len(shape))
+    whole = lambda *shape: pl.BlockSpec(shape, lambda i, m: (0,) * len(shape))
+    angle = jax.ShapeDtypeStruct((rows, HD // 2), F32)
     return pl.pallas_call(
         project_kernel,
-        grid=(width // HD,),
-        in_specs=[
-            whole(rows, rank),
-            pl.BlockSpec((rank, HD), lambda i: (0, i)),
-            whole(rows, HD // 2),
-            whole(rows, HD // 2),
-        ],
-        out_specs=pl.BlockSpec((rows, HD), lambda i: (0, i)),
-        out_shape=jax.ShapeDtypeStruct((rows, width), BF16),
+        grid_spec=pltpu.PrefetchScalarGridSpec(
+            num_scalar_prefetch=1,
+            grid=(width // HD,),
+            in_specs=[whole(rows, rank), pl.BlockSpec((rank, HD), lambda i, m: (0, i)), whole(1, HD // 2)],
+            out_specs=[
+                pl.BlockSpec((rows, HD), lambda i, m: (0, i)), whole(rows, HD // 2), whole(rows, HD // 2),
+            ],
+        ),
+        out_shape=[jax.ShapeDtypeStruct((rows, width), BF16), angle, angle],
         compiler_params=pltpu.CompilerParams(vmem_limit_bytes=10 * MIB),
         cost_estimate=BRIEF,
         name="project_rotate",
-    )(latent, weight, cos, sin)
+    )(lengths, latent, weight, freq)
 
 
 def hidden_kernel(x_ref, gate_ref, up_ref, gh_ref, hidden_ref, hidden_t_ref, gg_ref, gu_ref, gate_s, up_s):
@@ -408,12 +463,13 @@
     out_ref[0] = dot(left_ref[...], right_ref[...]).astype(BF16)
 
 
-def grad_by_columns(owner, left_t, right, count):
+def grad_by_columns(owner, left_t, right, count, part=0, parts=1):
     slots = owner.shape[0]
     rows, width = right.shape
     cut = width // count
-    tall = left_t.shape[0]
+    tall = left_t.shape[0] // parts
     if cut % 128:
+        left_t = left_t[part * tall : (part + 1) * tall]
         return in_order(dot(left_t, right).astype(BF16).reshape(tall, count, cut), owner, 1)
     return pl.pallas_call(
         columns_kernel,
@@ -421,7 +477,7 @@
             num_scalar_prefetch=1,
             grid=(slots,),
             in_specs=[
-                pl.BlockSpec((tall, rows), lambda i, o: (0, 0)),
+                pl.BlockSpec((tall, rows), lambda i, o: (part, 0)),
                 pl.BlockSpec((rows, cut), lambda i, o: (0, o[i])),
             ],
             out_specs=pl.BlockSpec((1, tall, cut), lambda i, o: (i, 0, 0)),
@@ -431,6 +487,39 @@
         cost_estimate=BRIEF,
         name="grad_by_columns",
     )(owner, left_t, right)
+
+
+def share_kernel(size, meta, x_ref, mine_ref, other_ref, turned_s):
+    turned_s[...] = x_ref[...].astype(F32).T
+    mine = meta[1, 0]
+    mine_ref[...] = turned_s[pl.ds(pl.multiple_of(mine * size, size), size), :].astype(BF16)
+    other_ref[...] = turned_s[pl.ds(pl.multiple_of((mine ^ 1) * size, size), size), :].astype(BF16)
+
+
+def share_of_columns(owner, mine, values, size, group):
+    slots = owner.shape[0]
+    rows, width = values.shape
+    cut = width // slots
+    if cut % 128:
+        turned = values.T.reshape(slots, group, size, rows)
+        return tuple(
+            in_order(at_index(turned, which, 1, keepdims=False), owner, 0).reshape(slots * size, rows)
+            for which in (mine, mine ^ 1)
+        )
+    return pl.pallas_call(
+        functools.partial(share_kernel, size),
+        grid_spec=pltpu.PrefetchScalarGridSpec(
+            num_scalar_prefetch=1,
+            grid=(slots,),
+            in_specs=[pl.BlockSpec((rows, cut), lambda i, m: (0, m[0, i]))],
+            out_specs=[pl.BlockSpec((size, rows), lambda i, m: (i, 0))] * 2,
+            scratch_shapes=[pltpu.VMEM((cut, rows), F32)],
+        ),
+        out_shape=[jax.ShapeDtypeStruct((slots * size, rows), BF16)] * 2,
+        compiler_params=pltpu.CompilerParams(vmem_limit_bytes=8 * MIB),
+        cost_estimate=BRIEF,
+        name="share_of_columns",
+    )(jnp.stack([owner, jnp.full((slots,), mine)]), values)
 
 
 def add(*parts):
@@ -542,50 +631,16 @@
     own = block_input.shape[0]
     rows = own * group
     heads = q_up.shape[1] // HD
-    place = jnp.where((seq & 1) == 0, seq >> 1, count - 1 - (seq >> 1))
-
-    starts = [jnp.int32(0)]
-    for i in range(lengths.shape[0] - 1):
-        starts.append(starts[-1] + lengths[i])
-    blocks = mine ^ jnp.array([0, 2, 1, 3], jnp.int32)
-    token = (seq * rows + blocks[:, None] * own + jnp.arange(own, dtype=jnp.int32)[None, :]).reshape(rows)
-    low = first_of_segment(token, starts)
-    cos_own, sin_own = angles((token - low)[:own].astype(F32))
-    offsets = [0]
-    for step in range(1, count // 2):
-        offsets += [-step, step]
-    offsets.append(count // 2)
-    slot_seq = seq_at((place + jnp.array(offsets, jnp.int32)) & (count - 1), count)
-    ends = first_of_segment(jnp.stack([seq * rows, seq * rows + rows - 1]), starts)
-    base = slot_seq * rows
-    needed = (slot_seq <= seq) & (slot_seq >= lax.div(ends[0], jnp.int32(rows)))
-    bounded = (slot_seq == seq) | (base < ends[1])
     bits, bits_two = bits_of(count), bits_of(count, 2)
-    apart = slot_seq ^ seq
-    slot_out = sum(((apart >> (bit.bit_length() - 1)) & 1) << (len(bits) - 1 - i) for i, bit in enumerate(bits))
-    meta = jnp.stack([base, needed * (1 + bounded), jnp.full((count,), mine), slot_out]).astype(jnp.int32)
-    q_index = jnp.broadcast_to(token[None, :], (8, rows))
-    q_low = jnp.broadcast_to(low[None, :], (8, rows))
     owner = seq ^ jnp.array(apart_of(bits), jnp.int32)
     owner_two = seq ^ jnp.array(apart_of(bits_two), jnp.int32)
 
     order = Order()
     half = count // 2
 
-    inputs = block_input.astype(F32)
-    scaled_one, inverse_one = rms_parts(inputs)
-    normed = (scaled_one * norm1_gain).astype(BF16)
-    kv_raw = dot(normed, kv_weight)
     mid = HD // 2
-    former, latter = kv_raw[:, :mid], kv_raw[:, mid:HD]
-    keyval = jnp.concatenate(
-        [
-            former * cos_own - latter * sin_own,
-            latter * cos_own + former * sin_own,
-            kv_raw[:, HD:],
-        ],
-        axis=1,
-    ).astype(BF16)
+    freq = 10000.0 ** (-(2.0 * jnp.arange(mid, dtype=F32)) / HD)[None, :]
+    keyval, normed = own_keys(lengths, block_input, norm1_gain[None, :], kv_weight, freq)
     order.ran(keyval)
     keyval_far = far(keyval)
     compressed = dot(order.after(normed), q_down)
@@ -595,21 +650,20 @@
     pair = jnp.concatenate([keyval, order.after(keyval_far)], axis=0)
     order.ran(pair)
     ahead, back = ring_shift(pair, 1, count), ring_shift(pair, -1, count)
-    pair_near = near(pair)
-    cos, sin = angles((order.after(token) - low).astype(F32))
-    order.ran(cos, sin)
-    latent_half = jnp.concatenate([latent, order.after(latent_far)], axis=0)
-    order.ran(latent_half)
-    latent_near = near(latent_half)
-    input_far = far(order.after(block_input))
-    grad_far = far(order.after(cotangent))
-    kv_a = jnp.zeros((count,) + pair.shape, BF16)
-    kv_b = jnp.zeros((count,) + pair.shape, BF16)
-
-    def put(kept, piece, slot):
-        return lax.dynamic_update_slice(kept, piece, (slot, 0, 0))
-
-    kv_a, kv_b = put(kv_a, pair[None], 0), put(kv_b, order.after(pair_near)[None], 0)
+    empty = jnp.zeros((count,) + pair.shape, BF16)
+    kv_a, kv_b = lax.dynamic_update_slice(empty, order.after(pair)[None], (0, 0, 0)), empty
+    waiting, moving = [pair[None]], []
+
+    def send_near(first):
+        piece = waiting[0] if len(waiting) == 1 else jnp.concatenate(waiting)
+        moving.append((first, near(order.after(piece))))
+        return first + piece.shape[0]
+
+    def take_near(kept):
+        first, piece = moving.pop(0)
+        return lax.dynamic_update_slice(kept, order.after(piece), (first, 0, 0))
+
+    sent = 0
     for step in range(1, half + 1):
         ahead, back = order.after(ahead, back)
         slot = 2 * step - 1
@@ -622,22 +676,31 @@
                 ahead, back = ring_shift(ahead[:own], 1, count), ring_shift(back[own:], -1, count)
         else:
             piece = jnp.concatenate([ahead, back], axis=0)[None]
-        piece_near = near(order.after(piece))
-        kv_a = put(kv_a, piece, slot)
+        waiting.append(piece)
+        if step != half - 1:
+            sent = send_near(sent)
+            waiting = []
+        kv_a = lax.dynamic_update_slice(kv_a, piece, (slot, 0, 0))
         if step == 1:
+            latent_half = jnp.concatenate([latent, order.after(latent_far)], axis=0)
+            order.ran(latent_half)
+            latent_near = near(latent_half)
+            both_far = far(jnp.concatenate(order.after(block_input, cotangent), axis=0))
+        if step == min(2, half - 1):
             latent_all = jnp.concatenate([latent_half, order.after(latent_near)], axis=0)
-            query = project_rotate(latent_all, q_up, cos, sin)
+            query, cos, sin = project_rotate(lengths, latent_all, q_up, freq)
             order.ran(query)
-        if step == half - 1:
-            input_half = jnp.concatenate([block_input, order.after(input_far)], axis=0)
-            order.ran(input_half)
-        if step == half:
-            grad_half = jnp.concatenate([cotangent, order.after(grad_far)], axis=0)
-            order.ran(grad_half)
-            grad_near = near(grad_half)
-        kv_b = put(kv_b, order.after(piece_near), slot)
+        if step > 2 and moving and step < half:
+            kv_b = take_near(kv_b)
+    while moving:
+        kv_b = take_near(kv_b)
+    both_far = order.after(both_far)
+    input_half = jnp.concatenate([block_input, both_far[:own]], axis=0)
+    grad_half = jnp.concatenate([cotangent, both_far[own:]], axis=0)
+    order.ran(input_half, grad_half)
+    grad_near = near(grad_half)
     kv_a, kv_b = order.after(kv_a, kv_b)
-    attended, attended_t, lse = attend(meta, 0, order.after(query), kv_a, kv_b, q_index, q_low, (), True)
+    attended, attended_t, lse = attend(lengths, order.after(query), kv_a, kv_b)
     order.ran(attended)
 
     def sum_half(lefts, rights, dims, meanwhile):
@@ -651,22 +714,21 @@
         return add(chip, order.after(moving)), made
 
     share = q_down.shape[0] // (count * group)
+    width = block_input.shape[1]
 
     def before_residual():
         normed_half = (rms_parts(order.after(input_half).astype(F32))[0] * norm1_gain).astype(BF16)
         scaled_q, inverse_q = rms_parts(dot(normed_half, q_down))
         order.ran(scaled_q)
 
-        def picked(which):
-            blocks = normed_half.reshape(2 * own, count, group, share)
-            return at_index(blocks, which, 2, keepdims=False).reshape(2 * own, count * share)
-
-        picked_near = near(picked(mine ^ 1))
+        picked_mine, picked_other = share_of_columns(owner, mine, normed_half, share, group)
+        order.ran(picked_mine)
+        picked_near = near(picked_other)
         grad_all = jnp.concatenate([grad_half, order.after(grad_near)], axis=0)
         grad_hidden = dot(grad_all, down_weight, NT)
         order.ran(grad_hidden)
-        picked_all = jnp.concatenate([picked(mine), order.after(picked_near)], axis=0)
-        order.ran(picked_all)
+        picked_all = jnp.concatenate([picked_mine, order.after(picked_near)], axis=1)
+        order.wait(picked_all)
         return scaled_q, inverse_q, picked_all, grad_all, grad_hidden
 
     branch, (scaled_q, inverse_q, picked, grad_all, grad_hidden) = sum_half(
@@ -712,19 +774,23 @@
     [send] = grad_by_rows(owner[half:], order.after(normed_two), [grad_gate], count)
     order.ran(send)
     gate_sum = Halving(order, bits, count, send)
+    down_sum.hop()
     grad_branch = jnp.concatenate([branch_half, order.after(branch_near)], axis=0)
     grad_attended, delta = attended_grad(grad_branch, out_weight, attended)
     order.ran(grad_attended)
-    send_out = grad_by_columns(owner[half:], order.after(attended_t), grad_branch, count)
+    send_out = grad_by_columns(owner[half:], order.after(attended_t), grad_branch, count, 0, 2)
     order.ran(send_out)
-    down_sum.hop()
+    send_out_two = grad_by_columns(owner[half:], order.after(attended_t), grad_branch, count, 1, 2)
+    order.ran(send_out_two)
     [keep] = grad_by_rows(owner[:half], order.after(normed_two), [grad_gate], count)
     order.ran(keep)
     gate_sum.keep(keep)
     up_sum.hop(go=False)
 
+    slot_out = slot_of(jnp.arange(count, dtype=jnp.int32), count, seq) ^ seq
+    slot_out = sum(((slot_out >> (bit.bit_length() - 1)) & 1) << (len(bits) - 1 - i) for i, bit in enumerate(bits))
     grad_query_raw, dkv_a, dkv_b = attend_back(
-        meta, query, order.after(grad_attended), kv_a, kv_b, q_index, q_low, lse, delta, cos, sin
+        lengths, slot_out, query, order.after(grad_attended), kv_a, kv_b, lse, delta, cos, sin
     )
     order.ran(grad_query_raw)
     dkv_near = near(dkv_b)
@@ -732,113 +798,118 @@
     latent_keep, latent_send = product([order.after(grad_query_raw)], [q_up], NT)
     order.ran(latent_send)
     latent_near = near(latent_send)
+    feed_out = add(feed_chip[:own], order.after(feed_far))
+    block_output = (residual[:own] + feed_out).astype(BF16)
+    order.ran(block_output)
     down_sum.hop()
     gate_sum.hop()
-    up_sum.go()
     chip_kv = add(dkv_a, order.after(dkv_near)).astype(BF16)
     order.ran(chip_kv)
     kv_far = far(chip_kv[:, own:])
     latent_chip = add(latent_keep, order.after(latent_near)).astype(BF16)
     order.ran(latent_chip)
-    latent_far = far(swap(latent_chip))
-    feed_out = add(feed_chip[:own], order.after(feed_far))
-    block_output = (residual[:own] + feed_out).astype(BF16)
-    order.ran(block_output)
-    keep = grad_by_columns(owner[:half], order.after(attended_t), grad_branch, count)
-    order.ran(keep)
-    out_sum = Halving(order, bits, count, order.after(send_out), keep)
+    up_sum.go()
+    keep_out = grad_by_columns(owner[:half], order.after(attended_t), grad_branch, count, 0, 2)
+    order.ran(keep_out)
+    keep_out_two = grad_by_columns(owner[:half], order.after(attended_t), grad_branch, count, 1, 2)
+    order.ran(keep_out_two)
     [send_query] = grad_by_rows(owner[half:], order.after(latent_all), [grad_query_raw], count)
     order.ran(send_query)
     [keep_query] = grad_by_rows(owner[:half], order.after(latent_all), [grad_query_raw], count)
     order.ran(keep_query)
-
+    down_grad = down_sum.finish()
     chips_kv = add(chip_kv[:, :own], order.after(kv_far)).astype(BF16)
     order.ran(chips_kv)
     kv_sum = Halving(order, bits, count, chips_kv[half:], chips_kv[:half])
+    latent_far = far(swap(order.after(latent_chip)))
     up_sum.hop()
-
+    out_sum = Halving(order, bits, count, order.after(send_out), keep_out)
+    kv_sum.hop()
     grad_latent = add(latent_chip, order.after(latent_far))
     grad_compressed = rms_back(grad_latent, scaled_q, inverse_q, q_gain).astype(BF16)
     order.ran(grad_compressed)
     compressed_near = near(grad_compressed)
-    down_grad = down_sum.finish()
     kv_sum.hop()
-
-
-    def shared(values, size):
-        blocks = values.reshape(count, group, size)
-        return at_index(blocks, mine, 1, keepdims=False)
-
+    gain_two = jnp.sum(order.after(back_two) * scaled_two, axis=0)
+    gain_q = jnp.sum(grad_latent * scaled_q, axis=0)
+    gains = jnp.concatenate([gain_two, gain_q])
+    up_grad = up_sum.finish()
     compressed_all = jnp.concatenate([grad_compressed, order.after(compressed_near)], axis=0)
-    q_down_parts = dot(picked, compressed_all, TN).astype(BF16).reshape(count, share, -1)
+    q_down_parts = dot(picked, compressed_all).astype(BF16)
     order.ran(q_down_parts)
-    q_down_parts = in_order(q_down_parts, owner, 0)
-    q_down_sum = Halving(order, bits, count, q_down_parts[half:], q_down_parts[:half])
-
-    out_sum.hop()
-    query_sum = Halving(order, bits, count, order.after(send_query), keep_query)
-    kv_sum.hop()
-    gate_sum.hop()
-    up_grad = up_sum.finish()
+    gate_sum.hop(go=False)
+
+    def by_owner(values, size):
+        blocks = lax.dynamic_slice(values.reshape(count, group, size), (0, mine, 0), (count, 1, size))
+        same = owner[:, None, None] == jnp.arange(count, dtype=jnp.int32)[None, :, None]
+        return jnp.sum(jnp.where(same, blocks[:, 0][None], 0.0), axis=1)[:, None, :]
+
     kv_own = kv_sum.finish()
     former, latter = kv_own[:, :mid], kv_own[:, mid:HD]
     grad_kv_raw = jnp.concatenate(
         [
-            former * cos_own + latter * sin_own,
-            latter * cos_own - former * sin_own,
+            former * cos[:own] + latter * sin[:own],
+            latter * cos[:own] - former * sin[:own],
             kv_own[:, HD:],
         ],
         axis=1,
     ).astype(BF16)
     order.ran(grad_kv_raw)
     kv_raw_far = far(grad_kv_raw)
+    out_sum.hop()
+    out_sum_two = Halving(order, bits, count, order.after(send_out_two), keep_out_two)
+    gate_sum.go()
+    kv_half = jnp.concatenate([grad_kv_raw, order.after(kv_raw_far)], axis=0)
+    order.ran(kv_half)
+    kv_half_near = near(kv_half)
+    q_down_parts = order.after(q_down_parts).reshape(count, share, -1)
+    q_down_sum = Halving(order, bits, count, q_down_parts[half:], q_down_parts[:half])
+    kv_half_near = order.after(kv_half_near)
+    order.ran(kv_half_near)
+    scaled_one, inverse_one = rms_parts(order.after(block_input).astype(F32))
     grad_normed = dot(grad_compressed[:own], q_down, NT) + dot(order.after(grad_kv_raw), kv_weight, NT)
     input_grad = grad_residual[:own] + rms_back(grad_normed, scaled_one, inverse_one, norm1_gain)
     gain_one = jnp.sum(grad_normed * scaled_one, axis=0)
-    order.ran(input_grad, gain_one)
+    order.ran(gain_one)
+    out_sum.hop()
     gain_far = far(gain_one)
-    kv_half = jnp.concatenate([grad_kv_raw, order.after(kv_raw_far)], axis=0)
-    order.ran(kv_half)
-    kv_half_near = near(kv_half)
+    kv_all = jnp.concatenate([kv_half, kv_half_near], axis=0)
+    kv_parts = dot(picked, order.after(kv_all)).astype(BF16)
+    order.ran(kv_parts)
+    out_sum_two.hop()
+    query_sum = Halving(order, bits, count, order.after(send_query), keep_query)
     gain_one = gain_one + order.after(gain_far)
-    gain_two = jnp.sum(back_two * scaled_two, axis=0)
-    gain_q = jnp.sum(grad_latent * scaled_q, axis=0)
-    gains = jnp.concatenate([gain_one, gain_two, gain_q])
+    gains = jnp.concatenate([gain_one, gains])
     order.ran(gains)
     gains_near = near(gains)
-    kv_parts = dot(
-        picked, jnp.concatenate([kv_half, order.after(kv_half_near)], axis=0), TN
-    ).astype(BF16).reshape(count, share, -1)
-    order.ran(kv_parts)
-    kv_parts = in_order(kv_parts, owner, 0)
+    q_down_sum.hop()
+    kv_parts = order.after(kv_parts).reshape(count, share, -1)
     kv_weight_sum = Halving(order, bits, count, kv_parts[half:], kv_parts[:half])
+    gate_grad = gate_sum.finish()
+    query_sum.hop()
     gains = gains + order.after(gains_near)
-    width = block_input.shape[1]
     gains = jnp.concatenate(
         [
-            shared(gains[:width], share),
-            shared(gains[width : 2 * width], share),
-            shared(gains[2 * width :], q_gain.shape[0] // (count * group)),
+            by_owner(gains[:width], share),
+            by_owner(gains[width : 2 * width], share),
+            by_owner(gains[2 * width :], q_gain.shape[0] // (count * group)),
         ],
-        axis=1,
+        axis=2,
     )
     order.ran(gains)
-    gains = in_order(gains, owner, 0)[:, None, :]
     gains_sum = Halving(order, bits, count, gains[half:], gains[:half])
+    kv_weight_sum.hop()
+    out_sum_two.hop()
     q_down_sum.hop()
     query_sum.hop()
+    gains_sum.hop()
     kv_weight_sum.hop()
+    out_one = out_sum.finish()
     gains_sum.hop()
-    out_sum.hop()
-    gate_grad = gate_sum.finish()
-    q_down_sum.hop()
-    kv_weight_sum.hop()
-    gains_sum.hop()
-    query_sum.hop()
-    out_weight_grad = out_sum.finish()
     q_down_grad = q_down_sum.finish()
     kv_weight_grad = kv_weight_sum.finish()
     gains = gains_sum.finish()[0]
+    out_weight_grad = jnp.concatenate([out_one, out_sum_two.finish()], axis=0)
     q_up_grad = query_sum.finish()
     return (
         block_output,

time: 490 us -> 463 us (0.945)
  waiting for transfers between devices: 198 us -> 178 us
  starting transfers between devices: 80.4 us -> 93 us
  local copies, waits for them, and re-layouts: 37.6 us -> 25.6 us
  other arithmetic: 68.1 us -> 58.4 us
  Pallas kernels: 59.9 us -> 65.3 us
    ppermute x11 -> x10, waiting for transfers between devices: 60.9 us -> 47.7 us  [far(): return lax.ppermute(values, 'tensor', [(i, i ^ 2) for i in range(4)])]
    ppermute x27 -> x30, starting transfers between devices: 56 us -> 69 us  [swap_seq(): return lax.ppermute(values, 'seq', [(i, i ^ bit) for i in range(count)])]
    dynamic_slice x7 -> x3, local copies, waits for them, and re-layouts: 12.6 us -> 2.18 us  [by_owner(): lax.dynamic_slice(values.reshape(count, group, size), (0, mine, 0), (coun...]
    pallas_call x2 -> x4, Pallas kernels: 5.98 us -> 10.9 us  [the longest x1 3.94 us: project_rotate(): pl.pallas_call(project_kernel, grid_spec=pltpu.PrefetchScalarGridSpec(num...]
    convert_element_type x18 -> x20, other arithmetic: 23.5 us -> 19 us  [hop(): send = add(*[t[cut:] for t in self.terms]).astype(BF16)]
    pallas_call x4 -> x6, Pallas kernels: 12 us -> 14.8 us  [grad_by_columns(): pl.pallas_call(columns_kernel, grid_spec=pltpu.PrefetchScalarGridSpec(num...]
    ppermute x27 -> x30, waiting for transfers between devices: 116 us -> 114 us  [swap_seq(): return lax.ppermute(values, 'seq', [(i, i ^ bit) for i in range(count)])]
    dot_general x18 -> x17, matrix products: 33 us -> 34.8 us  [dot(): return lax.dot_general(left, right, dims, preferred_element_type=F32)]
  transfers between devices with their start and end apart: 64 -> 64, of which waited for: 24 -> 30; matrix products, arithmetic and copies ran while one was open for 23% -> 21% of each run, Pallas kernels for 7% -> 10%
where the time goes in v2:
time: 463 us; the launch traced here: 458 us
  waiting for transfers between devices  178 us (38%)
  starting transfers between devices  93 us (20%)
  Pallas kernels  65.3 us (14%)
  other arithmetic  58.4 us (13%)
  matrix products  34.8 us (8%)
  local copies, waits for them, and re-layouts  25.6 us (6%)
    ppermute x30, waiting for transfers between devices, swap_seq(): return lax.ppermute(values, 'seq', [(i, i ^ bit) for i in range(count)])  114 us
    ppermute x30, starting transfers between devices, swap_seq(): return lax.ppermute(values, 'seq', [(i, i ^ bit) for i in range(count)])  69 us
    ppermute x10, waiting for transfers between devices, far(): return lax.ppermute(values, 'tensor', [(i, i ^ 2) for i in range(4)])  47.7 us
    dot_general x17, matrix products, dot(): return lax.dot_general(left, right, dims, preferred_element_type=F32)  34.8 us
    convert_element_type x20, other arithmetic, hop(): send = add(*[t[cut:] for t in self.terms]).astype(BF16)  19 us
    pallas_call x6, Pallas kernels, grad_by_rows(): pl.pallas_call(rows_kernel, grid_spec=pltpu.PrefetchScalarGridSpec(num_sc...  18.4 us
    unnamed x164, local copies, waits for them, and re-layouts  17.1 us
    add x11, other arithmetic, add(): total = total + part.astype(F32)  16.4 us
  transfers between devices with their start and end apart: 64, of which 30 were waited for; matrix products, arithmetic and copies ran while one was open for 21% of the time, Pallas kernels for 10%

profile of v2, /device:TPU:0, one launch (start us, length us, event | category | flops | bytes accessed | tf_op | source)
XLA Modules:
  0.0 457.6 jit_solution(15631040337601281249)
XLA Ops:
  6.0 3.0 collective-permute-start.1
  9.0 3.0 multiply_reduce_fusion.6
  16.5 3.5 collective-permute-done.2
  25.5 2.2 collective-permute-done.5
  31.6 3.9 project_rotate.1
  39.4 2.8 collective-permute-done.10
  44.3 4.9 %collective-permute-done.4 = bf16[256,2048]{1,0:T(8,128)(2,1)S(1)} collective-permute-done((bf16[256,2048]{1,0:T(8,128)(2,1)S(1)}, bf16[256,2048]{1,0:T(8,128)(2,1)S(1)}, u32[]{:S(2)}, u32[]{:S(2)}) %collective-permute-start.4) | collective-permute-done | bytes 1048608 | tf_op jit(solution)/shard_map/ppermute | solution.py:537
  50.7 3.9 attend.1
  54.7 2.2 convolution_convert_fusion
  57.5 3.6 fusion.3
  67.9 5.1 %fusion.56.gh_ref = f32[512,1408]{1,0:T(8,128)} fusion(bf16[1408,2048]{1,0:T(8,128)(2,1)S(1)} %bitcast.119, bf16[256,2048]{1,0:T(8,128)(2,1)S(1)} %collective-permute-done.17, bf16[128,2048]{1,0:T(8,128)(2,1)S(1)} %copy-done.48, bf16[128,2048]{1,0:T(8,128)(2,1)S(1)} %copy-done.45), kind=kOutput, calls=%fused_computation.186 | convolution fusion | flops 2959081472 | bytes 10747904 | tf_op jit(solution)/shard_map/dot_general | solution.py:27
  73.1 15.1 %collective-permute-done.16 = bf16[256,2048]{1,0:T(8,128)(2,1)S(1)} collective-permute-done((bf16[256,2048]{1,0:T(8,128)(2,1)S(1)}, bf16[256,2048]{1,0:T(8,128)(2,1)S(1)}, u32[]{:S(2)}, u32[]{:S(2)}) %collective-permute-start.16) | collective-permute-done | bytes 1048608 | tf_op jit(solution)/shard_map/ppermute | solution.py:537
  95.1 2.6 copy-done.18
  97.7 12.5 %hidden_units.1 = (bf16[512,1408]{1,0:T(8,128)(2,1)S(1)}, bf16[1408,512]{1,0:T(8,128)(2,1)S(1)}, bf16[512,1408]{1,0:T(8,128)(2,1)S(1)}, bf16[512,1408]{1,0:T(8,128)(2,1)S(1)}) custom-call(bf16[512,2048]{1,0:T(8,128)(2,1)S(1)} %pad_maximum_fusion.1.x_ref.left_ref, bf16[2048,1408]{1,0:T(8,128)(2,1)S(1)} %copy-done.18, bf16[2048,1408]{1,0:T(8,128)(2,1)} %up_ref.1, ...), custom_call_target="tpu_custom_call" | custom-call | flops 1000 | bytes 1000 | tf_op jit(solution)/shard_map/hidden_units/pallas_call | solution.py:414
  110.2 4.1 grad_by_columns.6
  114.2 2.7 collective-permute-start.25
  116.9 2.9 grad_by_columns.7
  121.5 4.3 grad_by_rows.6
  125.7 5.7 %collective-permute-start.26 = (bf16[4,256,1408]{2,1,0:T(8,128)(2,1)}, bf16[4,256,1408]{2,1,0:T(8,128)(2,1)}, u32[]{:S(2)}, u32[]{:S(2)}) collective-permute-start(bf16[4,256,1408]{2,1,0:T(8,128)(2,1)} %grad_by_rows.6), channel_id=1, source_target_pairs={{0,8},{4,12},{8,0},{12,4},{16,24},{20,28},{24,16},{28,20},{1,9},{5... | collective-permute-start | bytes 8650760 | tf_op jit(solution)/shard_map/ppermute | solution.py:556
  131.5 3.1 grad_by_rows.7
  151.6 20.5 %collective-permute-done.22 = bf16[256,2048]{1,0:T(8,128)(2,1)S(1)} collective-permute-done((bf16[256,2048]{1,0:T(8,128)(2,1)S(1)}, bf16[256,2048]{1,0:T(8,128)(2,1)S(1)}, u32[]{:S(2)}, u32[]{:S(2)}) %collective-permute-start.22) | collective-permute-done | bytes 1048608 | tf_op jit(solution)/shard_map/ppermute | solution.py:537
  174.0 2.6 fusion.57
  177.2 4.9 %multiply_reduce_fusion.5 = (f32[256]{0:T(256)S(1)}, f32[256,1024]{1,0:T(8,128)}) fusion(bf16[256,2048]{1,0:T(8,128)(2,1)} %copy-done.25, bf16[2048,1024]{1,0:T(8,128)(2,1)} %param.18), kind=kOutput, calls=%fused_computation.76 | convolution fusion | flops 1074265856 | bytes 6292480 | tf_op jit(solution)/shard_map/dot_general | solution.py:27
  183.7 3.4 grad_by_rows.8
  187.2 2.9 add_convert_fusion.3
  192.9 3.7 attended_grad.1
  196.6 1.9 grad_by_columns.8
  199.5 1.9 grad_by_columns.9
  201.5 3.2 grad_by_rows.9
  204.7 2.9 add_convert_fusion.2
  207.7 5.2 %attend_back.1 = (bf16[512,1024]{1,0:T(8,128)(2,1)S(1)}, bf16[8,256,512]{2,1,0:T(8,128)(2,1)S(1)}, bf16[8,256,512]{2,1,0:T(8,128)(2,1)S(1)}) custom-call(s32[4]{0:T(128)S(1)} %copy-done.38, s32[8]{0:T(128)S(1)} %get-tuple-element.299._, bf16[512,1024]{1,0:T(8,128)(2,1)S(1)} %copy-done.27, bf16[512,1024]{1,0:T(8,128)(2,1)S(1)} %get-tuple-element.197.do_ref, ...), custom_call_target="tpu_custom_call" | custom-call | flops 1000 | bytes 1000 | tf_op jit(solution)/shard_map/attend_back/pallas_call | solution.py:277
  216.8 9.4 %collective-permute-done.29 = bf16[2,1408,256]{2,1,0:T(8,128)(2,1)} collective-permute-done((bf16[2,1408,256]{2,1,0:T(8,128)(2,1)}, bf16[2,1408,256]{2,1,0:T(8,128)(2,1)}, u32[]{:S(2)}, u32[]{:S(2)}) %collective-permute-start.29) | collective-permute-done | bytes 1441824 | tf_op jit(solution)/shard_map/ppermute | solution.py:556
  227.7 13.9 %collective-permute-start.31 = (bf16[1,1408,256]{2,1,0:T(8,128)(2,1)S(1)}, bf16[1,1408,256]{2,1,0:T(8,128)(2,1)S(1)}, u32[]{:S(2)}, u32[]{:S(2)}) collective-permute-start(bf16[1,1408,256]{2,1,0:T(8,128)(2,1)S(1)} %add_convert_fusion.10), channel_id=1, source_target_pairs={{0,16},{4,20},{8,24},{12,28},{16,0},{20,4},{24,8},{28,12},{1,17},{... | collective-permute-start | bytes 2162696 | tf_op jit(solution)/shard_map/ppermute | solution.py:556
  241.6 10.2 %collective-permute-done.28 = bf16[4,256,1408]{2,1,0:T(8,128)(2,1)} collective-permute-done((bf16[4,256,1408]{2,1,0:T(8,128)(2,1)S(1)}, bf16[4,256,1408]{2,1,0:T(8,128)(2,1)}, u32[]{:S(2)}, u32[]{:S(2)}) %collective-permute-start.28) | collective-permute-done | bytes 2883616 | tf_op jit(solution)/shard_map/ppermute | solution.py:556
  255.8 2.3 collective-permute-start.38
  260.2 2.0 grad_by_columns.11
  262.1 2.1 grad_by_rows.10
  264.2 2.3 grad_by_rows.11
  266.6 7.2 %collective-permute-done.31 = bf16[1,1408,256]{2,1,0:T(8,128)(2,1)S(1)} collective-permute-done((bf16[1,1408,256]{2,1,0:T(8,128)(2,1)S(1)}, bf16[1,1408,256]{2,1,0:T(8,128)(2,1)S(1)}, u32[]{:S(2)}, u32[]{:S(2)}) %collective-permute-start.31) | collective-permute-done | bytes 720928 | tf_op jit(solution)/shard_map/ppermute | solution.py:556
  273.8 2.8 add_bitcast_fusion.2
  276.5 2.3 collective-permute-done.30
  279.2 2.7 collective-permute-start.33
  282.6 7.5 %collective-permute-done.34 = bf16[2,256,1408]{2,1,0:T(8,128)(2,1)S(1)} collective-permute-done((bf16[2,256,1408]{2,1,0:T(8,128)(2,1)S(1)}, bf16[2,256,1408]{2,1,0:T(8,128)(2,1)S(1)}, u32[]{:S(2)}, u32[]{:S(2)}) %collective-permute-start.34) | collective-permute-done | bytes 1441824 | tf_op jit(solution)/shard_map/ppermute | solution.py:556
  291.4 11.5 %collective-permute-start.40 = (bf16[1,256,1408]{2,1,0:T(8,128)(2,1)S(1)}, bf16[1,256,1408]{2,1,0:T(8,128)(2,1)S(1)}, u32[]{:S(2)}, u32[]{:S(2)}) collective-permute-start(bf16[1,256,1408]{2,1,0:T(8,128)(2,1)S(1)} %add_convert_fusion.9), channel_id=1, source_target_pairs={{0,16},{4,20},{8,24},{12,28},{16,0},{20,4},{24,8},{28,12},{1,17},{... | collective-permute-start | bytes 2162696 | tf_op jit(solution)/shard_map/ppermute | solution.py:556
  307.1 15.4 %collective-permute-done.35 = bf16[2,128,512]{2,1,0:T(8,128)(2,1)S(1)} collective-permute-done((bf16[2,128,512]{2,1,0:T(8,128)(2,1)S(1)}, bf16[2,128,512]{2,1,0:T(8,128)(2,1)S(1)}, u32[]{:S(2)}, u32[]{:S(2)}) %collective-permute-start.35) | collective-permute-done | bytes 262176 | tf_op jit(solution)/shard_map/ppermute | solution.py:556
  322.6 11.3 %collective-permute-done.40 = bf16[1,256,1408]{2,1,0:T(8,128)(2,1)S(1)} collective-permute-done((bf16[1,256,1408]{2,1,0:T(8,128)(2,1)S(1)}, bf16[1,256,1408]{2,1,0:T(8,128)(2,1)S(1)}, u32[]{:S(2)}, u32[]{:S(2)}) %collective-permute-start.40) | collective-permute-done | bytes 720928 | tf_op jit(solution)/shard_map/ppermute | solution.py:556
  333.9 2.5 add_bitcast_fusion.1
  339.8 4.7 %collective-permute-done.41 = bf16[128,512]{1,0:T(8,128)(2,1)S(1)} collective-permute-done((bf16[128,512]{1,0:T(8,128)(2,1)S(1)}, bf16[128,512]{1,0:T(8,128)(2,1)S(1)}, u32[]{:S(2)}, u32[]{:S(2)}) %collective-permute-start.41) | collective-permute-done | bytes 131104 | tf_op jit(solution)/shard_map/ppermute | solution.py:537
  347.0 3.0 collective-permute-start.49
  353.2 16.7 %collective-permute-done.46 = bf16[2,512,256]{2,1,0:T(8,128)(2,1)S(1)} collective-permute-done((bf16[2,512,256]{2,1,0:T(8,128)(2,1)S(1)}, bf16[2,512,256]{2,1,0:T(8,128)(2,1)S(1)}, u32[]{:S(2)}, u32[]{:S(2)}) %collective-permute-start.46) | collective-permute-done | bytes 524320 | tf_op jit(solution)/shard_map/ppermute | solution.py:556
  375.5 2.9 collective-permute-start.57
  378.5 4.7 %collective-permute-done.50 = bf16[4,64,1024]{2,1,0:T(8,128)(2,1)S(1)} collective-permute-done((bf16[4,64,1024]{2,1,0:T(8,128)(2,1)S(1)}, bf16[4,64,1024]{2,1,0:T(8,128)(2,1)S(1)}, u32[]{:S(2)}, u32[]{:S(2)}) %collective-permute-start.50) | collective-permute-done | bytes 524320 | tf_op jit(solution)/shard_map/ppermute | solution.py:556
  386.0 2.1 collective-permute-done.49
  388.3 2.5 add_bitcast_fusion
  390.8 14.1 %collective-permute-done.48 = bf16[4,128,1024]{2,1,0:T(8,128)(2,1)S(1)} collective-permute-done((bf16[4,128,1024]{2,1,0:T(8,128)(2,1)S(1)}, bf16[4,128,1024]{2,1,0:T(8,128)(2,1)S(1)}, u32[]{:S(2)}, u32[]{:S(2)}) %collective-permute-start.48) | collective-permute-done | bytes 1048608 | tf_op jit(solution)/shard_map/ppermute | solution.py:556
  417.8 3.4 collective-permute-start.63
  422.3 3.4 collective-permute-done.52
  426.9 3.0 collective-permute-start.62
  430.0 2.2 collective-permute-start.60
  433.4 2.8 collective-permute-done.56
  436.3 4.5 collective-permute-start.59
  440.8 4.0 collective-permute-done.61
  446.6 4.8 %collective-permute-done.60 = bf16[1,64,512]{2,1,0:T(8,128)(2,1)S(1)} collective-permute-done((bf16[1,64,512]{2,1,0:T(8,128)(2,1)S(1)}, bf16[1,64,512]{2,1,0:T(8,128)(2,1)S(1)}, u32[]{:S(2)}, u32[]{:S(2)}) %collective-permute-start.60) | collective-permute-done | bytes 65568 | tf_op jit(solution)/shard_map/ppermute | solution.py:556
  455.4 2.0 add_bitcast_fusion.3
  (393 shorter events, 124.4 us)
Async XLA Ops:
  6.0 6.5 %collective-permute-start.1 = (bf16[128,512]{1,0:T(8,128)(2,1)S(1)}, bf16[128,512]{1,0:T(8,128)(2,1)S(1)}, u32[]{:S(2)}, u32[]{:S(2)}) collective-permute-start(bf16[128,512]{1,0:T(8,128)(2,1)S(1)} %get-tuple-element.137), channel_id=1, source_target_pairs={{0,2},{1,3},{2,0},{3,1},{4,6},{5,7},{6,4},{7,5},{8,10},{9,11},{10,... | collective-permute-start | bytes 393224 | tf_op jit(solution)/shard_map/ppermute | solution.py:537
  12.5 7.5 %collective-permute-start.2 = (bf16[256,512]{1,0:T(8,128)(2,1)S(1)}, bf16[256,512]{1,0:T(8,128)(2,1)S(1)}, u32[]{:S(2)}, u32[]{:S(2)}) collective-permute-start(bf16[256,512]{1,0:T(8,128)(2,1)S(1)} %constant_dynamic-update-slice_fusion), channel_id=1, source_target_pairs={{0,8},{8,16},{16,24},{24,28},{28,20},{20,12},{12,4},{4,0},{1,9},{9... | collective-permute-start | bytes 786440 | tf_op jit(solution)/shard_map/ppermute | solution.py:546
  14.4 6.9 %collective-permute-start.3 = (bf16[256,512]{1,0:T(8,128)(2,1)S(1)}, bf16[256,512]{1,0:T(8,128)(2,1)S(1)}, u32[]{:S(2)}, u32[]{:S(2)}) collective-permute-start(bf16[256,512]{1,0:T(8,128)(2,1)S(1)} %constant_dynamic-update-slice_fusion), channel_id=1, source_target_pairs={{0,4},{8,0},{16,8},{24,16},{28,24},{20,28},{12,20},{4,12},{1,5},{9... | collective-permute-start | bytes 786440 | tf_op jit(solution)/shard_map/ppermute | solution.py:546
  14.6 8.8 %collective-permute-start = (bf16[128,1024]{1,0:T(8,128)(2,1)S(1)}, bf16[128,1024]{1,0:T(8,128)(2,1)S(1)}, u32[]{:S(2)}, u32[]{:S(2)}) collective-permute-start(bf16[128,1024]{1,0:T(8,128)(2,1)S(1)} %multiply_convert_fusion.2), channel_id=1, source_target_pairs={{0,2},{1,3},{2,0},{3,1},{4,6},{5,7},{6,4},{7,5},{8,10},{9,11},{10,... | collective-permute-start | bytes 786440 | tf_op jit(solution)/shard_map/ppermute | solution.py:537
  21.3 6.4 %collective-permute-start.5 = (bf16[256,512]{1,0:T(8,128)(2,1)S(1)}, bf16[256,512]{1,0:T(8,128)(2,1)S(1)}, u32[]{:S(2)}, u32[]{:S(2)}) collective-permute-start(bf16[256,512]{1,0:T(8,128)(2,1)S(1)} %collective-permute-done.2), channel_id=1, source_target_pairs={{0,8},{8,16},{16,24},{24,28},{28,20},{20,12},{12,4},{4,0},{1,9},{9... | collective-permute-start | bytes 786440 | tf_op jit(solution)/shard_map/ppermute | solution.py:546
  22.9 6.4 %collective-permute-start.6 = (bf16[256,512]{1,0:T(8,128)(2,1)S(1)}, bf16[256,512]{1,0:T(8,128)(2,1)S(1)}, u32[]{:S(2)}, u32[]{:S(2)}) collective-permute-start(bf16[256,512]{1,0:T(8,128)(2,1)S(1)} %collective-permute-done.3), channel_id=1, source_target_pairs={{0,4},{8,0},{16,8},{24,16},{28,24},{20,28},{12,20},{4,12},{1,5},{9... | collective-permute-start | bytes 786440 | tf_op jit(solution)/shard_map/ppermute | solution.py:546
  23.4 8.0 %collective-permute-start.9 = (bf16[256,1024]{1,0:T(8,128)(2,1)S(1)}, bf16[256,1024]{1,0:T(8,128)(2,1)S(1)}, u32[]{:S(2)}, u32[]{:S(2)}) collective-permute-start(bf16[256,1024]{1,0:T(8,128)(2,1)S(1)} %pad_maximum_fusion.12), channel_id=1, source_target_pairs={{0,1},{1,0},{2,3},{3,2},{4,5},{5,4},{6,7},{7,6},{8,9},{9,8},{10,11... | collective-permute-start | bytes 1572872 | tf_op jit(solution)/shard_map/ppermute | solution.py:533
  23.6 25.6 %collective-permute-start.4 = (bf16[256,2048]{1,0:T(8,128)(2,1)S(1)}, bf16[256,2048]{1,0:T(8,128)(2,1)S(1)}, u32[]{:S(2)}, u32[]{:S(2)}) collective-permute-start(bf16[256,2048]{1,0:T(8,128)(2,1)S(1)} %pad_maximum_fusion.3), channel_id=1, source_target_pairs={{0,2},{1,3},{2,0},{3,1},{4,6},{5,7},{6,4},{7,5},{8,10},{9,11},{10,... | collective-permute-start | bytes 3145736 | tf_op jit(solution)/shard_map/ppermute | solution.py:537
  25.2 18.9 %collective-permute-start.12 = (bf16[3,256,512]{2,1,0:T(8,128)(2,1)S(1)}, bf16[3,256,512]{2,1,0:T(8,128)(2,1)S(1)}, u32[]{:S(2)}, u32[]{:S(2)}) collective-permute-start(bf16[3,256,512]{2,1,0:T(8,128)(2,1)S(1)} %pad_maximum_fusion.10), channel_id=1, source_target_pairs={{0,1},{1,0},{2,3},{3,2},{4,5},{5,4},{6,7},{7,6},{8,9},{9,8},{10,11... | collective-permute-start | bytes 2359304 | tf_op jit(solution)/shard_map/ppermute | solution.py:533
  29.3 6.4 %collective-permute-start.7 = (bf16[256,512]{1,0:T(8,128)(2,1)S(1)}, bf16[256,512]{1,0:T(8,128)(2,1)S(1)}, u32[]{:S(2)}, u32[]{:S(2)}) collective-permute-start(bf16[256,512]{1,0:T(8,128)(2,1)S(1)} %collective-permute-done.5), channel_id=1, source_target_pairs={{0,8},{8,16},{16,24},{24,28},{28,20},{20,12},{12,4},{4,0},{1,9},{9... | collective-permute-start | bytes 786440 | tf_op jit(solution)/shard_map/ppermute | solution.py:546
  30.8 6.4 %collective-permute-start.8 = (bf16[256,512]{1,0:T(8,128)(2,1)S(1)}, bf16[256,512]{1,0:T(8,128)(2,1)S(1)}, u32[]{:S(2)}, u32[]{:S(2)}) collective-permute-start(bf16[256,512]{1,0:T(8,128)(2,1)S(1)} %collective-permute-done.6), channel_id=1, source_target_pairs={{0,4},{8,0},{16,8},{24,16},{28,24},{20,28},{12,20},{4,12},{1,5},{9... | collective-permute-start | bytes 786440 | tf_op jit(solution)/shard_map/ppermute | solution.py:546
  31.4 12.9 %collective-permute-start.13 = (bf16[2,256,512]{2,1,0:T(8,128)(2,1)S(1)}, bf16[2,256,512]{2,1,0:T(8,128)(2,1)S(1)}, u32[]{:S(2)}, u32[]{:S(2)}) collective-permute-start(bf16[2,256,512]{2,1,0:T(8,128)(2,1)S(1)} %get-tuple-element.158), channel_id=1, source_target_pairs={{0,1},{1,0},{2,3},{3,2},{4,5},{5,4},{6,7},{7,6},{8,9},{9,8},{10,11... | collective-permute-start | bytes 1572872 | tf_op jit(solution)/shard_map/ppermute | solution.py:533
  37.2 5.0 %collective-permute-start.10 = (bf16[128,512]{1,0:T(8,128)(2,1)S(1)}, bf16[128,512]{1,0:T(8,128)(2,1)S(1)}, u32[]{:S(2)}, u32[]{:S(2)}) collective-permute-start(bf16[128,512]{1,0:T(8,128)(2,1)S(1)} %slice.518), channel_id=1, source_target_pairs={{0,8},{8,16},{16,24},{24,28},{28,20},{20,12},{12,4},{4,0},{1,9},{9... | collective-permute-start | bytes 393224 | tf_op jit(solution)/shard_map/ppermute | solution.py:546
  38.8 5.0 %collective-permute-start.11 = (bf16[128,512]{1,0:T(8,128)(2,1)S(1)}, bf16[128,512]{1,0:T(8,128)(2,1)S(1)}, u32[]{:S(2)}, u32[]{:S(2)}) collective-permute-start(bf16[128,512]{1,0:T(8,128)(2,1)S(1)} %slice.519), channel_id=1, source_target_pairs={{0,4},{8,0},{16,8},{24,16},{28,24},{20,28},{12,20},{4,12},{1,5},{9... | collective-permute-start | bytes 393224 | tf_op jit(solution)/shard_map/ppermute | solution.py:546
  44.0 6.7 %collective-permute-start.14 = (bf16[3,256,512]{2,1,0:T(8,128)(2,1)S(1)}, bf16[3,256,512]{2,1,0:T(8,128)(2,1)S(1)}, u32[]{:S(2)}, u32[]{:S(2)}) collective-permute-start(bf16[3,256,512]{2,1,0:T(8,128)(2,1)S(1)} %pad_maximum_fusion.11), channel_id=1, source_target_pairs={{0,1},{1,0},{2,3},{3,2},{4,5},{5,4},{6,7},{7,6},{8,9},{9,8},{10,11... | collective-permute-start | bytes 2359304 | tf_op jit(solution)/shard_map/ppermute | solution.py:533
  56.9 4.2 collective-permute-start.15
  56.9 10.9 %collective-permute-start.17 = (bf16[256,2048]{1,0:T(8,128)(2,1)}, bf16[256,2048]{1,0:T(8,128)(2,1)S(1)}, u32[]{:S(2)}, u32[]{:S(2)}) collective-permute-start(bf16[256,2048]{1,0:T(8,128)(2,1)} %pad_maximum_fusion.6), channel_id=1, source_target_pairs={{0,1},{1,0},{2,3},{3,2},{4,5},{5,4},{6,7},{7,6},{8,9},{9,8},{10,11... | collective-permute-start | bytes 3145736 | tf_op jit(solution)/shard_map/ppermute | solution.py:533
  63.0 25.2 %collective-permute-start.16 = (bf16[256,2048]{1,0:T(8,128)(2,1)S(1)}, bf16[256,2048]{1,0:T(8,128)(2,1)S(1)}, u32[]{:S(2)}, u32[]{:S(2)}) collective-permute-start(bf16[256,2048]{1,0:T(8,128)(2,1)S(1)} %pad_maximum_fusion.7), channel_id=1, source_target_pairs={{0,2},{1,3},{2,0},{3,1},{4,6},{5,7},{6,4},{7,5},{8,10},{9,11},{10,... | collective-permute-start | bytes 3145736 | tf_op jit(solution)/shard_map/ppermute | solution.py:537
  67.9 5.1 %collective-permute-start.18 = (bf16[512,256]{1,0:T(8,128)(2,1)S(1)}, bf16[512,256]{1,0:T(8,128)(2,1)S(1)}, u32[]{:S(2)}, u32[]{:S(2)}) collective-permute-start(bf16[512,256]{1,0:T(8,128)(2,1)S(1)} %get-tuple-element.170), channel_id=1, source_target_pairs={{0,1},{1,0},{2,3},{3,2},{4,5},{5,4},{6,7},{7,6},{8,9},{9,8},{10,11... | collective-permute-start | bytes 786440 | tf_op jit(solution)/shard_map/ppermute | solution.py:533
  90.5 2.9 collective-permute-start.19
  114.2 72.9 %collective-permute-start.25 = (bf16[4,1408,256]{2,1,0:T(8,128)(2,1)}, bf16[4,1408,256]{2,1,0:T(8,128)(2,1)}, u32[]{:S(2)}, u32[]{:S(2)}) collective-permute-start(bf16[4,1408,256]{2,1,0:T(8,128)(2,1)} %grad_by_columns.6), channel_id=1, source_target_pairs={{0,4},{4,0},{8,12},{12,8},{16,20},{20,16},{24,28},{28,24},{1,5},{5... | collective-permute-start | bytes 8650760 | tf_op jit(solution)/shard_map/ppermute | solution.py:556
  125.7 79.0 %collective-permute-start.26 = (bf16[4,256,1408]{2,1,0:T(8,128)(2,1)}, bf16[4,256,1408]{2,1,0:T(8,128)(2,1)}, u32[]{:S(2)}, u32[]{:S(2)}) collective-permute-start(bf16[4,256,1408]{2,1,0:T(8,128)(2,1)} %grad_by_rows.6), channel_id=1, source_target_pairs={{0,8},{4,12},{8,0},{12,4},{16,24},{20,28},{24,16},{28,20},{1,9},{5... | collective-permute-start | bytes 8650760 | tf_op jit(solution)/shard_map/ppermute | solution.py:556
  140.3 3.8 collective-permute-start.20
  146.2 4.2 collective-permute-start.21
  147.0 25.2 %collective-permute-start.22 = (bf16[256,2048]{1,0:T(8,128)(2,1)S(1)}, bf16[256,2048]{1,0:T(8,128)(2,1)S(1)}, u32[]{:S(2)}, u32[]{:S(2)}) collective-permute-start(bf16[256,2048]{1,0:T(8,128)(2,1)S(1)} %pad_maximum_fusion.8), channel_id=1, source_target_pairs={{0,2},{1,3},{2,0},{3,1},{4,6},{5,7},{6,4},{7,5},{8,10},{9,11},{10,... | collective-permute-start | bytes 3145736 | tf_op jit(solution)/shard_map/ppermute | solution.py:537
  176.6 13.5 %collective-permute-start.24 = (bf16[256,2048]{1,0:T(8,128)(2,1)}, bf16[256,2048]{1,0:T(8,128)(2,1)}, u32[]{:S(2)}, u32[]{:S(2)}) collective-permute-start(bf16[256,2048]{1,0:T(8,128)(2,1)} %get-tuple-element.266), channel_id=1, source_target_pairs={{0,1},{1,0},{2,3},{3,2},{4,5},{5,4},{6,7},{7,6},{8,9},{9,8},{10,11... | collective-permute-start | bytes 3145736 | tf_op jit(solution)/shard_map/ppermute | solution.py:533
  182.2 32.1 %collective-permute-start.23 = (bf16[128,2048]{1,0:T(8,128)(2,1)S(1)}, bf16[128,2048]{1,0:T(8,128)(2,1)S(1)}, u32[]{:S(2)}, u32[]{:S(2)}) collective-permute-start(bf16[128,2048]{1,0:T(8,128)(2,1)S(1)} %slice.538), channel_id=1, source_target_pairs={{0,2},{1,3},{2,0},{3,1},{4,6},{5,7},{6,4},{7,5},{8,10},{9,11},{10,... | collective-permute-start | bytes 1572872 | tf_op jit(solution)/shard_map/ppermute | solution.py:537
  187.0 64.8 %collective-permute-start.28 = (bf16[4,256,1408]{2,1,0:T(8,128)(2,1)S(1)}, bf16[4,256,1408]{2,1,0:T(8,128)(2,1)}, u32[]{:S(2)}, u32[]{:S(2)}) collective-permute-start(bf16[4,256,1408]{2,1,0:T(8,128)(2,1)S(1)} %grad_by_rows.8), channel_id=1, source_target_pairs={{0,4},{4,0},{8,12},{12,8},{16,20},{20,16},{24,28},{28,24},{1,5},{5... | collective-permute-start | bytes 8650760 | tf_op jit(solution)/shard_map/ppermute | solution.py:556
  192.0 34.1 %collective-permute-start.29 = (bf16[2,1408,256]{2,1,0:T(8,128)(2,1)}, bf16[2,1408,256]{2,1,0:T(8,128)(2,1)}, u32[]{:S(2)}, u32[]{:S(2)}) collective-permute-start(bf16[2,1408,256]{2,1,0:T(8,128)(2,1)} %add_convert_fusion.3), channel_id=1, source_target_pairs={{0,8},{4,12},{8,0},{12,4},{16,24},{20,28},{24,16},{28,20},{1,9},{5... | collective-permute-start | bytes 4325384 | tf_op jit(solution)/shard_map/ppermute | solution.py:556
  212.9 40.7 %collective-permute-start.27 = (bf16[8,256,512]{2,1,0:T(8,128)(2,1)S(1)}, bf16[8,256,512]{2,1,0:T(8,128)(2,1)S(1)}, u32[]{:S(2)}, u32[]{:S(2)}) collective-permute-start(bf16[8,256,512]{2,1,0:T(8,128)(2,1)S(1)} %get-tuple-element.206), channel_id=1, source_target_pairs={{0,1},{1,0},{2,3},{3,2},{4,5},{5,4},{6,7},{7,6},{8,9},{9,8},{10,11... | collective-permute-start | bytes 6291464 | tf_op jit(solution)/shard_map/ppermute | solution.py:533
  213.9 41.0 %collective-permute-start.32 = (bf16[256,1024]{1,0:T(8,128)(2,1)S(1)}, bf16[256,1024]{1,0:T(8,128)(2,1)S(1)}, u32[]{:S(2)}, u32[]{:S(2)}) collective-permute-start(bf16[256,1024]{1,0:T(8,128)(2,1)S(1)} %convolution_convert_fusion.7), channel_id=1, source_target_pairs={{0,1},{1,0},{2,3},{3,2},{4,5},{5,4},{6,7},{7,6},{8,9},{9,8},{10,11... | collective-permute-start | bytes 1572872 | tf_op jit(solution)/shard_map/ppermute | solution.py:533
  227.7 46.1 %collective-permute-start.31 = (bf16[1,1408,256]{2,1,0:T(8,128)(2,1)S(1)}, bf16[1,1408,256]{2,1,0:T(8,128)(2,1)S(1)}, u32[]{:S(2)}, u32[]{:S(2)}) collective-permute-start(bf16[1,1408,256]{2,1,0:T(8,128)(2,1)S(1)} %add_convert_fusion.10), channel_id=1, source_target_pairs={{0,16},{4,20},{8,24},{12,28},{16,0},{20,4},{24,8},{28,12},{1,17},{... | collective-permute-start | bytes 2162696 | tf_op jit(solution)/shard_map/ppermute | solution.py:556
  254.3 24.5 %collective-permute-start.30 = (bf16[8,128,512]{2,1,0:T(8,128)(2,1)S(1)}, bf16[8,128,512]{2,1,0:T(8,128)(2,1)S(1)}, u32[]{:S(2)}, u32[]{:S(2)}) collective-permute-start(bf16[8,128,512]{2,1,0:T(8,128)(2,1)S(1)} %slice.662), channel_id=1, source_target_pairs={{0,2},{1,3},{2,0},{3,1},{4,6},{5,7},{6,4},{7,5},{8,10},{9,11},{10,... | collective-permute-start | bytes 3145736 | tf_op jit(solution)/shard_map/ppermute | solution.py:537
  255.5 34.5 %collective-permute-start.34 = (bf16[2,256,1408]{2,1,0:T(8,128)(2,1)S(1)}, bf16[2,256,1408]{2,1,0:T(8,128)(2,1)S(1)}, u32[]{:S(2)}, u32[]{:S(2)}) collective-permute-start(bf16[2,256,1408]{2,1,0:T(8,128)(2,1)S(1)} %copy-done.57), channel_id=1, source_target_pairs={{0,4},{4,0},{8,12},{12,8},{16,20},{20,16},{24,28},{28,24},{1,5},{5... | collective-permute-start | bytes 4325384 | tf_op jit(solution)/shard_map/ppermute | solution.py:556
  255.8 81.4 %collective-permute-start.38 = (bf16[2,256,1408]{2,1,0:T(8,128)(2,1)S(1)}, bf16[2,256,1408]{2,1,0:T(8,128)(2,1)S(1)}, u32[]{:S(2)}, u32[]{:S(2)}) collective-permute-start(bf16[2,256,1408]{2,1,0:T(8,128)(2,1)S(1)} %add_convert_fusion.1), channel_id=1, source_target_pairs={{0,8},{4,12},{8,0},{12,4},{16,24},{20,28},{24,16},{28,20},{1,9},{5... | collective-permute-start | bytes 4325384 | tf_op jit(solution)/shard_map/ppermute | solution.py:556
  279.2 24.1 %collective-permute-start.33 = (bf16[4,128,512]{2,1,0:T(8,128)(2,1)S(1)}, bf16[4,128,512]{2,1,0:T(8,128)(2,1)S(1)}, u32[]{:S(2)}, u32[]{:S(2)}) collective-permute-start(bf16[4,128,512]{2,1,0:T(8,128)(2,1)S(1)} %slice.665), channel_id=1, source_target_pairs={{0,4},{4,0},{8,12},{12,8},{16,20},{20,16},{24,28},{28,24},{1,5},{5... | collective-permute-start | bytes 1572872 | tf_op jit(solution)/shard_map/ppermute | solution.py:556
  282.0 21.4 %collective-permute-start.36 = (bf16[256,1024]{1,0:T(8,128)(2,1)S(1)}, bf16[256,1024]{1,0:T(8,128)(2,1)S(1)}, u32[]{:S(2)}, u32[]{:S(2)}) collective-permute-start(bf16[256,1024]{1,0:T(8,128)(2,1)S(1)} %pad_maximum_fusion.14), channel_id=1, source_target_pairs={{0,2},{1,3},{2,0},{3,1},{4,6},{5,7},{6,4},{7,5},{8,10},{9,11},{10,... | collective-permute-start | bytes 1572872 | tf_op jit(solution)/shard_map/ppermute | solution.py:537
  291.4 42.5 %collective-permute-start.40 = (bf16[1,256,1408]{2,1,0:T(8,128)(2,1)S(1)}, bf16[1,256,1408]{2,1,0:T(8,128)(2,1)S(1)}, u32[]{:S(2)}, u32[]{:S(2)}) collective-permute-start(bf16[1,256,1408]{2,1,0:T(8,128)(2,1)S(1)} %add_convert_fusion.9), channel_id=1, source_target_pairs={{0,16},{4,20},{8,24},{12,28},{16,0},{20,4},{24,8},{28,12},{1,17},{... | collective-permute-start | bytes 2162696 | tf_op jit(solution)/shard_map/ppermute | solution.py:556
  303.0 36.7 %collective-permute-start.42 = (bf16[4,512,256]{2,1,0:T(8,128)(2,1)S(1)}, bf16[4,512,256]{2,1,0:T(8,128)(2,1)S(1)}, u32[]{:S(2)}, u32[]{:S(2)}) collective-permute-start(bf16[4,512,256]{2,1,0:T(8,128)(2,1)S(1)} %copy-done.34), channel_id=1, source_target_pairs={{0,4},{4,0},{8,12},{12,8},{16,20},{20,16},{24,28},{28,24},{1,5},{5... | collective-permute-start | bytes 3145736 | tf_op jit(solution)/shard_map/ppermute | solution.py:556
  303.3 19.2 %collective-permute-start.35 = (bf16[2,128,512]{2,1,0:T(8,128)(2,1)S(1)}, bf16[2,128,512]{2,1,0:T(8,128)(2,1)S(1)}, u32[]{:S(2)}, u32[]{:S(2)}) collective-permute-start(bf16[2,128,512]{2,1,0:T(8,128)(2,1)S(1)} %add_convert_fusion.18), channel_id=1, source_target_pairs={{0,8},{4,12},{8,0},{12,4},{16,24},{20,28},{24,16},{28,20},{1,9},{5... | collective-permute-start | bytes 786440 | tf_op jit(solution)/shard_map/ppermute | solution.py:556
  304.2 32.2 %collective-permute-start.39 = (bf16[256,1024]{1,0:T(8,128)(2,1)S(1)}, bf16[256,1024]{1,0:T(8,128)(2,1)S(1)}, u32[]{:S(2)}, u32[]{:S(2)}) collective-permute-start(bf16[256,1024]{1,0:T(8,128)(2,1)S(1)} %multiply_convert_fusion.1), channel_id=1, source_target_pairs={{0,1},{1,0},{2,3},{3,2},{4,5},{5,4},{6,7},{7,6},{8,9},{9,8},{10,11... | collective-permute-start | bytes 1572872 | tf_op jit(solution)/shard_map/ppermute | solution.py:533
  322.5 16.5 %collective-permute-start.37 = (bf16[1,128,512]{2,1,0:T(8,128)(2,1)S(1)}, bf16[1,128,512]{2,1,0:T(8,128)(2,1)S(1)}, u32[]{:S(2)}, u32[]{:S(2)}) collective-permute-start(bf16[1,128,512]{2,1,0:T(8,128)(2,1)S(1)} %add_convert_fusion.19), channel_id=1, source_target_pairs={{0,16},{4,20},{8,24},{12,28},{16,0},{20,4},{24,8},{28,12},{1,17},{... | collective-permute-start | bytes 393224 | tf_op jit(solution)/shard_map/ppermute | solution.py:556
  339.1 5.4 %collective-permute-start.41 = (bf16[128,512]{1,0:T(8,128)(2,1)S(1)}, bf16[128,512]{1,0:T(8,128)(2,1)S(1)}, u32[]{:S(2)}, u32[]{:S(2)}) collective-permute-start(bf16[128,512]{1,0:T(8,128)(2,1)S(1)} %pad_maximum_fusion.17), channel_id=1, source_target_pairs={{0,2},{1,3},{2,0},{3,1},{4,6},{5,7},{6,4},{7,5},{8,10},{9,11},{10,... | collective-permute-start | bytes 393224 | tf_op jit(solution)/shard_map/ppermute | solution.py:537
  344.6 6.8 %collective-permute-start.43 = (bf16[256,512]{1,0:T(8,128)(2,1)S(1)}, bf16[256,512]{1,0:T(8,128)(2,1)S(1)}, u32[]{:S(2)}, u32[]{:S(2)}) collective-permute-start(bf16[256,512]{1,0:T(8,128)(2,1)S(1)} %pad_maximum_fusion.16), channel_id=1, source_target_pairs={{0,1},{1,0},{2,3},{3,2},{4,5},{5,4},{6,7},{7,6},{8,9},{9,8},{10,11... | collective-permute-start | bytes 786440 | tf_op jit(solution)/shard_map/ppermute | solution.py:533
  345.0 24.9 %collective-permute-start.46 = (bf16[2,512,256]{2,1,0:T(8,128)(2,1)S(1)}, bf16[2,512,256]{2,1,0:T(8,128)(2,1)S(1)}, u32[]{:S(2)}, u32[]{:S(2)}) collective-permute-start(bf16[2,512,256]{2,1,0:T(8,128)(2,1)S(1)} %add_convert_fusion.13), channel_id=1, source_target_pairs={{0,8},{4,12},{8,0},{12,4},{16,24},{20,28},{24,16},{28,20},{1,9},{5... | collective-permute-start | bytes 1572872 | tf_op jit(solution)/shard_map/ppermute | solution.py:556
  345.9 26.1 %collective-permute-start.45 = (bf16[4,512,256]{2,1,0:T(8,128)(2,1)S(1)}, bf16[4,512,256]{2,1,0:T(8,128)(2,1)S(1)}, u32[]{:S(2)}, u32[]{:S(2)}) collective-permute-start(bf16[4,512,256]{2,1,0:T(8,128)(2,1)S(1)} %copy-done.30), channel_id=1, source_target_pairs={{0,4},{4,0},{8,12},{12,8},{16,20},{20,16},{24,28},{28,24},{1,5},{5... | collective-permute-start | bytes 3145736 | tf_op jit(solution)/shard_map/ppermute | solution.py:556
  347.0 41.2 %collective-permute-start.49 = (bf16[1,256,1408]{2,1,0:T(8,128)(2,1)S(1)}, bf16[1,256,1408]{2,1,0:T(8,128)(2,1)S(1)}, u32[]{:S(2)}, u32[]{:S(2)}) collective-permute-start(bf16[1,256,1408]{2,1,0:T(8,128)(2,1)S(1)} %add_convert_fusion.8), channel_id=1, source_target_pairs={{0,16},{4,20},{8,24},{12,28},{16,0},{20,4},{24,8},{28,12},{1,17},{... | collective-permute-start | bytes 2162696 | tf_op jit(solution)/shard_map/ppermute | solution.py:556
  350.0 33.2 %collective-permute-start.50 = (bf16[4,64,1024]{2,1,0:T(8,128)(2,1)S(1)}, bf16[4,64,1024]{2,1,0:T(8,128)(2,1)S(1)}, u32[]{:S(2)}, u32[]{:S(2)}) collective-permute-start(bf16[4,64,1024]{2,1,0:T(8,128)(2,1)S(1)} %bitcast.109), channel_id=1, source_target_pairs={{0,4},{4,0},{8,12},{12,8},{16,20},{20,16},{24,28},{28,24},{1,5},{5... | collective-permute-start | bytes 1572872 | tf_op jit(solution)/shard_map/ppermute | solution.py:556
  352.5 25.9 %collective-permute-start.44 = (f32[2048]{0:T(1024)S(1)}, f32[2048]{0:T(1024)S(1)}, u32[]{:S(2)}, u32[]{:S(2)}) collective-permute-start(f32[2048]{0:T(1024)S(1)} %get-tuple-element.262), channel_id=1, source_target_pairs={{0,2},{1,3},{2,0},{3,1},{4,6},{5,7},{6,4},{7,5},{8,10},{9,11},{10,... | collective-permute-start | bytes 24584 | tf_op jit(solution)/shard_map/ppermute | solution.py:537
  373.0 31.9 %collective-permute-start.48 = (bf16[4,128,1024]{2,1,0:T(8,128)(2,1)S(1)}, bf16[4,128,1024]{2,1,0:T(8,128)(2,1)S(1)}, u32[]{:S(2)}, u32[]{:S(2)}) collective-permute-start(bf16[4,128,1024]{2,1,0:T(8,128)(2,1)S(1)} %grad_by_rows.10), channel_id=1, source_target_pairs={{0,4},{4,0},{8,12},{12,8},{16,20},{20,16},{24,28},{28,24},{1,5},{5... | collective-permute-start | bytes 3145736 | tf_op jit(solution)/shard_map/ppermute | solution.py:556
  375.5 54.6 %collective-permute-start.57 = (bf16[1,512,256]{2,1,0:T(8,128)(2,1)}, bf16[1,512,256]{2,1,0:T(8,128)(2,1)}, u32[]{:S(2)}, u32[]{:S(2)}) collective-permute-start(bf16[1,512,256]{2,1,0:T(8,128)(2,1)} %add_convert_fusion.17), channel_id=1, source_target_pairs={{0,16},{4,20},{8,24},{12,28},{16,0},{20,4},{24,8},{28,12},{1,17},{... | collective-permute-start | bytes 786440 | tf_op jit(solution)/shard_map/ppermute | solution.py:556
  378.4 27.5 %collective-permute-start.47 = (f32[5120]{0:T(1024)S(1)}, f32[5120]{0:T(1024)S(1)}, u32[]{:S(2)}, u32[]{:S(2)}) collective-permute-start(f32[5120]{0:T(1024)S(1)} %pad_maximum_fusion.18), channel_id=1, source_target_pairs={{0,1},{1,0},{2,3},{3,2},{4,5},{5,4},{6,7},{7,6},{8,9},{9,8},{10,11... | collective-permute-start | bytes 61448 | tf_op jit(solution)/shard_map/ppermute | solution.py:533
  384.1 33.7 %collective-permute-start.53 = (bf16[2,64,1024]{2,1,0:T(8,128)(2,1)}, bf16[2,64,1024]{2,1,0:T(8,128)(2,1)}, u32[]{:S(2)}, u32[]{:S(2)}) collective-permute-start(bf16[2,64,1024]{2,1,0:T(8,128)(2,1)} %fusion.31), channel_id=1, source_target_pairs={{0,8},{4,12},{8,0},{12,4},{16,24},{20,28},{24,16},{28,20},{1,9},{5... | collective-permute-start | bytes 786440 | tf_op jit(solution)/shard_map/ppermute | solution.py:556
  388.1 27.6 %collective-permute-start.54 = (bf16[2,512,256]{2,1,0:T(8,128)(2,1)}, bf16[2,512,256]{2,1,0:T(8,128)(2,1)}, u32[]{:S(2)}, u32[]{:S(2)}) collective-permute-start(bf16[2,512,256]{2,1,0:T(8,128)(2,1)} %add_convert_fusion.12), channel_id=1, source_target_pairs={{0,8},{4,12},{8,0},{12,4},{16,24},{20,28},{24,16},{28,20},{1,9},{5... | collective-permute-start | bytes 1572872 | tf_op jit(solution)/shard_map/ppermute | solution.py:556
  404.9 9.9 %collective-permute-start.55 = (bf16[4,64,512]{2,1,0:T(8,128)(2,1)}, bf16[4,64,512]{2,1,0:T(8,128)(2,1)S(1)}, u32[]{:S(2)}, u32[]{:S(2)}) collective-permute-start(bf16[4,64,512]{2,1,0:T(8,128)(2,1)} %bitcast.25), channel_id=1, source_target_pairs={{0,4},{4,0},{8,12},{12,8},{16,20},{20,16},{24,28},{28,24},{1,5},{5... | collective-permute-start | bytes 786440 | tf_op jit(solution)/shard_map/ppermute | solution.py:556
  406.5 19.2 %collective-permute-start.52 = (bf16[2,128,1024]{2,1,0:T(8,128)(2,1)S(1)}, bf16[2,128,1024]{2,1,0:T(8,128)(2,1)}, u32[]{:S(2)}, u32[]{:S(2)}) collective-permute-start(bf16[2,128,1024]{2,1,0:T(8,128)(2,1)S(1)} %add_convert_fusion.11), channel_id=1, source_target_pairs={{0,8},{4,12},{8,0},{12,4},{16,24},{20,28},{24,16},{28,20},{1,9},{5... | collective-permute-start | bytes 1572872 | tf_op jit(solution)/shard_map/ppermute | solution.py:556
  414.8 12.1 %collective-permute-start.51 = (f32[4,1,160]{2,0,1:T(4,128)S(1)}, f32[4,1,160]{2,0,1:T(4,128)S(1)}, u32[]{:S(2)}, u32[]{:S(2)}) collective-permute-start(f32[4,1,160]{2,0,1:T(4,128)S(1)} %slice.684), channel_id=1, source_target_pairs={{0,4},{4,0},{8,12},{12,8},{16,20},{20,16},{24,28},{28,24},{1,5},{5... | collective-permute-start | bytes 7688 | tf_op jit(solution)/shard_map/ppermute | solution.py:556
  415.8 14.1 %collective-permute-start.58 = (bf16[2,64,512]{2,1,0:T(8,128)(2,1)S(1)}, bf16[2,64,512]{2,1,0:T(8,128)(2,1)S(1)}, u32[]{:S(2)}, u32[]{:S(2)}) collective-permute-start(bf16[2,64,512]{2,1,0:T(8,128)(2,1)S(1)} %fusion.38), channel_id=1, source_target_pairs={{0,8},{4,12},{8,0},{12,4},{16,24},{20,28},{24,16},{28,20},{1,9},{5... | collective-permute-start | bytes 393224 | tf_op jit(solution)/shard_map/ppermute | solution.py:556
  417.8 34.8 %collective-permute-start.63 = (bf16[1,512,256]{2,1,0:T(8,128)(2,1)S(1)}, bf16[1,512,256]{2,1,0:T(8,128)(2,1)S(1)}, u32[]{:S(2)}, u32[]{:S(2)}) collective-permute-start(bf16[1,512,256]{2,1,0:T(8,128)(2,1)S(1)} %add_convert_fusion.16), channel_id=1, source_target_pairs={{0,16},{4,20},{8,24},{12,28},{16,0},{20,4},{24,8},{28,12},{1,17},{... | collective-permute-start | bytes 786440 | tf_op jit(solution)/shard_map/ppermute | solution.py:556
  425.7 19.1 %collective-permute-start.61 = (bf16[1,64,1024]{2,1,0:T(8,128)(2,1)S(1)}, bf16[1,64,1024]{2,1,0:T(8,128)(2,1)S(1)}, u32[]{:S(2)}, u32[]{:S(2)}) collective-permute-start(bf16[1,64,1024]{2,1,0:T(8,128)(2,1)S(1)} %fusion.40), channel_id=1, source_target_pairs={{0,16},{4,20},{8,24},{12,28},{16,0},{20,4},{24,8},{28,12},{1,17},{... | collective-permute-start | bytes 393224 | tf_op jit(solution)/shard_map/ppermute | solution.py:556
  426.9 28.4 %collective-permute-start.62 = (bf16[1,128,1024]{2,1,0:T(8,128)(2,1)S(1)}, bf16[1,128,1024]{2,1,0:T(8,128)(2,1)S(1)}, u32[]{:S(2)}, u32[]{:S(2)}) collective-permute-start(bf16[1,128,1024]{2,1,0:T(8,128)(2,1)S(1)} %add_convert_fusion.15), channel_id=1, source_target_pairs={{0,16},{4,20},{8,24},{12,28},{16,0},{20,4},{24,8},{28,12},{1,17},{... | collective-permute-start | bytes 786440 | tf_op jit(solution)/shard_map/ppermute | solution.py:556
  429.9 6.3 %collective-permute-start.56 = (bf16[2,1,160]{2,0,1:T(2,128)(2,1)S(1)}, bf16[2,1,160]{2,0,1:T(2,128)(2,1)S(1)}, u32[]{:S(2)}, u32[]{:S(2)}) collective-permute-start(bf16[2,1,160]{2,0,1:T(2,128)(2,1)S(1)} %fusion.43), channel_id=1, source_target_pairs={{0,8},{4,12},{8,0},{12,4},{16,24},{20,28},{24,16},{28,20},{1,9},{5... | collective-permute-start | bytes 1928 | tf_op jit(solution)/shard_map/ppermute | solution.py:556
  430.0 21.3 %collective-permute-start.60 = (bf16[1,64,512]{2,1,0:T(8,128)(2,1)S(1)}, bf16[1,64,512]{2,1,0:T(8,128)(2,1)S(1)}, u32[]{:S(2)}, u32[]{:S(2)}) collective-permute-start(bf16[1,64,512]{2,1,0:T(8,128)(2,1)S(1)} %fusion.42), channel_id=1, source_target_pairs={{0,16},{4,20},{8,24},{12,28},{16,0},{20,4},{24,8},{28,12},{1,17},{... | collective-permute-start | bytes 196616 | tf_op jit(solution)/shard_map/ppermute | solution.py:556
  436.3 15.8 %collective-permute-start.59 = (bf16[1,1,160]{2,0,1:T(2,128)(2,1)S(1)}, bf16[1,1,160]{2,0,1:T(2,128)(2,1)S(1)}, u32[]{:S(2)}, u32[]{:S(2)}) collective-permute-start(bf16[1,1,160]{2,0,1:T(2,128)(2,1)S(1)} %fusion.47), channel_id=1, source_target_pairs={{0,16},{4,20},{8,24},{12,28},{16,0},{20,4},{24,8},{28,12},{1,17},{... | collective-permute-start | bytes 968 | tf_op jit(solution)/shard_map/ppermute | solution.py:556
  (82 other events, 730.8 us)

commit v3 on v2

--- a/solution.py
+++ b/solution.py
@@ -17,6 +17,17 @@
 SCALE = 1.0 / math.sqrt(HD)
 MIB = 1 << 20
 BRIEF = pl.CostEstimate(flops=1000, bytes_accessed=1000, transcendentals=0)
+
+STEPS = (
+    "down", "down_keep", "up", "up_keep", "units_back", "units_chip", "feed_product", "feed_chip",
+    "branch_grad", "feed_far", "gate", "down_1", "attended_back", "out_send0", "out_send1", "gate_keep",
+    "up_1", "attention_back", "latent_product", "feed", "down_2", "gate_1", "chip_keys", "latent_chip",
+    "up_go", "out_keep0", "out_keep1", "query_send", "query_keep", "down_end", "keys", "latent_far", "up_2",
+    "out_a", "kv_1", "compressed", "kv_2", "out_a_1", "out_b", "up_end", "down_q_parts", "own_keys_grad",
+    "gate_2", "half_keys", "normed_grad", "out_b_1", "query", "gains_own", "kv_parts", "kv_w", "out_a_2",
+    "gains_1", "kv_w_1", "gate_end", "q_down", "out_a_end", "kv_w_2", "out_b_2", "query_1", "gains_2",
+    "q_down_1", "kv_w_end", "gains_3", "q_down_2", "query_2", "out_b_end", "q_down_end", "query_end",
+)
 
 NN = (((1,), (0,)), ((), ()))
 NT = (((1,), (1,)), ((), ()))
@@ -593,8 +604,10 @@
         self.terms += values
 
     def hop(self, go=True):
+        assert self.terms and self.moving is not None
         arrived = self.order.after(self.moving)
         self.terms.append(arrived)
+        self.moving = None
         cut = arrived.shape[0] // 2
         send = add(*[t[cut:] for t in self.terms]).astype(BF16)
         self.terms = [t[:cut] for t in self.terms]
@@ -609,6 +622,7 @@
     def finish(self):
         while self.bits:
             self.hop()
+        assert self.terms and self.moving is not None
         arrived = self.order.after(self.moving)
         total = add(*[t[0] for t in self.terms], arrived[0])
         self.order.ran(total)
@@ -650,6 +664,7 @@
     pair = jnp.concatenate([keyval, order.after(keyval_far)], axis=0)
     order.ran(pair)
     ahead, back = ring_shift(pair, 1, count), ring_shift(pair, -1, count)
+    both_far = far(jnp.concatenate(order.after(block_input, cotangent), axis=0))
     empty = jnp.zeros((count,) + pair.shape, BF16)
     kv_a, kv_b = lax.dynamic_update_slice(empty, order.after(pair)[None], (0, 0, 0)), empty
     waiting, moving = [pair[None]], []
@@ -685,7 +700,6 @@
             latent_half = jnp.concatenate([latent, order.after(latent_far)], axis=0)
             order.ran(latent_half)
             latent_near = near(latent_half)
-            both_far = far(jnp.concatenate(order.after(block_input, cotangent), axis=0))
         if step == min(2, half - 1):
             latent_all = jnp.concatenate([latent_half, order.after(latent_near)], axis=0)
             query, cos, sin = project_rotate(lengths, latent_all, q_up, freq)
@@ -743,187 +757,231 @@
     hidden, hidden_t, grad_gate, grad_up = hidden_units(normed_two, gate_weight, up_weight, grad_hidden)
     order.ran(hidden)
 
-    send = grad_by_columns(owner[half:], order.after(hidden_t), grad_all, count)
-    order.ran(send)
-    down_sum = Halving(order, bits, count, send)
-    keep = grad_by_columns(owner[:half], order.after(hidden_t), grad_all, count)
-    order.ran(keep)
-    down_sum.keep(keep)
-
-    [send] = grad_by_rows(owner_two[half:], order.after(normed_two), [grad_up], count)
-    order.ran(send)
-    up_sum = Halving(order, bits_two, count, send)
-    [keep] = grad_by_rows(owner_two[:half], order.after(normed_two), [grad_up], count)
-    order.ran(keep)
-    up_sum.keep(keep)
-
-    def after_feed():
-        keep, send = product([order.after(hidden)], [down_weight], NN)
-        order.ran(send)
-        feed_chip = add(keep, order.after(near(send))).astype(BF16)
-        order.ran(feed_chip)
-        return feed_chip
-
-    back_two, feed_chip = sum_half([grad_gate, grad_up], [gate_weight, up_weight], NT, after_feed)
-    grad_residual = grad_half.astype(F32) + rms_back(back_two, scaled_two, inverse_two, norm2_gain)
-    branch_half = grad_residual.astype(BF16)
-    order.ran(branch_half)
-    branch_near = near(branch_half)
-    feed_far = far(order.after(feed_chip)[own:])
-
-    [send] = grad_by_rows(owner[half:], order.after(normed_two), [grad_gate], count)
-    order.ran(send)
-    gate_sum = Halving(order, bits, count, send)
-    down_sum.hop()
-    grad_branch = jnp.concatenate([branch_half, order.after(branch_near)], axis=0)
-    grad_attended, delta = attended_grad(grad_branch, out_weight, attended)
-    order.ran(grad_attended)
-    send_out = grad_by_columns(owner[half:], order.after(attended_t), grad_branch, count, 0, 2)
-    order.ran(send_out)
-    send_out_two = grad_by_columns(owner[half:], order.after(attended_t), grad_branch, count, 1, 2)
-    order.ran(send_out_two)
-    [keep] = grad_by_rows(owner[:half], order.after(normed_two), [grad_gate], count)
-    order.ran(keep)
-    gate_sum.keep(keep)
-    up_sum.hop(go=False)
-
     slot_out = slot_of(jnp.arange(count, dtype=jnp.int32), count, seq) ^ seq
     slot_out = sum(((slot_out >> (bit.bit_length() - 1)) & 1) << (len(bits) - 1 - i) for i, bit in enumerate(bits))
-    grad_query_raw, dkv_a, dkv_b = attend_back(
-        lengths, slot_out, query, order.after(grad_attended), kv_a, kv_b, lse, delta, cos, sin
-    )
-    order.ran(grad_query_raw)
-    dkv_near = near(dkv_b)
-
-    latent_keep, latent_send = product([order.after(grad_query_raw)], [q_up], NT)
-    order.ran(latent_send)
-    latent_near = near(latent_send)
-    feed_out = add(feed_chip[:own], order.after(feed_far))
-    block_output = (residual[:own] + feed_out).astype(BF16)
-    order.ran(block_output)
-    down_sum.hop()
-    gate_sum.hop()
-    chip_kv = add(dkv_a, order.after(dkv_near)).astype(BF16)
-    order.ran(chip_kv)
-    kv_far = far(chip_kv[:, own:])
-    latent_chip = add(latent_keep, order.after(latent_near)).astype(BF16)
-    order.ran(latent_chip)
-    up_sum.go()
-    keep_out = grad_by_columns(owner[:half], order.after(attended_t), grad_branch, count, 0, 2)
-    order.ran(keep_out)
-    keep_out_two = grad_by_columns(owner[:half], order.after(attended_t), grad_branch, count, 1, 2)
-    order.ran(keep_out_two)
-    [send_query] = grad_by_rows(owner[half:], order.after(latent_all), [grad_query_raw], count)
-    order.ran(send_query)
-    [keep_query] = grad_by_rows(owner[:half], order.after(latent_all), [grad_query_raw], count)
-    order.ran(keep_query)
-    down_grad = down_sum.finish()
-    chips_kv = add(chip_kv[:, :own], order.after(kv_far)).astype(BF16)
-    order.ran(chips_kv)
-    kv_sum = Halving(order, bits, count, chips_kv[half:], chips_kv[:half])
-    latent_far = far(swap(order.after(latent_chip)))
-    up_sum.hop()
-    out_sum = Halving(order, bits, count, order.after(send_out), keep_out)
-    kv_sum.hop()
-    grad_latent = add(latent_chip, order.after(latent_far))
-    grad_compressed = rms_back(grad_latent, scaled_q, inverse_q, q_gain).astype(BF16)
-    order.ran(grad_compressed)
-    compressed_near = near(grad_compressed)
-    kv_sum.hop()
-    gain_two = jnp.sum(order.after(back_two) * scaled_two, axis=0)
-    gain_q = jnp.sum(grad_latent * scaled_q, axis=0)
-    gains = jnp.concatenate([gain_two, gain_q])
-    up_grad = up_sum.finish()
-    compressed_all = jnp.concatenate([grad_compressed, order.after(compressed_near)], axis=0)
-    q_down_parts = dot(picked, compressed_all).astype(BF16)
-    order.ran(q_down_parts)
-    gate_sum.hop(go=False)
-
-    def by_owner(values, size):
-        blocks = lax.dynamic_slice(values.reshape(count, group, size), (0, mine, 0), (count, 1, size))
-        same = owner[:, None, None] == jnp.arange(count, dtype=jnp.int32)[None, :, None]
-        return jnp.sum(jnp.where(same, blocks[:, 0][None], 0.0), axis=1)[:, None, :]
-
-    kv_own = kv_sum.finish()
-    former, latter = kv_own[:, :mid], kv_own[:, mid:HD]
-    grad_kv_raw = jnp.concatenate(
-        [
+
+    h = {}
+
+    def keep(name, value):
+        h[name] = value
+        order.ran(value)
+
+    def halving(name, send, kept, bits=bits):
+        h[name] = Halving(order, bits, count, order.after(send), kept)
+
+    def started(name, make, bits=bits):
+        def step():
+            parts = make()
+            order.ran(parts)
+            h[name] = Halving(order, bits, count, parts)
+
+        return step
+
+    def kept(name, make):
+        def step():
+            parts = make()
+            order.ran(parts)
+            h[name].keep(parts)
+
+        return step
+
+    def down_parts(which):
+        return lambda: grad_by_columns(which, order.after(hidden_t), grad_all, count)
+
+    def rows_parts(which, right):
+        return lambda: grad_by_rows(which, order.after(normed_two), [right], count)[0]
+
+    def units_back():
+        h["units_keep"], send = product(
+            [order.after(grad_gate), grad_up], [gate_weight, up_weight], NT
+        )
+        order.ran(send)
+        h["units_near"] = near(send)
+
+    def units_chip():
+        keep("units_chip", add(h["units_keep"], order.after(h["units_near"])).astype(BF16))
+        h["units_far"] = far(swap(h["units_chip"]))
+
+    def feed_product():
+        h["feed_keep"], send = product([order.after(hidden)], [down_weight], NN)
+        order.ran(send)
+        h["feed_near"] = near(send)
+
+    def feed_chip():
+        keep("feed_chip", add(h["feed_keep"], order.after(h["feed_near"])).astype(BF16))
+
+    def feed_far():
+        h["feed_far"] = far(order.after(h["feed_chip"])[own:])
+
+    def branch_grad():
+        h["back_two"] = add(h["units_chip"], order.after(h["units_far"]))
+        h["grad_residual"] = grad_half.astype(F32) + rms_back(h["back_two"], scaled_two, inverse_two, norm2_gain)
+        keep("branch_half", h["grad_residual"].astype(BF16))
+        h["branch_near"] = near(h["branch_half"])
+
+    def attended_back():
+        h["grad_branch"] = jnp.concatenate([h["branch_half"], order.after(h["branch_near"])], axis=0)
+        h["grad_attended"], h["delta"] = attended_grad(h["grad_branch"], out_weight, attended)
+        order.ran(h["grad_attended"])
+
+    def out_part(name, which, part):
+        return lambda: keep(
+            name, grad_by_columns(which, order.after(attended_t), h["grad_branch"], count, part, 2)
+        )
+
+    def attention_back():
+        h["grad_query"], h["dkv_a"], dkv_b = attend_back(
+            lengths, slot_out, query, order.after(h["grad_attended"]), kv_a, kv_b, lse, h["delta"], cos, sin
+        )
+        order.ran(h["grad_query"])
+        h["dkv_near"] = near(dkv_b)
+
+    def latent_product():
+        h["latent_keep"], send = product([order.after(h["grad_query"])], [q_up], NT)
+        order.ran(send)
+        h["latent_near"] = near(send)
+
+    def latent_chip():
+        keep("latent_chip", add(h["latent_keep"], order.after(h["latent_near"])).astype(BF16))
+
+    def latent_far():
+        h["latent_far"] = far(swap(order.after(h["latent_chip"])))
+
+    def compressed():
+        h["grad_latent"] = add(h["latent_chip"], order.after(h["latent_far"]))
+        keep("grad_compressed", rms_back(h["grad_latent"], scaled_q, inverse_q, q_gain).astype(BF16))
+        h["compressed_near"] = near(h["grad_compressed"])
+
+    def down_q_parts():
+        both = jnp.concatenate([h["grad_compressed"], order.after(h["compressed_near"])], axis=0)
+        keep("down_q_parts", dot(picked, both).astype(BF16))
+
+    def feed():
+        total = add(h["feed_chip"][:own], order.after(h["feed_far"]))
+        keep("block_output", (residual[:own] + total).astype(BF16))
+
+    def chip_keys():
+        keep("chip_kv", add(h["dkv_a"], order.after(h["dkv_near"])).astype(BF16))
+        h["kv_far"] = far(h["chip_kv"][:, own:])
+
+    def keys():
+        keep("chips_kv", add(h["chip_kv"][:, :own], order.after(h["kv_far"])).astype(BF16))
+        halving("kv", h["chips_kv"][half:], h["chips_kv"][:half])
+
+    def own_keys_grad():
+        total = h["kv"].finish()
+        former, latter = total[:, :mid], total[:, mid:HD]
+        turned = [
             former * cos[:own] + latter * sin[:own],
             latter * cos[:own] - former * sin[:own],
-            kv_own[:, HD:],
-        ],
-        axis=1,
-    ).astype(BF16)
-    order.ran(grad_kv_raw)
-    kv_raw_far = far(grad_kv_raw)
-    out_sum.hop()
-    out_sum_two = Halving(order, bits, count, order.after(send_out_two), keep_out_two)
-    gate_sum.go()
-    kv_half = jnp.concatenate([grad_kv_raw, order.after(kv_raw_far)], axis=0)
-    order.ran(kv_half)
-    kv_half_near = near(kv_half)
-    q_down_parts = order.after(q_down_parts).reshape(count, share, -1)
-    q_down_sum = Halving(order, bits, count, q_down_parts[half:], q_down_parts[:half])
-    kv_half_near = order.after(kv_half_near)
-    order.ran(kv_half_near)
-    scaled_one, inverse_one = rms_parts(order.after(block_input).astype(F32))
-    grad_normed = dot(grad_compressed[:own], q_down, NT) + dot(order.after(grad_kv_raw), kv_weight, NT)
-    input_grad = grad_residual[:own] + rms_back(grad_normed, scaled_one, inverse_one, norm1_gain)
-    gain_one = jnp.sum(grad_normed * scaled_one, axis=0)
-    order.ran(gain_one)
-    out_sum.hop()
-    gain_far = far(gain_one)
-    kv_all = jnp.concatenate([kv_half, kv_half_near], axis=0)
-    kv_parts = dot(picked, order.after(kv_all)).astype(BF16)
-    order.ran(kv_parts)
-    out_sum_two.hop()
-    query_sum = Halving(order, bits, count, order.after(send_query), keep_query)
-    gain_one = gain_one + order.after(gain_far)
-    gains = jnp.concatenate([gain_one, gains])
-    order.ran(gains)
-    gains_near = near(gains)
-    q_down_sum.hop()
-    kv_parts = order.after(kv_parts).reshape(count, share, -1)
-    kv_weight_sum = Halving(order, bits, count, kv_parts[half:], kv_parts[:half])
-    gate_grad = gate_sum.finish()
-    query_sum.hop()
-    gains = gains + order.after(gains_near)
-    gains = jnp.concatenate(
-        [
-            by_owner(gains[:width], share),
-            by_owner(gains[width : 2 * width], share),
-            by_owner(gains[2 * width :], q_gain.shape[0] // (count * group)),
-        ],
-        axis=2,
-    )
-    order.ran(gains)
-    gains_sum = Halving(order, bits, count, gains[half:], gains[:half])
-    kv_weight_sum.hop()
-    out_sum_two.hop()
-    q_down_sum.hop()
-    query_sum.hop()
-    gains_sum.hop()
-    kv_weight_sum.hop()
-    out_one = out_sum.finish()
-    gains_sum.hop()
-    q_down_grad = q_down_sum.finish()
-    kv_weight_grad = kv_weight_sum.finish()
-    gains = gains_sum.finish()[0]
-    out_weight_grad = jnp.concatenate([out_one, out_sum_two.finish()], axis=0)
-    q_up_grad = query_sum.finish()
+            total[:, HD:],
+        ]
+        keep("kv_raw", jnp.concatenate(turned, axis=1).astype(BF16))
+        h["kv_raw_far"] = far(h["kv_raw"])
+
+    def half_keys():
+        keep("kv_half", jnp.concatenate([h["kv_raw"], order.after(h["kv_raw_far"])], axis=0))
+        h["kv_half_near"] = near(h["kv_half"])
+
+    def kv_parts():
+        both = jnp.concatenate([h["kv_half"], order.after(h["kv_half_near"])], axis=0)
+        keep("kv_parts", dot(picked, both).astype(BF16))
+
+    def normed_grad():
+        scaled_one, inverse_one = rms_parts(order.after(block_input).astype(F32))
+        grad_normed = dot(h["grad_compressed"][:own], q_down, NT) + dot(h["kv_raw"], kv_weight, NT)
+        h["input_grad"] = h["grad_residual"][:own] + rms_back(grad_normed, scaled_one, inverse_one, norm1_gain)
+        keep("gain_one", jnp.sum(grad_normed * scaled_one, axis=0))
+        h["gain_far"] = far(h["gain_one"])
+
+    def gains_own():
+        gain_one = h["gain_one"] + order.after(h["gain_far"])
+        gain_two = jnp.sum(h["back_two"] * scaled_two, axis=0)
+        gain_q = jnp.sum(h["grad_latent"] * scaled_q, axis=0)
+        keep("gains", jnp.concatenate([gain_one, gain_two, gain_q]))
+        h["gains_moved"] = near(h["gains"])
+
+    def gains_step(bit):
+        def step():
+            keep("gains", h["gains"] + order.after(h["gains_moved"]))
+            if bit:
+                h["gains_moved"] = swap_seq(h["gains"], bit, count)
+
+        return step
+
+    def gains_later():
+        for bit in bits[2:]:
+            gains_step(bit)()
+        gains_step(None)()
+
+    def query_send():
+        [parts] = grad_by_rows(owner[half:], order.after(latent_all), [h["grad_query"]], count)
+        keep("query_send", parts)
+
+    def query_keep():
+        [parts] = grad_by_rows(owner[:half], order.after(latent_all), [h["grad_query"]], count)
+        keep("query_keep", parts)
+
+    def shares(name, parts):
+        def step():
+            by_owner = h[parts].reshape(count, share, -1)
+            halving(name, by_owner[half:], by_owner[:half])
+
+        return step
+
+    hop = lambda name: lambda: h[name].hop()
+    finish = lambda name: lambda: h.update({name: h[name].finish()})
+    steps = {
+        "latent_product": latent_product, "latent_chip": latent_chip, "latent_far": latent_far,
+        "compressed": compressed, "down_q_parts": down_q_parts, "feed": feed,
+        "chip_keys": chip_keys, "keys": keys, "own_keys_grad": own_keys_grad, "half_keys": half_keys,
+        "kv_parts": kv_parts, "normed_grad": normed_grad, "gains_own": gains_own,
+        "gains_1": gains_step(bits[0]), "gains_2": gains_step(bits[1]), "gains_3": gains_later,
+        "out_keep0": out_part("out_keep0", owner[:half], 0), "out_keep1": out_part("out_keep1", owner[:half], 1),
+        "out_send0": out_part("out_send0", owner[half:], 0), "out_send1": out_part("out_send1", owner[half:], 1),
+        "down": started("down", down_parts(owner[half:])), "down_keep": kept("down", down_parts(owner[:half])),
+        "up": started("up", rows_parts(owner_two[half:], grad_up), bits_two),
+        "up_keep": kept("up", rows_parts(owner_two[:half], grad_up)),
+        "gate": started("gate", rows_parts(owner[half:], grad_gate)),
+        "gate_keep": kept("gate", rows_parts(owner[:half], grad_gate)),
+        "units_back": units_back, "units_chip": units_chip, "feed_product": feed_product, "feed_chip": feed_chip,
+        "feed_far": feed_far, "branch_grad": branch_grad, "attended_back": attended_back,
+        "attention_back": attention_back, "down_1": hop("down"), "up_1": lambda: h["up"].hop(go=False),
+        "query_send": query_send, "query_keep": query_keep,
+        "up_go": lambda: h["up"].go(), "down_2": hop("down"), "down_end": finish("down"), "gate_1": hop("gate"),
+        "gate_2": hop("gate"), "gate_end": finish("gate"), "up_2": hop("up"), "up_end": finish("up"),
+        "kv_1": hop("kv"), "kv_2": hop("kv"),
+        "out_a": lambda: halving("out_a", h["out_send0"], h["out_keep0"]),
+        "out_a_1": hop("out_a"), "out_a_2": hop("out_a"), "out_a_end": finish("out_a"),
+        "out_b": lambda: halving("out_b", h["out_send1"], h["out_keep1"]),
+        "out_b_1": hop("out_b"), "out_b_2": hop("out_b"), "out_b_end": finish("out_b"),
+        "query": lambda: halving("query", h["query_send"], h["query_keep"]),
+        "query_1": hop("query"), "query_2": hop("query"), "query_end": finish("query"),
+        "q_down": shares("q_down", "down_q_parts"),
+        "q_down_1": hop("q_down"), "q_down_2": hop("q_down"), "q_down_end": finish("q_down"),
+        "kv_w": shares("kv_w", "kv_parts"),
+        "kv_w_1": hop("kv_w"), "kv_w_2": hop("kv_w"), "kv_w_end": finish("kv_w"),
+    }
+    assert sorted(steps) == sorted(STEPS)
+    for name in STEPS:
+        steps[name]()
+
+    place = seq * group + mine
+    q_share = q_gain.shape[0] // (count * group)
+    part_of = lambda first, size: lax.dynamic_slice(h["gains"], (first + place * size,), (size,))
     return (
-        block_output,
-        input_grad,
-        gains[:share],
-        q_down_grad,
-        gains[2 * share :],
-        q_up_grad,
-        kv_weight_grad,
-        out_weight_grad,
-        gains[share : 2 * share],
-        gate_grad,
-        up_grad,
-        down_grad,
+        h["block_output"],
+        h["input_grad"],
+        part_of(0, share),
+        h["q_down"],
+        part_of(2 * width, q_share),
+        h["query"],
+        h["kv_w"],
+        jnp.concatenate([h["out_a"], h["out_b"]], axis=0),
+        part_of(width, share),
+        h["gate"],
+        h["up"],
+        h["down"],
     )
 
 

time: 463 us -> 453 us (0.978)
  other arithmetic: 58.4 us -> 45.4 us
  waiting for transfers between devices: 178 us -> 187 us
  local copies, waits for them, and re-layouts: 25.6 us -> 20.3 us
    ppermute x30, waiting for transfers between devices: 114 us -> 129 us  [swap_seq(): return lax.ppermute(values, 'seq', [(i, i ^ bit) for i in range(count)])]
    convert_element_type x20 -> x18, other arithmetic: 19 us -> 12.4 us  [hop(): send = add(*[t[cut:] for t in self.terms]).astype(BF16)]
    ppermute x10, waiting for transfers between devices: 47.7 us -> 42 us  [far(): return lax.ppermute(values, 'tensor', [(i, i ^ 2) for i in range(4)])]
    add x11 -> x9, other arithmetic: 16.4 us -> 10.9 us  [add(): total = total + part.astype(F32)]
    unnamed x164 -> x140, local copies, waits for them, and re-layouts: 17.1 us -> 17.2 us
  transfers between devices with their start and end apart: 64 -> 64, of which waited for: 30 -> 32; matrix products, arithmetic and copies ran while one was open for 21% -> 17% of each run, Pallas kernels for 10% -> 10%
where the time goes in v3:
time: 453 us; the launch traced here: 448 us
  waiting for transfers between devices  187 us (41%)
  starting transfers between devices  91.6 us (20%)
  Pallas kernels  65.5 us (14%)
  other arithmetic  45.4 us (10%)
  matrix products  35 us (8%)
  local copies, waits for them, and re-layouts  20.3 us (4%)
    ppermute x30, waiting for transfers between devices, swap_seq(): return lax.ppermute(values, 'seq', [(i, i ^ bit) for i in range(count)])  129 us
    ppermute x30, starting transfers between devices, swap_seq(): return lax.ppermute(values, 'seq', [(i, i ^ bit) for i in range(count)])  66.1 us
    ppermute x10, waiting for transfers between devices, far(): return lax.ppermute(values, 'tensor', [(i, i ^ 2) for i in range(4)])  42 us
    dot_general x17, matrix products, dot(): return lax.dot_general(left, right, dims, preferred_element_type=F32)  35 us
    pallas_call x6, Pallas kernels, grad_by_rows(): pl.pallas_call(rows_kernel, grid_spec=pltpu.PrefetchScalarGridSpec(num_sc...  18.5 us
    unnamed x140, local copies, waits for them, and re-layouts  17.2 us
    ppermute x8, waiting for transfers between devices, ring_shift(): lax.ppermute(values, 'seq', [(order[i], order[(i + step) % count]) for i...  15 us
    pallas_call x6, Pallas kernels, grad_by_columns(): pl.pallas_call(columns_kernel, grid_spec=pltpu.PrefetchScalarGridSpec(num...  14.8 us
  transfers between devices with their start and end apart: 64, of which 32 were waited for; matrix products, arithmetic and copies ran while one was open for 17% of the time, Pallas kernels for 10%

profile of v3, /device:TPU:0, one launch (start us, length us, event | category | flops | bytes accessed | tf_op | source)
XLA Modules:
  0.0 447.6 jit_solution(17815459135495893644)
XLA Ops:
  6.0 3.0 collective-permute-start
  9.0 3.0 multiply_reduce_fusion.6
  12.5 1.9 collective-permute-start.2
  16.3 3.7 collective-permute-done.2
  25.7 2.0 collective-permute-done.4
  31.4 3.9 project_rotate.1
  39.9 2.7 collective-permute-done.10
  44.4 4.8 %collective-permute-done.1 = bf16[256,2048]{1,0:T(8,128)(2,1)S(1)} collective-permute-done((bf16[256,2048]{1,0:T(8,128)(2,1)S(1)}, bf16[256,2048]{1,0:T(8,128)(2,1)S(1)}, u32[]{:S(2)}, u32[]{:S(2)}) %collective-permute-start.1) | collective-permute-done | bytes 1048608 | tf_op jit(solution)/shard_map/ppermute | solution.py:548
  50.9 3.9 attend.1
  54.9 2.3 convolution_convert_fusion
  57.7 3.6 fusion.3
  68.3 5.0 %fusion.61.gh_ref = f32[512,1408]{1,0:T(8,128)} fusion(bf16[1408,2048]{1,0:T(8,128)(2,1)S(1)} %bitcast.102, bf16[256,2048]{1,0:T(8,128)(2,1)S(1)} %collective-permute-done.17, bf16[128,2048]{1,0:T(8,128)(2,1)S(1)} %copy-done.46, bf16[128,2048]{1,0:T(8,128)(2,1)S(1)} %copy-done.42), kind=kOutput, calls=%fused_computation.178 | convolution fusion | flops 2959081472 | bytes 10747904 | tf_op jit(solution)/shard_map/dot_general | solution.py:38
  73.4 15.0 %collective-permute-done.16 = bf16[256,2048]{1,0:T(8,128)(2,1)S(1)} collective-permute-done((bf16[256,2048]{1,0:T(8,128)(2,1)S(1)}, bf16[256,2048]{1,0:T(8,128)(2,1)S(1)}, u32[]{:S(2)}, u32[]{:S(2)}) %collective-permute-start.16) | collective-permute-done | bytes 1048608 | tf_op jit(solution)/shard_map/ppermute | solution.py:548
  95.3 2.6 copy-done.18
  97.9 12.5 %hidden_units.1 = (bf16[512,1408]{1,0:T(8,128)(2,1)S(1)}, bf16[1408,512]{1,0:T(8,128)(2,1)S(1)}, bf16[512,1408]{1,0:T(8,128)(2,1)S(1)}, bf16[512,1408]{1,0:T(8,128)(2,1)S(1)}) custom-call(bf16[512,2048]{1,0:T(8,128)(2,1)S(1)} %pad_maximum_fusion.1.x_ref.left_ref, bf16[2048,1408]{1,0:T(8,128)(2,1)S(1)} %copy-done.18, bf16[2048,1408]{1,0:T(8,128)(2,1)} %up_ref.1, ...), custom_call_target="tpu_custom_call" | custom-call | flops 1000 | bytes 1000 | tf_op jit(solution)/shard_map/hidden_units/pallas_call | solution.py:425
  110.4 4.1 grad_by_columns.6
  114.5 2.6 collective-permute-start.25
  117.1 2.9 grad_by_columns.7
  121.6 4.3 grad_by_rows.6
  125.9 5.8 %collective-permute-start.26 = (bf16[4,256,1408]{2,1,0:T(8,128)(2,1)}, bf16[4,256,1408]{2,1,0:T(8,128)(2,1)}, u32[]{:S(2)}, u32[]{:S(2)}) collective-permute-start(bf16[4,256,1408]{2,1,0:T(8,128)(2,1)} %grad_by_rows.6), channel_id=1, source_target_pairs={{0,8},{4,12},{8,0},{12,4},{16,24},{20,28},{24,16},{28,20},{1,9},{5... | collective-permute-start | bytes 8650760 | tf_op jit(solution)/shard_map/ppermute | solution.py:567
  131.8 3.2 grad_by_rows.7
  148.9 1.9 fusion.4
  152.1 20.5 %collective-permute-done.22 = bf16[256,2048]{1,0:T(8,128)(2,1)S(1)} collective-permute-done((bf16[256,2048]{1,0:T(8,128)(2,1)S(1)}, bf16[256,2048]{1,0:T(8,128)(2,1)S(1)}, u32[]{:S(2)}, u32[]{:S(2)}) %collective-permute-start.22) | collective-permute-done | bytes 1048608 | tf_op jit(solution)/shard_map/ppermute | solution.py:548
  173.3 2.7 fusion.62
  176.0 4.9 %multiply_reduce_fusion.5 = (f32[256]{0:T(256)S(1)}, f32[256,1024]{1,0:T(8,128)}) fusion(bf16[256,2048]{1,0:T(8,128)(2,1)} %copy-done.23, bf16[2048,1024]{1,0:T(8,128)(2,1)} %param.18), kind=kOutput, calls=%fused_computation.77 | convolution fusion | flops 1074265856 | bytes 6292480 | tf_op jit(solution)/shard_map/dot_general | solution.py:38
  183.2 3.4 grad_by_rows.8
  186.7 3.0 add_convert_fusion.3
  189.7 1.9 pad_maximum_fusion.2.gb_ref.right_ref
  192.5 3.7 attended_grad.1
  196.2 2.0 grad_by_columns.8
  199.1 1.9 grad_by_columns.9
  201.1 3.2 grad_by_rows.9
  204.4 1.9 add_convert_fusion.2
  207.0 5.2 %attend_back.1 = (bf16[512,1024]{1,0:T(8,128)(2,1)S(1)}, bf16[8,256,512]{2,1,0:T(8,128)(2,1)S(1)}, bf16[8,256,512]{2,1,0:T(8,128)(2,1)S(1)}) custom-call(s32[4]{0:T(128)S(1)} %copy-done.36, s32[8]{0:T(128)S(1)} %get-tuple-element.289._, bf16[512,1024]{1,0:T(8,128)(2,1)S(1)} %copy-done.25, bf16[512,1024]{1,0:T(8,128)(2,1)S(1)} %get-tuple-element.194.do_ref, ...), custom_call_target="tpu_custom_call" | custom-call | flops 1000 | bytes 1000 | tf_op jit(solution)/shard_map/attend_back/pallas_call | solution.py:288
  215.1 2.0 fusion.19
  217.2 8.6 %collective-permute-done.29 = bf16[2,1408,256]{2,1,0:T(8,128)(2,1)} collective-permute-done((bf16[2,1408,256]{2,1,0:T(8,128)(2,1)}, bf16[2,1408,256]{2,1,0:T(8,128)(2,1)}, u32[]{:S(2)}, u32[]{:S(2)}) %collective-permute-start.29) | collective-permute-done | bytes 1441824 | tf_op jit(solution)/shard_map/ppermute | solution.py:567
  227.4 14.6 %collective-permute-start.31 = (bf16[1,1408,256]{2,1,0:T(8,128)(2,1)S(1)}, bf16[1,1408,256]{2,1,0:T(8,128)(2,1)S(1)}, u32[]{:S(2)}, u32[]{:S(2)}) collective-permute-start(bf16[1,1408,256]{2,1,0:T(8,128)(2,1)S(1)} %add_convert_fusion.10), channel_id=1, source_target_pairs={{0,16},{4,20},{8,24},{12,28},{16,0},{20,4},{24,8},{28,12},{1,17},{... | collective-permute-start | bytes 2162696 | tf_op jit(solution)/shard_map/ppermute | solution.py:567
  242.0 9.4 %collective-permute-done.28 = bf16[4,256,1408]{2,1,0:T(8,128)(2,1)} collective-permute-done((bf16[4,256,1408]{2,1,0:T(8,128)(2,1)S(1)}, bf16[4,256,1408]{2,1,0:T(8,128)(2,1)}, u32[]{:S(2)}, u32[]{:S(2)}) %collective-permute-start.28) | collective-permute-done | bytes 2883616 | tf_op jit(solution)/shard_map/ppermute | solution.py:567
  255.0 3.5 collective-permute-start.42
  258.5 2.0 grad_by_columns.10
  260.5 2.0 grad_by_columns.11
  262.5 2.1 grad_by_rows.10
  264.6 2.3 grad_by_rows.11
  266.9 7.2 %collective-permute-done.31 = bf16[1,1408,256]{2,1,0:T(8,128)(2,1)S(1)} collective-permute-done((bf16[1,1408,256]{2,1,0:T(8,128)(2,1)S(1)}, bf16[1,1408,256]{2,1,0:T(8,128)(2,1)S(1)}, u32[]{:S(2)}, u32[]{:S(2)}) %collective-permute-start.31) | collective-permute-done | bytes 720928 | tf_op jit(solution)/shard_map/ppermute | solution.py:567
  274.2 2.9 add_bitcast_fusion.2
  278.7 3.6 collective-permute-start.33
  283.1 6.1 %collective-permute-done.34 = bf16[2,256,1408]{2,1,0:T(8,128)(2,1)S(1)} collective-permute-done((bf16[2,256,1408]{2,1,0:T(8,128)(2,1)S(1)}, bf16[2,256,1408]{2,1,0:T(8,128)(2,1)S(1)}, u32[]{:S(2)}, u32[]{:S(2)}) %collective-permute-start.34) | collective-permute-done | bytes 1441824 | tf_op jit(solution)/shard_map/ppermute | solution.py:567
  290.7 11.6 %collective-permute-start.39 = (bf16[1,256,1408]{2,1,0:T(8,128)(2,1)S(1)}, bf16[1,256,1408]{2,1,0:T(8,128)(2,1)S(1)}, u32[]{:S(2)}, u32[]{:S(2)}) collective-permute-start(bf16[1,256,1408]{2,1,0:T(8,128)(2,1)S(1)} %add_convert_fusion.9), channel_id=1, source_target_pairs={{0,16},{4,20},{8,24},{12,28},{16,0},{20,4},{24,8},{28,12},{1,17},{... | collective-permute-start | bytes 2162696 | tf_op jit(solution)/shard_map/ppermute | solution.py:567
  306.5 15.4 %collective-permute-done.35 = bf16[2,128,512]{2,1,0:T(8,128)(2,1)S(1)} collective-permute-done((bf16[2,128,512]{2,1,0:T(8,128)(2,1)S(1)}, bf16[2,128,512]{2,1,0:T(8,128)(2,1)S(1)}, u32[]{:S(2)}, u32[]{:S(2)}) %collective-permute-start.35) | collective-permute-done | bytes 262176 | tf_op jit(solution)/shard_map/ppermute | solution.py:567
  324.7 8.2 %collective-permute-done.39 = bf16[1,256,1408]{2,1,0:T(8,128)(2,1)S(1)} collective-permute-done((bf16[1,256,1408]{2,1,0:T(8,128)(2,1)S(1)}, bf16[1,256,1408]{2,1,0:T(8,128)(2,1)S(1)}, u32[]{:S(2)}, u32[]{:S(2)}) %collective-permute-start.39) | collective-permute-done | bytes 720928 | tf_op jit(solution)/shard_map/ppermute | solution.py:567
  332.8 2.6 add_bitcast_fusion.1
  339.4 2.7 collective-permute-start.44
  344.5 19.6 %collective-permute-done.44 = bf16[4,512,256]{2,1,0:T(8,128)(2,1)S(1)} collective-permute-done((bf16[4,512,256]{2,1,0:T(8,128)(2,1)S(1)}, bf16[4,512,256]{2,1,0:T(8,128)(2,1)S(1)}, u32[]{:S(2)}, u32[]{:S(2)}) %collective-permute-start.44) | collective-permute-done | bytes 1048608 | tf_op jit(solution)/shard_map/ppermute | solution.py:567
  368.3 3.4 collective-permute-start.53
  371.7 3.5 collective-permute-done.51
  377.4 2.6 add_bitcast_fusion
  380.0 4.5 %collective-permute-done.53 = bf16[1,512,256]{2,1,0:T(8,128)(2,1)S(1)} collective-permute-done((bf16[1,512,256]{2,1,0:T(8,128)(2,1)S(1)}, bf16[1,512,256]{2,1,0:T(8,128)(2,1)S(1)}, u32[]{:S(2)}, u32[]{:S(2)}) %collective-permute-start.53) | collective-permute-done | bytes 262176 | tf_op jit(solution)/shard_map/ppermute | solution.py:567
  385.0 9.0 %collective-permute-done.52 = bf16[2,64,512]{2,1,0:T(8,128)(2,1)S(1)} collective-permute-done((bf16[2,64,512]{2,1,0:T(8,128)(2,1)S(1)}, bf16[2,64,512]{2,1,0:T(8,128)(2,1)S(1)}, u32[]{:S(2)}, u32[]{:S(2)}) %collective-permute-start.52) | collective-permute-done | bytes 131104 | tf_op jit(solution)/shard_map/ppermute | solution.py:567
  394.3 3.4 collective-permute-done.49
  400.0 8.9 %collective-permute-done.57 = bf16[4,64,1024]{2,1,0:T(8,128)(2,1)S(1)} collective-permute-done((bf16[4,64,1024]{2,1,0:T(8,128)(2,1)S(1)}, bf16[4,64,1024]{2,1,0:T(8,128)(2,1)S(1)}, u32[]{:S(2)}, u32[]{:S(2)}) %collective-permute-start.57) | collective-permute-done | bytes 524320 | tf_op jit(solution)/shard_map/ppermute | solution.py:567
  411.6 3.4 collective-permute-start.58
  418.4 3.5 collective-permute-start.60
  422.1 17.8 %collective-permute-done.61 = bf16[1,512,256]{2,1,0:T(8,128)(2,1)S(1)} collective-permute-done((bf16[1,512,256]{2,1,0:T(8,128)(2,1)S(1)}, bf16[1,512,256]{2,1,0:T(8,128)(2,1)S(1)}, u32[]{:S(2)}, u32[]{:S(2)}) %collective-permute-start.61) | collective-permute-done | bytes 262176 | tf_op jit(solution)/shard_map/ppermute | solution.py:567
  443.5 2.9 collective-permute-done.63
  (352 shorter events, 106.7 us)
Async XLA Ops:
  6.0 6.5 %collective-permute-start = (bf16[128,512]{1,0:T(8,128)(2,1)S(1)}, bf16[128,512]{1,0:T(8,128)(2,1)S(1)}, u32[]{:S(2)}, u32[]{:S(2)}) collective-permute-start(bf16[128,512]{1,0:T(8,128)(2,1)S(1)} %get-tuple-element.133), channel_id=1, source_target_pairs={{0,2},{1,3},{2,0},{3,1},{4,6},{5,7},{6,4},{7,5},{8,10},{9,11},{10,... | collective-permute-start | bytes 393224 | tf_op jit(solution)/shard_map/ppermute | solution.py:548
  12.5 7.5 %collective-permute-start.2 = (bf16[256,512]{1,0:T(8,128)(2,1)S(1)}, bf16[256,512]{1,0:T(8,128)(2,1)S(1)}, u32[]{:S(2)}, u32[]{:S(2)}) collective-permute-start(bf16[256,512]{1,0:T(8,128)(2,1)S(1)} %constant_dynamic-update-slice_fusion), channel_id=1, source_target_pairs={{0,8},{8,16},{16,24},{24,28},{28,20},{20,12},{12,4},{4,0},{1,9},{9... | collective-permute-start | bytes 786440 | tf_op jit(solution)/shard_map/ppermute | solution.py:557
  14.4 6.9 %collective-permute-start.3 = (bf16[256,512]{1,0:T(8,128)(2,1)S(1)}, bf16[256,512]{1,0:T(8,128)(2,1)S(1)}, u32[]{:S(2)}, u32[]{:S(2)}) collective-permute-start(bf16[256,512]{1,0:T(8,128)(2,1)S(1)} %constant_dynamic-update-slice_fusion), channel_id=1, source_target_pairs={{0,4},{8,0},{16,8},{24,16},{28,24},{20,28},{12,20},{4,12},{1,5},{9... | collective-permute-start | bytes 786440 | tf_op jit(solution)/shard_map/ppermute | solution.py:557
  14.6 8.8 %collective-permute-start.6 = (bf16[128,1024]{1,0:T(8,128)(2,1)S(1)}, bf16[128,1024]{1,0:T(8,128)(2,1)S(1)}, u32[]{:S(2)}, u32[]{:S(2)}) collective-permute-start(bf16[128,1024]{1,0:T(8,128)(2,1)S(1)} %multiply_convert_fusion.2), channel_id=1, source_target_pairs={{0,2},{1,3},{2,0},{3,1},{4,6},{5,7},{6,4},{7,5},{8,10},{9,11},{10,... | collective-permute-start | bytes 786440 | tf_op jit(solution)/shard_map/ppermute | solution.py:548
  21.3 6.4 %collective-permute-start.4 = (bf16[256,512]{1,0:T(8,128)(2,1)S(1)}, bf16[256,512]{1,0:T(8,128)(2,1)S(1)}, u32[]{:S(2)}, u32[]{:S(2)}) collective-permute-start(bf16[256,512]{1,0:T(8,128)(2,1)S(1)} %collective-permute-done.2), channel_id=1, source_target_pairs={{0,8},{8,16},{16,24},{24,28},{28,20},{20,12},{12,4},{4,0},{1,9},{9... | collective-permute-start | bytes 786440 | tf_op jit(solution)/shard_map/ppermute | solution.py:557
  22.9 6.4 %collective-permute-start.5 = (bf16[256,512]{1,0:T(8,128)(2,1)S(1)}, bf16[256,512]{1,0:T(8,128)(2,1)S(1)}, u32[]{:S(2)}, u32[]{:S(2)}) collective-permute-start(bf16[256,512]{1,0:T(8,128)(2,1)S(1)} %collective-permute-done.3), channel_id=1, source_target_pairs={{0,4},{8,0},{16,8},{24,16},{28,24},{20,28},{12,20},{4,12},{1,5},{9... | collective-permute-start | bytes 786440 | tf_op jit(solution)/shard_map/ppermute | solution.py:557
  23.4 7.9 %collective-permute-start.9 = (bf16[256,1024]{1,0:T(8,128)(2,1)S(1)}, bf16[256,1024]{1,0:T(8,128)(2,1)S(1)}, u32[]{:S(2)}, u32[]{:S(2)}) collective-permute-start(bf16[256,1024]{1,0:T(8,128)(2,1)S(1)} %pad_maximum_fusion.12), channel_id=1, source_target_pairs={{0,1},{1,0},{2,3},{3,2},{4,5},{5,4},{6,7},{7,6},{8,9},{9,8},{10,11... | collective-permute-start | bytes 1572872 | tf_op jit(solution)/shard_map/ppermute | solution.py:544
  23.6 25.6 %collective-permute-start.1 = (bf16[256,2048]{1,0:T(8,128)(2,1)S(1)}, bf16[256,2048]{1,0:T(8,128)(2,1)S(1)}, u32[]{:S(2)}, u32[]{:S(2)}) collective-permute-start(bf16[256,2048]{1,0:T(8,128)(2,1)S(1)} %pad_maximum_fusion.3), channel_id=1, source_target_pairs={{0,2},{1,3},{2,0},{3,1},{4,6},{5,7},{6,4},{7,5},{8,10},{9,11},{10,... | collective-permute-start | bytes 3145736 | tf_op jit(solution)/shard_map/ppermute | solution.py:548
  25.4 25.2 %collective-permute-start.12 = (bf16[3,256,512]{2,1,0:T(8,128)(2,1)S(1)}, bf16[3,256,512]{2,1,0:T(8,128)(2,1)S(1)}, u32[]{:S(2)}, u32[]{:S(2)}) collective-permute-start(bf16[3,256,512]{2,1,0:T(8,128)(2,1)S(1)} %pad_maximum_fusion.10), channel_id=1, source_target_pairs={{0,1},{1,0},{2,3},{3,2},{4,5},{5,4},{6,7},{7,6},{8,9},{9,8},{10,11... | collective-permute-start | bytes 2359304 | tf_op jit(solution)/shard_map/ppermute | solution.py:544
  29.3 6.5 %collective-permute-start.7 = (bf16[256,512]{1,0:T(8,128)(2,1)S(1)}, bf16[256,512]{1,0:T(8,128)(2,1)S(1)}, u32[]{:S(2)}, u32[]{:S(2)}) collective-permute-start(bf16[256,512]{1,0:T(8,128)(2,1)S(1)} %collective-permute-done.4), channel_id=1, source_target_pairs={{0,8},{8,16},{16,24},{24,28},{28,20},{20,12},{12,4},{4,0},{1,9},{9... | collective-permute-start | bytes 786440 | tf_op jit(solution)/shard_map/ppermute | solution.py:557
  30.8 6.7 %collective-permute-start.8 = (bf16[256,512]{1,0:T(8,128)(2,1)S(1)}, bf16[256,512]{1,0:T(8,128)(2,1)S(1)}, u32[]{:S(2)}, u32[]{:S(2)}) collective-permute-start(bf16[256,512]{1,0:T(8,128)(2,1)S(1)} %collective-permute-done.5), channel_id=1, source_target_pairs={{0,4},{8,0},{16,8},{24,16},{28,24},{20,28},{12,20},{4,12},{1,5},{9... | collective-permute-start | bytes 786440 | tf_op jit(solution)/shard_map/ppermute | solution.py:557
  37.6 5.0 %collective-permute-start.10 = (bf16[128,512]{1,0:T(8,128)(2,1)S(1)}, bf16[128,512]{1,0:T(8,128)(2,1)S(1)}, u32[]{:S(2)}, u32[]{:S(2)}) collective-permute-start(bf16[128,512]{1,0:T(8,128)(2,1)S(1)} %slice.425), channel_id=1, source_target_pairs={{0,8},{8,16},{16,24},{24,28},{28,20},{20,12},{12,4},{4,0},{1,9},{9... | collective-permute-start | bytes 393224 | tf_op jit(solution)/shard_map/ppermute | solution.py:557
  39.1 5.0 %collective-permute-start.11 = (bf16[128,512]{1,0:T(8,128)(2,1)S(1)}, bf16[128,512]{1,0:T(8,128)(2,1)S(1)}, u32[]{:S(2)}, u32[]{:S(2)}) collective-permute-start(bf16[128,512]{1,0:T(8,128)(2,1)S(1)} %slice.426), channel_id=1, source_target_pairs={{0,4},{8,0},{16,8},{24,16},{28,24},{20,28},{12,20},{4,12},{1,5},{9... | collective-permute-start | bytes 393224 | tf_op jit(solution)/shard_map/ppermute | solution.py:557
  39.8 11.0 %collective-permute-start.13 = (bf16[2,256,512]{2,1,0:T(8,128)(2,1)S(1)}, bf16[2,256,512]{2,1,0:T(8,128)(2,1)S(1)}, u32[]{:S(2)}, u32[]{:S(2)}) collective-permute-start(bf16[2,256,512]{2,1,0:T(8,128)(2,1)S(1)} %get-tuple-element.155), channel_id=1, source_target_pairs={{0,1},{1,0},{2,3},{3,2},{4,5},{5,4},{6,7},{7,6},{8,9},{9,8},{10,11... | collective-permute-start | bytes 1572872 | tf_op jit(solution)/shard_map/ppermute | solution.py:544
  44.3 6.5 %collective-permute-start.14 = (bf16[3,256,512]{2,1,0:T(8,128)(2,1)S(1)}, bf16[3,256,512]{2,1,0:T(8,128)(2,1)S(1)}, u32[]{:S(2)}, u32[]{:S(2)}) collective-permute-start(bf16[3,256,512]{2,1,0:T(8,128)(2,1)S(1)} %pad_maximum_fusion.11), channel_id=1, source_target_pairs={{0,1},{1,0},{2,3},{3,2},{4,5},{5,4},{6,7},{7,6},{8,9},{9,8},{10,11... | collective-permute-start | bytes 2359304 | tf_op jit(solution)/shard_map/ppermute | solution.py:544
  57.1 4.2 collective-permute-start.15
  57.2 11.0 %collective-permute-start.17 = (bf16[256,2048]{1,0:T(8,128)(2,1)}, bf16[256,2048]{1,0:T(8,128)(2,1)S(1)}, u32[]{:S(2)}, u32[]{:S(2)}) collective-permute-start(bf16[256,2048]{1,0:T(8,128)(2,1)} %pad_maximum_fusion.6), channel_id=1, source_target_pairs={{0,1},{1,0},{2,3},{3,2},{4,5},{5,4},{6,7},{7,6},{8,9},{9,8},{10,11... | collective-permute-start | bytes 3145736 | tf_op jit(solution)/shard_map/ppermute | solution.py:544
  63.3 25.2 %collective-permute-start.16 = (bf16[256,2048]{1,0:T(8,128)(2,1)S(1)}, bf16[256,2048]{1,0:T(8,128)(2,1)S(1)}, u32[]{:S(2)}, u32[]{:S(2)}) collective-permute-start(bf16[256,2048]{1,0:T(8,128)(2,1)S(1)} %pad_maximum_fusion.7), channel_id=1, source_target_pairs={{0,2},{1,3},{2,0},{3,1},{4,6},{5,7},{6,4},{7,5},{8,10},{9,11},{10,... | collective-permute-start | bytes 3145736 | tf_op jit(solution)/shard_map/ppermute | solution.py:548
  68.2 5.1 %collective-permute-start.18 = (bf16[512,256]{1,0:T(8,128)(2,1)S(1)}, bf16[512,256]{1,0:T(8,128)(2,1)S(1)}, u32[]{:S(2)}, u32[]{:S(2)}) collective-permute-start(bf16[512,256]{1,0:T(8,128)(2,1)S(1)} %get-tuple-element.167), channel_id=1, source_target_pairs={{0,1},{1,0},{2,3},{3,2},{4,5},{5,4},{6,7},{7,6},{8,9},{9,8},{10,11... | collective-permute-start | bytes 786440 | tf_op jit(solution)/shard_map/ppermute | solution.py:544
  90.6 2.9 collective-permute-start.19
  114.5 72.2 %collective-permute-start.25 = (bf16[4,1408,256]{2,1,0:T(8,128)(2,1)}, bf16[4,1408,256]{2,1,0:T(8,128)(2,1)}, u32[]{:S(2)}, u32[]{:S(2)}) collective-permute-start(bf16[4,1408,256]{2,1,0:T(8,128)(2,1)} %grad_by_columns.6), channel_id=1, source_target_pairs={{0,4},{4,0},{8,12},{12,8},{16,20},{20,16},{24,28},{28,24},{1,5},{5... | collective-permute-start | bytes 8650760 | tf_op jit(solution)/shard_map/ppermute | solution.py:567
  125.9 78.4 %collective-permute-start.26 = (bf16[4,256,1408]{2,1,0:T(8,128)(2,1)}, bf16[4,256,1408]{2,1,0:T(8,128)(2,1)}, u32[]{:S(2)}, u32[]{:S(2)}) collective-permute-start(bf16[4,256,1408]{2,1,0:T(8,128)(2,1)} %grad_by_rows.6), channel_id=1, source_target_pairs={{0,8},{4,12},{8,0},{12,4},{16,24},{20,28},{24,16},{28,20},{1,9},{5... | collective-permute-start | bytes 8650760 | tf_op jit(solution)/shard_map/ppermute | solution.py:567
  140.6 3.8 collective-permute-start.20
  146.6 4.2 collective-permute-start.21
  147.4 25.2 %collective-permute-start.22 = (bf16[256,2048]{1,0:T(8,128)(2,1)S(1)}, bf16[256,2048]{1,0:T(8,128)(2,1)S(1)}, u32[]{:S(2)}, u32[]{:S(2)}) collective-permute-start(bf16[256,2048]{1,0:T(8,128)(2,1)S(1)} %pad_maximum_fusion.8), channel_id=1, source_target_pairs={{0,2},{1,3},{2,0},{3,1},{4,6},{5,7},{6,4},{7,5},{8,10},{9,11},{10,... | collective-permute-start | bytes 3145736 | tf_op jit(solution)/shard_map/ppermute | solution.py:548
  176.0 13.7 %collective-permute-start.24 = (bf16[256,2048]{1,0:T(8,128)(2,1)}, bf16[256,2048]{1,0:T(8,128)(2,1)}, u32[]{:S(2)}, u32[]{:S(2)}) collective-permute-start(bf16[256,2048]{1,0:T(8,128)(2,1)} %get-tuple-element.260), channel_id=1, source_target_pairs={{0,1},{1,0},{2,3},{3,2},{4,5},{5,4},{6,7},{7,6},{8,9},{9,8},{10,11... | collective-permute-start | bytes 3145736 | tf_op jit(solution)/shard_map/ppermute | solution.py:544
  181.8 31.8 %collective-permute-start.23 = (bf16[128,2048]{1,0:T(8,128)(2,1)}, bf16[128,2048]{1,0:T(8,128)(2,1)}, u32[]{:S(2)}, u32[]{:S(2)}) collective-permute-start(bf16[128,2048]{1,0:T(8,128)(2,1)} %slice.445), channel_id=1, source_target_pairs={{0,2},{1,3},{2,0},{3,1},{4,6},{5,7},{6,4},{7,5},{8,10},{9,11},{10,... | collective-permute-start | bytes 1572872 | tf_op jit(solution)/shard_map/ppermute | solution.py:548
  186.6 64.8 %collective-permute-start.28 = (bf16[4,256,1408]{2,1,0:T(8,128)(2,1)S(1)}, bf16[4,256,1408]{2,1,0:T(8,128)(2,1)}, u32[]{:S(2)}, u32[]{:S(2)}) collective-permute-start(bf16[4,256,1408]{2,1,0:T(8,128)(2,1)S(1)} %grad_by_rows.8), channel_id=1, source_target_pairs={{0,4},{4,0},{8,12},{12,8},{16,20},{20,16},{24,28},{28,24},{1,5},{5... | collective-permute-start | bytes 8650760 | tf_op jit(solution)/shard_map/ppermute | solution.py:567
  191.7 34.1 %collective-permute-start.29 = (bf16[2,1408,256]{2,1,0:T(8,128)(2,1)}, bf16[2,1408,256]{2,1,0:T(8,128)(2,1)}, u32[]{:S(2)}, u32[]{:S(2)}) collective-permute-start(bf16[2,1408,256]{2,1,0:T(8,128)(2,1)} %add_convert_fusion.3), channel_id=1, source_target_pairs={{0,8},{4,12},{8,0},{12,4},{16,24},{20,28},{24,16},{28,20},{1,9},{5... | collective-permute-start | bytes 4325384 | tf_op jit(solution)/shard_map/ppermute | solution.py:567
  212.2 41.0 %collective-permute-start.27 = (bf16[8,256,512]{2,1,0:T(8,128)(2,1)S(1)}, bf16[8,256,512]{2,1,0:T(8,128)(2,1)S(1)}, u32[]{:S(2)}, u32[]{:S(2)}) collective-permute-start(bf16[8,256,512]{2,1,0:T(8,128)(2,1)S(1)} %get-tuple-element.203), channel_id=1, source_target_pairs={{0,1},{1,0},{2,3},{3,2},{4,5},{5,4},{6,7},{7,6},{8,9},{9,8},{10,11... | collective-permute-start | bytes 6291464 | tf_op jit(solution)/shard_map/ppermute | solution.py:544
  213.3 41.2 %collective-permute-start.32 = (bf16[256,1024]{1,0:T(8,128)(2,1)S(1)}, bf16[256,1024]{1,0:T(8,128)(2,1)S(1)}, u32[]{:S(2)}, u32[]{:S(2)}) collective-permute-start(bf16[256,1024]{1,0:T(8,128)(2,1)S(1)} %convolution_convert_fusion.7), channel_id=1, source_target_pairs={{0,1},{1,0},{2,3},{3,2},{4,5},{5,4},{6,7},{7,6},{8,9},{9,8},{10,11... | collective-permute-start | bytes 1572872 | tf_op jit(solution)/shard_map/ppermute | solution.py:544
  227.4 46.7 %collective-permute-start.31 = (bf16[1,1408,256]{2,1,0:T(8,128)(2,1)S(1)}, bf16[1,1408,256]{2,1,0:T(8,128)(2,1)S(1)}, u32[]{:S(2)}, u32[]{:S(2)}) collective-permute-start(bf16[1,1408,256]{2,1,0:T(8,128)(2,1)S(1)} %add_convert_fusion.10), channel_id=1, source_target_pairs={{0,16},{4,20},{8,24},{12,28},{16,0},{20,4},{24,8},{28,12},{1,17},{... | collective-permute-start | bytes 2162696 | tf_op jit(solution)/shard_map/ppermute | solution.py:567
  253.9 24.5 %collective-permute-start.30 = (bf16[8,128,512]{2,1,0:T(8,128)(2,1)S(1)}, bf16[8,128,512]{2,1,0:T(8,128)(2,1)S(1)}, u32[]{:S(2)}, u32[]{:S(2)}) collective-permute-start(bf16[8,128,512]{2,1,0:T(8,128)(2,1)S(1)} %slice.548), channel_id=1, source_target_pairs={{0,2},{1,3},{2,0},{3,1},{4,6},{5,7},{6,4},{7,5},{8,10},{9,11},{10,... | collective-permute-start | bytes 3145736 | tf_op jit(solution)/shard_map/ppermute | solution.py:548
  254.7 34.6 %collective-permute-start.34 = (bf16[2,256,1408]{2,1,0:T(8,128)(2,1)S(1)}, bf16[2,256,1408]{2,1,0:T(8,128)(2,1)S(1)}, u32[]{:S(2)}, u32[]{:S(2)}) collective-permute-start(bf16[2,256,1408]{2,1,0:T(8,128)(2,1)S(1)} %add_convert_fusion.2), channel_id=1, source_target_pairs={{0,4},{4,0},{8,12},{12,8},{16,20},{20,16},{24,28},{28,24},{1,5},{5... | collective-permute-start | bytes 4325384 | tf_op jit(solution)/shard_map/ppermute | solution.py:567
  255.0 82.9 %collective-permute-start.42 = (bf16[2,256,1408]{2,1,0:T(8,128)(2,1)S(1)}, bf16[2,256,1408]{2,1,0:T(8,128)(2,1)S(1)}, u32[]{:S(2)}, u32[]{:S(2)}) collective-permute-start(bf16[2,256,1408]{2,1,0:T(8,128)(2,1)S(1)} %add_convert_fusion.1), channel_id=1, source_target_pairs={{0,8},{4,12},{8,0},{12,4},{16,24},{20,28},{24,16},{28,20},{1,9},{5... | collective-permute-start | bytes 4325384 | tf_op jit(solution)/shard_map/ppermute | solution.py:567
  278.7 23.8 %collective-permute-start.33 = (bf16[4,128,512]{2,1,0:T(8,128)(2,1)S(1)}, bf16[4,128,512]{2,1,0:T(8,128)(2,1)S(1)}, u32[]{:S(2)}, u32[]{:S(2)}) collective-permute-start(bf16[4,128,512]{2,1,0:T(8,128)(2,1)S(1)} %slice.551), channel_id=1, source_target_pairs={{0,4},{4,0},{8,12},{12,8},{16,20},{20,16},{24,28},{28,24},{1,5},{5... | collective-permute-start | bytes 1572872 | tf_op jit(solution)/shard_map/ppermute | solution.py:567
  282.5 20.3 %collective-permute-start.36 = (bf16[256,1024]{1,0:T(8,128)(2,1)S(1)}, bf16[256,1024]{1,0:T(8,128)(2,1)S(1)}, u32[]{:S(2)}, u32[]{:S(2)}) collective-permute-start(bf16[256,1024]{1,0:T(8,128)(2,1)S(1)} %pad_maximum_fusion.14), channel_id=1, source_target_pairs={{0,2},{1,3},{2,0},{3,1},{4,6},{5,7},{6,4},{7,5},{8,10},{9,11},{10,... | collective-permute-start | bytes 1572872 | tf_op jit(solution)/shard_map/ppermute | solution.py:548
  290.7 42.1 %collective-permute-start.39 = (bf16[1,256,1408]{2,1,0:T(8,128)(2,1)S(1)}, bf16[1,256,1408]{2,1,0:T(8,128)(2,1)S(1)}, u32[]{:S(2)}, u32[]{:S(2)}) collective-permute-start(bf16[1,256,1408]{2,1,0:T(8,128)(2,1)S(1)} %add_convert_fusion.9), channel_id=1, source_target_pairs={{0,16},{4,20},{8,24},{12,28},{16,0},{20,4},{24,8},{28,12},{1,17},{... | collective-permute-start | bytes 2162696 | tf_op jit(solution)/shard_map/ppermute | solution.py:567
  302.3 21.1 %collective-permute-start.40 = (bf16[4,512,256]{2,1,0:T(8,128)(2,1)S(1)}, bf16[4,512,256]{2,1,0:T(8,128)(2,1)S(1)}, u32[]{:S(2)}, u32[]{:S(2)}) collective-permute-start(bf16[4,512,256]{2,1,0:T(8,128)(2,1)S(1)} %copy-done.32), channel_id=1, source_target_pairs={{0,4},{4,0},{8,12},{12,8},{16,20},{20,16},{24,28},{28,24},{1,5},{5... | collective-permute-start | bytes 3145736 | tf_op jit(solution)/shard_map/ppermute | solution.py:567
  302.7 19.2 %collective-permute-start.35 = (bf16[2,128,512]{2,1,0:T(8,128)(2,1)S(1)}, bf16[2,128,512]{2,1,0:T(8,128)(2,1)S(1)}, u32[]{:S(2)}, u32[]{:S(2)}) collective-permute-start(bf16[2,128,512]{2,1,0:T(8,128)(2,1)S(1)} %add_convert_fusion.18), channel_id=1, source_target_pairs={{0,8},{4,12},{8,0},{12,4},{16,24},{20,28},{24,16},{28,20},{1,9},{5... | collective-permute-start | bytes 786440 | tf_op jit(solution)/shard_map/ppermute | solution.py:567
  303.6 31.9 %collective-permute-start.38 = (bf16[256,1024]{1,0:T(8,128)(2,1)S(1)}, bf16[256,1024]{1,0:T(8,128)(2,1)S(1)}, u32[]{:S(2)}, u32[]{:S(2)}) collective-permute-start(bf16[256,1024]{1,0:T(8,128)(2,1)S(1)} %multiply_convert_fusion.1), channel_id=1, source_target_pairs={{0,1},{1,0},{2,3},{3,2},{4,5},{5,4},{6,7},{7,6},{8,9},{9,8},{10,11... | collective-permute-start | bytes 1572872 | tf_op jit(solution)/shard_map/ppermute | solution.py:544
  321.9 14.3 %collective-permute-start.37 = (bf16[1,128,512]{2,1,0:T(8,128)(2,1)S(1)}, bf16[1,128,512]{2,1,0:T(8,128)(2,1)S(1)}, u32[]{:S(2)}, u32[]{:S(2)}) collective-permute-start(bf16[1,128,512]{2,1,0:T(8,128)(2,1)S(1)} %add_convert_fusion.19), channel_id=1, source_target_pairs={{0,16},{4,20},{8,24},{12,28},{16,0},{20,4},{24,8},{28,12},{1,17},{... | collective-permute-start | bytes 393224 | tf_op jit(solution)/shard_map/ppermute | solution.py:567
  323.5 42.5 %collective-permute-start.46 = (bf16[2,512,256]{2,1,0:T(8,128)(2,1)S(1)}, bf16[2,512,256]{2,1,0:T(8,128)(2,1)S(1)}, u32[]{:S(2)}, u32[]{:S(2)}) collective-permute-start(bf16[2,512,256]{2,1,0:T(8,128)(2,1)S(1)} %add_convert_fusion.13), channel_id=1, source_target_pairs={{0,8},{4,12},{8,0},{12,4},{16,24},{20,28},{24,16},{28,20},{1,9},{5... | collective-permute-start | bytes 1572872 | tf_op jit(solution)/shard_map/ppermute | solution.py:567
  336.4 5.8 %collective-permute-start.41 = (bf16[128,512]{1,0:T(8,128)(2,1)S(1)}, bf16[128,512]{1,0:T(8,128)(2,1)S(1)}, u32[]{:S(2)}, u32[]{:S(2)}) collective-permute-start(bf16[128,512]{1,0:T(8,128)(2,1)S(1)} %pad_maximum_fusion.16), channel_id=1, source_target_pairs={{0,2},{1,3},{2,0},{3,1},{4,6},{5,7},{6,4},{7,5},{8,10},{9,11},{10,... | collective-permute-start | bytes 393224 | tf_op jit(solution)/shard_map/ppermute | solution.py:548
  339.4 24.7 %collective-permute-start.44 = (bf16[4,512,256]{2,1,0:T(8,128)(2,1)S(1)}, bf16[4,512,256]{2,1,0:T(8,128)(2,1)S(1)}, u32[]{:S(2)}, u32[]{:S(2)}) collective-permute-start(bf16[4,512,256]{2,1,0:T(8,128)(2,1)S(1)} %copy-done.30), channel_id=1, source_target_pairs={{0,4},{4,0},{8,12},{12,8},{16,20},{20,16},{24,28},{28,24},{1,5},{5... | collective-permute-start | bytes 3145736 | tf_op jit(solution)/shard_map/ppermute | solution.py:567
  342.1 34.9 %collective-permute-start.54 = (bf16[1,256,1408]{2,1,0:T(8,128)(2,1)S(1)}, bf16[1,256,1408]{2,1,0:T(8,128)(2,1)S(1)}, u32[]{:S(2)}, u32[]{:S(2)}) collective-permute-start(bf16[1,256,1408]{2,1,0:T(8,128)(2,1)S(1)} %add_convert_fusion.8), channel_id=1, source_target_pairs={{0,16},{4,20},{8,24},{12,28},{16,0},{20,4},{24,8},{28,12},{1,17},{... | collective-permute-start | bytes 2162696 | tf_op jit(solution)/shard_map/ppermute | solution.py:567
  342.1 23.4 %collective-permute-start.47 = (bf16[256,512]{1,0:T(8,128)(2,1)S(1)}, bf16[256,512]{1,0:T(8,128)(2,1)S(1)}, u32[]{:S(2)}, u32[]{:S(2)}) collective-permute-start(bf16[256,512]{1,0:T(8,128)(2,1)S(1)} %pad_maximum_fusion.15), channel_id=1, source_target_pairs={{0,1},{1,0},{2,3},{3,2},{4,5},{5,4},{6,7},{7,6},{8,9},{9,8},{10,11... | collective-permute-start | bytes 786440 | tf_op jit(solution)/shard_map/ppermute | solution.py:544
  343.4 22.1 %collective-permute-start.43 = (f32[2048]{0:T(1024)S(1)}, f32[2048]{0:T(1024)S(1)}, u32[]{:S(2)}, u32[]{:S(2)}) collective-permute-start(f32[2048]{0:T(1024)S(1)} %get-tuple-element.258), channel_id=1, source_target_pairs={{0,2},{1,3},{2,0},{3,1},{4,6},{5,7},{6,4},{7,5},{8,10},{9,11},{10,... | collective-permute-start | bytes 24584 | tf_op jit(solution)/shard_map/ppermute | solution.py:548
  364.3 29.9 %collective-permute-start.50 = (bf16[2,512,256]{2,1,0:T(8,128)(2,1)S(1)}, bf16[2,512,256]{2,1,0:T(8,128)(2,1)S(1)}, u32[]{:S(2)}, u32[]{:S(2)}) collective-permute-start(bf16[2,512,256]{2,1,0:T(8,128)(2,1)S(1)} %add_convert_fusion.12), channel_id=1, source_target_pairs={{0,8},{4,12},{8,0},{12,4},{16,24},{20,28},{24,16},{28,20},{1,9},{5... | collective-permute-start | bytes 1572872 | tf_op jit(solution)/shard_map/ppermute | solution.py:567
  365.5 2.9 collective-permute-start.45
  366.0 9.2 %collective-permute-start.51 = (bf16[4,64,512]{2,1,0:T(8,128)(2,1)S(1)}, bf16[4,64,512]{2,1,0:T(8,128)(2,1)S(1)}, u32[]{:S(2)}, u32[]{:S(2)}) collective-permute-start(bf16[4,64,512]{2,1,0:T(8,128)(2,1)S(1)} %bitcast.98), channel_id=1, source_target_pairs={{0,4},{4,0},{8,12},{12,8},{16,20},{20,16},{24,28},{28,24},{1,5},{5... | collective-permute-start | bytes 786440 | tf_op jit(solution)/shard_map/ppermute | solution.py:567
  368.0 29.7 %collective-permute-start.49 = (bf16[4,128,1024]{2,1,0:T(8,128)(2,1)S(1)}, bf16[4,128,1024]{2,1,0:T(8,128)(2,1)S(1)}, u32[]{:S(2)}, u32[]{:S(2)}) collective-permute-start(bf16[4,128,1024]{2,1,0:T(8,128)(2,1)S(1)} %grad_by_rows.10), channel_id=1, source_target_pairs={{0,4},{4,0},{8,12},{12,8},{16,20},{20,16},{24,28},{28,24},{1,5},{5... | collective-permute-start | bytes 3145736 | tf_op jit(solution)/shard_map/ppermute | solution.py:567
  368.3 16.2 %collective-permute-start.53 = (bf16[1,512,256]{2,1,0:T(8,128)(2,1)S(1)}, bf16[1,512,256]{2,1,0:T(8,128)(2,1)S(1)}, u32[]{:S(2)}, u32[]{:S(2)}) collective-permute-start(bf16[1,512,256]{2,1,0:T(8,128)(2,1)S(1)} %add_convert_fusion.17), channel_id=1, source_target_pairs={{0,16},{4,20},{8,24},{12,28},{16,0},{20,4},{24,8},{28,12},{1,17},{... | collective-permute-start | bytes 786440 | tf_op jit(solution)/shard_map/ppermute | solution.py:567
  375.2 23.6 %collective-permute-start.48 = (f32[5120]{0:T(1024)S(1)}, f32[5120]{0:T(1024)S(1)}, u32[]{:S(2)}, u32[]{:S(2)}) collective-permute-start(f32[5120]{0:T(1024)S(1)} %fusion.60), channel_id=1, source_target_pairs={{0,4},{4,0},{8,12},{12,8},{16,20},{20,16},{24,28},{28,24},{1,5},{5... | collective-permute-start | bytes 61448 | tf_op jit(solution)/shard_map/ppermute | solution.py:567
  377.0 17.0 %collective-permute-start.52 = (bf16[2,64,512]{2,1,0:T(8,128)(2,1)S(1)}, bf16[2,64,512]{2,1,0:T(8,128)(2,1)S(1)}, u32[]{:S(2)}, u32[]{:S(2)}) collective-permute-start(bf16[2,64,512]{2,1,0:T(8,128)(2,1)S(1)} %fusion.50), channel_id=1, source_target_pairs={{0,8},{4,12},{8,0},{12,4},{16,24},{20,28},{24,16},{28,20},{1,9},{5... | collective-permute-start | bytes 393224 | tf_op jit(solution)/shard_map/ppermute | solution.py:567
  384.7 24.3 %collective-permute-start.57 = (bf16[4,64,1024]{2,1,0:T(8,128)(2,1)S(1)}, bf16[4,64,1024]{2,1,0:T(8,128)(2,1)S(1)}, u32[]{:S(2)}, u32[]{:S(2)}) collective-permute-start(bf16[4,64,1024]{2,1,0:T(8,128)(2,1)S(1)} %bitcast.97), channel_id=1, source_target_pairs={{0,4},{4,0},{8,12},{12,8},{16,20},{20,16},{24,28},{28,24},{1,5},{5... | collective-permute-start | bytes 1572872 | tf_op jit(solution)/shard_map/ppermute | solution.py:567
  394.1 15.9 %collective-permute-start.56 = (bf16[1,64,512]{2,1,0:T(8,128)(2,1)S(1)}, bf16[1,64,512]{2,1,0:T(8,128)(2,1)S(1)}, u32[]{:S(2)}, u32[]{:S(2)}) collective-permute-start(bf16[1,64,512]{2,1,0:T(8,128)(2,1)S(1)} %fusion.52), channel_id=1, source_target_pairs={{0,16},{4,20},{8,24},{12,28},{16,0},{20,4},{24,8},{28,12},{1,17},{... | collective-permute-start | bytes 196616 | tf_op jit(solution)/shard_map/ppermute | solution.py:567
  397.9 24.1 %collective-permute-start.62 = (bf16[2,128,1024]{2,1,0:T(8,128)(2,1)S(1)}, bf16[2,128,1024]{2,1,0:T(8,128)(2,1)S(1)}, u32[]{:S(2)}, u32[]{:S(2)}) collective-permute-start(bf16[2,128,1024]{2,1,0:T(8,128)(2,1)S(1)} %add_convert_fusion.11), channel_id=1, source_target_pairs={{0,8},{4,12},{8,0},{12,4},{16,24},{20,28},{24,16},{28,20},{1,9},{5... | collective-permute-start | bytes 1572872 | tf_op jit(solution)/shard_map/ppermute | solution.py:567
  398.8 12.7 %collective-permute-start.55 = (f32[5120]{0:T(1024)S(1)}, f32[5120]{0:T(1024)S(1)}, u32[]{:S(2)}, u32[]{:S(2)}) collective-permute-start(f32[5120]{0:T(1024)S(1)} %add.419), channel_id=1, source_target_pairs={{0,8},{4,12},{8,0},{12,4},{16,24},{20,28},{24,16},{28,20},{1,9},{5... | collective-permute-start | bytes 61448 | tf_op jit(solution)/shard_map/ppermute | solution.py:567
  409.0 9.3 %collective-permute-start.59 = (bf16[2,64,1024]{2,1,0:T(8,128)(2,1)S(1)}, bf16[2,64,1024]{2,1,0:T(8,128)(2,1)S(1)}, u32[]{:S(2)}, u32[]{:S(2)}) collective-permute-start(bf16[2,64,1024]{2,1,0:T(8,128)(2,1)S(1)} %fusion.41), channel_id=1, source_target_pairs={{0,8},{4,12},{8,0},{12,4},{16,24},{20,28},{24,16},{28,20},{1,9},{5... | collective-permute-start | bytes 786440 | tf_op jit(solution)/shard_map/ppermute | solution.py:567
  411.6 5.6 %collective-permute-start.58 = (f32[5120]{0:T(1024)S(1)}, f32[5120]{0:T(1024)S(1)}, u32[]{:S(2)}, u32[]{:S(2)}) collective-permute-start(f32[5120]{0:T(1024)S(1)} %add.424), channel_id=1, source_target_pairs={{0,16},{4,20},{8,24},{12,28},{16,0},{20,4},{24,8},{28,12},{1,17},{... | collective-permute-start | bytes 61448 | tf_op jit(solution)/shard_map/ppermute | solution.py:567
  416.3 23.6 %collective-permute-start.61 = (bf16[1,512,256]{2,1,0:T(8,128)(2,1)S(1)}, bf16[1,512,256]{2,1,0:T(8,128)(2,1)S(1)}, u32[]{:S(2)}, u32[]{:S(2)}) collective-permute-start(bf16[1,512,256]{2,1,0:T(8,128)(2,1)S(1)} %add_convert_fusion.16), channel_id=1, source_target_pairs={{0,16},{4,20},{8,24},{12,28},{16,0},{20,4},{24,8},{28,12},{1,17},{... | collective-permute-start | bytes 786440 | tf_op jit(solution)/shard_map/ppermute | solution.py:567
  418.4 24.4 %collective-permute-start.60 = (bf16[1,64,1024]{2,1,0:T(8,128)(2,1)S(1)}, bf16[1,64,1024]{2,1,0:T(8,128)(2,1)S(1)}, u32[]{:S(2)}, u32[]{:S(2)}) collective-permute-start(bf16[1,64,1024]{2,1,0:T(8,128)(2,1)S(1)} %fusion.49), channel_id=1, source_target_pairs={{0,16},{4,20},{8,24},{12,28},{16,0},{20,4},{24,8},{28,12},{1,17},{... | collective-permute-start | bytes 393224 | tf_op jit(solution)/shard_map/ppermute | solution.py:567
  422.1 24.3 %collective-permute-start.63 = (bf16[1,128,1024]{2,1,0:T(8,128)(2,1)S(1)}, bf16[1,128,1024]{2,1,0:T(8,128)(2,1)S(1)}, u32[]{:S(2)}, u32[]{:S(2)}) collective-permute-start(bf16[1,128,1024]{2,1,0:T(8,128)(2,1)S(1)} %add_convert_fusion.15), channel_id=1, source_target_pairs={{0,16},{4,20},{8,24},{12,28},{16,0},{20,4},{24,8},{28,12},{1,17},{... | collective-permute-start | bytes 786440 | tf_op jit(solution)/shard_map/ppermute | solution.py:567
  (69 other events, 457.4 us)

commit v4 on v3

--- a/solution.py
+++ b/solution.py
@@ -23,10 +23,11 @@
     "branch_grad", "feed_far", "gate", "down_1", "attended_back", "out_send0", "out_send1", "gate_keep",
     "up_1", "attention_back", "latent_product", "feed", "down_2", "gate_1", "chip_keys", "latent_chip",
     "up_go", "out_keep0", "out_keep1", "query_send", "query_keep", "down_end", "keys", "latent_far", "up_2",
-    "out_a", "kv_1", "compressed", "kv_2", "out_a_1", "out_b", "up_end", "down_q_parts", "own_keys_grad",
-    "gate_2", "half_keys", "normed_grad", "out_b_1", "query", "gains_own", "kv_parts", "kv_w", "out_a_2",
-    "gains_1", "kv_w_1", "gate_end", "q_down", "out_a_end", "kv_w_2", "out_b_2", "query_1", "gains_2",
-    "q_down_1", "kv_w_end", "gains_3", "q_down_2", "query_2", "out_b_end", "q_down_end", "query_end",
+    "out_a", "kv_1", "compressed", "kv_2", "gate_2", "out_a_1", "out_b", "up_end", "gate_go", "down_q_parts",
+    "own_keys_grad", "half_keys", "normed_grad", "out_b_1", "query", "gains_own", "kv_parts", "kv_w",
+    "out_a_2", "gains_1", "kv_w_1", "gate_end", "q_down", "out_a_end", "kv_w_2", "out_b_2", "query_1",
+    "gains_2", "q_down_1", "gains_3", "query_2", "kv_w_end", "out_b_end", "q_down_2", "gains_4", "q_down_end",
+    "query_end",
 )
 
 NN = (((1,), (0,)), ((), ()))
@@ -144,14 +145,18 @@
     )(lengths, values, gain, weight, freq)
 
 
-def fwd_kernel(heads, lengths, q_ref, a_ref, b_ref, o_ref, ot_ref, lse_ref, m_s, l_s, acc_s, bias_s):
+def fwd_kernel(heads, lengths, q_ref, a_ref, b_ref, w_ref, o_ref, ot_ref, lse_ref, keep_ref, send_ref,
+               m_s, l_s, acc_s, bias_s, w_s, w_sem):
     slot = pl.program_id(0)
     count = pl.num_programs(0)
     keys, rows = bias_s.shape
     base, needed, bounded = slot_state(lengths, slot, count, rows)
 
+    fetch = pltpu.make_async_copy(w_ref, w_s, w_sem)
+
     @pl.when(slot == 0)
     def _():
+        fetch.start()
         m_s[...] = jnp.full_like(m_s, NEG)
         l_s[...] = jnp.zeros_like(l_s)
         acc_s[...] = jnp.zeros_like(acc_s)
@@ -192,9 +197,16 @@
             ot_ref[h * HD : (h + 1) * HD, :] = out_t
             o_ref[:, h * HD : (h + 1) * HD] = out_t.T
             lse_ref[h] = jnp.broadcast_to(m_s[h, 0:1, :] + jnp.log2(total), lse_ref.shape[1:])
-
-
-def attend(lengths, query, kv_a, kv_b):
+        fetch.wait()
+        cut = min(512, w_s.shape[1])
+        for first in range(0, w_s.shape[1], cut):
+            at = slice(first, first + cut)
+            part = dot(o_ref[...], w_s[:, at]).astype(BF16)
+            keep_ref[:, at] = part[: rows // 2]
+            send_ref[:, at] = part[rows // 2 :]
+
+
+def attend(lengths, query, kv_a, kv_b, weight):
     rows, width = query.shape
     heads = width // HD
     slots, half, wide = kv_a.shape
@@ -202,21 +214,23 @@
     whole = lambda *shape: pl.BlockSpec(shape, lambda i, m: (0,) * len(shape))
     tile = pl.BlockSpec((1, half, wide), lambda i, m: (i, 0, 0))
     state = [(heads, 8, rows), (heads, 8, rows), (heads, HD, rows), (keys, rows)]
-    out = [((rows, width), BF16), ((width, rows), BF16), ((heads, 8, rows), F32)]
+    branch = ((rows // 2, weight.shape[1]), BF16)
+    out = [((rows, width), BF16), ((width, rows), BF16), ((heads, 8, rows), F32), branch, branch]
     return pl.pallas_call(
         functools.partial(fwd_kernel, heads),
         grid_spec=pltpu.PrefetchScalarGridSpec(
             num_scalar_prefetch=1,
             grid=(slots,),
-            in_specs=[whole(rows, width), tile, tile],
+            in_specs=[whole(rows, width), tile, tile, pl.BlockSpec(memory_space=pl.ANY)],
             out_specs=[whole(*shape) for shape, _ in out],
-            scratch_shapes=[pltpu.VMEM(shape, F32) for shape in state],
+            scratch_shapes=[pltpu.VMEM(shape, F32) for shape in state]
+            + [pltpu.VMEM(weight.shape, BF16), pltpu.SemaphoreType.DMA],
         ),
         out_shape=[jax.ShapeDtypeStruct(*o) for o in out],
-        compiler_params=pltpu.CompilerParams(vmem_limit_bytes=24 * MIB),
+        compiler_params=pltpu.CompilerParams(vmem_limit_bytes=32 * MIB),
         cost_estimate=BRIEF,
         name="attend",
-    )(lengths, query, kv_a, kv_b)
+    )(lengths, query, kv_a, kv_b, weight)
 
 
 def bwd_kernel(heads, lengths, _, q_ref, do_ref, a_ref, b_ref, lse_ref, delta_ref, cos_ref, sin_ref,
@@ -664,7 +678,7 @@
     pair = jnp.concatenate([keyval, order.after(keyval_far)], axis=0)
     order.ran(pair)
     ahead, back = ring_shift(pair, 1, count), ring_shift(pair, -1, count)
-    both_far = far(jnp.concatenate(order.after(block_input, cotangent), axis=0))
+    input_far = far(order.after(block_input))
     empty = jnp.zeros((count,) + pair.shape, BF16)
     kv_a, kv_b = lax.dynamic_update_slice(empty, order.after(pair)[None], (0, 0, 0)), empty
     waiting, moving = [pair[None]], []
@@ -708,29 +722,24 @@
             kv_b = take_near(kv_b)
     while moving:
         kv_b = take_near(kv_b)
-    both_far = order.after(both_far)
-    input_half = jnp.concatenate([block_input, both_far[:own]], axis=0)
-    grad_half = jnp.concatenate([cotangent, both_far[own:]], axis=0)
-    order.ran(input_half, grad_half)
-    grad_near = near(grad_half)
+    grad_far = far(order.after(cotangent))
+    input_half = jnp.concatenate([block_input, order.after(input_far)], axis=0)
+    order.ran(input_half)
     kv_a, kv_b = order.after(kv_a, kv_b)
-    attended, attended_t, lse = attend(lengths, order.after(query), kv_a, kv_b)
+    attended, attended_t, lse, branch_keep, branch_send = attend(
+        lengths, order.after(query), kv_a, kv_b, out_weight
+    )
     order.ran(attended)
-
-    def sum_half(lefts, rights, dims, meanwhile):
-        lefts[0] = order.after(lefts[0])
-        keep, send = product(lefts, rights, dims)
-        order.ran(send)
-        chip = add(keep, order.after(near(send))).astype(BF16)
-        order.ran(chip)
-        moving = far(swap(chip))
-        made = meanwhile()
-        return add(chip, order.after(moving)), made
+    grad_far = order.after(grad_far)
+    order.wait(grad_far)
 
     share = q_down.shape[0] // (count * group)
     width = block_input.shape[1]
 
     def before_residual():
+        grad_half = jnp.concatenate([cotangent, order.after(grad_far)], axis=0)
+        order.ran(grad_half)
+        grad_near = near(grad_half)
         normed_half = (rms_parts(order.after(input_half).astype(F32))[0] * norm1_gain).astype(BF16)
         scaled_q, inverse_q = rms_parts(dot(normed_half, q_down))
         order.ran(scaled_q)
@@ -743,11 +752,14 @@
         order.ran(grad_hidden)
         picked_all = jnp.concatenate([picked_mine, order.after(picked_near)], axis=1)
         order.wait(picked_all)
-        return scaled_q, inverse_q, picked_all, grad_all, grad_hidden
-
-    branch, (scaled_q, inverse_q, picked, grad_all, grad_hidden) = sum_half(
-        [attended], [out_weight], NN, before_residual
-    )
+        return scaled_q, inverse_q, picked_all, grad_half, grad_all, grad_hidden
+
+    branch_near = near(order.after(branch_send))
+    branch_chip = add(branch_keep, order.after(branch_near)).astype(BF16)
+    order.ran(branch_chip)
+    branch_far = far(swap(branch_chip))
+    scaled_q, inverse_q, picked, grad_half, grad_all, grad_hidden = before_residual()
+    branch = add(branch_chip, order.after(branch_far))
     residual = input_half.astype(F32) + branch
     scaled_two, inverse_two = rms_parts(residual)
     normed_half = (scaled_two * norm2_gain).astype(BF16)
@@ -910,7 +922,7 @@
         return step
 
     def gains_later():
-        for bit in bits[2:]:
+        for bit in bits[3:]:
             gains_step(bit)()
         gains_step(None)()
 
@@ -936,7 +948,7 @@
         "compressed": compressed, "down_q_parts": down_q_parts, "feed": feed,
         "chip_keys": chip_keys, "keys": keys, "own_keys_grad": own_keys_grad, "half_keys": half_keys,
         "kv_parts": kv_parts, "normed_grad": normed_grad, "gains_own": gains_own,
-        "gains_1": gains_step(bits[0]), "gains_2": gains_step(bits[1]), "gains_3": gains_later,
+        "gains_1": gains_step(bits[0]), "gains_2": gains_step(bits[1]), "gains_3": gains_step(bits[2]), "gains_4": gains_later,
         "out_keep0": out_part("out_keep0", owner[:half], 0), "out_keep1": out_part("out_keep1", owner[:half], 1),
         "out_send0": out_part("out_send0", owner[half:], 0), "out_send1": out_part("out_send1", owner[half:], 1),
         "down": started("down", down_parts(owner[half:])), "down_keep": kept("down", down_parts(owner[:half])),
@@ -949,7 +961,7 @@
         "attention_back": attention_back, "down_1": hop("down"), "up_1": lambda: h["up"].hop(go=False),
         "query_send": query_send, "query_keep": query_keep,
         "up_go": lambda: h["up"].go(), "down_2": hop("down"), "down_end": finish("down"), "gate_1": hop("gate"),
-        "gate_2": hop("gate"), "gate_end": finish("gate"), "up_2": hop("up"), "up_end": finish("up"),
+        "gate_2": lambda: h["gate"].hop(go=False), "gate_go": lambda: h["gate"].go(), "gate_end": finish("gate"), "up_2": hop("up"), "up_end": finish("up"),
         "kv_1": hop("kv"), "kv_2": hop("kv"),
         "out_a": lambda: halving("out_a", h["out_send0"], h["out_keep0"]),
         "out_a_1": hop("out_a"), "out_a_2": hop("out_a"), "out_a_end": finish("out_a"),

time: 453 us -> 447 us (0.987)
  starting transfers between devices: 91.6 us -> 75.3 us
  waiting for transfers between devices: 187 us -> 199 us
    ppermute x30, starting transfers between devices: 66.1 us -> 50 us  [swap_seq(): return lax.ppermute(values, 'seq', [(i, i ^ bit) for i in range(count)])]
    ppermute x30, waiting for transfers between devices: 129 us -> 136 us  [swap_seq(): return lax.ppermute(values, 'seq', [(i, i ^ bit) for i in range(count)])]
    dot_general x17 -> x15, matrix products: 35 us -> 32.3 us  [dot(): return lax.dot_general(left, right, dims, preferred_element_type=F32)]
    unnamed x140 -> x130, local copies, waits for them, and re-layouts: 17.2 us -> 19.7 us
    ppermute x10 -> x11, waiting for transfers between devices: 42 us -> 40.8 us  [far(): return lax.ppermute(values, 'tensor', [(i, i ^ 2) for i in range(4)])]
    ppermute x10 -> x11, starting transfers between devices: 14.6 us -> 15 us  [far(): return lax.ppermute(values, 'tensor', [(i, i ^ 2) for i in range(4)])]
  transfers between devices with their start and end apart: 64 -> 65, of which waited for: 32 -> 33; matrix products, arithmetic and copies ran while one was open for 17% -> 16% of each run, Pallas kernels for 10% -> 11%
where the time goes in v4:
time: 447 us; the launch traced here: 442 us
  waiting for transfers between devices  199 us (45%)
  starting transfers between devices  75.3 us (17%)
  Pallas kernels  68.3 us (15%)
  other arithmetic  42.5 us (10%)
  matrix products  32.3 us (7%)
  local copies, waits for them, and re-layouts  22.1 us (5%)
    ppermute x30, waiting for transfers between devices, swap_seq(): return lax.ppermute(values, 'seq', [(i, i ^ bit) for i in range(count)])  136 us
    ppermute x30, starting transfers between devices, swap_seq(): return lax.ppermute(values, 'seq', [(i, i ^ bit) for i in range(count)])  50 us
    ppermute x11, waiting for transfers between devices, far(): return lax.ppermute(values, 'tensor', [(i, i ^ 2) for i in range(4)])  40.8 us
    dot_general x15, matrix products, dot(): return lax.dot_general(left, right, dims, preferred_element_type=F32)  32.3 us
    unnamed x130, local copies, waits for them, and re-layouts  19.7 us
    pallas_call x6, Pallas kernels, grad_by_rows(): pl.pallas_call(rows_kernel, grid_spec=pltpu.PrefetchScalarGridSpec(num_sc...  18.5 us
    ppermute x8, waiting for transfers between devices, ring_shift(): lax.ppermute(values, 'seq', [(order[i], order[(i + step) % count]) for i...  18.2 us
    ppermute x11, starting transfers between devices, far(): return lax.ppermute(values, 'tensor', [(i, i ^ 2) for i in range(4)])  15 us
  transfers between devices with their start and end apart: 65, of which 33 were waited for; matrix products, arithmetic and copies ran while one was open for 16% of the time, Pallas kernels for 11%

profile of v4, /device:TPU:0, one launch (start us, length us, event | category | flops | bytes accessed | tf_op | source)
XLA Modules:
  0.0 441.8 jit_solution(6662545963153706942)
XLA Ops:
  6.0 3.0 collective-permute-start
  9.0 3.0 multiply_reduce_fusion.6
  12.5 1.9 collective-permute-start.2
  16.3 3.7 collective-permute-done.2
  25.5 4.8 %collective-permute-done.4 = bf16[256,512]{1,0:T(8,128)(2,1)S(1)} collective-permute-done((bf16[256,512]{1,0:T(8,128)(2,1)S(1)}, bf16[256,512]{1,0:T(8,128)(2,1)S(1)}, u32[]{:S(2)}, u32[]{:S(2)}) %collective-permute-start.4) | collective-permute-done | bytes 262176 | tf_op jit(solution)/shard_map/ppermute | solution.py:571
  33.8 3.9 project_rotate.1
  42.8 2.7 collective-permute-done.10
  52.9 6.6 %attend.1 = (bf16[512,1024]{1,0:T(8,128)(2,1)S(1)}, bf16[1024,512]{1,0:T(8,128)(2,1)S(1)}, f32[4,8,512]{2,1,0:T(8,128)S(1)}, bf16[256,2048]{1,0:T(8,128)(2,1)S(1)}, bf16[256,2048]{1,0:T(8,128)(2,1)S(1)}) custom-call(s32[4]{0:T(128)S(1)} %copy-done.37, bf16[512,1024]{1,0:T(8,128)(2,1)S(1)} %get-tuple-element.153.q_ref, ...), custom_call_target="tpu_custom_call" | custom-call | flops 1000 | bytes 1000 | tf_op jit(solution)/shard_map/attend/pallas_call | solution.py:219
  71.9 8.4 %fusion.65.gh_ref = f32[512,1408]{1,0:T(8,128)} fusion(bf16[512,2048]{1,0:T(8,128)(2,1)S(1)} %constant_dynamic-update-slice_fusion.6.right_ref, bf16[1408,2048]{1,0:T(8,128)(2,1)} %param.26), kind=kOutput, calls=%fused_computation.183 | convolution fusion | flops 2952790016 | bytes 10747904 | tf_op jit(solution)/shard_map/dot_general | solution.py:39
  80.3 13.4 %collective-permute-done.17 = bf16[256,2048]{1,0:T(8,128)(2,1)S(1)} collective-permute-done((bf16[256,2048]{1,0:T(8,128)(2,1)S(1)}, bf16[256,2048]{1,0:T(8,128)(2,1)S(1)}, u32[]{:S(2)}, u32[]{:S(2)}) %collective-permute-start.17) | collective-permute-done | bytes 1048608 | tf_op jit(solution)/shard_map/ppermute | solution.py:562
  96.0 2.8 collective-permute-done.20
  100.6 2.6 copy-done.21
  103.2 12.7 %hidden_units.1 = (bf16[512,1408]{1,0:T(8,128)(2,1)S(1)}, bf16[1408,512]{1,0:T(8,128)(2,1)S(1)}, bf16[512,1408]{1,0:T(8,128)(2,1)S(1)}, bf16[512,1408]{1,0:T(8,128)(2,1)S(1)}) custom-call(bf16[512,2048]{1,0:T(8,128)(2,1)S(1)} %pad_maximum_fusion.x_ref.left_ref, bf16[2048,1408]{1,0:T(8,128)(2,1)S(1)} %copy-done.21, bf16[2048,1408]{1,0:T(8,128)(2,1)} %up_ref.1, ...), custom_call_target="tpu_custom_call" | custom-call | flops 1000 | bytes 1000 | tf_op jit(solution)/shard_map/hidden_units/pallas_call | solution.py:439
  115.9 4.0 grad_by_columns.6
  121.3 2.9 grad_by_columns.7
  125.8 4.3 grad_by_rows.6
  130.1 4.8 %collective-permute-start.27 = (bf16[4,256,1408]{2,1,0:T(8,128)(2,1)}, bf16[4,256,1408]{2,1,0:T(8,128)(2,1)}, u32[]{:S(2)}, u32[]{:S(2)}) collective-permute-start(bf16[4,256,1408]{2,1,0:T(8,128)(2,1)} %grad_by_rows.6), channel_id=1, source_target_pairs={{0,8},{4,12},{8,0},{12,4},{16,24},{20,28},{24,16},{28,20},{1,9},{5... | collective-permute-start | bytes 8650760 | tf_op jit(solution)/shard_map/ppermute | solution.py:581
  134.9 3.2 grad_by_rows.7
  139.7 1.8 fusion.26
  141.9 1.8 fusion.2
  143.8 1.8 fusion.29
  145.6 1.8 fusion.1
  147.8 1.8 convolution_convert_fusion
  154.1 21.4 %collective-permute-done.23 = bf16[256,2048]{1,0:T(8,128)(2,1)S(1)} collective-permute-done((bf16[256,2048]{1,0:T(8,128)(2,1)S(1)}, bf16[256,2048]{1,0:T(8,128)(2,1)S(1)}, u32[]{:S(2)}, u32[]{:S(2)}) %collective-permute-start.23) | collective-permute-done | bytes 1048608 | tf_op jit(solution)/shard_map/ppermute | solution.py:562
  176.3 2.7 fusion.58
  179.0 4.9 %multiply_reduce_fusion.5 = (f32[256]{0:T(256)S(1)}, f32[256,1024]{1,0:T(8,128)}) fusion(bf16[256,2048]{1,0:T(8,128)(2,1)} %copy-done.26, bf16[2048,1024]{1,0:T(8,128)(2,1)} %param.18), kind=kOutput, calls=%fused_computation.70 | convolution fusion | flops 1074265856 | bytes 6292480 | tf_op jit(solution)/shard_map/dot_general | solution.py:39
  184.6 3.4 grad_by_rows.8
  188.5 3.0 add_convert_fusion.3
  191.5 1.9 pad_maximum_fusion.1.gb_ref.right_ref
  194.4 3.6 attended_grad.1
  198.0 2.0 grad_by_columns.8
  200.0 2.0 grad_by_columns.9
  202.0 3.2 grad_by_rows.9
  205.3 1.9 add_convert_fusion.2
  207.9 5.2 %attend_back.1 = (bf16[512,1024]{1,0:T(8,128)(2,1)S(1)}, bf16[8,256,512]{2,1,0:T(8,128)(2,1)S(1)}, bf16[8,256,512]{2,1,0:T(8,128)(2,1)S(1)}) custom-call(s32[4]{0:T(128)S(1)} %copy-done.37, s32[8]{0:T(128)S(1)} %get-tuple-element.301._, bf16[512,1024]{1,0:T(8,128)(2,1)S(1)} %copy-done.25, bf16[512,1024]{1,0:T(8,128)(2,1)S(1)} %get-tuple-element.203.do_ref, ...), custom_call_target="tpu_custom_call" | custom-call | flops 1000 | bytes 1000 | tf_op jit(solution)/shard_map/attend_back/pallas_call | solution.py:302
  216.8 11.9 %collective-permute-done.30 = bf16[2,1408,256]{2,1,0:T(8,128)(2,1)} collective-permute-done((bf16[2,1408,256]{2,1,0:T(8,128)(2,1)}, bf16[2,1408,256]{2,1,0:T(8,128)(2,1)}, u32[]{:S(2)}, u32[]{:S(2)}) %collective-permute-start.30) | collective-permute-done | bytes 1441824 | tf_op jit(solution)/shard_map/ppermute | solution.py:581
  230.3 10.3 %collective-permute-start.32 = (bf16[1,1408,256]{2,1,0:T(8,128)(2,1)S(1)}, bf16[1,1408,256]{2,1,0:T(8,128)(2,1)S(1)}, u32[]{:S(2)}, u32[]{:S(2)}) collective-permute-start(bf16[1,1408,256]{2,1,0:T(8,128)(2,1)S(1)} %add_convert_fusion.10), channel_id=1, source_target_pairs={{0,16},{4,20},{8,24},{12,28},{16,0},{20,4},{24,8},{28,12},{1,17},{... | collective-permute-start | bytes 2162696 | tf_op jit(solution)/shard_map/ppermute | solution.py:581
  240.6 12.2 %collective-permute-done.29 = bf16[4,256,1408]{2,1,0:T(8,128)(2,1)} collective-permute-done((bf16[4,256,1408]{2,1,0:T(8,128)(2,1)S(1)}, bf16[4,256,1408]{2,1,0:T(8,128)(2,1)}, u32[]{:S(2)}, u32[]{:S(2)}) %collective-permute-start.29) | collective-permute-done | bytes 2883616 | tf_op jit(solution)/shard_map/ppermute | solution.py:581
  257.4 2.0 grad_by_columns.10
  259.4 2.0 grad_by_columns.11
  261.4 2.1 grad_by_rows.10
  263.5 2.3 grad_by_rows.11
  265.9 6.8 %collective-permute-done.32 = bf16[1,1408,256]{2,1,0:T(8,128)(2,1)S(1)} collective-permute-done((bf16[1,1408,256]{2,1,0:T(8,128)(2,1)S(1)}, bf16[1,1408,256]{2,1,0:T(8,128)(2,1)S(1)}, u32[]{:S(2)}, u32[]{:S(2)}) %collective-permute-start.32) | collective-permute-done | bytes 720928 | tf_op jit(solution)/shard_map/ppermute | solution.py:581
  272.7 2.9 add_bitcast_fusion.2
  275.6 4.2 collective-permute-done.31
  282.3 9.2 %collective-permute-done.35 = bf16[2,256,1408]{2,1,0:T(8,128)(2,1)S(1)} collective-permute-done((bf16[2,256,1408]{2,1,0:T(8,128)(2,1)S(1)}, bf16[2,256,1408]{2,1,0:T(8,128)(2,1)S(1)}, u32[]{:S(2)}, u32[]{:S(2)}) %collective-permute-start.35) | collective-permute-done | bytes 1441824 | tf_op jit(solution)/shard_map/ppermute | solution.py:581
  292.9 10.3 %collective-permute-start.40 = (bf16[1,256,1408]{2,1,0:T(8,128)(2,1)S(1)}, bf16[1,256,1408]{2,1,0:T(8,128)(2,1)S(1)}, u32[]{:S(2)}, u32[]{:S(2)}) collective-permute-start(bf16[1,256,1408]{2,1,0:T(8,128)(2,1)S(1)} %add_convert_fusion.9), channel_id=1, source_target_pairs={{0,16},{4,20},{8,24},{12,28},{16,0},{20,4},{24,8},{28,12},{1,17},{... | collective-permute-start | bytes 2162696 | tf_op jit(solution)/shard_map/ppermute | solution.py:581
  304.5 17.6 %collective-permute-done.36 = bf16[2,128,512]{2,1,0:T(8,128)(2,1)S(1)} collective-permute-done((bf16[2,128,512]{2,1,0:T(8,128)(2,1)S(1)}, bf16[2,128,512]{2,1,0:T(8,128)(2,1)S(1)}, u32[]{:S(2)}, u32[]{:S(2)}) %collective-permute-start.36) | collective-permute-done | bytes 262176 | tf_op jit(solution)/shard_map/ppermute | solution.py:581
  324.4 9.2 %collective-permute-done.40 = bf16[1,256,1408]{2,1,0:T(8,128)(2,1)S(1)} collective-permute-done((bf16[1,256,1408]{2,1,0:T(8,128)(2,1)S(1)}, bf16[1,256,1408]{2,1,0:T(8,128)(2,1)S(1)}, u32[]{:S(2)}, u32[]{:S(2)}) %collective-permute-start.40) | collective-permute-done | bytes 720928 | tf_op jit(solution)/shard_map/ppermute | solution.py:581
  333.6 2.6 add_bitcast_fusion.1
  342.0 3.4 collective-permute-start.55
  347.6 17.6 %collective-permute-done.45 = bf16[4,512,256]{2,1,0:T(8,128)(2,1)S(1)} collective-permute-done((bf16[4,512,256]{2,1,0:T(8,128)(2,1)S(1)}, bf16[4,512,256]{2,1,0:T(8,128)(2,1)S(1)}, u32[]{:S(2)}, u32[]{:S(2)}) %collective-permute-start.45) | collective-permute-done | bytes 1048608 | tf_op jit(solution)/shard_map/ppermute | solution.py:581
  365.3 1.8 collective-permute-start.51
  370.0 6.8 %collective-permute-done.52 = bf16[4,64,512]{2,1,0:T(8,128)(2,1)S(1)} collective-permute-done((bf16[4,64,512]{2,1,0:T(8,128)(2,1)S(1)}, bf16[4,64,512]{2,1,0:T(8,128)(2,1)S(1)}, u32[]{:S(2)}, u32[]{:S(2)}) %collective-permute-start.52) | collective-permute-done | bytes 262176 | tf_op jit(solution)/shard_map/ppermute | solution.py:581
  378.3 2.6 add_bitcast_fusion
  380.9 4.1 collective-permute-done.54
  386.4 5.8 %collective-permute-done.53 = bf16[2,64,512]{2,1,0:T(8,128)(2,1)S(1)} collective-permute-done((bf16[2,64,512]{2,1,0:T(8,128)(2,1)S(1)}, bf16[2,64,512]{2,1,0:T(8,128)(2,1)S(1)}, u32[]{:S(2)}, u32[]{:S(2)}) %collective-permute-start.53) | collective-permute-done | bytes 131104 | tf_op jit(solution)/shard_map/ppermute | solution.py:581
  392.3 7.0 %collective-permute-done.50 = bf16[4,128,1024]{2,1,0:T(8,128)(2,1)S(1)} collective-permute-done((bf16[4,128,1024]{2,1,0:T(8,128)(2,1)S(1)}, bf16[4,128,1024]{2,1,0:T(8,128)(2,1)S(1)}, u32[]{:S(2)}, u32[]{:S(2)}) %collective-permute-start.50) | collective-permute-done | bytes 1048608 | tf_op jit(solution)/shard_map/ppermute | solution.py:581
  404.1 1.8 collective-permute-start.56
  405.9 4.6 %collective-permute-done.57 = bf16[4,64,1024]{2,1,0:T(8,128)(2,1)S(1)} collective-permute-done((bf16[4,64,1024]{2,1,0:T(8,128)(2,1)S(1)}, bf16[4,64,1024]{2,1,0:T(8,128)(2,1)S(1)}, u32[]{:S(2)}, u32[]{:S(2)}) %collective-permute-start.57) | collective-permute-done | bytes 524320 | tf_op jit(solution)/shard_map/ppermute | solution.py:581
  411.0 10.9 %collective-permute-done.56 = f32[5120]{0:T(1024)S(1)} collective-permute-done((f32[5120]{0:T(1024)S(1)}, f32[5120]{0:T(1024)S(1)}, u32[]{:S(2)}, u32[]{:S(2)}) %collective-permute-start.56) | collective-permute-done | bytes 20512 | tf_op jit(solution)/shard_map/ppermute | solution.py:581
  422.1 2.9 collective-permute-start.64
  425.8 3.2 collective-permute-done.59
  431.4 8.4 %collective-permute-done.63 = bf16[1,64,1024]{2,1,0:T(8,128)(2,1)S(1)} collective-permute-done((bf16[1,64,1024]{2,1,0:T(8,128)(2,1)S(1)}, bf16[1,64,1024]{2,1,0:T(8,128)(2,1)S(1)}, u32[]{:S(2)}, u32[]{:S(2)}) %collective-permute-start.63) | collective-permute-done | bytes 131104 | tf_op jit(solution)/shard_map/ppermute | solution.py:581
  (339 shorter events, 100.2 us)
Async XLA Ops:
  6.0 6.5 %collective-permute-start = (bf16[128,512]{1,0:T(8,128)(2,1)S(1)}, bf16[128,512]{1,0:T(8,128)(2,1)S(1)}, u32[]{:S(2)}, u32[]{:S(2)}) collective-permute-start(bf16[128,512]{1,0:T(8,128)(2,1)S(1)} %get-tuple-element.138), channel_id=1, source_target_pairs={{0,2},{1,3},{2,0},{3,1},{4,6},{5,7},{6,4},{7,5},{8,10},{9,11},{10,... | collective-permute-start | bytes 393224 | tf_op jit(solution)/shard_map/ppermute | solution.py:562
  12.5 7.5 %collective-permute-start.2 = (bf16[256,512]{1,0:T(8,128)(2,1)S(1)}, bf16[256,512]{1,0:T(8,128)(2,1)S(1)}, u32[]{:S(2)}, u32[]{:S(2)}) collective-permute-start(bf16[256,512]{1,0:T(8,128)(2,1)S(1)} %constant_dynamic-update-slice_fusion), channel_id=1, source_target_pairs={{0,8},{8,16},{16,24},{24,28},{28,20},{20,12},{12,4},{4,0},{1,9},{9... | collective-permute-start | bytes 786440 | tf_op jit(solution)/shard_map/ppermute | solution.py:571
  14.4 7.0 %collective-permute-start.3 = (bf16[256,512]{1,0:T(8,128)(2,1)S(1)}, bf16[256,512]{1,0:T(8,128)(2,1)S(1)}, u32[]{:S(2)}, u32[]{:S(2)}) collective-permute-start(bf16[256,512]{1,0:T(8,128)(2,1)S(1)} %constant_dynamic-update-slice_fusion), channel_id=1, source_target_pairs={{0,4},{8,0},{16,8},{24,16},{28,24},{20,28},{12,20},{4,12},{1,5},{9... | collective-permute-start | bytes 786440 | tf_op jit(solution)/shard_map/ppermute | solution.py:571
  14.6 6.9 %collective-permute-start.6 = (bf16[128,1024]{1,0:T(8,128)(2,1)S(1)}, bf16[128,1024]{1,0:T(8,128)(2,1)S(1)}, u32[]{:S(2)}, u32[]{:S(2)}) collective-permute-start(bf16[128,1024]{1,0:T(8,128)(2,1)S(1)} %multiply_convert_fusion.2), channel_id=1, source_target_pairs={{0,2},{1,3},{2,0},{3,1},{4,6},{5,7},{6,4},{7,5},{8,10},{9,11},{10,... | collective-permute-start | bytes 786440 | tf_op jit(solution)/shard_map/ppermute | solution.py:562
  21.6 12.1 %collective-permute-start.9 = (bf16[256,1024]{1,0:T(8,128)(2,1)S(1)}, bf16[256,1024]{1,0:T(8,128)(2,1)S(1)}, u32[]{:S(2)}, u32[]{:S(2)}) collective-permute-start(bf16[256,1024]{1,0:T(8,128)(2,1)S(1)} %pad_maximum_fusion.8), channel_id=1, source_target_pairs={{0,1},{1,0},{2,3},{3,2},{4,5},{5,4},{6,7},{7,6},{8,9},{9,8},{10,11... | collective-permute-start | bytes 1572872 | tf_op jit(solution)/shard_map/ppermute | solution.py:558
  21.7 8.7 %collective-permute-start.4 = (bf16[256,512]{1,0:T(8,128)(2,1)S(1)}, bf16[256,512]{1,0:T(8,128)(2,1)S(1)}, u32[]{:S(2)}, u32[]{:S(2)}) collective-permute-start(bf16[256,512]{1,0:T(8,128)(2,1)S(1)} %collective-permute-done.2), channel_id=1, source_target_pairs={{0,8},{8,16},{16,24},{24,28},{28,20},{20,12},{12,4},{4,0},{1,9},{9... | collective-permute-start | bytes 786440 | tf_op jit(solution)/shard_map/ppermute | solution.py:571
  23.3 8.4 %collective-permute-start.5 = (bf16[256,512]{1,0:T(8,128)(2,1)S(1)}, bf16[256,512]{1,0:T(8,128)(2,1)S(1)}, u32[]{:S(2)}, u32[]{:S(2)}) collective-permute-start(bf16[256,512]{1,0:T(8,128)(2,1)S(1)} %collective-permute-done.3), channel_id=1, source_target_pairs={{0,4},{8,0},{16,8},{24,16},{28,24},{20,28},{12,20},{4,12},{1,5},{9... | collective-permute-start | bytes 786440 | tf_op jit(solution)/shard_map/ppermute | solution.py:571
  23.7 23.7 %collective-permute-start.1 = (bf16[128,2048]{1,0:T(8,128)(2,1)S(1)}, bf16[128,2048]{1,0:T(8,128)(2,1)S(1)}, u32[]{:S(2)}, u32[]{:S(2)}) collective-permute-start(bf16[128,2048]{1,0:T(8,128)(2,1)S(1)} %copy-done.9), channel_id=1, source_target_pairs={{0,2},{1,3},{2,0},{3,1},{4,6},{5,7},{6,4},{7,5},{8,10},{9,11},{10,... | collective-permute-start | bytes 1572872 | tf_op jit(solution)/shard_map/ppermute | solution.py:562
  25.5 24.5 %collective-permute-start.12 = (bf16[3,256,512]{2,1,0:T(8,128)(2,1)S(1)}, bf16[3,256,512]{2,1,0:T(8,128)(2,1)S(1)}, u32[]{:S(2)}, u32[]{:S(2)}) collective-permute-start(bf16[3,256,512]{2,1,0:T(8,128)(2,1)S(1)} %pad_maximum_fusion.6), channel_id=1, source_target_pairs={{0,1},{1,0},{2,3},{3,2},{4,5},{5,4},{6,7},{7,6},{8,9},{9,8},{10,11... | collective-permute-start | bytes 2359304 | tf_op jit(solution)/shard_map/ppermute | solution.py:558
  31.7 7.5 %collective-permute-start.7 = (bf16[256,512]{1,0:T(8,128)(2,1)S(1)}, bf16[256,512]{1,0:T(8,128)(2,1)S(1)}, u32[]{:S(2)}, u32[]{:S(2)}) collective-permute-start(bf16[256,512]{1,0:T(8,128)(2,1)S(1)} %collective-permute-done.4), channel_id=1, source_target_pairs={{0,8},{8,16},{16,24},{24,28},{28,20},{20,12},{12,4},{4,0},{1,9},{9... | collective-permute-start | bytes 786440 | tf_op jit(solution)/shard_map/ppermute | solution.py:571
  33.2 7.3 %collective-permute-start.8 = (bf16[256,512]{1,0:T(8,128)(2,1)S(1)}, bf16[256,512]{1,0:T(8,128)(2,1)S(1)}, u32[]{:S(2)}, u32[]{:S(2)}) collective-permute-start(bf16[256,512]{1,0:T(8,128)(2,1)S(1)} %collective-permute-done.5), channel_id=1, source_target_pairs={{0,4},{8,0},{16,8},{24,16},{28,24},{20,28},{12,20},{4,12},{1,5},{9... | collective-permute-start | bytes 786440 | tf_op jit(solution)/shard_map/ppermute | solution.py:571
  40.5 5.0 %collective-permute-start.10 = (bf16[128,512]{1,0:T(8,128)(2,1)S(1)}, bf16[128,512]{1,0:T(8,128)(2,1)S(1)}, u32[]{:S(2)}, u32[]{:S(2)}) collective-permute-start(bf16[128,512]{1,0:T(8,128)(2,1)S(1)} %slice.411), channel_id=1, source_target_pairs={{0,8},{8,16},{16,24},{24,28},{28,20},{20,12},{12,4},{4,0},{1,9},{9... | collective-permute-start | bytes 393224 | tf_op jit(solution)/shard_map/ppermute | solution.py:571
  42.2 5.0 %collective-permute-start.11 = (bf16[128,512]{1,0:T(8,128)(2,1)S(1)}, bf16[128,512]{1,0:T(8,128)(2,1)S(1)}, u32[]{:S(2)}, u32[]{:S(2)}) collective-permute-start(bf16[128,512]{1,0:T(8,128)(2,1)S(1)} %slice.412), channel_id=1, source_target_pairs={{0,4},{8,0},{16,8},{24,16},{28,24},{20,28},{12,20},{4,12},{1,5},{9... | collective-permute-start | bytes 393224 | tf_op jit(solution)/shard_map/ppermute | solution.py:571
  42.8 7.4 %collective-permute-start.13 = (bf16[2,256,512]{2,1,0:T(8,128)(2,1)S(1)}, bf16[2,256,512]{2,1,0:T(8,128)(2,1)S(1)}, u32[]{:S(2)}, u32[]{:S(2)}) collective-permute-start(bf16[2,256,512]{2,1,0:T(8,128)(2,1)S(1)} %get-tuple-element.159), channel_id=1, source_target_pairs={{0,1},{1,0},{2,3},{3,2},{4,5},{5,4},{6,7},{7,6},{8,9},{9,8},{10,11... | collective-permute-start | bytes 1572872 | tf_op jit(solution)/shard_map/ppermute | solution.py:558
  47.3 2.9 collective-permute-start.14
  47.5 14.4 %collective-permute-start.15 = (bf16[128,2048]{1,0:T(8,128)(2,1)S(1)}, bf16[128,2048]{1,0:T(8,128)(2,1)S(1)}, u32[]{:S(2)}, u32[]{:S(2)}) collective-permute-start(bf16[128,2048]{1,0:T(8,128)(2,1)S(1)} %copy-done.50), channel_id=1, source_target_pairs={{0,2},{1,3},{2,0},{3,1},{4,6},{5,7},{6,4},{7,5},{8,10},{9,11},{10,... | collective-permute-start | bytes 1572872 | tf_op jit(solution)/shard_map/ppermute | solution.py:562
  66.4 5.3 %collective-permute-start.18 = (bf16[256,2048]{1,0:T(8,128)(2,1)S(1)}, bf16[256,2048]{1,0:T(8,128)(2,1)S(1)}, u32[]{:S(2)}, u32[]{:S(2)}) collective-permute-start(bf16[256,2048]{1,0:T(8,128)(2,1)S(1)} %get-tuple-element.282), channel_id=1, source_target_pairs={{0,1},{1,0},{2,3},{3,2},{4,5},{5,4},{6,7},{7,6},{8,9},{9,8},{10,11... | collective-permute-start | bytes 3145736 | tf_op jit(solution)/shard_map/ppermute | solution.py:558
  68.4 25.3 %collective-permute-start.17 = (bf16[256,2048]{1,0:T(8,128)(2,1)S(1)}, bf16[256,2048]{1,0:T(8,128)(2,1)S(1)}, u32[]{:S(2)}, u32[]{:S(2)}) collective-permute-start(bf16[256,2048]{1,0:T(8,128)(2,1)S(1)} %pad_maximum_fusion.3), channel_id=1, source_target_pairs={{0,2},{1,3},{2,0},{3,1},{4,6},{5,7},{6,4},{7,5},{8,10},{9,11},{10,... | collective-permute-start | bytes 3145736 | tf_op jit(solution)/shard_map/ppermute | solution.py:562
  71.7 8.6 %collective-permute-start.19 = (bf16[512,256]{1,0:T(8,128)(2,1)S(1)}, bf16[512,256]{1,0:T(8,128)(2,1)S(1)}, u32[]{:S(2)}, u32[]{:S(2)}) collective-permute-start(bf16[512,256]{1,0:T(8,128)(2,1)S(1)} %get-tuple-element.176), channel_id=1, source_target_pairs={{0,1},{1,0},{2,3},{3,2},{4,5},{5,4},{6,7},{7,6},{8,9},{9,8},{10,11... | collective-permute-start | bytes 786440 | tf_op jit(solution)/shard_map/ppermute | solution.py:558
  95.8 3.0 collective-permute-start.20
  120.0 68.6 %collective-permute-start.26 = (bf16[4,1408,256]{2,1,0:T(8,128)(2,1)}, bf16[4,1408,256]{2,1,0:T(8,128)(2,1)}, u32[]{:S(2)}, u32[]{:S(2)}) collective-permute-start(bf16[4,1408,256]{2,1,0:T(8,128)(2,1)} %grad_by_columns.6), channel_id=1, source_target_pairs={{0,4},{4,0},{8,12},{12,8},{16,20},{20,16},{24,28},{28,24},{1,5},{5... | collective-permute-start | bytes 8650760 | tf_op jit(solution)/shard_map/ppermute | solution.py:581
  130.1 75.1 %collective-permute-start.27 = (bf16[4,256,1408]{2,1,0:T(8,128)(2,1)}, bf16[4,256,1408]{2,1,0:T(8,128)(2,1)}, u32[]{:S(2)}, u32[]{:S(2)}) collective-permute-start(bf16[4,256,1408]{2,1,0:T(8,128)(2,1)} %grad_by_rows.6), channel_id=1, source_target_pairs={{0,8},{4,12},{8,0},{12,4},{16,24},{20,28},{24,16},{28,20},{1,9},{5... | collective-permute-start | bytes 8650760 | tf_op jit(solution)/shard_map/ppermute | solution.py:581
  143.7 3.8 collective-permute-start.21
  149.6 3.2 collective-permute-start.22
  150.3 25.2 %collective-permute-start.23 = (bf16[256,2048]{1,0:T(8,128)(2,1)S(1)}, bf16[256,2048]{1,0:T(8,128)(2,1)S(1)}, u32[]{:S(2)}, u32[]{:S(2)}) collective-permute-start(bf16[256,2048]{1,0:T(8,128)(2,1)S(1)} %pad_maximum_fusion.4), channel_id=1, source_target_pairs={{0,2},{1,3},{2,0},{3,1},{4,6},{5,7},{6,4},{7,5},{8,10},{9,11},{10,... | collective-permute-start | bytes 3145736 | tf_op jit(solution)/shard_map/ppermute | solution.py:562
  179.0 12.5 %collective-permute-start.25 = (bf16[256,2048]{1,0:T(8,128)(2,1)}, bf16[256,2048]{1,0:T(8,128)(2,1)}, u32[]{:S(2)}, u32[]{:S(2)}) collective-permute-start(bf16[256,2048]{1,0:T(8,128)(2,1)} %get-tuple-element.270), channel_id=1, source_target_pairs={{0,1},{1,0},{2,3},{3,2},{4,5},{5,4},{6,7},{7,6},{8,9},{9,8},{10,11... | collective-permute-start | bytes 3145736 | tf_op jit(solution)/shard_map/ppermute | solution.py:558
  183.9 30.6 %collective-permute-start.24 = (bf16[128,2048]{1,0:T(8,128)(2,1)S(1)}, bf16[128,2048]{1,0:T(8,128)(2,1)S(1)}, u32[]{:S(2)}, u32[]{:S(2)}) collective-permute-start(bf16[128,2048]{1,0:T(8,128)(2,1)S(1)} %slice.429), channel_id=1, source_target_pairs={{0,2},{1,3},{2,0},{3,1},{4,6},{5,7},{6,4},{7,5},{8,10},{9,11},{10,... | collective-permute-start | bytes 1572872 | tf_op jit(solution)/shard_map/ppermute | solution.py:562
  188.0 64.8 %collective-permute-start.29 = (bf16[4,256,1408]{2,1,0:T(8,128)(2,1)S(1)}, bf16[4,256,1408]{2,1,0:T(8,128)(2,1)}, u32[]{:S(2)}, u32[]{:S(2)}) collective-permute-start(bf16[4,256,1408]{2,1,0:T(8,128)(2,1)S(1)} %grad_by_rows.8), channel_id=1, source_target_pairs={{0,4},{4,0},{8,12},{12,8},{16,20},{20,16},{24,28},{28,24},{1,5},{5... | collective-permute-start | bytes 8650760 | tf_op jit(solution)/shard_map/ppermute | solution.py:581
  193.5 35.2 %collective-permute-start.30 = (bf16[2,1408,256]{2,1,0:T(8,128)(2,1)}, bf16[2,1408,256]{2,1,0:T(8,128)(2,1)}, u32[]{:S(2)}, u32[]{:S(2)}) collective-permute-start(bf16[2,1408,256]{2,1,0:T(8,128)(2,1)} %add_convert_fusion.3), channel_id=1, source_target_pairs={{0,8},{4,12},{8,0},{12,4},{16,24},{20,28},{24,16},{28,20},{1,9},{5... | collective-permute-start | bytes 4325384 | tf_op jit(solution)/shard_map/ppermute | solution.py:581
  213.1 41.4 %collective-permute-start.28 = (bf16[8,256,512]{2,1,0:T(8,128)(2,1)S(1)}, bf16[8,256,512]{2,1,0:T(8,128)(2,1)S(1)}, u32[]{:S(2)}, u32[]{:S(2)}) collective-permute-start(bf16[8,256,512]{2,1,0:T(8,128)(2,1)S(1)} %get-tuple-element.212), channel_id=1, source_target_pairs={{0,1},{1,0},{2,3},{3,2},{4,5},{5,4},{6,7},{7,6},{8,9},{9,8},{10,11... | collective-permute-start | bytes 6291464 | tf_op jit(solution)/shard_map/ppermute | solution.py:558
  214.0 42.7 %collective-permute-start.33 = (bf16[256,1024]{1,0:T(8,128)(2,1)S(1)}, bf16[256,1024]{1,0:T(8,128)(2,1)S(1)}, u32[]{:S(2)}, u32[]{:S(2)}) collective-permute-start(bf16[256,1024]{1,0:T(8,128)(2,1)S(1)} %convolution_convert_fusion.5), channel_id=1, source_target_pairs={{0,1},{1,0},{2,3},{3,2},{4,5},{5,4},{6,7},{7,6},{8,9},{9,8},{10,11... | collective-permute-start | bytes 1572872 | tf_op jit(solution)/shard_map/ppermute | solution.py:558
  230.3 42.4 %collective-permute-start.32 = (bf16[1,1408,256]{2,1,0:T(8,128)(2,1)S(1)}, bf16[1,1408,256]{2,1,0:T(8,128)(2,1)S(1)}, u32[]{:S(2)}, u32[]{:S(2)}) collective-permute-start(bf16[1,1408,256]{2,1,0:T(8,128)(2,1)S(1)} %add_convert_fusion.10), channel_id=1, source_target_pairs={{0,16},{4,20},{8,24},{12,28},{16,0},{20,4},{24,8},{28,12},{1,17},{... | collective-permute-start | bytes 2162696 | tf_op jit(solution)/shard_map/ppermute | solution.py:581
  255.2 24.5 %collective-permute-start.31 = (bf16[8,128,512]{2,1,0:T(8,128)(2,1)S(1)}, bf16[8,128,512]{2,1,0:T(8,128)(2,1)S(1)}, u32[]{:S(2)}, u32[]{:S(2)}) collective-permute-start(bf16[8,128,512]{2,1,0:T(8,128)(2,1)S(1)} %slice.532), channel_id=1, source_target_pairs={{0,2},{1,3},{2,0},{3,1},{4,6},{5,7},{6,4},{7,5},{8,10},{9,11},{10,... | collective-permute-start | bytes 3145736 | tf_op jit(solution)/shard_map/ppermute | solution.py:562
  256.9 34.6 %collective-permute-start.35 = (bf16[2,256,1408]{2,1,0:T(8,128)(2,1)S(1)}, bf16[2,256,1408]{2,1,0:T(8,128)(2,1)S(1)}, u32[]{:S(2)}, u32[]{:S(2)}) collective-permute-start(bf16[2,256,1408]{2,1,0:T(8,128)(2,1)S(1)} %add_convert_fusion.2), channel_id=1, source_target_pairs={{0,4},{4,0},{8,12},{12,8},{16,20},{20,16},{24,28},{28,24},{1,5},{5... | collective-permute-start | bytes 4325384 | tf_op jit(solution)/shard_map/ppermute | solution.py:581
  257.4 64.8 %collective-permute-start.42 = (bf16[2,256,1408]{2,1,0:T(8,128)(2,1)S(1)}, bf16[2,256,1408]{2,1,0:T(8,128)(2,1)S(1)}, u32[]{:S(2)}, u32[]{:S(2)}) collective-permute-start(bf16[2,256,1408]{2,1,0:T(8,128)(2,1)S(1)} %add_convert_fusion.1), channel_id=1, source_target_pairs={{0,8},{4,12},{8,0},{12,4},{16,24},{20,28},{24,16},{28,20},{1,9},{5... | collective-permute-start | bytes 4325384 | tf_op jit(solution)/shard_map/ppermute | solution.py:581
  280.1 23.4 %collective-permute-start.34 = (bf16[4,128,512]{2,1,0:T(8,128)(2,1)S(1)}, bf16[4,128,512]{2,1,0:T(8,128)(2,1)S(1)}, u32[]{:S(2)}, u32[]{:S(2)}) collective-permute-start(bf16[4,128,512]{2,1,0:T(8,128)(2,1)S(1)} %slice.535), channel_id=1, source_target_pairs={{0,4},{4,0},{8,12},{12,8},{16,20},{20,16},{24,28},{28,24},{1,5},{5... | collective-permute-start | bytes 1572872 | tf_op jit(solution)/shard_map/ppermute | solution.py:581
  280.8 22.8 %collective-permute-start.37 = (bf16[256,1024]{1,0:T(8,128)(2,1)S(1)}, bf16[256,1024]{1,0:T(8,128)(2,1)S(1)}, u32[]{:S(2)}, u32[]{:S(2)}) collective-permute-start(bf16[256,1024]{1,0:T(8,128)(2,1)S(1)} %pad_maximum_fusion.10), channel_id=1, source_target_pairs={{0,2},{1,3},{2,0},{3,1},{4,6},{5,7},{6,4},{7,5},{8,10},{9,11},{10,... | collective-permute-start | bytes 1572872 | tf_op jit(solution)/shard_map/ppermute | solution.py:562
  292.9 40.7 %collective-permute-start.40 = (bf16[1,256,1408]{2,1,0:T(8,128)(2,1)S(1)}, bf16[1,256,1408]{2,1,0:T(8,128)(2,1)S(1)}, u32[]{:S(2)}, u32[]{:S(2)}) collective-permute-start(bf16[1,256,1408]{2,1,0:T(8,128)(2,1)S(1)} %add_convert_fusion.9), channel_id=1, source_target_pairs={{0,16},{4,20},{8,24},{12,28},{16,0},{20,4},{24,8},{28,12},{1,17},{... | collective-permute-start | bytes 2162696 | tf_op jit(solution)/shard_map/ppermute | solution.py:581
  303.2 21.1 %collective-permute-start.41 = (bf16[4,512,256]{2,1,0:T(8,128)(2,1)S(1)}, bf16[4,512,256]{2,1,0:T(8,128)(2,1)S(1)}, u32[]{:S(2)}, u32[]{:S(2)}) collective-permute-start(bf16[4,512,256]{2,1,0:T(8,128)(2,1)S(1)} %copy-done.31), channel_id=1, source_target_pairs={{0,4},{4,0},{8,12},{12,8},{16,20},{20,16},{24,28},{28,24},{1,5},{5... | collective-permute-start | bytes 3145736 | tf_op jit(solution)/shard_map/ppermute | solution.py:581
  303.5 18.6 %collective-permute-start.36 = (bf16[2,128,512]{2,1,0:T(8,128)(2,1)S(1)}, bf16[2,128,512]{2,1,0:T(8,128)(2,1)S(1)}, u32[]{:S(2)}, u32[]{:S(2)}) collective-permute-start(bf16[2,128,512]{2,1,0:T(8,128)(2,1)S(1)} %add_convert_fusion.18), channel_id=1, source_target_pairs={{0,8},{4,12},{8,0},{12,4},{16,24},{20,28},{24,16},{28,20},{1,9},{5... | collective-permute-start | bytes 786440 | tf_op jit(solution)/shard_map/ppermute | solution.py:581
  304.4 31.8 %collective-permute-start.39 = (bf16[256,1024]{1,0:T(8,128)(2,1)S(1)}, bf16[256,1024]{1,0:T(8,128)(2,1)S(1)}, u32[]{:S(2)}, u32[]{:S(2)}) collective-permute-start(bf16[256,1024]{1,0:T(8,128)(2,1)S(1)} %multiply_convert_fusion.1), channel_id=1, source_target_pairs={{0,1},{1,0},{2,3},{3,2},{4,5},{5,4},{6,7},{7,6},{8,9},{9,8},{10,11... | collective-permute-start | bytes 1572872 | tf_op jit(solution)/shard_map/ppermute | solution.py:558
  322.2 14.8 %collective-permute-start.38 = (bf16[1,128,512]{2,1,0:T(8,128)(2,1)S(1)}, bf16[1,128,512]{2,1,0:T(8,128)(2,1)S(1)}, u32[]{:S(2)}, u32[]{:S(2)}) collective-permute-start(bf16[1,128,512]{2,1,0:T(8,128)(2,1)S(1)} %add_convert_fusion.19), channel_id=1, source_target_pairs={{0,16},{4,20},{8,24},{12,28},{16,0},{20,4},{24,8},{28,12},{1,17},{... | collective-permute-start | bytes 393224 | tf_op jit(solution)/shard_map/ppermute | solution.py:581
  337.1 8.3 %collective-permute-start.43 = (bf16[128,512]{1,0:T(8,128)(2,1)S(1)}, bf16[128,512]{1,0:T(8,128)(2,1)S(1)}, u32[]{:S(2)}, u32[]{:S(2)}) collective-permute-start(bf16[128,512]{1,0:T(8,128)(2,1)S(1)} %pad_maximum_fusion.12), channel_id=1, source_target_pairs={{0,2},{1,3},{2,0},{3,1},{4,6},{5,7},{6,4},{7,5},{8,10},{9,11},{10,... | collective-permute-start | bytes 393224 | tf_op jit(solution)/shard_map/ppermute | solution.py:562
  339.9 27.7 %collective-permute-start.47 = (bf16[2,512,256]{2,1,0:T(8,128)(2,1)S(1)}, bf16[2,512,256]{2,1,0:T(8,128)(2,1)S(1)}, u32[]{:S(2)}, u32[]{:S(2)}) collective-permute-start(bf16[2,512,256]{2,1,0:T(8,128)(2,1)S(1)} %add_convert_fusion.13), channel_id=1, source_target_pairs={{0,8},{4,12},{8,0},{12,4},{16,24},{20,28},{24,16},{28,20},{1,9},{5... | collective-permute-start | bytes 1572872 | tf_op jit(solution)/shard_map/ppermute | solution.py:581
  341.2 23.9 %collective-permute-start.45 = (bf16[4,512,256]{2,1,0:T(8,128)(2,1)S(1)}, bf16[4,512,256]{2,1,0:T(8,128)(2,1)S(1)}, u32[]{:S(2)}, u32[]{:S(2)}) collective-permute-start(bf16[4,512,256]{2,1,0:T(8,128)(2,1)S(1)} %grad_by_columns.9), channel_id=1, source_target_pairs={{0,4},{4,0},{8,12},{12,8},{16,20},{20,16},{24,28},{28,24},{1,5},{5... | collective-permute-start | bytes 3145736 | tf_op jit(solution)/shard_map/ppermute | solution.py:581
  342.0 36.2 %collective-permute-start.55 = (bf16[1,256,1408]{2,1,0:T(8,128)(2,1)S(1)}, bf16[1,256,1408]{2,1,0:T(8,128)(2,1)S(1)}, u32[]{:S(2)}, u32[]{:S(2)}) collective-permute-start(bf16[1,256,1408]{2,1,0:T(8,128)(2,1)S(1)} %add_convert_fusion.8), channel_id=1, source_target_pairs={{0,16},{4,20},{8,24},{12,28},{16,0},{20,4},{24,8},{28,12},{1,17},{... | collective-permute-start | bytes 2162696 | tf_op jit(solution)/shard_map/ppermute | solution.py:581
  345.4 21.7 %collective-permute-start.48 = (bf16[256,512]{1,0:T(8,128)(2,1)S(1)}, bf16[256,512]{1,0:T(8,128)(2,1)S(1)}, u32[]{:S(2)}, u32[]{:S(2)}) collective-permute-start(bf16[256,512]{1,0:T(8,128)(2,1)S(1)} %pad_maximum_fusion.11), channel_id=1, source_target_pairs={{0,1},{1,0},{2,3},{3,2},{4,5},{5,4},{6,7},{7,6},{8,9},{9,8},{10,11... | collective-permute-start | bytes 786440 | tf_op jit(solution)/shard_map/ppermute | solution.py:558
  346.7 20.4 %collective-permute-start.44 = (f32[2048]{0:T(1024)S(1)}, f32[2048]{0:T(1024)S(1)}, u32[]{:S(2)}, u32[]{:S(2)}) collective-permute-start(f32[2048]{0:T(1024)S(1)} %get-tuple-element.268), channel_id=1, source_target_pairs={{0,2},{1,3},{2,0},{3,1},{4,6},{5,7},{6,4},{7,5},{8,10},{9,11},{10,... | collective-permute-start | bytes 24584 | tf_op jit(solution)/shard_map/ppermute | solution.py:562
  365.3 26.9 %collective-permute-start.51 = (bf16[2,512,256]{2,1,0:T(8,128)(2,1)S(1)}, bf16[2,512,256]{2,1,0:T(8,128)(2,1)S(1)}, u32[]{:S(2)}, u32[]{:S(2)}) collective-permute-start(bf16[2,512,256]{2,1,0:T(8,128)(2,1)S(1)} %add_convert_fusion.12), channel_id=1, source_target_pairs={{0,8},{4,12},{8,0},{12,4},{16,24},{20,28},{24,16},{28,20},{1,9},{5... | collective-permute-start | bytes 1572872 | tf_op jit(solution)/shard_map/ppermute | solution.py:581
  367.1 2.9 collective-permute-start.46
  367.7 9.2 %collective-permute-start.52 = (bf16[4,64,512]{2,1,0:T(8,128)(2,1)S(1)}, bf16[4,64,512]{2,1,0:T(8,128)(2,1)S(1)}, u32[]{:S(2)}, u32[]{:S(2)}) collective-permute-start(bf16[4,64,512]{2,1,0:T(8,128)(2,1)S(1)} %bitcast.97), channel_id=1, source_target_pairs={{0,4},{4,0},{8,12},{12,8},{16,20},{20,16},{24,28},{28,24},{1,5},{5... | collective-permute-start | bytes 786440 | tf_op jit(solution)/shard_map/ppermute | solution.py:581
  368.9 30.4 %collective-permute-start.50 = (bf16[4,128,1024]{2,1,0:T(8,128)(2,1)S(1)}, bf16[4,128,1024]{2,1,0:T(8,128)(2,1)S(1)}, u32[]{:S(2)}, u32[]{:S(2)}) collective-permute-start(bf16[4,128,1024]{2,1,0:T(8,128)(2,1)S(1)} %grad_by_rows.10), channel_id=1, source_target_pairs={{0,4},{4,0},{8,12},{12,8},{16,20},{20,16},{24,28},{28,24},{1,5},{5... | collective-permute-start | bytes 3145736 | tf_op jit(solution)/shard_map/ppermute | solution.py:581
  369.9 15.1 %collective-permute-start.54 = (bf16[1,512,256]{2,1,0:T(8,128)(2,1)S(1)}, bf16[1,512,256]{2,1,0:T(8,128)(2,1)S(1)}, u32[]{:S(2)}, u32[]{:S(2)}) collective-permute-start(bf16[1,512,256]{2,1,0:T(8,128)(2,1)S(1)} %add_convert_fusion.17), channel_id=1, source_target_pairs={{0,16},{4,20},{8,24},{12,28},{16,0},{20,4},{24,8},{28,12},{1,17},{... | collective-permute-start | bytes 786440 | tf_op jit(solution)/shard_map/ppermute | solution.py:581
  376.8 27.3 %collective-permute-start.49 = (f32[5120]{0:T(1024)S(1)}, f32[5120]{0:T(1024)S(1)}, u32[]{:S(2)}, u32[]{:S(2)}) collective-permute-start(f32[5120]{0:T(1024)S(1)} %fusion.57), channel_id=1, source_target_pairs={{0,4},{4,0},{8,12},{12,8},{16,20},{20,16},{24,28},{28,24},{1,5},{5... | collective-permute-start | bytes 61448 | tf_op jit(solution)/shard_map/ppermute | solution.py:581
  378.2 13.9 %collective-permute-start.53 = (bf16[2,64,512]{2,1,0:T(8,128)(2,1)S(1)}, bf16[2,64,512]{2,1,0:T(8,128)(2,1)S(1)}, u32[]{:S(2)}, u32[]{:S(2)}) collective-permute-start(bf16[2,64,512]{2,1,0:T(8,128)(2,1)S(1)} %fusion.47), channel_id=1, source_target_pairs={{0,8},{4,12},{8,0},{12,4},{16,24},{20,28},{24,16},{28,20},{1,9},{5... | collective-permute-start | bytes 393224 | tf_op jit(solution)/shard_map/ppermute | solution.py:581
  385.2 25.4 %collective-permute-start.57 = (bf16[4,64,1024]{2,1,0:T(8,128)(2,1)S(1)}, bf16[4,64,1024]{2,1,0:T(8,128)(2,1)S(1)}, u32[]{:S(2)}, u32[]{:S(2)}) collective-permute-start(bf16[4,64,1024]{2,1,0:T(8,128)(2,1)S(1)} %bitcast.96), channel_id=1, source_target_pairs={{0,4},{4,0},{8,12},{12,8},{16,20},{20,16},{24,28},{28,24},{1,5},{5... | collective-permute-start | bytes 1572872 | tf_op jit(solution)/shard_map/ppermute | solution.py:581
  399.5 22.4 %collective-permute-start.62 = (bf16[2,128,1024]{2,1,0:T(8,128)(2,1)S(1)}, bf16[2,128,1024]{2,1,0:T(8,128)(2,1)S(1)}, u32[]{:S(2)}, u32[]{:S(2)}) collective-permute-start(bf16[2,128,1024]{2,1,0:T(8,128)(2,1)S(1)} %add_convert_fusion.11), channel_id=1, source_target_pairs={{0,8},{4,12},{8,0},{12,4},{16,24},{20,28},{24,16},{28,20},{1,9},{5... | collective-permute-start | bytes 1572872 | tf_op jit(solution)/shard_map/ppermute | solution.py:581
  401.2 23.8 %collective-permute-start.61 = (bf16[1,64,512]{2,1,0:T(8,128)(2,1)S(1)}, bf16[1,64,512]{2,1,0:T(8,128)(2,1)S(1)}, u32[]{:S(2)}, u32[]{:S(2)}) collective-permute-start(bf16[1,64,512]{2,1,0:T(8,128)(2,1)S(1)} %fusion.49), channel_id=1, source_target_pairs={{0,16},{4,20},{8,24},{12,28},{16,0},{20,4},{24,8},{28,12},{1,17},{... | collective-permute-start | bytes 196616 | tf_op jit(solution)/shard_map/ppermute | solution.py:581
  402.7 23.0 %collective-permute-start.60 = (bf16[1,512,256]{2,1,0:T(8,128)(2,1)S(1)}, bf16[1,512,256]{2,1,0:T(8,128)(2,1)S(1)}, u32[]{:S(2)}, u32[]{:S(2)}) collective-permute-start(bf16[1,512,256]{2,1,0:T(8,128)(2,1)S(1)} %add_convert_fusion.16), channel_id=1, source_target_pairs={{0,16},{4,20},{8,24},{12,28},{16,0},{20,4},{24,8},{28,12},{1,17},{... | collective-permute-start | bytes 786440 | tf_op jit(solution)/shard_map/ppermute | solution.py:581
  404.1 17.7 %collective-permute-start.56 = (f32[5120]{0:T(1024)S(1)}, f32[5120]{0:T(1024)S(1)}, u32[]{:S(2)}, u32[]{:S(2)}) collective-permute-start(f32[5120]{0:T(1024)S(1)} %add.419), channel_id=1, source_target_pairs={{0,8},{4,12},{8,0},{12,4},{16,24},{20,28},{24,16},{28,20},{1,9},{5... | collective-permute-start | bytes 61448 | tf_op jit(solution)/shard_map/ppermute | solution.py:581
  410.6 18.4 %collective-permute-start.59 = (bf16[2,64,1024]{2,1,0:T(8,128)(2,1)S(1)}, bf16[2,64,1024]{2,1,0:T(8,128)(2,1)S(1)}, u32[]{:S(2)}, u32[]{:S(2)}) collective-permute-start(bf16[2,64,1024]{2,1,0:T(8,128)(2,1)S(1)} %fusion.40), channel_id=1, source_target_pairs={{0,8},{4,12},{8,0},{12,4},{16,24},{20,28},{24,16},{28,20},{1,9},{5... | collective-permute-start | bytes 786440 | tf_op jit(solution)/shard_map/ppermute | solution.py:581
  421.9 8.3 %collective-permute-start.58 = (f32[5120]{0:T(1024)S(1)}, f32[5120]{0:T(1024)S(1)}, u32[]{:S(2)}, u32[]{:S(2)}) collective-permute-start(f32[5120]{0:T(1024)S(1)} %add.421), channel_id=1, source_target_pairs={{0,16},{4,20},{8,24},{12,28},{16,0},{20,4},{24,8},{28,12},{1,17},{... | collective-permute-start | bytes 61448 | tf_op jit(solution)/shard_map/ppermute | solution.py:581
  422.1 18.5 %collective-permute-start.64 = (bf16[1,128,1024]{2,1,0:T(8,128)(2,1)S(1)}, bf16[1,128,1024]{2,1,0:T(8,128)(2,1)S(1)}, u32[]{:S(2)}, u32[]{:S(2)}) collective-permute-start(bf16[1,128,1024]{2,1,0:T(8,128)(2,1)S(1)} %add_convert_fusion.15), channel_id=1, source_target_pairs={{0,16},{4,20},{8,24},{12,28},{16,0},{20,4},{24,8},{28,12},{1,17},{... | collective-permute-start | bytes 786440 | tf_op jit(solution)/shard_map/ppermute | solution.py:581
  429.1 10.7 %collective-permute-start.63 = (bf16[1,64,1024]{2,1,0:T(8,128)(2,1)S(1)}, bf16[1,64,1024]{2,1,0:T(8,128)(2,1)S(1)}, u32[]{:S(2)}, u32[]{:S(2)}) collective-permute-start(bf16[1,64,1024]{2,1,0:T(8,128)(2,1)S(1)} %fusion.46), channel_id=1, source_target_pairs={{0,16},{4,20},{8,24},{12,28},{16,0},{20,4},{24,8},{28,12},{1,17},{... | collective-permute-start | bytes 393224 | tf_op jit(solution)/shard_map/ppermute | solution.py:581
  (64 other events, 402.8 us)

commit v5 on v4

--- a/solution.py
+++ b/solution.py
@@ -402,24 +402,25 @@
 
 def hidden_kernel(x_ref, gate_ref, up_ref, gh_ref, hidden_ref, hidden_t_ref, gg_ref, gu_ref, gate_s, up_s):
     step = pl.program_id(0)
-    gate = dot(x_ref[...], gate_ref[...])
-    up = dot(x_ref[...], up_ref[...])
+    final = pl.num_programs(0) - 1
 
     @pl.when(step == 0)
     def _():
-        gate_s[...] = gate
-        up_s[...] = up
-
-    @pl.when(step > 0)
+        gate_s[...] = dot(x_ref[...], gate_ref[...])
+        up_s[...] = dot(x_ref[...], up_ref[...])
+
+    @pl.when((step > 0) & (step < final))
     def _():
-        gate_s[...] += gate
-        up_s[...] += up
-
-    @pl.when(step == pl.num_programs(0) - 1)
+        gate_s[...] += dot(x_ref[...], gate_ref[...])
+        up_s[...] += dot(x_ref[...], up_ref[...])
+
+    @pl.when(step == final)
     def _():
-        for first in range(0, gate_s.shape[0], 128):
-            at = slice(first, first + 128)
-            gate_pre, up_pre, grad = gate_s[at, :], up_s[at, :], gh_ref[at, :]
+        for first in range(0, gate_s.shape[0], 256):
+            at = slice(first, first + 256)
+            gate_pre = gate_s[at, :] + dot(x_ref[at, :], gate_ref[...])
+            up_pre = up_s[at, :] + dot(x_ref[at, :], up_ref[...])
+            grad = gh_ref[at, :]
             sigmoid = jax.nn.sigmoid(gate_pre)
             silu = gate_pre * sigmoid
             hidden = (silu * up_pre).astype(BF16)

time: 447 us -> 446 us (level)
  no operation moved by 1% of the time
where the time goes in v5:
time: 446 us; the launch traced here: 440 us
  waiting for transfers between devices  198 us (44%)
  starting transfers between devices  76 us (17%)
  Pallas kernels  66.4 us (15%)
  other arithmetic  42.5 us (10%)
  matrix products  32.3 us (7%)
  local copies, waits for them, and re-layouts  22.3 us (5%)
    ppermute x30, waiting for transfers between devices, swap_seq(): return lax.ppermute(values, 'seq', [(i, i ^ bit) for i in range(count)])  136 us
    ppermute x30, starting transfers between devices, swap_seq(): return lax.ppermute(values, 'seq', [(i, i ^ bit) for i in range(count)])  50.7 us
    ppermute x11, waiting for transfers between devices, far(): return lax.ppermute(values, 'tensor', [(i, i ^ 2) for i in range(4)])  40.7 us
    dot_general x15, matrix products, dot(): return lax.dot_general(left, right, dims, preferred_element_type=F32)  32.3 us
    unnamed x130, local copies, waits for them, and re-layouts  19.9 us
    pallas_call x6, Pallas kernels, grad_by_rows(): pl.pallas_call(rows_kernel, grid_spec=pltpu.PrefetchScalarGridSpec(num_sc...  18.7 us
    ppermute x8, waiting for transfers between devices, ring_shift(): lax.ppermute(values, 'seq', [(order[i], order[(i + step) % count]) for i...  18.2 us
    ppermute x11, starting transfers between devices, far(): return lax.ppermute(values, 'tensor', [(i, i ^ 2) for i in range(4)])  15 us
  transfers between devices with their start and end apart: 65, of which 33 were waited for; matrix products, arithmetic and copies ran while one was open for 16% of the time, Pallas kernels for 11%

profile of v5, /device:TPU:0, one launch (start us, length us, event | category | flops | bytes accessed | tf_op | source)
XLA Modules:
  0.0 440.2 jit_solution(14786826940582419962)
XLA Ops:
  6.0 3.0 collective-permute-start
  9.0 3.0 multiply_reduce_fusion.6
  12.5 1.9 collective-permute-start.2
  16.3 3.7 collective-permute-done.2
  25.5 4.8 %collective-permute-done.4 = bf16[256,512]{1,0:T(8,128)(2,1)S(1)} collective-permute-done((bf16[256,512]{1,0:T(8,128)(2,1)S(1)}, bf16[256,512]{1,0:T(8,128)(2,1)S(1)}, u32[]{:S(2)}, u32[]{:S(2)}) %collective-permute-start.4) | collective-permute-done | bytes 262176 | tf_op jit(solution)/shard_map/ppermute | solution.py:572
  33.8 3.9 project_rotate.1
  42.8 2.7 collective-permute-done.10
  52.9 6.6 %attend.1 = (bf16[512,1024]{1,0:T(8,128)(2,1)S(1)}, bf16[1024,512]{1,0:T(8,128)(2,1)S(1)}, f32[4,8,512]{2,1,0:T(8,128)S(1)}, bf16[256,2048]{1,0:T(8,128)(2,1)S(1)}, bf16[256,2048]{1,0:T(8,128)(2,1)S(1)}) custom-call(s32[4]{0:T(128)S(1)} %copy-done.37, bf16[512,1024]{1,0:T(8,128)(2,1)S(1)} %get-tuple-element.153.q_ref, ...), custom_call_target="tpu_custom_call" | custom-call | flops 1000 | bytes 1000 | tf_op jit(solution)/shard_map/attend/pallas_call | solution.py:219
  71.9 8.4 %fusion.65.gh_ref = f32[512,1408]{1,0:T(8,128)} fusion(bf16[512,2048]{1,0:T(8,128)(2,1)S(1)} %constant_dynamic-update-slice_fusion.6.right_ref, bf16[1408,2048]{1,0:T(8,128)(2,1)} %param.26), kind=kOutput, calls=%fused_computation.183 | convolution fusion | flops 2952790016 | bytes 10747904 | tf_op jit(solution)/shard_map/dot_general | solution.py:39
  80.3 13.4 %collective-permute-done.17 = bf16[256,2048]{1,0:T(8,128)(2,1)S(1)} collective-permute-done((bf16[256,2048]{1,0:T(8,128)(2,1)S(1)}, bf16[256,2048]{1,0:T(8,128)(2,1)S(1)}, u32[]{:S(2)}, u32[]{:S(2)}) %collective-permute-start.17) | collective-permute-done | bytes 1048608 | tf_op jit(solution)/shard_map/ppermute | solution.py:563
  96.0 2.8 collective-permute-done.20
  100.6 2.6 copy-done.21
  103.2 10.4 %hidden_units.1 = (bf16[512,1408]{1,0:T(8,128)(2,1)S(1)}, bf16[1408,512]{1,0:T(8,128)(2,1)S(1)}, bf16[512,1408]{1,0:T(8,128)(2,1)S(1)}, bf16[512,1408]{1,0:T(8,128)(2,1)S(1)}) custom-call(bf16[512,2048]{1,0:T(8,128)(2,1)S(1)} %pad_maximum_fusion.x_ref.left_ref, bf16[2048,1408]{1,0:T(8,128)(2,1)S(1)} %copy-done.21, bf16[2048,1408]{1,0:T(8,128)(2,1)} %up_ref.1, ...), custom_call_target="tpu_custom_call" | custom-call | flops 1000 | bytes 1000 | tf_op jit(solution)/shard_map/hidden_units/pallas_call | solution.py:440
  113.7 4.0 grad_by_columns.6
  119.1 2.9 grad_by_columns.7
  123.6 4.3 grad_by_rows.6
  127.9 4.7 %collective-permute-start.27 = (bf16[4,256,1408]{2,1,0:T(8,128)(2,1)}, bf16[4,256,1408]{2,1,0:T(8,128)(2,1)}, u32[]{:S(2)}, u32[]{:S(2)}) collective-permute-start(bf16[4,256,1408]{2,1,0:T(8,128)(2,1)} %grad_by_rows.6), channel_id=1, source_target_pairs={{0,8},{4,12},{8,0},{12,4},{16,24},{20,28},{24,16},{28,20},{1,9},{5... | collective-permute-start | bytes 8650760 | tf_op jit(solution)/shard_map/ppermute | solution.py:582
  132.7 3.4 grad_by_rows.7
  137.6 1.8 fusion.26
  139.8 1.8 fusion.2
  141.7 1.8 fusion.29
  143.6 1.8 fusion.1
  145.7 1.8 convolution_convert_fusion
  152.0 21.4 %collective-permute-done.23 = bf16[256,2048]{1,0:T(8,128)(2,1)S(1)} collective-permute-done((bf16[256,2048]{1,0:T(8,128)(2,1)S(1)}, bf16[256,2048]{1,0:T(8,128)(2,1)S(1)}, u32[]{:S(2)}, u32[]{:S(2)}) %collective-permute-start.23) | collective-permute-done | bytes 1048608 | tf_op jit(solution)/shard_map/ppermute | solution.py:563
  174.2 2.7 fusion.58
  176.9 4.9 %multiply_reduce_fusion.5 = (f32[256]{0:T(256)S(1)}, f32[256,1024]{1,0:T(8,128)}) fusion(bf16[256,2048]{1,0:T(8,128)(2,1)} %copy-done.26, bf16[2048,1024]{1,0:T(8,128)(2,1)} %param.18), kind=kOutput, calls=%fused_computation.70 | convolution fusion | flops 1074265856 | bytes 6292480 | tf_op jit(solution)/shard_map/dot_general | solution.py:39
  182.5 3.4 grad_by_rows.8
  186.5 3.0 add_convert_fusion.3
  189.5 1.9 pad_maximum_fusion.1.gb_ref.right_ref
  192.3 3.6 attended_grad.1
  195.9 2.0 grad_by_columns.8
  197.9 2.0 grad_by_columns.9
  199.9 3.2 grad_by_rows.9
  203.2 1.9 add_convert_fusion.2
  205.8 5.2 %attend_back.1 = (bf16[512,1024]{1,0:T(8,128)(2,1)S(1)}, bf16[8,256,512]{2,1,0:T(8,128)(2,1)S(1)}, bf16[8,256,512]{2,1,0:T(8,128)(2,1)S(1)}) custom-call(s32[4]{0:T(128)S(1)} %copy-done.37, s32[8]{0:T(128)S(1)} %get-tuple-element.301._, bf16[512,1024]{1,0:T(8,128)(2,1)S(1)} %copy-done.25, bf16[512,1024]{1,0:T(8,128)(2,1)S(1)} %get-tuple-element.203.do_ref, ...), custom_call_target="tpu_custom_call" | custom-call | flops 1000 | bytes 1000 | tf_op jit(solution)/shard_map/attend_back/pallas_call | solution.py:302
  214.7 11.7 %collective-permute-done.30 = bf16[2,1408,256]{2,1,0:T(8,128)(2,1)} collective-permute-done((bf16[2,1408,256]{2,1,0:T(8,128)(2,1)}, bf16[2,1408,256]{2,1,0:T(8,128)(2,1)}, u32[]{:S(2)}, u32[]{:S(2)}) %collective-permute-start.30) | collective-permute-done | bytes 1441824 | tf_op jit(solution)/shard_map/ppermute | solution.py:582
  228.1 10.5 %collective-permute-start.32 = (bf16[1,1408,256]{2,1,0:T(8,128)(2,1)S(1)}, bf16[1,1408,256]{2,1,0:T(8,128)(2,1)S(1)}, u32[]{:S(2)}, u32[]{:S(2)}) collective-permute-start(bf16[1,1408,256]{2,1,0:T(8,128)(2,1)S(1)} %add_convert_fusion.10), channel_id=1, source_target_pairs={{0,16},{4,20},{8,24},{12,28},{16,0},{20,4},{24,8},{28,12},{1,17},{... | collective-permute-start | bytes 2162696 | tf_op jit(solution)/shard_map/ppermute | solution.py:582
  238.6 12.1 %collective-permute-done.29 = bf16[4,256,1408]{2,1,0:T(8,128)(2,1)} collective-permute-done((bf16[4,256,1408]{2,1,0:T(8,128)(2,1)S(1)}, bf16[4,256,1408]{2,1,0:T(8,128)(2,1)}, u32[]{:S(2)}, u32[]{:S(2)}) %collective-permute-start.29) | collective-permute-done | bytes 2883616 | tf_op jit(solution)/shard_map/ppermute | solution.py:582
  255.6 2.0 grad_by_columns.10
  257.6 2.0 grad_by_columns.11
  259.5 2.1 grad_by_rows.10
  261.7 2.4 grad_by_rows.11
  264.0 6.7 %collective-permute-done.32 = bf16[1,1408,256]{2,1,0:T(8,128)(2,1)S(1)} collective-permute-done((bf16[1,1408,256]{2,1,0:T(8,128)(2,1)S(1)}, bf16[1,1408,256]{2,1,0:T(8,128)(2,1)S(1)}, u32[]{:S(2)}, u32[]{:S(2)}) %collective-permute-start.32) | collective-permute-done | bytes 720928 | tf_op jit(solution)/shard_map/ppermute | solution.py:582
  270.7 2.9 add_bitcast_fusion.2
  273.6 4.1 collective-permute-done.31
  280.4 9.0 %collective-permute-done.35 = bf16[2,256,1408]{2,1,0:T(8,128)(2,1)S(1)} collective-permute-done((bf16[2,256,1408]{2,1,0:T(8,128)(2,1)S(1)}, bf16[2,256,1408]{2,1,0:T(8,128)(2,1)S(1)}, u32[]{:S(2)}, u32[]{:S(2)}) %collective-permute-start.35) | collective-permute-done | bytes 1441824 | tf_op jit(solution)/shard_map/ppermute | solution.py:582
  290.9 10.5 %collective-permute-start.40 = (bf16[1,256,1408]{2,1,0:T(8,128)(2,1)S(1)}, bf16[1,256,1408]{2,1,0:T(8,128)(2,1)S(1)}, u32[]{:S(2)}, u32[]{:S(2)}) collective-permute-start(bf16[1,256,1408]{2,1,0:T(8,128)(2,1)S(1)} %add_convert_fusion.9), channel_id=1, source_target_pairs={{0,16},{4,20},{8,24},{12,28},{16,0},{20,4},{24,8},{28,12},{1,17},{... | collective-permute-start | bytes 2162696 | tf_op jit(solution)/shard_map/ppermute | solution.py:582
  302.8 17.6 %collective-permute-done.36 = bf16[2,128,512]{2,1,0:T(8,128)(2,1)S(1)} collective-permute-done((bf16[2,128,512]{2,1,0:T(8,128)(2,1)S(1)}, bf16[2,128,512]{2,1,0:T(8,128)(2,1)S(1)}, u32[]{:S(2)}, u32[]{:S(2)}) %collective-permute-start.36) | collective-permute-done | bytes 262176 | tf_op jit(solution)/shard_map/ppermute | solution.py:582
  322.6 9.2 %collective-permute-done.40 = bf16[1,256,1408]{2,1,0:T(8,128)(2,1)S(1)} collective-permute-done((bf16[1,256,1408]{2,1,0:T(8,128)(2,1)S(1)}, bf16[1,256,1408]{2,1,0:T(8,128)(2,1)S(1)}, u32[]{:S(2)}, u32[]{:S(2)}) %collective-permute-start.40) | collective-permute-done | bytes 720928 | tf_op jit(solution)/shard_map/ppermute | solution.py:582
  331.8 2.6 add_bitcast_fusion.1
  340.2 3.4 collective-permute-start.55
  345.8 17.6 %collective-permute-done.45 = bf16[4,512,256]{2,1,0:T(8,128)(2,1)S(1)} collective-permute-done((bf16[4,512,256]{2,1,0:T(8,128)(2,1)S(1)}, bf16[4,512,256]{2,1,0:T(8,128)(2,1)S(1)}, u32[]{:S(2)}, u32[]{:S(2)}) %collective-permute-start.45) | collective-permute-done | bytes 1048608 | tf_op jit(solution)/shard_map/ppermute | solution.py:582
  363.5 1.8 collective-permute-start.51
  368.2 6.8 %collective-permute-done.52 = bf16[4,64,512]{2,1,0:T(8,128)(2,1)S(1)} collective-permute-done((bf16[4,64,512]{2,1,0:T(8,128)(2,1)S(1)}, bf16[4,64,512]{2,1,0:T(8,128)(2,1)S(1)}, u32[]{:S(2)}, u32[]{:S(2)}) %collective-permute-start.52) | collective-permute-done | bytes 262176 | tf_op jit(solution)/shard_map/ppermute | solution.py:582
  376.5 2.6 add_bitcast_fusion
  379.2 4.1 collective-permute-done.54
  384.6 5.8 %collective-permute-done.53 = bf16[2,64,512]{2,1,0:T(8,128)(2,1)S(1)} collective-permute-done((bf16[2,64,512]{2,1,0:T(8,128)(2,1)S(1)}, bf16[2,64,512]{2,1,0:T(8,128)(2,1)S(1)}, u32[]{:S(2)}, u32[]{:S(2)}) %collective-permute-start.53) | collective-permute-done | bytes 131104 | tf_op jit(solution)/shard_map/ppermute | solution.py:582
  390.5 7.0 %collective-permute-done.50 = bf16[4,128,1024]{2,1,0:T(8,128)(2,1)S(1)} collective-permute-done((bf16[4,128,1024]{2,1,0:T(8,128)(2,1)S(1)}, bf16[4,128,1024]{2,1,0:T(8,128)(2,1)S(1)}, u32[]{:S(2)}, u32[]{:S(2)}) %collective-permute-start.50) | collective-permute-done | bytes 1048608 | tf_op jit(solution)/shard_map/ppermute | solution.py:582
  402.4 1.8 collective-permute-start.56
  404.2 4.6 %collective-permute-done.57 = bf16[4,64,1024]{2,1,0:T(8,128)(2,1)S(1)} collective-permute-done((bf16[4,64,1024]{2,1,0:T(8,128)(2,1)S(1)}, bf16[4,64,1024]{2,1,0:T(8,128)(2,1)S(1)}, u32[]{:S(2)}, u32[]{:S(2)}) %collective-permute-start.57) | collective-permute-done | bytes 524320 | tf_op jit(solution)/shard_map/ppermute | solution.py:582
  409.2 10.9 %collective-permute-done.56 = f32[5120]{0:T(1024)S(1)} collective-permute-done((f32[5120]{0:T(1024)S(1)}, f32[5120]{0:T(1024)S(1)}, u32[]{:S(2)}, u32[]{:S(2)}) %collective-permute-start.56) | collective-permute-done | bytes 20512 | tf_op jit(solution)/shard_map/ppermute | solution.py:582
  420.3 2.9 collective-permute-start.64
  424.1 3.2 collective-permute-done.59
  429.6 8.4 %collective-permute-done.63 = bf16[1,64,1024]{2,1,0:T(8,128)(2,1)S(1)} collective-permute-done((bf16[1,64,1024]{2,1,0:T(8,128)(2,1)S(1)}, bf16[1,64,1024]{2,1,0:T(8,128)(2,1)S(1)}, u32[]{:S(2)}, u32[]{:S(2)}) %collective-permute-start.63) | collective-permute-done | bytes 131104 | tf_op jit(solution)/shard_map/ppermute | solution.py:582
  (339 shorter events, 100.4 us)
Async XLA Ops:
  6.0 6.5 %collective-permute-start = (bf16[128,512]{1,0:T(8,128)(2,1)S(1)}, bf16[128,512]{1,0:T(8,128)(2,1)S(1)}, u32[]{:S(2)}, u32[]{:S(2)}) collective-permute-start(bf16[128,512]{1,0:T(8,128)(2,1)S(1)} %get-tuple-element.138), channel_id=1, source_target_pairs={{0,2},{1,3},{2,0},{3,1},{4,6},{5,7},{6,4},{7,5},{8,10},{9,11},{10,... | collective-permute-start | bytes 393224 | tf_op jit(solution)/shard_map/ppermute | solution.py:563
  12.5 7.5 %collective-permute-start.2 = (bf16[256,512]{1,0:T(8,128)(2,1)S(1)}, bf16[256,512]{1,0:T(8,128)(2,1)S(1)}, u32[]{:S(2)}, u32[]{:S(2)}) collective-permute-start(bf16[256,512]{1,0:T(8,128)(2,1)S(1)} %constant_dynamic-update-slice_fusion), channel_id=1, source_target_pairs={{0,8},{8,16},{16,24},{24,28},{28,20},{20,12},{12,4},{4,0},{1,9},{9... | collective-permute-start | bytes 786440 | tf_op jit(solution)/shard_map/ppermute | solution.py:572
  14.4 7.0 %collective-permute-start.3 = (bf16[256,512]{1,0:T(8,128)(2,1)S(1)}, bf16[256,512]{1,0:T(8,128)(2,1)S(1)}, u32[]{:S(2)}, u32[]{:S(2)}) collective-permute-start(bf16[256,512]{1,0:T(8,128)(2,1)S(1)} %constant_dynamic-update-slice_fusion), channel_id=1, source_target_pairs={{0,4},{8,0},{16,8},{24,16},{28,24},{20,28},{12,20},{4,12},{1,5},{9... | collective-permute-start | bytes 786440 | tf_op jit(solution)/shard_map/ppermute | solution.py:572
  14.6 6.9 %collective-permute-start.6 = (bf16[128,1024]{1,0:T(8,128)(2,1)S(1)}, bf16[128,1024]{1,0:T(8,128)(2,1)S(1)}, u32[]{:S(2)}, u32[]{:S(2)}) collective-permute-start(bf16[128,1024]{1,0:T(8,128)(2,1)S(1)} %multiply_convert_fusion.2), channel_id=1, source_target_pairs={{0,2},{1,3},{2,0},{3,1},{4,6},{5,7},{6,4},{7,5},{8,10},{9,11},{10,... | collective-permute-start | bytes 786440 | tf_op jit(solution)/shard_map/ppermute | solution.py:563
  21.6 12.1 %collective-permute-start.9 = (bf16[256,1024]{1,0:T(8,128)(2,1)S(1)}, bf16[256,1024]{1,0:T(8,128)(2,1)S(1)}, u32[]{:S(2)}, u32[]{:S(2)}) collective-permute-start(bf16[256,1024]{1,0:T(8,128)(2,1)S(1)} %pad_maximum_fusion.8), channel_id=1, source_target_pairs={{0,1},{1,0},{2,3},{3,2},{4,5},{5,4},{6,7},{7,6},{8,9},{9,8},{10,11... | collective-permute-start | bytes 1572872 | tf_op jit(solution)/shard_map/ppermute | solution.py:559
  21.6 8.7 %collective-permute-start.4 = (bf16[256,512]{1,0:T(8,128)(2,1)S(1)}, bf16[256,512]{1,0:T(8,128)(2,1)S(1)}, u32[]{:S(2)}, u32[]{:S(2)}) collective-permute-start(bf16[256,512]{1,0:T(8,128)(2,1)S(1)} %collective-permute-done.2), channel_id=1, source_target_pairs={{0,8},{8,16},{16,24},{24,28},{28,20},{20,12},{12,4},{4,0},{1,9},{9... | collective-permute-start | bytes 786440 | tf_op jit(solution)/shard_map/ppermute | solution.py:572
  23.3 8.4 %collective-permute-start.5 = (bf16[256,512]{1,0:T(8,128)(2,1)S(1)}, bf16[256,512]{1,0:T(8,128)(2,1)S(1)}, u32[]{:S(2)}, u32[]{:S(2)}) collective-permute-start(bf16[256,512]{1,0:T(8,128)(2,1)S(1)} %collective-permute-done.3), channel_id=1, source_target_pairs={{0,4},{8,0},{16,8},{24,16},{28,24},{20,28},{12,20},{4,12},{1,5},{9... | collective-permute-start | bytes 786440 | tf_op jit(solution)/shard_map/ppermute | solution.py:572
  23.7 23.7 %collective-permute-start.1 = (bf16[128,2048]{1,0:T(8,128)(2,1)S(1)}, bf16[128,2048]{1,0:T(8,128)(2,1)S(1)}, u32[]{:S(2)}, u32[]{:S(2)}) collective-permute-start(bf16[128,2048]{1,0:T(8,128)(2,1)S(1)} %copy-done.9), channel_id=1, source_target_pairs={{0,2},{1,3},{2,0},{3,1},{4,6},{5,7},{6,4},{7,5},{8,10},{9,11},{10,... | collective-permute-start | bytes 1572872 | tf_op jit(solution)/shard_map/ppermute | solution.py:563
  25.5 24.5 %collective-permute-start.12 = (bf16[3,256,512]{2,1,0:T(8,128)(2,1)S(1)}, bf16[3,256,512]{2,1,0:T(8,128)(2,1)S(1)}, u32[]{:S(2)}, u32[]{:S(2)}) collective-permute-start(bf16[3,256,512]{2,1,0:T(8,128)(2,1)S(1)} %pad_maximum_fusion.6), channel_id=1, source_target_pairs={{0,1},{1,0},{2,3},{3,2},{4,5},{5,4},{6,7},{7,6},{8,9},{9,8},{10,11... | collective-permute-start | bytes 2359304 | tf_op jit(solution)/shard_map/ppermute | solution.py:559
  31.7 7.5 %collective-permute-start.7 = (bf16[256,512]{1,0:T(8,128)(2,1)S(1)}, bf16[256,512]{1,0:T(8,128)(2,1)S(1)}, u32[]{:S(2)}, u32[]{:S(2)}) collective-permute-start(bf16[256,512]{1,0:T(8,128)(2,1)S(1)} %collective-permute-done.4), channel_id=1, source_target_pairs={{0,8},{8,16},{16,24},{24,28},{28,20},{20,12},{12,4},{4,0},{1,9},{9... | collective-permute-start | bytes 786440 | tf_op jit(solution)/shard_map/ppermute | solution.py:572
  33.2 7.3 %collective-permute-start.8 = (bf16[256,512]{1,0:T(8,128)(2,1)S(1)}, bf16[256,512]{1,0:T(8,128)(2,1)S(1)}, u32[]{:S(2)}, u32[]{:S(2)}) collective-permute-start(bf16[256,512]{1,0:T(8,128)(2,1)S(1)} %collective-permute-done.5), channel_id=1, source_target_pairs={{0,4},{8,0},{16,8},{24,16},{28,24},{20,28},{12,20},{4,12},{1,5},{9... | collective-permute-start | bytes 786440 | tf_op jit(solution)/shard_map/ppermute | solution.py:572
  40.5 5.0 %collective-permute-start.10 = (bf16[128,512]{1,0:T(8,128)(2,1)S(1)}, bf16[128,512]{1,0:T(8,128)(2,1)S(1)}, u32[]{:S(2)}, u32[]{:S(2)}) collective-permute-start(bf16[128,512]{1,0:T(8,128)(2,1)S(1)} %slice.411), channel_id=1, source_target_pairs={{0,8},{8,16},{16,24},{24,28},{28,20},{20,12},{12,4},{4,0},{1,9},{9... | collective-permute-start | bytes 393224 | tf_op jit(solution)/shard_map/ppermute | solution.py:572
  42.2 5.0 %collective-permute-start.11 = (bf16[128,512]{1,0:T(8,128)(2,1)S(1)}, bf16[128,512]{1,0:T(8,128)(2,1)S(1)}, u32[]{:S(2)}, u32[]{:S(2)}) collective-permute-start(bf16[128,512]{1,0:T(8,128)(2,1)S(1)} %slice.412), channel_id=1, source_target_pairs={{0,4},{8,0},{16,8},{24,16},{28,24},{20,28},{12,20},{4,12},{1,5},{9... | collective-permute-start | bytes 393224 | tf_op jit(solution)/shard_map/ppermute | solution.py:572
  42.8 7.4 %collective-permute-start.13 = (bf16[2,256,512]{2,1,0:T(8,128)(2,1)S(1)}, bf16[2,256,512]{2,1,0:T(8,128)(2,1)S(1)}, u32[]{:S(2)}, u32[]{:S(2)}) collective-permute-start(bf16[2,256,512]{2,1,0:T(8,128)(2,1)S(1)} %get-tuple-element.159), channel_id=1, source_target_pairs={{0,1},{1,0},{2,3},{3,2},{4,5},{5,4},{6,7},{7,6},{8,9},{9,8},{10,11... | collective-permute-start | bytes 1572872 | tf_op jit(solution)/shard_map/ppermute | solution.py:559
  47.3 2.9 collective-permute-start.14
  47.5 14.4 %collective-permute-start.15 = (bf16[128,2048]{1,0:T(8,128)(2,1)S(1)}, bf16[128,2048]{1,0:T(8,128)(2,1)S(1)}, u32[]{:S(2)}, u32[]{:S(2)}) collective-permute-start(bf16[128,2048]{1,0:T(8,128)(2,1)S(1)} %copy-done.50), channel_id=1, source_target_pairs={{0,2},{1,3},{2,0},{3,1},{4,6},{5,7},{6,4},{7,5},{8,10},{9,11},{10,... | collective-permute-start | bytes 1572872 | tf_op jit(solution)/shard_map/ppermute | solution.py:563
  66.4 5.3 %collective-permute-start.18 = (bf16[256,2048]{1,0:T(8,128)(2,1)S(1)}, bf16[256,2048]{1,0:T(8,128)(2,1)S(1)}, u32[]{:S(2)}, u32[]{:S(2)}) collective-permute-start(bf16[256,2048]{1,0:T(8,128)(2,1)S(1)} %get-tuple-element.282), channel_id=1, source_target_pairs={{0,1},{1,0},{2,3},{3,2},{4,5},{5,4},{6,7},{7,6},{8,9},{9,8},{10,11... | collective-permute-start | bytes 3145736 | tf_op jit(solution)/shard_map/ppermute | solution.py:559
  68.4 25.3 %collective-permute-start.17 = (bf16[256,2048]{1,0:T(8,128)(2,1)S(1)}, bf16[256,2048]{1,0:T(8,128)(2,1)S(1)}, u32[]{:S(2)}, u32[]{:S(2)}) collective-permute-start(bf16[256,2048]{1,0:T(8,128)(2,1)S(1)} %pad_maximum_fusion.3), channel_id=1, source_target_pairs={{0,2},{1,3},{2,0},{3,1},{4,6},{5,7},{6,4},{7,5},{8,10},{9,11},{10,... | collective-permute-start | bytes 3145736 | tf_op jit(solution)/shard_map/ppermute | solution.py:563
  71.7 8.6 %collective-permute-start.19 = (bf16[512,256]{1,0:T(8,128)(2,1)S(1)}, bf16[512,256]{1,0:T(8,128)(2,1)S(1)}, u32[]{:S(2)}, u32[]{:S(2)}) collective-permute-start(bf16[512,256]{1,0:T(8,128)(2,1)S(1)} %get-tuple-element.176), channel_id=1, source_target_pairs={{0,1},{1,0},{2,3},{3,2},{4,5},{5,4},{6,7},{7,6},{8,9},{9,8},{10,11... | collective-permute-start | bytes 786440 | tf_op jit(solution)/shard_map/ppermute | solution.py:559
  95.8 3.0 collective-permute-start.20
  117.7 68.8 %collective-permute-start.26 = (bf16[4,1408,256]{2,1,0:T(8,128)(2,1)}, bf16[4,1408,256]{2,1,0:T(8,128)(2,1)}, u32[]{:S(2)}, u32[]{:S(2)}) collective-permute-start(bf16[4,1408,256]{2,1,0:T(8,128)(2,1)} %grad_by_columns.6), channel_id=1, source_target_pairs={{0,4},{4,0},{8,12},{12,8},{16,20},{20,16},{24,28},{28,24},{1,5},{5... | collective-permute-start | bytes 8650760 | tf_op jit(solution)/shard_map/ppermute | solution.py:582
  127.9 75.2 %collective-permute-start.27 = (bf16[4,256,1408]{2,1,0:T(8,128)(2,1)}, bf16[4,256,1408]{2,1,0:T(8,128)(2,1)}, u32[]{:S(2)}, u32[]{:S(2)}) collective-permute-start(bf16[4,256,1408]{2,1,0:T(8,128)(2,1)} %grad_by_rows.6), channel_id=1, source_target_pairs={{0,8},{4,12},{8,0},{12,4},{16,24},{20,28},{24,16},{28,20},{1,9},{5... | collective-permute-start | bytes 8650760 | tf_op jit(solution)/shard_map/ppermute | solution.py:582
  141.6 3.8 collective-permute-start.21
  147.5 3.2 collective-permute-start.22
  148.2 25.2 %collective-permute-start.23 = (bf16[256,2048]{1,0:T(8,128)(2,1)S(1)}, bf16[256,2048]{1,0:T(8,128)(2,1)S(1)}, u32[]{:S(2)}, u32[]{:S(2)}) collective-permute-start(bf16[256,2048]{1,0:T(8,128)(2,1)S(1)} %pad_maximum_fusion.4), channel_id=1, source_target_pairs={{0,2},{1,3},{2,0},{3,1},{4,6},{5,7},{6,4},{7,5},{8,10},{9,11},{10,... | collective-permute-start | bytes 3145736 | tf_op jit(solution)/shard_map/ppermute | solution.py:563
  176.9 12.6 %collective-permute-start.25 = (bf16[256,2048]{1,0:T(8,128)(2,1)}, bf16[256,2048]{1,0:T(8,128)(2,1)}, u32[]{:S(2)}, u32[]{:S(2)}) collective-permute-start(bf16[256,2048]{1,0:T(8,128)(2,1)} %get-tuple-element.270), channel_id=1, source_target_pairs={{0,1},{1,0},{2,3},{3,2},{4,5},{5,4},{6,7},{7,6},{8,9},{9,8},{10,11... | collective-permute-start | bytes 3145736 | tf_op jit(solution)/shard_map/ppermute | solution.py:559
  181.9 30.6 %collective-permute-start.24 = (bf16[128,2048]{1,0:T(8,128)(2,1)S(1)}, bf16[128,2048]{1,0:T(8,128)(2,1)S(1)}, u32[]{:S(2)}, u32[]{:S(2)}) collective-permute-start(bf16[128,2048]{1,0:T(8,128)(2,1)S(1)} %slice.429), channel_id=1, source_target_pairs={{0,2},{1,3},{2,0},{3,1},{4,6},{5,7},{6,4},{7,5},{8,10},{9,11},{10,... | collective-permute-start | bytes 1572872 | tf_op jit(solution)/shard_map/ppermute | solution.py:563
  185.9 64.8 %collective-permute-start.29 = (bf16[4,256,1408]{2,1,0:T(8,128)(2,1)S(1)}, bf16[4,256,1408]{2,1,0:T(8,128)(2,1)}, u32[]{:S(2)}, u32[]{:S(2)}) collective-permute-start(bf16[4,256,1408]{2,1,0:T(8,128)(2,1)S(1)} %grad_by_rows.8), channel_id=1, source_target_pairs={{0,4},{4,0},{8,12},{12,8},{16,20},{20,16},{24,28},{28,24},{1,5},{5... | collective-permute-start | bytes 8650760 | tf_op jit(solution)/shard_map/ppermute | solution.py:582
  191.4 35.0 %collective-permute-start.30 = (bf16[2,1408,256]{2,1,0:T(8,128)(2,1)}, bf16[2,1408,256]{2,1,0:T(8,128)(2,1)}, u32[]{:S(2)}, u32[]{:S(2)}) collective-permute-start(bf16[2,1408,256]{2,1,0:T(8,128)(2,1)} %add_convert_fusion.3), channel_id=1, source_target_pairs={{0,8},{4,12},{8,0},{12,4},{16,24},{20,28},{24,16},{28,20},{1,9},{5... | collective-permute-start | bytes 4325384 | tf_op jit(solution)/shard_map/ppermute | solution.py:582
  211.0 41.5 %collective-permute-start.28 = (bf16[8,256,512]{2,1,0:T(8,128)(2,1)S(1)}, bf16[8,256,512]{2,1,0:T(8,128)(2,1)S(1)}, u32[]{:S(2)}, u32[]{:S(2)}) collective-permute-start(bf16[8,256,512]{2,1,0:T(8,128)(2,1)S(1)} %get-tuple-element.212), channel_id=1, source_target_pairs={{0,1},{1,0},{2,3},{3,2},{4,5},{5,4},{6,7},{7,6},{8,9},{9,8},{10,11... | collective-permute-start | bytes 6291464 | tf_op jit(solution)/shard_map/ppermute | solution.py:559
  211.9 42.8 %collective-permute-start.33 = (bf16[256,1024]{1,0:T(8,128)(2,1)S(1)}, bf16[256,1024]{1,0:T(8,128)(2,1)S(1)}, u32[]{:S(2)}, u32[]{:S(2)}) collective-permute-start(bf16[256,1024]{1,0:T(8,128)(2,1)S(1)} %convolution_convert_fusion.5), channel_id=1, source_target_pairs={{0,1},{1,0},{2,3},{3,2},{4,5},{5,4},{6,7},{7,6},{8,9},{9,8},{10,11... | collective-permute-start | bytes 1572872 | tf_op jit(solution)/shard_map/ppermute | solution.py:559
  228.1 42.7 %collective-permute-start.32 = (bf16[1,1408,256]{2,1,0:T(8,128)(2,1)S(1)}, bf16[1,1408,256]{2,1,0:T(8,128)(2,1)S(1)}, u32[]{:S(2)}, u32[]{:S(2)}) collective-permute-start(bf16[1,1408,256]{2,1,0:T(8,128)(2,1)S(1)} %add_convert_fusion.10), channel_id=1, source_target_pairs={{0,16},{4,20},{8,24},{12,28},{16,0},{20,4},{24,8},{28,12},{1,17},{... | collective-permute-start | bytes 2162696 | tf_op jit(solution)/shard_map/ppermute | solution.py:582
  253.2 24.5 %collective-permute-start.31 = (bf16[8,128,512]{2,1,0:T(8,128)(2,1)S(1)}, bf16[8,128,512]{2,1,0:T(8,128)(2,1)S(1)}, u32[]{:S(2)}, u32[]{:S(2)}) collective-permute-start(bf16[8,128,512]{2,1,0:T(8,128)(2,1)S(1)} %slice.532), channel_id=1, source_target_pairs={{0,2},{1,3},{2,0},{3,1},{4,6},{5,7},{6,4},{7,5},{8,10},{9,11},{10,... | collective-permute-start | bytes 3145736 | tf_op jit(solution)/shard_map/ppermute | solution.py:563
  254.8 34.6 %collective-permute-start.35 = (bf16[2,256,1408]{2,1,0:T(8,128)(2,1)S(1)}, bf16[2,256,1408]{2,1,0:T(8,128)(2,1)S(1)}, u32[]{:S(2)}, u32[]{:S(2)}) collective-permute-start(bf16[2,256,1408]{2,1,0:T(8,128)(2,1)S(1)} %add_convert_fusion.2), channel_id=1, source_target_pairs={{0,4},{4,0},{8,12},{12,8},{16,20},{20,16},{24,28},{28,24},{1,5},{5... | collective-permute-start | bytes 4325384 | tf_op jit(solution)/shard_map/ppermute | solution.py:582
  255.4 65.1 %collective-permute-start.42 = (bf16[2,256,1408]{2,1,0:T(8,128)(2,1)S(1)}, bf16[2,256,1408]{2,1,0:T(8,128)(2,1)S(1)}, u32[]{:S(2)}, u32[]{:S(2)}) collective-permute-start(bf16[2,256,1408]{2,1,0:T(8,128)(2,1)S(1)} %add_convert_fusion.1), channel_id=1, source_target_pairs={{0,8},{4,12},{8,0},{12,4},{16,24},{20,28},{24,16},{28,20},{1,9},{5... | collective-permute-start | bytes 4325384 | tf_op jit(solution)/shard_map/ppermute | solution.py:582
  278.1 23.6 %collective-permute-start.34 = (bf16[4,128,512]{2,1,0:T(8,128)(2,1)S(1)}, bf16[4,128,512]{2,1,0:T(8,128)(2,1)S(1)}, u32[]{:S(2)}, u32[]{:S(2)}) collective-permute-start(bf16[4,128,512]{2,1,0:T(8,128)(2,1)S(1)} %slice.535), channel_id=1, source_target_pairs={{0,4},{4,0},{8,12},{12,8},{16,20},{20,16},{24,28},{28,24},{1,5},{5... | collective-permute-start | bytes 1572872 | tf_op jit(solution)/shard_map/ppermute | solution.py:582
  278.9 23.0 %collective-permute-start.37 = (bf16[256,1024]{1,0:T(8,128)(2,1)S(1)}, bf16[256,1024]{1,0:T(8,128)(2,1)S(1)}, u32[]{:S(2)}, u32[]{:S(2)}) collective-permute-start(bf16[256,1024]{1,0:T(8,128)(2,1)S(1)} %pad_maximum_fusion.10), channel_id=1, source_target_pairs={{0,2},{1,3},{2,0},{3,1},{4,6},{5,7},{6,4},{7,5},{8,10},{9,11},{10,... | collective-permute-start | bytes 1572872 | tf_op jit(solution)/shard_map/ppermute | solution.py:563
  290.9 40.9 %collective-permute-start.40 = (bf16[1,256,1408]{2,1,0:T(8,128)(2,1)S(1)}, bf16[1,256,1408]{2,1,0:T(8,128)(2,1)S(1)}, u32[]{:S(2)}, u32[]{:S(2)}) collective-permute-start(bf16[1,256,1408]{2,1,0:T(8,128)(2,1)S(1)} %add_convert_fusion.9), channel_id=1, source_target_pairs={{0,16},{4,20},{8,24},{12,28},{16,0},{20,4},{24,8},{28,12},{1,17},{... | collective-permute-start | bytes 2162696 | tf_op jit(solution)/shard_map/ppermute | solution.py:582
  301.4 21.1 %collective-permute-start.41 = (bf16[4,512,256]{2,1,0:T(8,128)(2,1)S(1)}, bf16[4,512,256]{2,1,0:T(8,128)(2,1)S(1)}, u32[]{:S(2)}, u32[]{:S(2)}) collective-permute-start(bf16[4,512,256]{2,1,0:T(8,128)(2,1)S(1)} %copy-done.31), channel_id=1, source_target_pairs={{0,4},{4,0},{8,12},{12,8},{16,20},{20,16},{24,28},{28,24},{1,5},{5... | collective-permute-start | bytes 3145736 | tf_op jit(solution)/shard_map/ppermute | solution.py:582
  301.8 18.6 %collective-permute-start.36 = (bf16[2,128,512]{2,1,0:T(8,128)(2,1)S(1)}, bf16[2,128,512]{2,1,0:T(8,128)(2,1)S(1)}, u32[]{:S(2)}, u32[]{:S(2)}) collective-permute-start(bf16[2,128,512]{2,1,0:T(8,128)(2,1)S(1)} %add_convert_fusion.18), channel_id=1, source_target_pairs={{0,8},{4,12},{8,0},{12,4},{16,24},{20,28},{24,16},{28,20},{1,9},{5... | collective-permute-start | bytes 786440 | tf_op jit(solution)/shard_map/ppermute | solution.py:582
  302.7 31.8 %collective-permute-start.39 = (bf16[256,1024]{1,0:T(8,128)(2,1)S(1)}, bf16[256,1024]{1,0:T(8,128)(2,1)S(1)}, u32[]{:S(2)}, u32[]{:S(2)}) collective-permute-start(bf16[256,1024]{1,0:T(8,128)(2,1)S(1)} %multiply_convert_fusion.1), channel_id=1, source_target_pairs={{0,1},{1,0},{2,3},{3,2},{4,5},{5,4},{6,7},{7,6},{8,9},{9,8},{10,11... | collective-permute-start | bytes 1572872 | tf_op jit(solution)/shard_map/ppermute | solution.py:559
  320.4 14.8 %collective-permute-start.38 = (bf16[1,128,512]{2,1,0:T(8,128)(2,1)S(1)}, bf16[1,128,512]{2,1,0:T(8,128)(2,1)S(1)}, u32[]{:S(2)}, u32[]{:S(2)}) collective-permute-start(bf16[1,128,512]{2,1,0:T(8,128)(2,1)S(1)} %add_convert_fusion.19), channel_id=1, source_target_pairs={{0,16},{4,20},{8,24},{12,28},{16,0},{20,4},{24,8},{28,12},{1,17},{... | collective-permute-start | bytes 393224 | tf_op jit(solution)/shard_map/ppermute | solution.py:582
  335.3 8.3 %collective-permute-start.43 = (bf16[128,512]{1,0:T(8,128)(2,1)S(1)}, bf16[128,512]{1,0:T(8,128)(2,1)S(1)}, u32[]{:S(2)}, u32[]{:S(2)}) collective-permute-start(bf16[128,512]{1,0:T(8,128)(2,1)S(1)} %pad_maximum_fusion.12), channel_id=1, source_target_pairs={{0,2},{1,3},{2,0},{3,1},{4,6},{5,7},{6,4},{7,5},{8,10},{9,11},{10,... | collective-permute-start | bytes 393224 | tf_op jit(solution)/shard_map/ppermute | solution.py:563
  338.2 27.7 %collective-permute-start.47 = (bf16[2,512,256]{2,1,0:T(8,128)(2,1)S(1)}, bf16[2,512,256]{2,1,0:T(8,128)(2,1)S(1)}, u32[]{:S(2)}, u32[]{:S(2)}) collective-permute-start(bf16[2,512,256]{2,1,0:T(8,128)(2,1)S(1)} %add_convert_fusion.13), channel_id=1, source_target_pairs={{0,8},{4,12},{8,0},{12,4},{16,24},{20,28},{24,16},{28,20},{1,9},{5... | collective-permute-start | bytes 1572872 | tf_op jit(solution)/shard_map/ppermute | solution.py:582
  339.5 23.9 %collective-permute-start.45 = (bf16[4,512,256]{2,1,0:T(8,128)(2,1)S(1)}, bf16[4,512,256]{2,1,0:T(8,128)(2,1)S(1)}, u32[]{:S(2)}, u32[]{:S(2)}) collective-permute-start(bf16[4,512,256]{2,1,0:T(8,128)(2,1)S(1)} %grad_by_columns.9), channel_id=1, source_target_pairs={{0,4},{4,0},{8,12},{12,8},{16,20},{20,16},{24,28},{28,24},{1,5},{5... | collective-permute-start | bytes 3145736 | tf_op jit(solution)/shard_map/ppermute | solution.py:582
  340.2 36.1 %collective-permute-start.55 = (bf16[1,256,1408]{2,1,0:T(8,128)(2,1)S(1)}, bf16[1,256,1408]{2,1,0:T(8,128)(2,1)S(1)}, u32[]{:S(2)}, u32[]{:S(2)}) collective-permute-start(bf16[1,256,1408]{2,1,0:T(8,128)(2,1)S(1)} %add_convert_fusion.8), channel_id=1, source_target_pairs={{0,16},{4,20},{8,24},{12,28},{16,0},{20,4},{24,8},{28,12},{1,17},{... | collective-permute-start | bytes 2162696 | tf_op jit(solution)/shard_map/ppermute | solution.py:582
  343.7 21.7 %collective-permute-start.48 = (bf16[256,512]{1,0:T(8,128)(2,1)S(1)}, bf16[256,512]{1,0:T(8,128)(2,1)S(1)}, u32[]{:S(2)}, u32[]{:S(2)}) collective-permute-start(bf16[256,512]{1,0:T(8,128)(2,1)S(1)} %pad_maximum_fusion.11), channel_id=1, source_target_pairs={{0,1},{1,0},{2,3},{3,2},{4,5},{5,4},{6,7},{7,6},{8,9},{9,8},{10,11... | collective-permute-start | bytes 786440 | tf_op jit(solution)/shard_map/ppermute | solution.py:559
  344.9 20.4 %collective-permute-start.44 = (f32[2048]{0:T(1024)S(1)}, f32[2048]{0:T(1024)S(1)}, u32[]{:S(2)}, u32[]{:S(2)}) collective-permute-start(f32[2048]{0:T(1024)S(1)} %get-tuple-element.268), channel_id=1, source_target_pairs={{0,2},{1,3},{2,0},{3,1},{4,6},{5,7},{6,4},{7,5},{8,10},{9,11},{10,... | collective-permute-start | bytes 24584 | tf_op jit(solution)/shard_map/ppermute | solution.py:563
  363.5 26.9 %collective-permute-start.51 = (bf16[2,512,256]{2,1,0:T(8,128)(2,1)S(1)}, bf16[2,512,256]{2,1,0:T(8,128)(2,1)S(1)}, u32[]{:S(2)}, u32[]{:S(2)}) collective-permute-start(bf16[2,512,256]{2,1,0:T(8,128)(2,1)S(1)} %add_convert_fusion.12), channel_id=1, source_target_pairs={{0,8},{4,12},{8,0},{12,4},{16,24},{20,28},{24,16},{28,20},{1,9},{5... | collective-permute-start | bytes 1572872 | tf_op jit(solution)/shard_map/ppermute | solution.py:582
  365.3 2.9 collective-permute-start.46
  365.9 9.2 %collective-permute-start.52 = (bf16[4,64,512]{2,1,0:T(8,128)(2,1)S(1)}, bf16[4,64,512]{2,1,0:T(8,128)(2,1)S(1)}, u32[]{:S(2)}, u32[]{:S(2)}) collective-permute-start(bf16[4,64,512]{2,1,0:T(8,128)(2,1)S(1)} %bitcast.97), channel_id=1, source_target_pairs={{0,4},{4,0},{8,12},{12,8},{16,20},{20,16},{24,28},{28,24},{1,5},{5... | collective-permute-start | bytes 786440 | tf_op jit(solution)/shard_map/ppermute | solution.py:582
  367.1 30.4 %collective-permute-start.50 = (bf16[4,128,1024]{2,1,0:T(8,128)(2,1)S(1)}, bf16[4,128,1024]{2,1,0:T(8,128)(2,1)S(1)}, u32[]{:S(2)}, u32[]{:S(2)}) collective-permute-start(bf16[4,128,1024]{2,1,0:T(8,128)(2,1)S(1)} %grad_by_rows.10), channel_id=1, source_target_pairs={{0,4},{4,0},{8,12},{12,8},{16,20},{20,16},{24,28},{28,24},{1,5},{5... | collective-permute-start | bytes 3145736 | tf_op jit(solution)/shard_map/ppermute | solution.py:582
  368.2 15.1 %collective-permute-start.54 = (bf16[1,512,256]{2,1,0:T(8,128)(2,1)S(1)}, bf16[1,512,256]{2,1,0:T(8,128)(2,1)S(1)}, u32[]{:S(2)}, u32[]{:S(2)}) collective-permute-start(bf16[1,512,256]{2,1,0:T(8,128)(2,1)S(1)} %add_convert_fusion.17), channel_id=1, source_target_pairs={{0,16},{4,20},{8,24},{12,28},{16,0},{20,4},{24,8},{28,12},{1,17},{... | collective-permute-start | bytes 786440 | tf_op jit(solution)/shard_map/ppermute | solution.py:582
  375.0 27.3 %collective-permute-start.49 = (f32[5120]{0:T(1024)S(1)}, f32[5120]{0:T(1024)S(1)}, u32[]{:S(2)}, u32[]{:S(2)}) collective-permute-start(f32[5120]{0:T(1024)S(1)} %fusion.57), channel_id=1, source_target_pairs={{0,4},{4,0},{8,12},{12,8},{16,20},{20,16},{24,28},{28,24},{1,5},{5... | collective-permute-start | bytes 61448 | tf_op jit(solution)/shard_map/ppermute | solution.py:582
  376.4 14.0 %collective-permute-start.53 = (bf16[2,64,512]{2,1,0:T(8,128)(2,1)S(1)}, bf16[2,64,512]{2,1,0:T(8,128)(2,1)S(1)}, u32[]{:S(2)}, u32[]{:S(2)}) collective-permute-start(bf16[2,64,512]{2,1,0:T(8,128)(2,1)S(1)} %fusion.47), channel_id=1, source_target_pairs={{0,8},{4,12},{8,0},{12,4},{16,24},{20,28},{24,16},{28,20},{1,9},{5... | collective-permute-start | bytes 393224 | tf_op jit(solution)/shard_map/ppermute | solution.py:582
  383.4 25.4 %collective-permute-start.57 = (bf16[4,64,1024]{2,1,0:T(8,128)(2,1)S(1)}, bf16[4,64,1024]{2,1,0:T(8,128)(2,1)S(1)}, u32[]{:S(2)}, u32[]{:S(2)}) collective-permute-start(bf16[4,64,1024]{2,1,0:T(8,128)(2,1)S(1)} %bitcast.96), channel_id=1, source_target_pairs={{0,4},{4,0},{8,12},{12,8},{16,20},{20,16},{24,28},{28,24},{1,5},{5... | collective-permute-start | bytes 1572872 | tf_op jit(solution)/shard_map/ppermute | solution.py:582
  397.7 22.4 %collective-permute-start.62 = (bf16[2,128,1024]{2,1,0:T(8,128)(2,1)S(1)}, bf16[2,128,1024]{2,1,0:T(8,128)(2,1)S(1)}, u32[]{:S(2)}, u32[]{:S(2)}) collective-permute-start(bf16[2,128,1024]{2,1,0:T(8,128)(2,1)S(1)} %add_convert_fusion.11), channel_id=1, source_target_pairs={{0,8},{4,12},{8,0},{12,4},{16,24},{20,28},{24,16},{28,20},{1,9},{5... | collective-permute-start | bytes 1572872 | tf_op jit(solution)/shard_map/ppermute | solution.py:582
  399.4 23.8 %collective-permute-start.61 = (bf16[1,64,512]{2,1,0:T(8,128)(2,1)S(1)}, bf16[1,64,512]{2,1,0:T(8,128)(2,1)S(1)}, u32[]{:S(2)}, u32[]{:S(2)}) collective-permute-start(bf16[1,64,512]{2,1,0:T(8,128)(2,1)S(1)} %fusion.49), channel_id=1, source_target_pairs={{0,16},{4,20},{8,24},{12,28},{16,0},{20,4},{24,8},{28,12},{1,17},{... | collective-permute-start | bytes 196616 | tf_op jit(solution)/shard_map/ppermute | solution.py:582
  400.9 23.0 %collective-permute-start.60 = (bf16[1,512,256]{2,1,0:T(8,128)(2,1)S(1)}, bf16[1,512,256]{2,1,0:T(8,128)(2,1)S(1)}, u32[]{:S(2)}, u32[]{:S(2)}) collective-permute-start(bf16[1,512,256]{2,1,0:T(8,128)(2,1)S(1)} %add_convert_fusion.16), channel_id=1, source_target_pairs={{0,16},{4,20},{8,24},{12,28},{16,0},{20,4},{24,8},{28,12},{1,17},{... | collective-permute-start | bytes 786440 | tf_op jit(solution)/shard_map/ppermute | solution.py:582
  402.4 17.7 %collective-permute-start.56 = (f32[5120]{0:T(1024)S(1)}, f32[5120]{0:T(1024)S(1)}, u32[]{:S(2)}, u32[]{:S(2)}) collective-permute-start(f32[5120]{0:T(1024)S(1)} %add.419), channel_id=1, source_target_pairs={{0,8},{4,12},{8,0},{12,4},{16,24},{20,28},{24,16},{28,20},{1,9},{5... | collective-permute-start | bytes 61448 | tf_op jit(solution)/shard_map/ppermute | solution.py:582
  408.9 18.4 %collective-permute-start.59 = (bf16[2,64,1024]{2,1,0:T(8,128)(2,1)S(1)}, bf16[2,64,1024]{2,1,0:T(8,128)(2,1)S(1)}, u32[]{:S(2)}, u32[]{:S(2)}) collective-permute-start(bf16[2,64,1024]{2,1,0:T(8,128)(2,1)S(1)} %fusion.40), channel_id=1, source_target_pairs={{0,8},{4,12},{8,0},{12,4},{16,24},{20,28},{24,16},{28,20},{1,9},{5... | collective-permute-start | bytes 786440 | tf_op jit(solution)/shard_map/ppermute | solution.py:582
  420.1 8.3 %collective-permute-start.58 = (f32[5120]{0:T(1024)S(1)}, f32[5120]{0:T(1024)S(1)}, u32[]{:S(2)}, u32[]{:S(2)}) collective-permute-start(f32[5120]{0:T(1024)S(1)} %add.421), channel_id=1, source_target_pairs={{0,16},{4,20},{8,24},{12,28},{16,0},{20,4},{24,8},{28,12},{1,17},{... | collective-permute-start | bytes 61448 | tf_op jit(solution)/shard_map/ppermute | solution.py:582
  420.3 18.5 %collective-permute-start.64 = (bf16[1,128,1024]{2,1,0:T(8,128)(2,1)S(1)}, bf16[1,128,1024]{2,1,0:T(8,128)(2,1)S(1)}, u32[]{:S(2)}, u32[]{:S(2)}) collective-permute-start(bf16[1,128,1024]{2,1,0:T(8,128)(2,1)S(1)} %add_convert_fusion.15), channel_id=1, source_target_pairs={{0,16},{4,20},{8,24},{12,28},{16,0},{20,4},{24,8},{28,12},{1,17},{... | collective-permute-start | bytes 786440 | tf_op jit(solution)/shard_map/ppermute | solution.py:582
  427.3 10.7 %collective-permute-start.63 = (bf16[1,64,1024]{2,1,0:T(8,128)(2,1)S(1)}, bf16[1,64,1024]{2,1,0:T(8,128)(2,1)S(1)}, u32[]{:S(2)}, u32[]{:S(2)}) collective-permute-start(bf16[1,64,1024]{2,1,0:T(8,128)(2,1)S(1)} %fusion.46), channel_id=1, source_target_pairs={{0,16},{4,20},{8,24},{12,28},{16,0},{20,4},{24,8},{28,12},{1,17},{... | collective-permute-start | bytes 393224 | tf_op jit(solution)/shard_map/ppermute | solution.py:582
  (64 other events, 401.0 us)
